TPU v7x, 32 devices: a whole 2x2x4 slice. The times are simulated.
32 devices in a mesh: group: 2 (over x), adapter: 16 (over z, y, core).
Axes of the slice: x: 2, y: 2, z: 4, core: 2. Of those that a mesh axis runs over, the one named last changes fastest.
Arguments:
- hidden: bfloat16 [768, 8192], P(('group', 'adapter')), parts along dimension 0, may hold values from -6 to 6
- norm_weight: float32 [8192], replicated, may hold values from 0.5 to 1.5
- query_weight: bfloat16 [8192, 8192], P(None, 'adapter'), may hold values from -0.0625 to 0.0625
- down_weights: bfloat16 [16, 8192, 64], P('adapter'), may hold values from -0.0625 to 0.0625
- up_weights: bfloat16 [16, 64, 8192], P(None, None, 'adapter'), may hold values from -0.75 to 0.75
- adapter_index: int32 [768, 1], P(('group', 'adapter')), parts along dimension 0, may hold values from 0 to 15; in each aligned block of 384 rows (0 to 383, 384 to 767, ...) at most 96 rows name the same one
- adapter_slot: int32 [16], replicated, may hold values from 0 to 15, each once
Outputs:
- query: bfloat16 [768, 8192], P(('group', 'adapter')), parts along dimension 0
There are 2 independent parts, one for each index of `group`. A program takes and returns all parts, laid end to end along the dimension named above; an argument that names none is the same for every part. Nothing has to cross between parts.
Inputs may be any that keep to these rules, and one draw needn't show every extreme that they name: `adapter_index`: no adapter is named by more than 96 token rows of a part, a bound that some block reaches. `adapter_slot`: each slot holds exactly one adapter.
All inputs are finite; a program needn't handle non-finite values.
Results may differ from a plain program's by a relative error of at most 0.0052.
Values may be sent and summed in bfloat16 or wider, within the bound.
No kernel may reach another device: no remote copies, remote signals or barrier semaphores. Data moves between devices by JAX's collectives and lax.ppermute only.
A program may use at most 128 MiB of HBM per device.

v0:
```python
import jax
import jax.numpy as jnp
from jax import lax
from jax.sharding import PartitionSpec as P

ADAPTER_SCALE = 0.5
EPS = 1e-05


def shards(
    hidden, norm_weight, query_weight, down_weights, up_weights, adapter_index, adapter_slot
):
    wide32 = hidden.astype(jnp.float32)
    inv_rms = lax.rsqrt(jnp.mean(wide32 * wide32, axis=1, keepdims=True) + EPS)
    normalized_input = (wide32 * inv_rms * norm_weight).astype(jnp.bfloat16)
    collected_rows = lax.all_gather(normalized_input, "adapter", axis=0, tiled=True)
    ids_all = lax.all_gather(adapter_index, "adapter", axis=0, tiled=True)
    holding_devices = lax.axis_size("adapter")
    owner = lax.axis_index("adapter")
    rank_columns = down_weights.shape[2]
    total_rows = collected_rows.shape[0]
    slot_ids = jnp.arange(holding_devices, dtype=jnp.int32)
    id_hits = (ids_all[:, 0][:, None] == slot_ids[None, :]).astype(jnp.int32)
    slot_tok = jnp.sum(id_hits * adapter_slot[None, :], axis=1)
    slot_hits = slot_tok[:, None] == slot_ids[None, :]
    owned_rows = slot_tok == owner
    partial_output = jnp.dot(collected_rows, down_weights[0], preferred_element_type=jnp.float32)
    rounded = jnp.where(owned_rows[:, None], partial_output, jnp.float32(0.0)).astype(jnp.bfloat16)
    rounded = lax.optimization_barrier(rounded)
    shrink_all = lax.psum(rounded.astype(jnp.float32), "adapter").astype(jnp.bfloat16)
    scatter_rows = jnp.where(
        slot_hits[:, :, None], shrink_all[:, None, :], jnp.zeros((), jnp.bfloat16)
    )
    scatter_rows = scatter_rows.reshape(total_rows, holding_devices * rank_columns)
    up_weight_table = up_weights.reshape(holding_devices * rank_columns, up_weights.shape[2])
    adapter_update = jnp.dot(scatter_rows, up_weight_table, preferred_element_type=jnp.float32)
    base_columns = jnp.dot(collected_rows, query_weight, preferred_element_type=jnp.float32)
    query_columns = (base_columns + ADAPTER_SCALE * adapter_update).astype(jnp.bfloat16)
    return lax.all_to_all(query_columns, "adapter", split_axis=0, concat_axis=1, tiled=True)


def solution(mesh):
    in_specs = (
        P(("group", "adapter"), None),
        P(),
        P(None, "adapter"),
        P("adapter", None, None),
        P(None, None, "adapter"),
        P(("group", "adapter"), None),
        P(),
    )
    out_specs = P(("group", "adapter"), None)
    return jax.shard_map(shards, mesh=mesh, in_specs=in_specs, out_specs=out_specs, check_vma=False)
```

profile of v0, /device:TPU:0, one launch (start us, length us, event | category | flops | bytes accessed | tf_op | source)
XLA Modules:
  0.0 171.4 jit_solution(854716376491338598)
XLA Ops:
  6.5 0.0 copy-start
  6.5 0.0 all-gather.2.cloned.1.call-start
  6.5 1.3 fusion.4
  7.8 1.9 %fusion.6 = bf16[24,8192]{1,0:T(8,128)(2,1)} fusion(bf16[24,8192]{1,0:T(8,128)(2,1)} %param.7, f32[8192]{0:T(1024)} %param.8, f32[24]{0:T(128)S(1)} %add_rsqrt_fusion), kind=kLoop, calls=%fused_computation.11 | loop fusion | flops 786432 | bytes 819296 | tf_op jit(solution)/shard_map/convert_element_type | solution.py:15
  9.7 0.0 all-gather.2.cloned.1.call-update
  9.8 1.2 dynamic-slice
  11.6 0.8 bitcast_dynamic-update-slice_fusion
  12.4 13.8 %all-reduce = s32[384]{0:T(512)S(1)} all-reduce(s32[384]{0:T(512)S(1)} %bitcast_dynamic-update-slice_fusion), channel_id=1, replica_groups=mesh['group'=2,'adapter'=16] {'adapter'}, use_global_device_ids=true, to_apply=%add | all-reduce | flops 384 | bytes 3072
  26.1 0.7 select_reduce_fusion
  26.9 47.6 %all-gather.2.cloned.1.call-done = bf16[384,8192]{1,0:T(8,128)(2,1)} async-done(((bf16[24,8192]{1,0:T(8,128)(2,1)}), bf16[384,8192]{1,0:T(8,128)(2,1)}) %all-gather.2.cloned.1.call-update) | async-done | bytes 6291472 | tf_op jit(solution)/shard_map/all_gather | solution.py:16
  74.5 5.1 %fusion.2 = bf16[384,64]{0,1:T(8,128)(2,1)S(1)} fusion(bf16[384,8192]{1,0:T(8,128)(2,1)} %all-gather.2.cloned.1.call-done, bf16[1,8192,64]{1,2,0:T(8,128)(2,1)} %param.10, pred[384]{0:T(512)(128)(4,1)S(1)} %broadcast_compare_fusion), kind=kOutput, calls=%fused_computation.5 | convolution fusion | flops 402702336 | bytes 7389568 | tf_op jit(solution)/shard_map/dot_general | solution.py:27
  79.5 60.2 %psum.7 = bf16[384,64]{0,1:T(8,128)(2,1)S(1)} all-reduce(bf16[384,64]{0,1:T(8,128)(2,1)S(1)} %fusion.2), channel_id=1, replica_groups=mesh['group'=2,'adapter'=16] {'adapter'}, use_global_device_ids=true, to_apply=%region_2.3 | all-reduce | flops 24576 | bytes 98304 | tf_op jit(solution)/shard_map/psum | solution.py:30
  139.7 0.0 copy-done
  139.7 0.6 fusion
  140.4 8.6 %fusion.1 = bf16[384,512]{1,0:T(8,128)(2,1)S(1)} fusion(f32[384,512]{1,0:T(8,128)S(1)} %fusion, bf16[384,8192]{1,0:T(8,128)(2,1)} %all-gather.2.cloned.1.call-done, bf16[8192,512]{1,0:T(8,128)(2,1)} %param.9), kind=kOutput, calls=%fused_computation.3 | convolution fusion | flops 3221618688 | bytes 15859712 | tf_op jit(solution)/shard_map/dot_general | solution.py:37
  149.0 14.8 %all_to_all.19 = bf16[16,24,512]{2,1,0:T(8,128)(2,1)S(1)} all-to-all(bf16[16,24,512]{2,1,0:T(8,128)(2,1)S(1)} %bitcast.19), channel_id=1, replica_groups=mesh['group'=2,'adapter'=16] {'adapter'}, dimensions={0} | all-to-all | bytes 786432 | tf_op jit(solution)/shard_map/all_to_all | solution.py:39
  163.8 0.8 copy.10
  (4 shorter events, 0.0 us)
Async XLA Ops:
  6.5 133.2 %copy-start = (bf16[16,64,512]{2,1,0:T(8,128)(2,1)S(1)}, bf16[16,64,512]{2,1,0:T(8,128)(2,1)}, u32[]{:S(2)}) copy-start(bf16[16,64,512]{2,1,0:T(8,128)(2,1)} %param.11) | copy-start | bytes 3145732
  6.5 67.9 %all-gather.2.cloned.1.call-start = ((), (), s32[]{:S(2)}) async-start(), calls=%async_computation.1 | async-start | bytes 6684672 | tf_op jit(solution)/shard_map/all_gather | solution.py:16
Sparse Core Ops, SparseCore 0:
  9.9 64.5 all-gather.1
where the time goes:
time: 172 us; the launch traced here: 171 us
  blocking collectives  88.8 us (52%)
  waiting for transfers between devices  47.6 us (28%)
  matrix products  14.3 us (8%)
  between operations  14 us (8%)
  other arithmetic  3.95 us (2%)
  local copies, waits for them, and re-layouts  2.78 us (2%)
    psum x1, blocking collectives, shards(): lax.psum(rounded.astype(jnp.float32), 'adapter').astype(jnp.bfloat16)  60.2 us
    all_gather x1, waiting for transfers between devices, shards(): lax.all_gather(normalized_input, 'adapter', axis=0, tiled=True)  47.6 us
    all_to_all x1, blocking collectives, shards(): lax.all_to_all(query_columns, 'adapter', split_axis=0, concat_axis=1, til...  14.8 us
    unnamed x1, blocking collectives  13.8 us
    dot_general x1, matrix products, shards(): jnp.dot(collected_rows, query_weight, preferred_element_type=jnp.float32)  8.6 us
    dot_general x1, matrix products, shards(): jnp.dot(collected_rows, down_weights[0], preferred_element_type=jnp.float32)  5.08 us
  transfers between devices with their start and end apart: 1, of which 1 were waited for; matrix products, arithmetic and copies ran while one was open for 2% of the time, Pallas kernels for 0%

commit v1 on v0

v1 whole, which is shorter than its diff:
```python
import jax
import jax.numpy as jnp
from jax import lax
from jax.sharding import PartitionSpec as P

ADAPTER_SCALE = 0.5
EPS = 1e-05

SIDE = 2
CORES = 2


def line_ring(places):
    odd = list(range(1, places, 2))
    even = list(range(0, places, 2))
    return [0] + odd + even[:0:-1]


def pairs(places, move):
    steps, flip_y, flip_core = move
    ring = line_ring(places)
    out = []
    for at, place in enumerate(ring):
        target = ring[(at + steps) % places]
        for y in range(SIDE):
            for core in range(CORES):
                source = (place * SIDE + y) * CORES + core
                out.append((source, (target * SIDE + (y ^ flip_y)) * CORES + (core ^ flip_core)))
    return out


def shards(
    hidden, norm_weight, query_weight, down_weights, up_weights, adapter_index, adapter_slot
):
    devices = lax.axis_size("adapter")
    me = lax.axis_index("adapter")
    places = devices // (SIDE * CORES)
    own_rows, width = hidden.shape
    columns = query_weight.shape[1]
    rank = down_weights.shape[2]
    ring = line_ring(places)

    wide32 = hidden.astype(jnp.float32)
    inv_rms = lax.rsqrt(jnp.mean(wide32 * wide32, axis=1, keepdims=True) + EPS)
    normed = (wide32 * inv_rms * norm_weight).astype(jnp.bfloat16)

    slots = jnp.arange(devices, dtype=jnp.int32)
    hits = (adapter_index[:, 0][:, None] == slots[None, :]).astype(jnp.int32)
    slot_own = jnp.sum(hits * adapter_slot[None, :], axis=1)
    slot_all = lax.all_gather(slot_own, "adapter", axis=0, tiled=True)

    def move(x, *how):
        return lax.ppermute(x, "adapter", pairs(places, how))

    place_of = jnp.asarray(ring, jnp.int32)
    turn_of = jnp.asarray([ring.index(p) for p in range(places)], jnp.int32)
    turn = turn_of[me // (SIDE * CORES)]
    corner = me % (SIDE * CORES)

    chain = normed
    slot_blocks = slot_all.reshape(devices, own_rows)
    bases, shrinks, origins = [], [], []
    for step in range(places):
        if step:
            chain = move(chain, 1, 0, 0)
        other_y = move(chain, 0, 1, 0)
        other_core = move(chain, 0, 0, 1)
        both = move(other_y, 0, 0, 1)
        rows = jnp.concatenate([chain, other_core, other_y, both], axis=0)
        place = place_of[(turn - step + places) % places]
        origin = place * (SIDE * CORES) + (corner ^ jnp.arange(SIDE * CORES, dtype=jnp.int32))
        slot_here = slot_blocks[origin].reshape(-1)
        part = jnp.dot(rows, down_weights[0], preferred_element_type=jnp.float32)
        shrinks.append(jnp.where((slot_here == me)[:, None], part, 0.0).astype(jnp.bfloat16))
        bases.append(jnp.dot(rows, query_weight, preferred_element_type=jnp.float32))
        origins.append(origin)
    origin_all = jnp.concatenate(origins)
    base = jnp.concatenate(bases, axis=0)
    base = jnp.zeros((devices, own_rows, columns), jnp.float32).at[origin_all].set(
        base.reshape(devices, own_rows, columns)
    )
    shrink = jnp.concatenate(shrinks, axis=0).reshape(devices, own_rows, rank)
    shrink = jnp.zeros((devices, own_rows, rank), jnp.bfloat16).at[origin_all].set(shrink)
    shrink_all = lax.all_gather(shrink.reshape(devices * own_rows, rank), "adapter", axis=0)
    shrink_all = jnp.sum(shrink_all, axis=0, dtype=jnp.float32).astype(jnp.bfloat16)
    slot_hits = slot_all[:, None] == slots[None, :]
    spread = jnp.where(
        slot_hits[:, :, None], shrink_all[:, None, :], jnp.zeros((), jnp.bfloat16)
    ).reshape(devices * own_rows, devices * rank)
    update = jnp.dot(
        spread,
        up_weights.reshape(devices * rank, columns),
        preferred_element_type=jnp.float32,
    )
    query = (base.reshape(devices * own_rows, columns) + ADAPTER_SCALE * update).astype(jnp.bfloat16)
    return lax.all_to_all(query, "adapter", split_axis=0, concat_axis=1, tiled=True)


def solution(mesh):
    in_specs = (
        P(("group", "adapter"), None),
        P(),
        P(None, "adapter"),
        P("adapter", None, None),
        P(None, None, "adapter"),
        P(("group", "adapter"), None),
        P(),
    )
    out_specs = P(("group", "adapter"), None)
    return jax.shard_map(shards, mesh=mesh, in_specs=in_specs, out_specs=out_specs, check_vma=False)
```

time: 172 us -> 115 us (0.67)
  blocking collectives: 88.8 us -> 49.3 us
  waiting for transfers between devices: 47.6 us -> 20.7 us
  starting transfers between devices: 0.01 us -> 11.5 us
  between operations: 14 us -> 6.26 us
  local copies, waits for them, and re-layouts: 2.78 us -> 10.5 us
    psum x1 -> x0, blocking collectives: 60.2 us -> none  [shards(): lax.psum(rounded.astype(jnp.float32), 'adapter').astype(jnp.bfloat16)]
    all_gather x1 -> x0, waiting for transfers between devices: 47.6 us -> none  [shards(): lax.all_gather(normalized_input, 'adapter', axis=0, tiled=True)]
    all_gather x0 -> x1, blocking collectives: none -> 24 us  [shards(): lax.all_gather(shrink.reshape(devices * own_rows, rank), 'adapter', axis=0)]
    ppermute x0 -> x15, waiting for transfers between devices: none -> 20.7 us  [move(): return lax.ppermute(x, 'adapter', pairs(places, how))]
    ppermute x0 -> x15, starting transfers between devices: none -> 11.5 us  [move(): return lax.ppermute(x, 'adapter', pairs(places, how))]
    unnamed x1, blocking collectives: 13.8 us -> 10.5 us
    dynamic_slice x0 -> x2, local copies, waits for them, and re-layouts: none -> 2.71 us  [the longest x1 1.47 us: shards(): place = place_of[(turn - step + places) % places]]
    gather x0 -> x4, local copies, waits for them, and re-layouts: none -> 2.24 us  [shards(): slot_here = slot_blocks[origin].reshape(-1)]
  transfers between devices with their start and end apart: 1 -> 15, of which waited for: 1 -> 4; matrix products, arithmetic and copies ran while one was open for 2% -> 16% of each run, Pallas kernels for 0% -> 0%
where the time goes in v1:
time: 115 us
  blocking collectives  49.3 us (43%)
  waiting for transfers between devices  20.7 us (18%)
  matrix products  13.2 us (11%)
  starting transfers between devices  11.5 us (10%)
  local copies, waits for them, and re-layouts  10.5 us (9%)
  between operations  6.26 us (5%)
  other arithmetic  3.63 us (3%)
    all_gather x1, blocking collectives, shards(): lax.all_gather(shrink.reshape(devices * own_rows, rank), 'adapter', axis=0)  24 us
    ppermute x15, waiting for transfers between devices, move(): return lax.ppermute(x, 'adapter', pairs(places, how))  20.7 us
    all_to_all x1, blocking collectives, shards(): lax.all_to_all(query, 'adapter', split_axis=0, concat_axis=1, tiled=True)  14.8 us
    ppermute x15, starting transfers between devices, move(): return lax.ppermute(x, 'adapter', pairs(places, how))  11.5 us
    unnamed x1, blocking collectives  10.5 us
    dot_general x4, matrix products, shards(): jnp.dot(rows, query_weight, preferred_element_type=jnp.float32)  9.78 us
    dot_general x4, matrix products, shards(): part = jnp.dot(rows, down_weights[0], preferred_element_type=jnp.float32)  2.81 us
  transfers between devices with their start and end apart: 15, of which 4 were waited for; matrix products, arithmetic and copies ran while one was open for 16% of the time, Pallas kernels for 0%

profile of v1, /device:TPU:0, one launch (start us, length us, event | category | flops | bytes accessed | tf_op | source)
XLA Modules:
  0.0 115.2 jit_solution(13656324299198447872)
XLA Ops:
  0.0 1.3 %fusion.11 = f32[24]{0:T(128)S(1)} fusion(bf16[24,8192]{1,0:T(8,128)(2,1)} %param.9), kind=kLoop, calls=%fused_computation.25 | loop fusion | flops 589800 | bytes 393312 | tf_op jit(solution)/shard_map/reduce_sum | solution.py:44
  1.3 1.2 %fusion.13 = bf16[24,8192]{1,0:T(8,128)(2,1)S(1)} fusion(bf16[24,8192]{1,0:T(8,128)(2,1)} %param.9, f32[8192]{0:T(1024)} %param.10, f32[24]{0:T(128)S(1)} %add_rsqrt_fusion), kind=kLoop, calls=%fused_computation.27 | loop fusion | flops 786432 | bytes 819296 | tf_op jit(solution)/shard_map/convert_element_type | solution.py:45
  2.5 3.1 %collective-permute-start.3 = (bf16[24,8192]{1,0:T(8,128)(2,1)S(1)}, bf16[24,8192]{1,0:T(8,128)(2,1)S(1)}, u32[]{:S(2)}, u32[]{:S(2)}) collective-permute-start(bf16[24,8192]{1,0:T(8,128)(2,1)S(1)} %fusion.13), channel_id=1, source_target_pairs={{0,4},{1,5},{2,6},{3,7},{4,12},{5,13},{6,14},{7,15},{12,8},{13,9},... | collective-permute-start | bytes 1179656 | tf_op jit(solution)/shard_map/ppermute | solution.py:53
  5.5 1.5 %collective-permute-start.1 = (bf16[24,8192]{1,0:T(8,128)(2,1)S(1)}, bf16[24,8192]{1,0:T(8,128)(2,1)S(1)}, u32[]{:S(2)}, u32[]{:S(2)}) collective-permute-start(bf16[24,8192]{1,0:T(8,128)(2,1)S(1)} %fusion.13), channel_id=1, source_target_pairs={{0,2},{1,3},{2,0},{3,1},{4,6},{5,7},{6,4},{7,5},{12,14},{13,15},{1... | collective-permute-start | bytes 1179656 | tf_op jit(solution)/shard_map/ppermute | solution.py:53
  7.1 1.2 %dynamic_slice.15 = s32[1]{0:T(128)} dynamic-slice(s32[4]{0:T(128)} %constant.90.clone, s32[]{:T(128)S(6)} %select_n.111), dynamic_slice_sizes={1} | dynamic-slice | bytes 12 | tf_op jit(solution)/shard_map/dynamic_slice | solution.py:57
  11.0 1.5 %fusion.27 = (s32[1]{0:T(128)}, s32[1]{0:T(128)}, s32[1]{0:T(128)}, s32[1]{0:T(128)}) fusion(s32[4]{0:T(128)} %constant.90.clone, s32[]{:T(128)S(6)} %select_n.113, s32[]{:T(128)S(6)} %select_n.116, s32[]{:T(128)S(6)} %select_n.120, s32[]{:T(128)S(6)} %select_n.118), kind=kLoop, calls=%fused_computation.78 | loop fusion | bytes 48 | tf_op jit(solution)/shard_map/dynamic_slice | solution.py:70
  15.1 1.3 %dynamic-slice = u32[1]{0:T(128)} dynamic-slice(u32[32]{0:T(128)} %constant.96, u32[]{:T(128)S(6)} %add.284), dynamic_slice_sizes={1} | dynamic-slice | bytes 12
  18.0 10.5 %all-reduce = s32[384]{0:T(512)S(1)} all-reduce(s32[384]{0:T(512)S(1)} %dynamic-update-slice), channel_id=1, replica_groups=mesh['group'=2,'adapter'=16] {'adapter'}, use_global_device_ids=true, to_apply=%add | all-reduce | flops 384 | bytes 3072
  31.8 1.3 %collective-permute-start.5 = (bf16[24,8192]{1,0:T(8,128)(2,1)S(1)}, bf16[24,8192]{1,0:T(8,128)(2,1)S(1)}, u32[]{:S(2)}, u32[]{:S(2)}) collective-permute-start(bf16[24,8192]{1,0:T(8,128)(2,1)S(1)} %collective-permute-done.3), channel_id=1, source_target_pairs={{0,2},{1,3},{2,0},{3,1},{4,6},{5,7},{6,4},{7,5},{12,14},{13,15},{1... | collective-permute-start | bytes 1179656 | tf_op jit(solution)/shard_map/ppermute | solution.py:53
  33.2 7.7 %collective-permute-done.7 = bf16[24,8192]{1,0:T(8,128)(2,1)S(1)} collective-permute-done((bf16[24,8192]{1,0:T(8,128)(2,1)S(1)}, bf16[24,8192]{1,0:T(8,128)(2,1)S(1)}, u32[]{:S(2)}, u32[]{:S(2)}) %collective-permute-start.7) | collective-permute-done | bytes 393248 | tf_op jit(solution)/shard_map/ppermute | solution.py:53
  41.0 1.5 %collective-permute-start.9 = (bf16[24,8192]{1,0:T(8,128)(2,1)S(1)}, bf16[24,8192]{1,0:T(8,128)(2,1)S(1)}, u32[]{:S(2)}, u32[]{:S(2)}) collective-permute-start(bf16[24,8192]{1,0:T(8,128)(2,1)S(1)} %collective-permute-done.7), channel_id=1, source_target_pairs={{0,2},{1,3},{2,0},{3,1},{4,6},{5,7},{6,4},{7,5},{12,14},{13,15},{1... | collective-permute-start | bytes 1179656 | tf_op jit(solution)/shard_map/ppermute | solution.py:53
  42.5 0.8 collective-permute-done.5
  43.5 2.1 %collective-permute-start.11 = (bf16[24,8192]{1,0:T(8,128)(2,1)S(1)}, bf16[24,8192]{1,0:T(8,128)(2,1)S(1)}, u32[]{:S(2)}, u32[]{:S(2)}) collective-permute-start(bf16[24,8192]{1,0:T(8,128)(2,1)S(1)} %collective-permute-done.7), channel_id=1, source_target_pairs={{0,4},{1,5},{2,6},{3,7},{4,12},{5,13},{6,14},{7,15},{12,8},{13,9},... | collective-permute-start | bytes 1179656 | tf_op jit(solution)/shard_map/ppermute | solution.py:53
  45.5 5.4 %fusion.18 = f32[96,512]{1,0:T(8,128)S(1)} fusion(bf16[8192,512]{1,0:T(8,128)(2,1)} %param.11, bf16[24,8192]{1,0:T(8,128)(2,1)S(1)} %collective-permute-done.2, bf16[24,8192]{1,0:T(8,128)(2,1)S(1)} %collective-permute-done.1, bf16[24,8192]{1,0:T(8,128)(2,1)S(1)} %collective-permute-done, bf16[24,8192]{1,0:T(8,128)(2,1)S(1)} %fusion.13), kind=kOutput, calls=%fused_computation.33 | convolution fusion | flops 811597824 | bytes 10158080 | tf_op jit(solution)/shard_map/dot_general | solution.py:75
  51.7 4.3 %collective-permute-done.11 = bf16[24,8192]{1,0:T(8,128)(2,1)S(1)} collective-permute-done((bf16[24,8192]{1,0:T(8,128)(2,1)S(1)}, bf16[24,8192]{1,0:T(8,128)(2,1)S(1)}, u32[]{:S(2)}, u32[]{:S(2)}) %collective-permute-start.11) | collective-permute-done | bytes 393248 | tf_op jit(solution)/shard_map/ppermute | solution.py:53
  56.1 1.2 %collective-permute-start.13 = (bf16[24,8192]{1,0:T(8,128)(2,1)S(1)}, bf16[24,8192]{1,0:T(8,128)(2,1)S(1)}, u32[]{:S(2)}, u32[]{:S(2)}) collective-permute-start(bf16[24,8192]{1,0:T(8,128)(2,1)S(1)} %collective-permute-done.11), channel_id=1, source_target_pairs={{0,2},{1,3},{2,0},{3,1},{4,6},{5,7},{6,4},{7,5},{12,14},{13,15},{1... | collective-permute-start | bytes 1179656 | tf_op jit(solution)/shard_map/ppermute | solution.py:53
  57.5 1.4 %fusion.28 = f32[96,512]{1,0:T(8,128)S(1)} fusion(bf16[96,8192]{1,0:T(8,128)(2,1)S(1)} %constant_dynamic-update-slice_fusion, bf16[8192,512]{1,0:T(8,128)(2,1)S(1)} %bitcast.65), kind=kOutput, calls=%fused_computation.79 | convolution fusion | flops 805306368 | bytes 10158080 | tf_op jit(solution)/shard_map/dot_general | solution.py:75
  59.8 7.9 %collective-permute-done.13 = bf16[24,8192]{1,0:T(8,128)(2,1)S(1)} collective-permute-done((bf16[24,8192]{1,0:T(8,128)(2,1)S(1)}, bf16[24,8192]{1,0:T(8,128)(2,1)S(1)}, u32[]{:S(2)}, u32[]{:S(2)}) %collective-permute-start.13) | collective-permute-done | bytes 393248 | tf_op jit(solution)/shard_map/ppermute | solution.py:53
  67.8 1.4 %fusion.29 = f32[96,512]{1,0:T(8,128)S(1)} fusion(bf16[96,8192]{1,0:T(8,128)(2,1)S(1)} %constant_dynamic-update-slice_fusion.4, bf16[8192,512]{1,0:T(8,128)(2,1)S(1)} %bitcast.65), kind=kOutput, calls=%fused_computation.80 | convolution fusion | flops 805306368 | bytes 10158080 | tf_op jit(solution)/shard_map/dot_general | solution.py:75
  70.0 1.4 %fusion.30 = f32[96,512]{1,0:T(8,128)S(1)} fusion(bf16[96,8192]{1,0:T(8,128)(2,1)S(1)} %constant_dynamic-update-slice_fusion.8, bf16[8192,512]{1,0:T(8,128)(2,1)S(1)} %bitcast.65), kind=kOutput, calls=%fused_computation.81 | convolution fusion | flops 805306368 | bytes 10158080 | tf_op jit(solution)/shard_map/dot_general | solution.py:75
  72.4 1.0 scatter_fusion.1
  73.6 24.0 %all_gather.7 = bf16[16,384,64]{1,2,0:T(8,128)(2,1)S(1)} all-gather(bf16[1,384,64]{1,2,0:T(8,128)(2,1)S(1)} %copy.19), channel_id=1, replica_groups=mesh['group'=2,'adapter'=16] {'adapter'}, dimensions={0}, use_global_device_ids=true | all-gather | bytes 835584 | tf_op jit(solution)/shard_map/all_gather | solution.py:84
  97.8 1.1 scatter_fusion
  99.6 14.8 %all_to_all.19 = bf16[16,24,512]{2,1,0:T(8,128)(2,1)S(1)} all-to-all(bf16[16,24,512]{2,1,0:T(8,128)(2,1)S(1)} %bitcast.70), channel_id=1, replica_groups=mesh['group'=2,'adapter'=16] {'adapter'}, dimensions={0} | all-to-all | bytes 786432 | tf_op jit(solution)/shard_map/all_to_all | solution.py:96
  (81 shorter events, 10.0 us)
Async XLA Ops:
  0.0 99.0 %copy-start = (bf16[16,64,512]{2,1,0:T(8,128)(2,1)S(1)}, bf16[16,64,512]{2,1,0:T(8,128)(2,1)}, u32[]{:S(2)}) copy-start(bf16[16,64,512]{2,1,0:T(8,128)(2,1)} %param.13) | copy-start | bytes 3145732
  2.5 28.8 %collective-permute-start.3 = (bf16[24,8192]{1,0:T(8,128)(2,1)S(1)}, bf16[24,8192]{1,0:T(8,128)(2,1)S(1)}, u32[]{:S(2)}, u32[]{:S(2)}) collective-permute-start(bf16[24,8192]{1,0:T(8,128)(2,1)S(1)} %fusion.13), channel_id=1, source_target_pairs={{0,4},{1,5},{2,6},{3,7},{4,12},{5,13},{6,14},{7,15},{12,8},{13,9},... | collective-permute-start | bytes 1179656 | tf_op jit(solution)/shard_map/ppermute | solution.py:53
  5.5 27.5 %collective-permute-start.1 = (bf16[24,8192]{1,0:T(8,128)(2,1)S(1)}, bf16[24,8192]{1,0:T(8,128)(2,1)S(1)}, u32[]{:S(2)}, u32[]{:S(2)}) collective-permute-start(bf16[24,8192]{1,0:T(8,128)(2,1)S(1)} %fusion.13), channel_id=1, source_target_pairs={{0,2},{1,3},{2,0},{3,1},{4,6},{5,7},{6,4},{7,5},{12,14},{13,15},{1... | collective-permute-start | bytes 1179656 | tf_op jit(solution)/shard_map/ppermute | solution.py:53
  7.0 36.4 %collective-permute-start = (bf16[24,8192]{1,0:T(8,128)(2,1)S(1)}, bf16[24,8192]{1,0:T(8,128)(2,1)S(1)}, u32[]{:S(2)}, u32[]{:S(2)}) collective-permute-start(bf16[24,8192]{1,0:T(8,128)(2,1)S(1)} %fusion.13), channel_id=1, source_target_pairs={{0,1},{1,0},{2,3},{3,2},{4,5},{5,4},{6,7},{7,6},{12,13},{13,12},{1... | collective-permute-start | bytes 1179656 | tf_op jit(solution)/shard_map/ppermute | solution.py:53
  31.3 9.6 %collective-permute-start.7 = (bf16[24,8192]{1,0:T(8,128)(2,1)S(1)}, bf16[24,8192]{1,0:T(8,128)(2,1)S(1)}, u32[]{:S(2)}, u32[]{:S(2)}) collective-permute-start(bf16[24,8192]{1,0:T(8,128)(2,1)S(1)} %collective-permute-done.3), channel_id=1, source_target_pairs={{0,4},{1,5},{2,6},{3,7},{4,12},{5,13},{6,14},{7,15},{12,8},{13,9},... | collective-permute-start | bytes 1179656 | tf_op jit(solution)/shard_map/ppermute | solution.py:53
  31.7 9.3 %collective-permute-start.4 = (bf16[24,8192]{1,0:T(8,128)(2,1)S(1)}, bf16[24,8192]{1,0:T(8,128)(2,1)S(1)}, u32[]{:S(2)}, u32[]{:S(2)}) collective-permute-start(bf16[24,8192]{1,0:T(8,128)(2,1)S(1)} %collective-permute-done.3), channel_id=1, source_target_pairs={{0,1},{1,0},{2,3},{3,2},{4,5},{5,4},{6,7},{7,6},{12,13},{13,12},{1... | collective-permute-start | bytes 1179656 | tf_op jit(solution)/shard_map/ppermute | solution.py:53
  31.8 11.5 %collective-permute-start.5 = (bf16[24,8192]{1,0:T(8,128)(2,1)S(1)}, bf16[24,8192]{1,0:T(8,128)(2,1)S(1)}, u32[]{:S(2)}, u32[]{:S(2)}) collective-permute-start(bf16[24,8192]{1,0:T(8,128)(2,1)S(1)} %collective-permute-done.3), channel_id=1, source_target_pairs={{0,2},{1,3},{2,0},{3,1},{4,6},{5,7},{6,4},{7,5},{12,14},{13,15},{1... | collective-permute-start | bytes 1179656 | tf_op jit(solution)/shard_map/ppermute | solution.py:53
  33.1 12.5 %collective-permute-start.2 = (bf16[24,8192]{1,0:T(8,128)(2,1)S(1)}, bf16[24,8192]{1,0:T(8,128)(2,1)S(1)}, u32[]{:S(2)}, u32[]{:S(2)}) collective-permute-start(bf16[24,8192]{1,0:T(8,128)(2,1)S(1)} %collective-permute-done.1), channel_id=1, source_target_pairs={{0,1},{1,0},{2,3},{3,2},{4,5},{5,4},{6,7},{7,6},{12,13},{13,12},{1... | collective-permute-start | bytes 1179656 | tf_op jit(solution)/shard_map/ppermute | solution.py:53
  40.9 18.1 %collective-permute-start.8 = (bf16[24,8192]{1,0:T(8,128)(2,1)S(1)}, bf16[24,8192]{1,0:T(8,128)(2,1)S(1)}, u32[]{:S(2)}, u32[]{:S(2)}) collective-permute-start(bf16[24,8192]{1,0:T(8,128)(2,1)S(1)} %collective-permute-done.7), channel_id=1, source_target_pairs={{0,1},{1,0},{2,3},{3,2},{4,5},{5,4},{6,7},{7,6},{12,13},{13,12},{1... | collective-permute-start | bytes 1179656 | tf_op jit(solution)/shard_map/ppermute | solution.py:53
  41.0 16.3 %collective-permute-start.9 = (bf16[24,8192]{1,0:T(8,128)(2,1)S(1)}, bf16[24,8192]{1,0:T(8,128)(2,1)S(1)}, u32[]{:S(2)}, u32[]{:S(2)}) collective-permute-start(bf16[24,8192]{1,0:T(8,128)(2,1)S(1)} %collective-permute-done.7), channel_id=1, source_target_pairs={{0,2},{1,3},{2,0},{3,1},{4,6},{5,7},{6,4},{7,5},{12,14},{13,15},{1... | collective-permute-start | bytes 1179656 | tf_op jit(solution)/shard_map/ppermute | solution.py:53
  43.3 14.1 %collective-permute-start.6 = (bf16[24,8192]{1,0:T(8,128)(2,1)S(1)}, bf16[24,8192]{1,0:T(8,128)(2,1)S(1)}, u32[]{:S(2)}, u32[]{:S(2)}) collective-permute-start(bf16[24,8192]{1,0:T(8,128)(2,1)S(1)} %collective-permute-done.5), channel_id=1, source_target_pairs={{0,1},{1,0},{2,3},{3,2},{4,5},{5,4},{6,7},{7,6},{12,13},{13,12},{1... | collective-permute-start | bytes 1179656 | tf_op jit(solution)/shard_map/ppermute | solution.py:53
  43.4 14.1 %slice-start = ((s8[8388608]{0:T(1024)(128)(4,1)}), s8[4194304]{0:T(1024)(128)(4,1)S(1)}, s32[]{:S(2)}) async-start(s8[8388608]{0:T(1024)(128)(4,1)} %bitcast.64), calls=%async_computation.1 | async-start | bytes 8388608
  43.4 7.6 %copy-start.1 = (bf16[1,8192,64]{1,2,0:T(8,128)(2,1)S(1)}, bf16[1,8192,64]{1,2,0:T(8,128)(2,1)}, u32[]{:S(2)}) copy-start(bf16[1,8192,64]{1,2,0:T(8,128)(2,1)} %param.12) | copy-start | bytes 3145732
  43.4 14.1 %slice-start.1 = ((s8[8388608]{0:T(1024)(128)(4,1)}), s8[4194304]{0:T(1024)(128)(4,1)S(1)}, s32[]{:S(2)}) async-start(s8[8388608]{0:T(1024)(128)(4,1)} %bitcast.64), calls=%async_computation.2 | async-start | bytes 8388608
  43.5 12.6 %collective-permute-start.11 = (bf16[24,8192]{1,0:T(8,128)(2,1)S(1)}, bf16[24,8192]{1,0:T(8,128)(2,1)S(1)}, u32[]{:S(2)}, u32[]{:S(2)}) collective-permute-start(bf16[24,8192]{1,0:T(8,128)(2,1)S(1)} %collective-permute-done.7), channel_id=1, source_target_pairs={{0,4},{1,5},{2,6},{3,7},{4,12},{5,13},{6,14},{7,15},{12,8},{13,9},... | collective-permute-start | bytes 1179656 | tf_op jit(solution)/shard_map/ppermute | solution.py:53
  56.1 11.6 %collective-permute-start.12 = (bf16[24,8192]{1,0:T(8,128)(2,1)S(1)}, bf16[24,8192]{1,0:T(8,128)(2,1)S(1)}, u32[]{:S(2)}, u32[]{:S(2)}) collective-permute-start(bf16[24,8192]{1,0:T(8,128)(2,1)S(1)} %collective-permute-done.11), channel_id=1, source_target_pairs={{0,1},{1,0},{2,3},{3,2},{4,5},{5,4},{6,7},{7,6},{12,13},{13,12},{1... | collective-permute-start | bytes 1179656 | tf_op jit(solution)/shard_map/ppermute | solution.py:53
  56.1 11.5 %collective-permute-start.13 = (bf16[24,8192]{1,0:T(8,128)(2,1)S(1)}, bf16[24,8192]{1,0:T(8,128)(2,1)S(1)}, u32[]{:S(2)}, u32[]{:S(2)}) collective-permute-start(bf16[24,8192]{1,0:T(8,128)(2,1)S(1)} %collective-permute-done.11), channel_id=1, source_target_pairs={{0,2},{1,3},{2,0},{3,1},{4,6},{5,7},{6,4},{7,5},{12,14},{13,15},{1... | collective-permute-start | bytes 1179656 | tf_op jit(solution)/shard_map/ppermute | solution.py:53
  57.3 10.4 %collective-permute-start.10 = (bf16[24,8192]{1,0:T(8,128)(2,1)S(1)}, bf16[24,8192]{1,0:T(8,128)(2,1)S(1)}, u32[]{:S(2)}, u32[]{:S(2)}) collective-permute-start(bf16[24,8192]{1,0:T(8,128)(2,1)S(1)} %collective-permute-done.9), channel_id=1, source_target_pairs={{0,1},{1,0},{2,3},{3,2},{4,5},{5,4},{6,7},{7,6},{12,13},{13,12},{1... | collective-permute-start | bytes 1179656 | tf_op jit(solution)/shard_map/ppermute | solution.py:53
  67.7 2.3 %collective-permute-start.14 = (bf16[24,8192]{1,0:T(8,128)(2,1)S(1)}, bf16[24,8192]{1,0:T(8,128)(2,1)S(1)}, u32[]{:S(2)}, u32[]{:S(2)}) collective-permute-start(bf16[24,8192]{1,0:T(8,128)(2,1)S(1)} %collective-permute-done.13), channel_id=1, source_target_pairs={{0,1},{1,0},{2,3},{3,2},{4,5},{5,4},{6,7},{7,6},{12,13},{13,12},{1... | collective-permute-start | bytes 1179656 | tf_op jit(solution)/shard_map/ppermute | solution.py:53

commit v2 on v0

v2 whole, which is shorter than its diff:
```python
import jax
import jax.numpy as jnp
from jax import lax
from jax.experimental import pallas as pl
from jax.experimental.pallas import tpu as pltpu
from jax.sharding import PartitionSpec as P

ADAPTER_SCALE = 0.5
EPS = 1e-05

SIDE = 2
CORES = 2
CORNERS = SIDE * CORES
LANES = 128
CHUNK = 1024


def line_ring(places):
    odd = list(range(1, places, 2))
    even = list(range(0, places, 2))
    return [0] + odd + even[:0:-1]


def pairs(places, steps, flip):
    ring = line_ring(places)
    out = []
    for at, place in enumerate(ring):
        target = ring[(at + steps) % places]
        for corner in range(CORNERS):
            out.append((place * CORNERS + corner, target * CORNERS + (corner ^ flip)))
    return out


def ring_device(places, steps, flip):
    me = lax.axis_index("adapter")
    ring = line_ring(places)
    place, corner = me // CORNERS, me % CORNERS
    target = jnp.int32(0)
    for at, name in enumerate(ring):
        target = jnp.where(place == name, jnp.int32(ring[(at + steps) % places]), target)
    return target * CORNERS + (corner ^ flip)


def norm_kernel(hidden_ref, gain_ref, index_ref, slot_ref, keep_ref, give_ref, slots_ref):
    rows, width = hidden_ref.shape
    half = width // CORES
    core = lax.axis_index("adapter") % CORES
    squares = jnp.zeros((rows, LANES), jnp.float32)
    for start in range(0, width, CHUNK):
        wide = hidden_ref[:, start : start + CHUNK].astype(jnp.float32)
        wide = wide * wide
        for lane in range(0, CHUNK, LANES):
            squares = squares + wide[:, lane : lane + LANES]
    inv_rms = lax.rsqrt(jnp.sum(squares, axis=1, keepdims=True) / width + EPS)
    for which, out_ref in ((core, keep_ref), (1 - core, give_ref)):
        for start in range(0, half, CHUNK):
            at = pl.multiple_of(which * half + start, CHUNK)
            wide = hidden_ref[:, pl.ds(at, CHUNK)].astype(jnp.float32)
            gain = gain_ref[:, pl.ds(at, CHUNK)]
            out_ref[:, start : start + CHUNK] = (wide * inv_rms * gain).astype(jnp.bfloat16)
    index = index_ref[...]
    slot = jnp.zeros(index.shape, jnp.float32)
    for name in range(slot_ref.shape[0]):
        slot = jnp.where(index == name, slot_ref[name].astype(jnp.float32), slot)
    slots_ref[...] = jnp.zeros(slots_ref.shape, jnp.float32)
    slots_ref[0:1, 0:rows] = slot


def normalize(hidden, norm_weight, adapter_index, adapter_slot):
    rows, width = hidden.shape
    vmem = pl.BlockSpec(memory_space=pltpu.VMEM)
    return pl.pallas_call(
        norm_kernel,
        out_shape=(
            jax.ShapeDtypeStruct((rows, width // CORES), jnp.bfloat16),
            jax.ShapeDtypeStruct((rows, width // CORES), jnp.bfloat16),
            jax.ShapeDtypeStruct((8, LANES), jnp.float32),
        ),
        in_specs=[vmem, vmem, vmem, pl.BlockSpec(memory_space=pltpu.SMEM)],
        out_specs=(vmem, vmem, vmem),
    )(hidden, norm_weight.reshape(1, width), adapter_index.reshape(1, rows), adapter_slot)


def order_kernel(places, rows, slots_ref, out_ref):
    across = lax.broadcasted_iota(jnp.int32, (rows, LANES), 1)
    down = lax.broadcasted_iota(jnp.int32, (rows, LANES), 0)
    for step in range(places):
        for corner in range(CORNERS):
            origin = ring_device(places, -step, corner)
            row = slots_ref[origin, 0:1, :]
            column = jnp.sum(jnp.where(across == down, row, 0.0), axis=1, keepdims=True)
            out_ref[step, corner] = jnp.broadcast_to(column, (rows, LANES))


def order_slots(slots, places, rows):
    vmem = pl.BlockSpec(memory_space=pltpu.VMEM)
    return pl.pallas_call(
        lambda slots_ref, out_ref: order_kernel(places, rows, slots_ref, out_ref),
        out_shape=jax.ShapeDtypeStruct((places, CORNERS, rows, LANES), jnp.float32),
        in_specs=[vmem],
        out_specs=vmem,
    )(slots)


def assemble_kernel(places, columns, *refs):
    parts, out_ref, sems = refs[:-2], refs[-2], refs[-1]
    copies = []
    for step in range(places):
        for corner in range(CORNERS):
            which = step * CORNERS + corner
            at = pl.multiple_of(ring_device(places, step, corner) * columns, columns)
            copies.append(
                pltpu.make_async_copy(parts[which], out_ref.at[:, pl.ds(at, columns)], sems.at[which])
            )
    for copy in copies:
        copy.start()
    for copy in copies:
        copy.wait()


def assemble(parts, places):
    rows, columns = parts[0].shape
    anywhere = pl.BlockSpec(memory_space=pl.ANY)
    return pl.pallas_call(
        lambda *refs: assemble_kernel(places, columns, *refs),
        out_shape=jax.ShapeDtypeStruct((rows, columns * len(parts)), jnp.bfloat16),
        in_specs=[anywhere] * len(parts),
        out_specs=anywhere,
        scratch_shapes=[pltpu.SemaphoreType.DMA((len(parts),))],
    )(*parts)


def shards(
    hidden, norm_weight, query_weight, down_weights, up_weights, adapter_index, adapter_slot
):
    devices = lax.axis_size("adapter")
    me = lax.axis_index("adapter")
    core = me % CORES
    places = devices // CORNERS
    own_rows, width = hidden.shape
    half = width // CORES
    columns = query_weight.shape[1]
    rank = down_weights.shape[2]
    step_rows = CORNERS * own_rows

    def move(x, steps, flip):
        return lax.ppermute(x, "adapter", pairs(places, steps, flip))

    def matmul(x, y):
        return jnp.dot(x, y, preferred_element_type=jnp.float32)

    keep, give, slots_own = normalize(hidden, norm_weight, adapter_index, adapter_slot)
    slots_all = lax.all_gather(slots_own, "adapter", axis=0)

    first = [keep]
    second = [move(give, 0, 1)]
    first_y = [move(keep, 0, 2)]
    second_y = [move(second[0], 0, 2)]
    for step in range(1, places):
        first.append(move(first[-1], 1, 0))
        second.append(move(second[-1], 1, 0))
        first_y.append(move(first[-1], 0, 2))
        if step < places - 1:
            second_y.append(move(second[-1], 0, 2))
        else:
            second_y.append(move(second_y[-1], 1, 0))

    w_keep = lax.dynamic_slice_in_dim(query_weight, core * half, half, 0)
    w_got = move(lax.dynamic_slice_in_dim(query_weight, (1 - core) * half, half, 0), 0, 1)
    down = down_weights[0]
    d_keep = lax.dynamic_slice_in_dim(down, core * half, half, 0)
    d_got = move(lax.dynamic_slice_in_dim(down, (1 - core) * half, half, 0), 0, 1)
    d_both = jnp.concatenate([d_keep, d_got], axis=1)

    slots = order_slots(slots_all, places, own_rows).reshape(places, step_rows, LANES)
    holder = jnp.where(jnp.arange(2 * rank) < rank, me, me ^ 1).astype(jnp.float32)

    bases, travelling = [], None
    for step in range(places):
        a, b, c, d = first[step], second[step], first_y[step], second_y[step]
        mine = jnp.concatenate([a, b, c, d], axis=0)
        theirs = jnp.concatenate([b, a, d, c], axis=0)
        part = matmul(mine, d_both)
        part = jnp.where(slots[step][:, :1] == holder[None, :], part, 0.0)
        part = part[:, :rank] + part[:, rank:]
        travelling = part if travelling is None else part + move(travelling, 1, 0)
        bases.append(matmul(mine, w_keep) + move(matmul(theirs, w_got), 0, 1))

    def flipped(x, flip):
        blocks = x.reshape(CORNERS, own_rows, rank)
        return jnp.stack([blocks[k ^ flip] for k in range(CORNERS)]).reshape(step_rows, rank)

    shrink = (travelling + flipped(move(travelling, 0, 1), 1)).astype(jnp.bfloat16)
    shrink = shrink + flipped(move(shrink, 0, 2), 2)

    up = up_weights.reshape(devices * rank, columns)
    names = jnp.arange(devices, dtype=jnp.float32)
    parts = []
    for step in range(places):
        mine = shrink if step == places - 1 else move(shrink, step + 1, 0)
        hits = slots[step][:, :1] == names[None, :]
        spread = jnp.where(hits[:, :, None], mine[:, None, :], jnp.zeros((), jnp.bfloat16))
        update = matmul(spread.reshape(step_rows, devices * rank), up)
        query = (bases[step] + ADAPTER_SCALE * update).astype(jnp.bfloat16)
        for corner in range(CORNERS):
            piece = query[corner * own_rows : (corner + 1) * own_rows]
            parts.append(move(piece, -step, corner) if step or corner else piece)
    return assemble(parts, places)


def solution(mesh):
    in_specs = (
        P(("group", "adapter"), None),
        P(),
        P(None, "adapter"),
        P("adapter", None, None),
        P(None, None, "adapter"),
        P(("group", "adapter"), None),
        P(),
    )
    out_specs = P(("group", "adapter"), None)
    return jax.shard_map(shards, mesh=mesh, in_specs=in_specs, out_specs=out_specs, check_vma=False)
```

time: 172 us -> 157 us (0.913)
  blocking collectives: 88.8 us -> 21.2 us
  starting transfers between devices: 0.01 us -> 39.8 us
  Pallas kernels: 0 us -> 16.9 us
  between operations: 14 us -> 1 us
  local copies, waits for them, and re-layouts: 2.78 us -> 13.5 us
  matrix products: 14.3 us -> 24 us
  waiting for transfers between devices: 47.6 us -> 39.3 us
  other arithmetic: 3.95 us -> 0.42 us
    psum x1 -> x0, blocking collectives: 60.2 us -> none  [shards(): lax.psum(rounded.astype(jnp.float32), 'adapter').astype(jnp.bfloat16)]
    all_gather x1 -> x0, waiting for transfers between devices: 47.6 us -> none  [shards(): lax.all_gather(normalized_input, 'adapter', axis=0, tiled=True)]
    ppermute x0 -> x44, starting transfers between devices: none -> 39.8 us  [move(): return lax.ppermute(x, 'adapter', pairs(places, steps, flip))]
    ppermute x0 -> x44, waiting for transfers between devices: none -> 39.3 us  [move(): return lax.ppermute(x, 'adapter', pairs(places, steps, flip))]
    all_gather x0 -> x1, blocking collectives: none -> 21.2 us  [shards(): slots_all = lax.all_gather(slots_own, 'adapter', axis=0)]
    pallas_call x0 -> x3, Pallas kernels: none -> 16.9 us  [the longest x1 13.2 us: assemble(): pl.pallas_call(lambda *refs: assemble_kernel(places, columns, *refs), out...]
    all_to_all x1 -> x0, blocking collectives: 14.8 us -> none  [shards(): lax.all_to_all(query_columns, 'adapter', split_axis=0, concat_axis=1, til...]
    unnamed x1 -> x0, blocking collectives: 13.8 us -> none
  transfers between devices with their start and end apart: 1 -> 44, of which waited for: 1 -> 14; matrix products, arithmetic and copies ran while one was open for 2% -> 21% of each run, Pallas kernels for 0% -> 1%
where the time goes in v2:
time: 157 us; the launch traced here: 156 us
  starting transfers between devices  39.8 us (25%)
  waiting for transfers between devices  39.3 us (25%)
  matrix products  24 us (15%)
  blocking collectives  21.2 us (14%)
  Pallas kernels  16.9 us (11%)
  local copies, waits for them, and re-layouts  13.5 us (9%)
    ppermute x44, starting transfers between devices, move(): return lax.ppermute(x, 'adapter', pairs(places, steps, flip))  39.8 us
    ppermute x44, waiting for transfers between devices, move(): return lax.ppermute(x, 'adapter', pairs(places, steps, flip))  39.3 us
    dot_general x16, matrix products, matmul(): return jnp.dot(x, y, preferred_element_type=jnp.float32)  24 us
    all_gather x1, blocking collectives, shards(): slots_all = lax.all_gather(slots_own, 'adapter', axis=0)  21.2 us
    pallas_call x1, Pallas kernels, assemble(): pl.pallas_call(lambda *refs: assemble_kernel(places, columns, *refs), out...  13.2 us
    unnamed x120, local copies, waits for them, and re-layouts  4.76 us
    dynamic_slice x1, local copies, waits for them, and re-layouts, shards(): lax.dynamic_slice_in_dim(query_weight, (1 - core) * half, half, 0)  4.55 us
  transfers between devices with their start and end apart: 44, of which 14 were waited for; matrix products, arithmetic and copies ran while one was open for 21% of the time, Pallas kernels for 1%

profile of v2, /device:TPU:0, one launch (start us, length us, event | category | flops | bytes accessed | tf_op | source)
XLA Modules:
  0.0 156.0 jit_solution(4290267433830517011)
XLA Ops:
  0.0 2.1 %shard_map.73 = (bf16[24,4096]{1,0:T(8,128)(2,1)}, bf16[24,4096]{1,0:T(8,128)(2,1)}, f32[8,128]{1,0:T(8,128)}) custom-call(bf16[24,8192]{1,0:T(8,128)(2,1)} %hidden_ref.1, f32[1,8192]{1,0:T(1,128)} %bitcast.80, s32[1,24]{1,0:T(1,128)} %bitcast.89, s32[16]{0:T(128)} %slot_ref.1), custom_call_target="tpu_custom_call" | custom-call | tf_op jit(solution)/shard_map/pallas_call | solution.py:72
  2.1 3.0 %collective-permute-start.5 = (bf16[24,4096]{1,0:T(8,128)(2,1)}, bf16[24,4096]{1,0:T(8,128)(2,1)}, u32[]{:S(2)}, u32[]{:S(2)}) collective-permute-start(bf16[24,4096]{1,0:T(8,128)(2,1)} %get-tuple-element.8), channel_id=1, source_target_pairs={{0,4},{1,5},{2,6},{3,7},{4,12},{5,13},{6,14},{7,15},{12,8},{13,9},... | collective-permute-start | bytes 589832 | tf_op jit(solution)/shard_map/ppermute | solution.py:147
  6.6 2.3 %dynamic-slice_bitcast_fusion.1 = (bf16[4096,64]{0,1:T(8,128)(2,1)}, bf16[4096,64]{0,1:T(8,128)(2,1)}) fusion(bf16[1,8192,64]{1,2,0:T(8,128)(2,1)} %param.10, s32[]{:T(128)S(6)} %select_n.50, s32[]{:T(128)S(6)} %select_n.51), kind=kLoop, calls=%fused_computation.66 | loop fusion | bytes 2097160 | tf_op jit(solution)/shard_map/dynamic_slice | solution.py:171
  9.5 4.5 %constant_dynamic-slice_fusion = bf16[4096,512]{1,0:T(8,128)(2,1)} fusion(bf16[8192,512]{1,0:T(8,128)(2,1)} %param.9, s32[]{:T(128)S(6)} %select_n.51), kind=kLoop, calls=%fused_computation.127 | loop fusion | bytes 8388612 | tf_op jit(solution)/shard_map/dynamic_slice | solution.py:169
  14.2 21.2 %all-gather = f32[128,128]{1,0:T(8,128)} all-gather(f32[8,128]{1,0:T(8,128)S(1)} %copy-done.48), channel_id=2, replica_groups=mesh['group'=2,'adapter'=16] {'adapter'}, dimensions={0}, use_global_device_ids=true | all-gather | bytes 69632 | tf_op jit(solution)/shard_map/all_gather | solution.py:153
  41.2 5.9 %collective-permute-done.6 = bf16[24,4096]{1,0:T(8,128)(2,1)S(1)} collective-permute-done((bf16[24,4096]{1,0:T(8,128)(2,1)}, bf16[24,4096]{1,0:T(8,128)(2,1)S(1)}, u32[]{:S(2)}, u32[]{:S(2)}) %collective-permute-start.6) | collective-permute-done | bytes 196640 | tf_op jit(solution)/shard_map/ppermute | solution.py:147
  47.2 3.6 %collective-permute-done.8 = bf16[24,4096]{1,0:T(8,128)(2,1)S(1)} collective-permute-done((bf16[24,4096]{1,0:T(8,128)(2,1)}, bf16[24,4096]{1,0:T(8,128)(2,1)S(1)}, u32[]{:S(2)}, u32[]{:S(2)}) %collective-permute-start.8) | collective-permute-done | bytes 196640 | tf_op jit(solution)/shard_map/ppermute | solution.py:147
  50.9 2.2 %collective-permute-done.2 = bf16[24,4096]{1,0:T(8,128)(2,1)S(1)} collective-permute-done((bf16[24,4096]{1,0:T(8,128)(2,1)}, bf16[24,4096]{1,0:T(8,128)(2,1)S(1)}, u32[]{:S(2)}, u32[]{:S(2)}) %collective-permute-start.2) | collective-permute-done | bytes 196640 | tf_op jit(solution)/shard_map/ppermute | solution.py:147
  55.8 5.7 %collective-permute-done.17 = bf16[24,4096]{1,0:T(8,128)(2,1)S(1)} collective-permute-done((bf16[24,4096]{1,0:T(8,128)(2,1)S(1)}, bf16[24,4096]{1,0:T(8,128)(2,1)S(1)}, u32[]{:S(2)}, u32[]{:S(2)}) %collective-permute-start.17) | collective-permute-done | bytes 196640 | tf_op jit(solution)/shard_map/ppermute | solution.py:147
  63.2 3.3 %collective-permute-done.18 = f32[96,64]{1,0:T(8,128)S(1)} collective-permute-done((f32[96,64]{1,0:T(8,128)S(1)}, f32[96,64]{1,0:T(8,128)S(1)}, u32[]{:S(2)}, u32[]{:S(2)}) %collective-permute-start.18) | collective-permute-done | bytes 24608 | tf_op jit(solution)/shard_map/ppermute | solution.py:147
  67.1 3.2 %collective-permute-start.10 = (bf16[24,4096]{1,0:T(8,128)(2,1)S(1)}, bf16[24,4096]{1,0:T(8,128)(2,1)S(1)}, u32[]{:S(2)}, u32[]{:S(2)}) collective-permute-start(bf16[24,4096]{1,0:T(8,128)(2,1)S(1)} %collective-permute-done.9), channel_id=1, source_target_pairs={{0,4},{1,5},{2,6},{3,7},{4,12},{5,13},{6,14},{7,15},{12,8},{13,9},... | collective-permute-start | bytes 589832 | tf_op jit(solution)/shard_map/ppermute | solution.py:147
  72.2 2.3 %collective-permute-done.12 = bf16[24,4096]{1,0:T(8,128)(2,1)S(1)} collective-permute-done((bf16[24,4096]{1,0:T(8,128)(2,1)S(1)}, bf16[24,4096]{1,0:T(8,128)(2,1)S(1)}, u32[]{:S(2)}, u32[]{:S(2)}) %collective-permute-start.12) | collective-permute-done | bytes 196640 | tf_op jit(solution)/shard_map/ppermute | solution.py:147
  78.5 6.1 %collective-permute-done.13 = bf16[24,4096]{1,0:T(8,128)(2,1)S(1)} collective-permute-done((bf16[24,4096]{1,0:T(8,128)(2,1)S(1)}, bf16[24,4096]{1,0:T(8,128)(2,1)S(1)}, u32[]{:S(2)}, u32[]{:S(2)}) %collective-permute-start.13) | collective-permute-done | bytes 196640 | tf_op jit(solution)/shard_map/ppermute | solution.py:147
  89.8 3.2 %collective-permute-done.22 = bf16[96,64]{1,0:T(8,128)(2,1)S(1)} collective-permute-done((bf16[96,64]{1,0:T(8,128)(2,1)S(1)}, bf16[96,64]{1,0:T(8,128)(2,1)S(1)}, u32[]{:S(2)}, u32[]{:S(2)}) %collective-permute-start.22) | collective-permute-done | bytes 12320 | tf_op jit(solution)/shard_map/ppermute | solution.py:147
  101.3 3.0 %fusion.72 = f32[96,512]{1,0:T(8,128)S(1)} fusion(bf16[4096,512]{1,0:T(8,128)(2,1)} %collective-permute-done.3, bf16[24,4096]{1,0:T(8,128)(2,1)S(1)} %copy-done.30, bf16[24,4096]{1,0:T(8,128)(2,1)S(1)} %copy-done.32, bf16[24,4096]{1,0:T(8,128)(2,1)S(1)} %copy-done.24, bf16[24,4096]{1,0:T(8,128)(2,1)S(1)} %copy-done.28), kind=kOutput, calls=%fused_computation.57 | convolution fusion | flops 405798912 | bytes 5177344 | tf_op jit(solution)/shard_map/dot_general | solution.py:150
  104.5 3.1 %fusion.64 = f32[96,512]{1,0:T(8,128)S(1)} fusion(bf16[4096,512]{1,0:T(8,128)(2,1)} %collective-permute-done.3, bf16[24,4096]{1,0:T(8,128)(2,1)S(1)} %copy-done.22, bf16[24,4096]{1,0:T(8,128)(2,1)S(1)} %copy-done.26, bf16[24,4096]{1,0:T(8,128)(2,1)S(1)} %copy-done.12, bf16[24,4096]{1,0:T(8,128)(2,1)S(1)} %copy-done.18), kind=kOutput, calls=%fused_computation.49 | convolution fusion | flops 405798912 | bytes 5177344 | tf_op jit(solution)/shard_map/dot_general | solution.py:150
  108.2 3.2 %fusion.56 = f32[96,512]{1,0:T(8,128)S(1)} fusion(bf16[4096,512]{1,0:T(8,128)(2,1)} %collective-permute-done.3, bf16[24,4096]{1,0:T(8,128)(2,1)S(1)} %copy-done.16, bf16[24,4096]{1,0:T(8,128)(2,1)S(1)} %copy-done.20, bf16[24,4096]{1,0:T(8,128)(2,1)} %collective-permute-done.5, bf16[24,4096]{1,0:T(8,128)(2,1)S(1)} %copy-done.10), kind=kOutput, calls=%fused_computation.41 | convolution fusion | flops 405798912 | bytes 5177344 | tf_op jit(solution)/shard_map/dot_general | solution.py:150
  111.6 3.1 %fusion.48 = f32[96,512]{1,0:T(8,128)S(1)} fusion(bf16[4096,512]{1,0:T(8,128)(2,1)} %collective-permute-done.3, bf16[24,4096]{1,0:T(8,128)(2,1)S(1)} %copy-done.8, bf16[24,4096]{1,0:T(8,128)(2,1)S(1)} %copy-done.14, bf16[24,4096]{1,0:T(8,128)(2,1)S(1)} %copy-done.6, bf16[24,4096]{1,0:T(8,128)(2,1)} %collective-permute-done), kind=kOutput, calls=%fused_computation.33 | convolution fusion | flops 405798912 | bytes 5177344 | tf_op jit(solution)/shard_map/dot_general | solution.py:150
  119.5 2.8 %collective-permute-start.43 = (bf16[24,512]{1,0:T(8,128)(2,1)S(1)}, bf16[24,512]{1,0:T(8,128)(2,1)S(1)}, u32[]{:S(2)}, u32[]{:S(2)}) collective-permute-start(bf16[24,512]{1,0:T(8,128)(2,1)S(1)} %get-tuple-element.17), channel_id=1, source_target_pairs={{0,7},{1,6},{2,5},{3,4},{4,15},{5,14},{6,13},{7,12},{12,11},{13,10... | collective-permute-start | bytes 73736 | tf_op jit(solution)/shard_map/ppermute | solution.py:147
  123.1 2.1 %collective-permute-start.35 = (bf16[24,512]{1,0:T(8,128)(2,1)S(1)}, bf16[24,512]{1,0:T(8,128)(2,1)S(1)}, u32[]{:S(2)}, u32[]{:S(2)}) collective-permute-start(bf16[24,512]{1,0:T(8,128)(2,1)S(1)} %get-tuple-element.24), channel_id=1, source_target_pairs={{0,12},{1,13},{2,14},{3,15},{4,8},{5,9},{6,10},{7,11},{12,0},{13,1... | collective-permute-start | bytes 73736 | tf_op jit(solution)/shard_map/ppermute | solution.py:147
  129.3 2.8 %collective-permute-start.38 = (bf16[24,512]{1,0:T(8,128)(2,1)S(1)}, bf16[24,512]{1,0:T(8,128)(2,1)S(1)}, u32[]{:S(2)}, u32[]{:S(2)}) collective-permute-start(bf16[24,512]{1,0:T(8,128)(2,1)S(1)} %get-tuple-element.21), channel_id=1, source_target_pairs={{0,15},{1,14},{2,13},{3,12},{4,11},{5,10},{6,9},{7,8},{12,3},{13,2... | collective-permute-start | bytes 73736 | tf_op jit(solution)/shard_map/ppermute | solution.py:147
  135.3 2.8 %collective-permute-start.32 = (bf16[24,512]{1,0:T(8,128)(2,1)S(1)}, bf16[24,512]{1,0:T(8,128)(2,1)S(1)}, u32[]{:S(2)}, u32[]{:S(2)}) collective-permute-start(bf16[24,512]{1,0:T(8,128)(2,1)S(1)} %get-tuple-element.25), channel_id=1, source_target_pairs={{0,11},{1,10},{2,9},{3,8},{4,3},{5,2},{6,1},{7,0},{12,7},{13,6},{1... | collective-permute-start | bytes 73736 | tf_op jit(solution)/shard_map/ppermute | solution.py:147
  140.0 2.2 %collective-permute-done.25.refs_2_ = bf16[24,512]{1,0:T(8,128)(2,1)S(1)} collective-permute-done((bf16[24,512]{1,0:T(8,128)(2,1)S(1)}, bf16[24,512]{1,0:T(8,128)(2,1)S(1)}, u32[]{:S(2)}, u32[]{:S(2)}) %collective-permute-start.25) | collective-permute-done | bytes 24608 | tf_op jit(solution)/shard_map/ppermute | solution.py:147
  142.9 13.2 %shard_map.75 = bf16[24,8192]{1,0:T(8,128)(2,1)} custom-call(bf16[24,512]{1,0:T(8,128)(2,1)} %get-tuple-element.32.refs_0_, bf16[24,512]{1,0:T(8,128)(2,1)} %copy-done.45, bf16[24,512]{1,0:T(8,128)(2,1)} %copy-done.46, bf16[24,512]{1,0:T(8,128)(2,1)} %copy-done.47, bf16[24,512]{1,0:T(8,128)(2,1)} %copy-done.41, bf16[24,512]{1,0:T(8,128)(2,1)} %copy-done.42, ...), custom_call_target="tpu_custom_call" | custom-call | tf_op jit(solution)/shard_map/pallas_call | solution.py:124
  (235 shorter events, 48.1 us)
Async XLA Ops:
  2.1 36.1 %collective-permute-start.5 = (bf16[24,4096]{1,0:T(8,128)(2,1)}, bf16[24,4096]{1,0:T(8,128)(2,1)}, u32[]{:S(2)}, u32[]{:S(2)}) collective-permute-start(bf16[24,4096]{1,0:T(8,128)(2,1)} %get-tuple-element.8), channel_id=1, source_target_pairs={{0,4},{1,5},{2,6},{3,7},{4,12},{5,13},{6,14},{7,15},{12,8},{13,9},... | collective-permute-start | bytes 589832 | tf_op jit(solution)/shard_map/ppermute | solution.py:147
  5.1 35.5 %collective-permute-start.1 = (bf16[24,4096]{1,0:T(8,128)(2,1)}, bf16[24,4096]{1,0:T(8,128)(2,1)S(1)}, u32[]{:S(2)}, u32[]{:S(2)}) collective-permute-start(bf16[24,4096]{1,0:T(8,128)(2,1)} %get-tuple-element.8), channel_id=1, source_target_pairs={{0,2},{1,3},{2,0},{3,1},{4,6},{5,7},{6,4},{7,5},{12,14},{13,15},{1... | collective-permute-start | bytes 589832 | tf_op jit(solution)/shard_map/ppermute | solution.py:147
  8.9 44.5 %collective-permute-start.14 = (bf16[4096,64]{0,1:T(8,128)(2,1)}, bf16[4096,64]{0,1:T(8,128)(2,1)}, u32[]{:S(2)}, u32[]{:S(2)}) collective-permute-start(bf16[4096,64]{0,1:T(8,128)(2,1)} %get-tuple-element.12), channel_id=1, source_target_pairs={{0,1},{1,0},{2,3},{3,2},{4,5},{5,4},{6,7},{7,6},{12,13},{13,12},{1... | collective-permute-start | bytes 1572872 | tf_op jit(solution)/shard_map/ppermute | solution.py:147
  9.0 30.3 %collective-permute-start = (bf16[24,4096]{1,0:T(8,128)(2,1)S(1)}, bf16[24,4096]{1,0:T(8,128)(2,1)}, u32[]{:S(2)}, u32[]{:S(2)}) collective-permute-start(bf16[24,4096]{1,0:T(8,128)(2,1)S(1)} %copy-done.49), channel_id=1, source_target_pairs={{0,1},{1,0},{2,3},{3,2},{4,5},{5,4},{6,7},{7,6},{12,13},{13,12},{1... | collective-permute-start | bytes 589832 | tf_op jit(solution)/shard_map/ppermute | solution.py:147
  14.0 87.1 %collective-permute-start.3 = (bf16[4096,512]{1,0:T(8,128)(2,1)}, bf16[4096,512]{1,0:T(8,128)(2,1)}, u32[]{:S(2)}, u32[]{:S(2)}) collective-permute-start(bf16[4096,512]{1,0:T(8,128)(2,1)} %constant_dynamic-slice_fusion), channel_id=1, source_target_pairs={{0,1},{1,0},{2,3},{3,2},{4,5},{5,4},{6,7},{7,6},{12,13},{13,12},{1... | collective-permute-start | bytes 12582920 | tf_op jit(solution)/shard_map/ppermute | solution.py:147
  38.2 8.9 %collective-permute-start.6 = (bf16[24,4096]{1,0:T(8,128)(2,1)}, bf16[24,4096]{1,0:T(8,128)(2,1)S(1)}, u32[]{:S(2)}, u32[]{:S(2)}) collective-permute-start(bf16[24,4096]{1,0:T(8,128)(2,1)} %collective-permute-done.5), channel_id=1, source_target_pairs={{0,4},{1,5},{2,6},{3,7},{4,12},{5,13},{6,14},{7,15},{12,8},{13,9},... | collective-permute-start | bytes 589832 | tf_op jit(solution)/shard_map/ppermute | solution.py:147
  39.3 11.5 %collective-permute-start.8 = (bf16[24,4096]{1,0:T(8,128)(2,1)}, bf16[24,4096]{1,0:T(8,128)(2,1)S(1)}, u32[]{:S(2)}, u32[]{:S(2)}) collective-permute-start(bf16[24,4096]{1,0:T(8,128)(2,1)} %collective-permute-done), channel_id=1, source_target_pairs={{0,4},{1,5},{2,6},{3,7},{4,12},{5,13},{6,14},{7,15},{12,8},{13,9},... | collective-permute-start | bytes 589832 | tf_op jit(solution)/shard_map/ppermute | solution.py:147
  40.7 10.1 %collective-permute-start.16 = (bf16[24,4096]{1,0:T(8,128)(2,1)}, bf16[24,4096]{1,0:T(8,128)(2,1)S(1)}, u32[]{:S(2)}, u32[]{:S(2)}) collective-permute-start(bf16[24,4096]{1,0:T(8,128)(2,1)} %collective-permute-done.5), channel_id=1, source_target_pairs={{0,2},{1,3},{2,0},{3,1},{4,6},{5,7},{6,4},{7,5},{12,14},{13,15},{1... | collective-permute-start | bytes 589832 | tf_op jit(solution)/shard_map/ppermute | solution.py:147
  50.8 15.9 %collective-permute-start.9 = (bf16[24,4096]{1,0:T(8,128)(2,1)S(1)}, bf16[24,4096]{1,0:T(8,128)(2,1)S(1)}, u32[]{:S(2)}, u32[]{:S(2)}) collective-permute-start(bf16[24,4096]{1,0:T(8,128)(2,1)S(1)} %collective-permute-done.8), channel_id=1, source_target_pairs={{0,4},{1,5},{2,6},{3,7},{4,12},{5,13},{6,14},{7,15},{12,8},{13,9},... | collective-permute-start | bytes 589832 | tf_op jit(solution)/shard_map/ppermute | solution.py:147
  50.8 19.5 %collective-permute-start.15 = (bf16[24,4096]{1,0:T(8,128)(2,1)S(1)}, bf16[24,4096]{1,0:T(8,128)(2,1)S(1)}, u32[]{:S(2)}, u32[]{:S(2)}) collective-permute-start(bf16[24,4096]{1,0:T(8,128)(2,1)S(1)} %collective-permute-done.6), channel_id=1, source_target_pairs={{0,2},{1,3},{2,0},{3,1},{4,6},{5,7},{6,4},{7,5},{12,14},{13,15},{1... | collective-permute-start | bytes 589832 | tf_op jit(solution)/shard_map/ppermute | solution.py:147
  53.5 13.6 %collective-permute-start.7 = (bf16[24,4096]{1,0:T(8,128)(2,1)S(1)}, bf16[24,4096]{1,0:T(8,128)(2,1)S(1)}, u32[]{:S(2)}, u32[]{:S(2)}) collective-permute-start(bf16[24,4096]{1,0:T(8,128)(2,1)S(1)} %collective-permute-done.6), channel_id=1, source_target_pairs={{0,4},{1,5},{2,6},{3,7},{4,12},{5,13},{6,14},{7,15},{12,8},{13,9},... | collective-permute-start | bytes 589832 | tf_op jit(solution)/shard_map/ppermute | solution.py:147
  66.6 9.4 %collective-permute-start.19 = (f32[96,64]{1,0:T(8,128)S(1)}, f32[96,64]{1,0:T(8,128)S(1)}, u32[]{:S(2)}, u32[]{:S(2)}) collective-permute-start(f32[96,64]{1,0:T(8,128)S(1)} %fusion.96), channel_id=1, source_target_pairs={{0,4},{1,5},{2,6},{3,7},{4,12},{5,13},{6,14},{7,15},{12,8},{13,9},... | collective-permute-start | bytes 73736 | tf_op jit(solution)/shard_map/ppermute | solution.py:147
  67.1 11.3 %collective-permute-start.10 = (bf16[24,4096]{1,0:T(8,128)(2,1)S(1)}, bf16[24,4096]{1,0:T(8,128)(2,1)S(1)}, u32[]{:S(2)}, u32[]{:S(2)}) collective-permute-start(bf16[24,4096]{1,0:T(8,128)(2,1)S(1)} %collective-permute-done.9), channel_id=1, source_target_pairs={{0,4},{1,5},{2,6},{3,7},{4,12},{5,13},{6,14},{7,15},{12,8},{13,9},... | collective-permute-start | bytes 589832 | tf_op jit(solution)/shard_map/ppermute | solution.py:147
  76.1 11.6 %collective-permute-start.20 = (f32[96,64]{1,0:T(8,128)S(1)}, f32[96,64]{1,0:T(8,128)S(1)}, u32[]{:S(2)}, u32[]{:S(2)}) collective-permute-start(f32[96,64]{1,0:T(8,128)S(1)} %fusion.97), channel_id=1, source_target_pairs={{0,4},{1,5},{2,6},{3,7},{4,12},{5,13},{6,14},{7,15},{12,8},{13,9},... | collective-permute-start | bytes 73736 | tf_op jit(solution)/shard_map/ppermute | solution.py:147
  104.4 10.8 %collective-permute-start.39 = (f32[96,512]{1,0:T(8,128)S(1)}, f32[96,512]{1,0:T(8,128)S(1)}, u32[]{:S(2)}, u32[]{:S(2)}) collective-permute-start(f32[96,512]{1,0:T(8,128)S(1)} %fusion.72), channel_id=1, source_target_pairs={{0,1},{1,0},{2,3},{3,2},{4,5},{5,4},{6,7},{7,6},{12,13},{13,12},{1... | collective-permute-start | bytes 589832 | tf_op jit(solution)/shard_map/ppermute | solution.py:147
  107.7 10.4 %collective-permute-start.33 = (f32[96,512]{1,0:T(8,128)S(1)}, f32[96,512]{1,0:T(8,128)S(1)}, u32[]{:S(2)}, u32[]{:S(2)}) collective-permute-start(f32[96,512]{1,0:T(8,128)S(1)} %fusion.64), channel_id=1, source_target_pairs={{0,1},{1,0},{2,3},{3,2},{4,5},{5,4},{6,7},{7,6},{12,13},{13,12},{1... | collective-permute-start | bytes 589832 | tf_op jit(solution)/shard_map/ppermute | solution.py:147
  114.7 8.4 %collective-permute-start.4 = (f32[96,512]{1,0:T(8,128)S(1)}, f32[96,512]{1,0:T(8,128)S(1)}, u32[]{:S(2)}, u32[]{:S(2)}) collective-permute-start(f32[96,512]{1,0:T(8,128)S(1)} %fusion.48), channel_id=1, source_target_pairs={{0,1},{1,0},{2,3},{3,2},{4,5},{5,4},{6,7},{7,6},{12,13},{13,12},{1... | collective-permute-start | bytes 589832 | tf_op jit(solution)/shard_map/ppermute | solution.py:147
  116.1 9.9 %collective-permute-start.40 = (bf16[24,512]{1,0:T(8,128)(2,1)S(1)}, bf16[24,512]{1,0:T(8,128)(2,1)S(1)}, u32[]{:S(2)}, u32[]{:S(2)}) collective-permute-start(bf16[24,512]{1,0:T(8,128)(2,1)S(1)} %get-tuple-element.20), channel_id=1, source_target_pairs={{0,4},{1,5},{2,6},{3,7},{4,12},{5,13},{6,14},{7,15},{12,8},{13,9},... | collective-permute-start | bytes 73736 | tf_op jit(solution)/shard_map/ppermute | solution.py:147
  116.1 11.2 %collective-permute-start.41 = (bf16[24,512]{1,0:T(8,128)(2,1)S(1)}, bf16[24,512]{1,0:T(8,128)(2,1)S(1)}, u32[]{:S(2)}, u32[]{:S(2)}) collective-permute-start(bf16[24,512]{1,0:T(8,128)(2,1)S(1)} %get-tuple-element.19), channel_id=1, source_target_pairs={{0,5},{1,4},{2,7},{3,6},{4,13},{5,12},{6,15},{7,14},{12,9},{13,8},... | collective-permute-start | bytes 73736 | tf_op jit(solution)/shard_map/ppermute | solution.py:147
  118.1 11.2 %collective-permute-start.42 = (bf16[24,512]{1,0:T(8,128)(2,1)S(1)}, bf16[24,512]{1,0:T(8,128)(2,1)S(1)}, u32[]{:S(2)}, u32[]{:S(2)}) collective-permute-start(bf16[24,512]{1,0:T(8,128)(2,1)S(1)} %get-tuple-element.18), channel_id=1, source_target_pairs={{0,6},{1,7},{2,4},{3,5},{4,14},{5,15},{6,12},{7,13},{12,10},{13,11... | collective-permute-start | bytes 73736 | tf_op jit(solution)/shard_map/ppermute | solution.py:147
  119.5 12.6 %collective-permute-start.43 = (bf16[24,512]{1,0:T(8,128)(2,1)S(1)}, bf16[24,512]{1,0:T(8,128)(2,1)S(1)}, u32[]{:S(2)}, u32[]{:S(2)}) collective-permute-start(bf16[24,512]{1,0:T(8,128)(2,1)S(1)} %get-tuple-element.17), channel_id=1, source_target_pairs={{0,7},{1,6},{2,5},{3,4},{4,15},{5,14},{6,13},{7,12},{12,11},{13,10... | collective-permute-start | bytes 73736 | tf_op jit(solution)/shard_map/ppermute | solution.py:147
  123.1 9.0 %collective-permute-start.35 = (bf16[24,512]{1,0:T(8,128)(2,1)S(1)}, bf16[24,512]{1,0:T(8,128)(2,1)S(1)}, u32[]{:S(2)}, u32[]{:S(2)}) collective-permute-start(bf16[24,512]{1,0:T(8,128)(2,1)S(1)} %get-tuple-element.24), channel_id=1, source_target_pairs={{0,12},{1,13},{2,14},{3,15},{4,8},{5,9},{6,10},{7,11},{12,0},{13,1... | collective-permute-start | bytes 73736 | tf_op jit(solution)/shard_map/ppermute | solution.py:147
  126.0 8.7 %collective-permute-start.36 = (bf16[24,512]{1,0:T(8,128)(2,1)S(1)}, bf16[24,512]{1,0:T(8,128)(2,1)S(1)}, u32[]{:S(2)}, u32[]{:S(2)}) collective-permute-start(bf16[24,512]{1,0:T(8,128)(2,1)S(1)} %get-tuple-element.23), channel_id=1, source_target_pairs={{0,13},{1,12},{2,15},{3,14},{4,9},{5,8},{6,11},{7,10},{12,1},{13,0... | collective-permute-start | bytes 73736 | tf_op jit(solution)/shard_map/ppermute | solution.py:147
  129.3 8.8 %collective-permute-start.38 = (bf16[24,512]{1,0:T(8,128)(2,1)S(1)}, bf16[24,512]{1,0:T(8,128)(2,1)S(1)}, u32[]{:S(2)}, u32[]{:S(2)}) collective-permute-start(bf16[24,512]{1,0:T(8,128)(2,1)S(1)} %get-tuple-element.21), channel_id=1, source_target_pairs={{0,15},{1,14},{2,13},{3,12},{4,11},{5,10},{6,9},{7,8},{12,3},{13,2... | collective-permute-start | bytes 73736 | tf_op jit(solution)/shard_map/ppermute | solution.py:147
  (72 other events, 535.5 us)

commit v3 on v0

v3 whole, which is shorter than its diff:
```python
import jax
import jax.numpy as jnp
from jax import lax
from jax.experimental import pallas as pl
from jax.experimental.pallas import tpu as pltpu
from jax.sharding import PartitionSpec as P

ADAPTER_SCALE = 0.5
EPS = 1e-05

SIDE = 2
CORES = 2
CORNERS = SIDE * CORES
LANES = 128
CHUNK = 1024


def round_trip(devices):
    places = devices // CORNERS
    up = [place * CORNERS + core for place in range(places) for core in range(CORES)]
    back = [
        place * CORNERS + CORES + core for place in reversed(range(places)) for core in range(CORES)
    ]
    return up + back


def norm_kernel(hidden_ref, gain_ref, low_ref, high_ref):
    rows, width = hidden_ref.shape
    half = width // 2
    squares = jnp.zeros((rows, LANES), jnp.float32)
    for start in range(0, width, CHUNK):
        wide = hidden_ref[:, start : start + CHUNK].astype(jnp.float32)
        wide = wide * wide
        for lane in range(0, CHUNK, LANES):
            squares = squares + wide[:, lane : lane + LANES]
    inv_rms = lax.rsqrt(jnp.sum(squares, axis=1, keepdims=True) / width + EPS)
    for first, out_ref in ((0, low_ref), (half, high_ref)):
        for start in range(0, half, CHUNK):
            at = first + start
            wide = hidden_ref[:, at : at + CHUNK].astype(jnp.float32)
            gain = gain_ref[:, at : at + CHUNK]
            out_ref[:, start : start + CHUNK] = (wide * inv_rms * gain).astype(jnp.bfloat16)


def normalize(hidden, norm_weight):
    rows, width = hidden.shape
    vmem = pl.BlockSpec(memory_space=pltpu.VMEM)
    half = jax.ShapeDtypeStruct((rows, width // 2), jnp.bfloat16)
    return pl.pallas_call(
        norm_kernel, out_shape=(half, half), in_specs=[vmem, vmem], out_specs=(vmem, vmem)
    )(hidden, norm_weight.reshape(1, width))


def shards(
    hidden, norm_weight, query_weight, down_weights, up_weights, adapter_index, adapter_slot
):
    devices = lax.axis_size("adapter")
    me = lax.axis_index("adapter")
    places = devices // CORNERS
    own_rows, width = hidden.shape
    half = width // 2
    columns = query_weight.shape[1]
    rank = down_weights.shape[2]
    rows = devices * own_rows
    order = round_trip(devices)

    def matmul(x, y):
        return jnp.dot(x, y, preferred_element_type=jnp.float32)

    def flip(x, how):
        return lax.ppermute(x, "adapter", [(i, i ^ how) for i in range(devices)])

    def along(x, steps):
        step = steps * CORNERS
        return lax.ppermute(x, "adapter", [(i, (i + step) % devices) for i in range(devices)])

    low, high = normalize(hidden, norm_weight)
    low = lax.all_gather(low, "adapter", axis_index_groups=[order])
    high = lax.all_gather(high, "adapter", axis_index_groups=[order[::-1]])
    ids = lax.all_gather(adapter_index, "adapter")
    ids = ids[:, :, 0][jnp.asarray(order)].reshape(rows)

    names = jnp.arange(devices, dtype=jnp.int32)
    hits = (ids[:, None] == names[None, :]).astype(jnp.int32)
    slot_tok = jnp.sum(hits * adapter_slot[None, :], axis=1)
    slot_hits = slot_tok[:, None] == names[None, :]

    def project(weight):
        one = matmul(low.reshape(rows, half), weight[:half])
        other = matmul(high.reshape(rows, half), weight[half:])
        return one + other.reshape(devices, own_rows, -1)[::-1].reshape(rows, -1)

    shrink = project(down_weights[0])
    shrink = jnp.where((slot_tok == me)[:, None], shrink, 0.0).astype(jnp.bfloat16)
    shrink = shrink + flip(shrink, 1)
    shrink = shrink + flip(shrink, 2)
    parts = [along(shrink, steps) for steps in range(1, places)]
    for part in parts:
        shrink = shrink + part
    base = project(query_weight)
    spread = jnp.where(slot_hits[:, :, None], shrink[:, None, :], jnp.zeros((), jnp.bfloat16))
    update = matmul(spread.reshape(rows, devices * rank), up_weights.reshape(devices * rank, columns))
    query = (base + ADAPTER_SCALE * update).astype(jnp.bfloat16)
    query = query.reshape(devices, own_rows, columns)
    back = [order.index(i) for i in range(devices)]
    query = jnp.concatenate([query[i] for i in back], axis=0)
    return lax.all_to_all(query, "adapter", split_axis=0, concat_axis=1, tiled=True)


def solution(mesh):
    in_specs = (
        P(("group", "adapter"), None),
        P(),
        P(None, "adapter"),
        P("adapter", None, None),
        P(None, None, "adapter"),
        P(("group", "adapter"), None),
        P(),
    )
    out_specs = P(("group", "adapter"), None)
    return jax.shard_map(shards, mesh=mesh, in_specs=in_specs, out_specs=out_specs, check_vma=False)
```

time: 172 us -> 137 us (0.80)
  blocking collectives: 88.8 us -> 28.7 us
  waiting for transfers between devices: 47.6 us -> 64.6 us
  starting transfers between devices: 0.01 us -> 6.21 us
  other arithmetic: 3.95 us -> 1.48 us
  Pallas kernels: 0 us -> 2.1 us
    psum x1 -> x0, blocking collectives: 60.2 us -> none  [shards(): lax.psum(rounded.astype(jnp.float32), 'adapter').astype(jnp.bfloat16)]
    all_gather x1 -> x2, waiting for transfers between devices: 47.6 us -> 62.9 us  [the longest x1 33.3 us: shards(): low = lax.all_gather(low, 'adapter', axis_index_groups=[order])]
    ppermute x0 -> x5, starting transfers between devices: none -> 6.16 us  [the longest x3 4.44 us: along(): lax.ppermute(x, 'adapter', [(i, (i + step) % devices) for i in range(devi...]
    pallas_call x0 -> x1, Pallas kernels: none -> 2.1 us  [normalize(): pl.pallas_call(norm_kernel, out_shape=(half, half), in_specs=[vmem, vmem]...]
    convert_element_type x1 -> x0, other arithmetic: 1.91 us -> none  [shards(): normalized_input = (wide32 * inv_rms * norm_weight).astype(jnp.bfloat16)]
    dot_general x3 -> x5, matrix products: 14.3 us -> 15.7 us  [matmul(): return jnp.dot(x, y, preferred_element_type=jnp.float32)]
  transfers between devices with their start and end apart: 1 -> 7, of which waited for: 1 -> 3; matrix products, arithmetic and copies ran while one was open for 2% -> 12% of each run, Pallas kernels for 0% -> 0%
where the time goes in v3:
time: 137 us
  waiting for transfers between devices  64.6 us (47%)
  blocking collectives  28.7 us (21%)
  matrix products  15.7 us (11%)
  between operations  14.2 us (10%)
  starting transfers between devices  6.21 us (5%)
  local copies, waits for them, and re-layouts  3.74 us (3%)
  Pallas kernels  2.1 us (2%)
  other arithmetic  1.48 us (1%)
    all_gather x1, waiting for transfers between devices, shards(): low = lax.all_gather(low, 'adapter', axis_index_groups=[order])  33.3 us
    all_gather x1, waiting for transfers between devices, shards(): high = lax.all_gather(high, 'adapter', axis_index_groups=[order[::-1]])  29.6 us
    dot_general x5, matrix products, matmul(): return jnp.dot(x, y, preferred_element_type=jnp.float32)  15.7 us
    all_to_all x1, blocking collectives, shards(): lax.all_to_all(query, 'adapter', split_axis=0, concat_axis=1, tiled=True)  14.9 us
    unnamed x1, blocking collectives  13.8 us
    ppermute x3, starting transfers between devices, along(): lax.ppermute(x, 'adapter', [(i, (i + step) % devices) for i in range(devi...  4.44 us
  transfers between devices with their start and end apart: 7, of which 3 were waited for; matrix products, arithmetic and copies ran while one was open for 12% of the time, Pallas kernels for 0%

profile of v3, /device:TPU:0, one launch (start us, length us, event | category | flops | bytes accessed | tf_op | source)
XLA Modules:
  0.0 136.6 jit_solution(11583642112308181820)
XLA Ops:
  6.5 2.1 %shard_map.82 = (bf16[24,4096]{1,0:T(8,128)(2,1)}, bf16[24,4096]{1,0:T(8,128)(2,1)}) custom-call(bf16[24,8192]{1,0:T(8,128)(2,1)} %hidden_ref.1, f32[1,8192]{1,0:T(1,128)} %bitcast.38), custom_call_target="tpu_custom_call" | custom-call | tf_op jit(solution)/shard_map/pallas_call | solution.py:49
  8.7 0.7 all-gather.6.cloned.1.call-update
  9.4 1.2 dynamic-slice
  11.2 0.8 bitcast_dynamic-update-slice_fusion
  12.0 13.8 %all-reduce = s32[384]{0:T(512)S(1)} all-reduce(s32[384]{0:T(512)S(1)} %bitcast_dynamic-update-slice_fusion), channel_id=4, replica_groups=mesh['group'=2,'adapter'=16] {'adapter'}, use_global_device_ids=true, to_apply=%add | all-reduce | flops 384 | bytes 3072
  25.8 0.7 pad_clamp_fusion
  26.5 0.6 gather_fusion
  27.2 0.7 select_reduce_fusion
  27.9 29.6 %all-gather.8.cloned.1.call-done = bf16[384,4096]{1,0:T(8,128)(2,1)} async-done(((bf16[24,4096]{1,0:T(8,128)(2,1)}), bf16[384,4096]{1,0:T(8,128)(2,1)}) %all-gather.8.cloned.1.call-update) | async-done | bytes 3145744 | tf_op jit(solution)/shard_map/all_gather | solution.py:79
  57.5 3.0 %fusion.15 = f32[16,24,64]{2,1,0:T(8,128)S(1)} fusion(bf16[16,24,4096]{2,1,0:T(8,128)(2,1)} %bitcast.39, bf16[1,8192,64]{1,2,0:T(8,128)(2,1)} %param.11), kind=kOutput, calls=%fused_computation.16 | convolution fusion | flops 201326592 | bytes 3768320 | tf_op jit(solution)/shard_map/dot_general | solution.py:68
  60.5 0.1 copy.13
  60.6 33.3 %all-gather.6.cloned.1.call-done = bf16[384,4096]{1,0:T(8,128)(2,1)} async-done(((bf16[24,4096]{1,0:T(8,128)(2,1)}), bf16[384,4096]{1,0:T(8,128)(2,1)}) %all-gather.6.cloned.1.call-update) | async-done | bytes 3145744 | tf_op jit(solution)/shard_map/all_gather | solution.py:78
  93.9 3.1 %fusion.12 = bf16[384,64]{0,1:T(8,128)(2,1)S(1)} fusion(f32[384,64]{0,1:T(8,128)S(1)} %copy.13, bf16[384,4096]{1,0:T(8,128)(2,1)} %all-gather.6.cloned.1.call-done, bf16[1,8192,64]{1,2,0:T(8,128)(2,1)S(1)} %copy-done.1, pred[384]{0:T(512)(128)(4,1)S(1)} %broadcast_compare_fusion), kind=kOutput, calls=%fused_computation.13 | convolution fusion | flops 201400320 | bytes 3817984 | tf_op jit(solution)/shard_map/dot_general | solution.py:68
  97.0 0.3 collective-permute-start
  97.3 1.0 collective-permute-done
  98.3 1.4 %collective-permute-start.1 = (bf16[384,64]{0,1:T(8,128)(2,1)S(1)}, bf16[384,64]{0,1:T(8,128)(2,1)S(1)}, u32[]{:S(2)}, u32[]{:S(2)}) collective-permute-start(bf16[384,64]{0,1:T(8,128)(2,1)S(1)} %add.30), channel_id=1, source_target_pairs={{0,2},{1,3},{2,0},{3,1},{4,6},{5,7},{6,4},{7,5},{8,10},{9,11},{10,... | collective-permute-start | bytes 147464 | tf_op jit(solution)/shard_map/ppermute | solution.py:71
  99.8 4.0 %fusion = f32[16,24,512]{2,1,0:T(8,128)S(1)} fusion(bf16[16,24,4096]{2,1,0:T(8,128)(2,1)S(1)} %bitcast.40, bf16[8192,512]{1,0:T(8,128)(2,1)} %param.10), kind=kOutput, calls=%fused_computation.1 | convolution fusion | flops 1610612736 | bytes 8126464 | tf_op jit(solution)/shard_map/dot_general | solution.py:68
  103.9 0.7 collective-permute-start.2
  104.6 1.4 %collective-permute-start.3 = (bf16[384,64]{0,1:T(8,128)(2,1)S(1)}, bf16[384,64]{0,1:T(8,128)(2,1)S(1)}, u32[]{:S(2)}, u32[]{:S(2)}) collective-permute-start(bf16[384,64]{0,1:T(8,128)(2,1)S(1)} %add.31), channel_id=1, source_target_pairs={{0,8},{1,9},{2,10},{3,11},{4,12},{5,13},{6,14},{7,15},{8,0},{9,1},... | collective-permute-start | bytes 147464 | tf_op jit(solution)/shard_map/ppermute | solution.py:75
  106.0 2.3 %collective-permute-start.4 = (bf16[384,64]{0,1:T(8,128)(2,1)S(1)}, bf16[384,64]{0,1:T(8,128)(2,1)S(1)}, u32[]{:S(2)}, u32[]{:S(2)}) collective-permute-start(bf16[384,64]{0,1:T(8,128)(2,1)S(1)} %add.31), channel_id=1, source_target_pairs={{0,12},{1,13},{2,14},{3,15},{4,0},{5,1},{6,2},{7,3},{8,4},{9,5},{1... | collective-permute-start | bytes 147464 | tf_op jit(solution)/shard_map/ppermute | solution.py:75
  108.3 4.9 %fusion.6 = f32[384,512]{1,0:T(8,128)S(1)} fusion(f32[384,512]{1,0:T(8,128)S(1)} %bitcast.35, bf16[384,4096]{1,0:T(8,128)(2,1)} %all-gather.6.cloned.1.call-done, bf16[8192,512]{1,0:T(8,128)(2,1)} %param.10), kind=kOutput, calls=%fused_computation.8 | convolution fusion | flops 1610809344 | bytes 8912896 | tf_op jit(solution)/shard_map/dot_general | solution.py:68
  113.3 0.6 fusion.10
  114.1 14.9 %all_to_all.19 = bf16[16,24,512]{2,1,0:T(8,128)(2,1)S(1)} all-to-all(bf16[16,24,512]{2,1,0:T(8,128)(2,1)S(1)} %bitcast.37), channel_id=1, replica_groups=mesh['group'=2,'adapter'=16] {'adapter'}, dimensions={0} | all-to-all | bytes 786432 | tf_op jit(solution)/shard_map/all_to_all | solution.py:107
  129.0 0.8 copy.15
  (30 shorter events, 0.4 us)
Async XLA Ops:
  6.5 106.8 %copy-start = (bf16[16,64,512]{2,1,0:T(8,128)(2,1)S(1)}, bf16[16,64,512]{2,1,0:T(8,128)(2,1)}, u32[]{:S(2)}) copy-start(bf16[16,64,512]{2,1,0:T(8,128)(2,1)} %param.12) | copy-start | bytes 3145732
  6.5 87.3 %copy-start.1 = (bf16[1,8192,64]{1,2,0:T(8,128)(2,1)S(1)}, bf16[1,8192,64]{1,2,0:T(8,128)(2,1)}, u32[]{:S(2)}) copy-start(bf16[1,8192,64]{1,2,0:T(8,128)(2,1)} %param.11) | copy-start | bytes 3145732
  6.5 50.9 %all-gather.8.cloned.1.call-start = ((), (), s32[]{:S(2)}) async-start(), calls=%async_computation.2 | async-start | bytes 3342336 | tf_op jit(solution)/shard_map/all_gather | solution.py:79
  8.7 85.2 %all-gather.6.cloned.1.call-start = ((), (), s32[]{:S(2)}) async-start(), calls=%async_computation.1 | async-start | bytes 3342336 | tf_op jit(solution)/shard_map/all_gather | solution.py:78
  93.9 5.9 %copy-start.2 = (bf16[384,4096]{1,0:T(8,128)(2,1)S(1)}, bf16[384,4096]{1,0:T(8,128)(2,1)}, u32[]{:S(2)}) copy-start(bf16[384,4096]{1,0:T(8,128)(2,1)} %all-gather.8.cloned.1.call-done) | copy-start | bytes 9437188
  97.0 1.3 collective-permute-start
  98.3 5.5 %collective-permute-start.1 = (bf16[384,64]{0,1:T(8,128)(2,1)S(1)}, bf16[384,64]{0,1:T(8,128)(2,1)S(1)}, u32[]{:S(2)}, u32[]{:S(2)}) collective-permute-start(bf16[384,64]{0,1:T(8,128)(2,1)S(1)} %add.30), channel_id=1, source_target_pairs={{0,2},{1,3},{2,0},{3,1},{4,6},{5,7},{6,4},{7,5},{8,10},{9,11},{10,... | collective-permute-start | bytes 147464 | tf_op jit(solution)/shard_map/ppermute | solution.py:71
  103.9 9.4 %collective-permute-start.2 = (bf16[384,64]{0,1:T(8,128)(2,1)S(1)}, bf16[384,64]{0,1:T(8,128)(2,1)S(1)}, u32[]{:S(2)}, u32[]{:S(2)}) collective-permute-start(bf16[384,64]{0,1:T(8,128)(2,1)S(1)} %add.31), channel_id=1, source_target_pairs={{0,4},{1,5},{2,6},{3,7},{4,8},{5,9},{6,10},{7,11},{8,12},{9,13},{1... | collective-permute-start | bytes 147464 | tf_op jit(solution)/shard_map/ppermute | solution.py:75
  104.6 8.7 %collective-permute-start.3 = (bf16[384,64]{0,1:T(8,128)(2,1)S(1)}, bf16[384,64]{0,1:T(8,128)(2,1)S(1)}, u32[]{:S(2)}, u32[]{:S(2)}) collective-permute-start(bf16[384,64]{0,1:T(8,128)(2,1)S(1)} %add.31), channel_id=1, source_target_pairs={{0,8},{1,9},{2,10},{3,11},{4,12},{5,13},{6,14},{7,15},{8,0},{9,1},... | collective-permute-start | bytes 147464 | tf_op jit(solution)/shard_map/ppermute | solution.py:75
  106.0 7.3 %collective-permute-start.4 = (bf16[384,64]{0,1:T(8,128)(2,1)S(1)}, bf16[384,64]{0,1:T(8,128)(2,1)S(1)}, u32[]{:S(2)}, u32[]{:S(2)}) collective-permute-start(bf16[384,64]{0,1:T(8,128)(2,1)S(1)} %add.31), channel_id=1, source_target_pairs={{0,12},{1,13},{2,14},{3,15},{4,0},{5,1},{6,2},{7,3},{8,4},{9,5},{1... | collective-permute-start | bytes 147464 | tf_op jit(solution)/shard_map/ppermute | solution.py:75
Sparse Core Ops, SparseCore 0:
  8.9 48.5 all-gather.7
  59.1 34.7 all-gather.5

commit v4 on v0

v4 whole, which is shorter than its diff:
```python
import jax
import jax.numpy as jnp
from jax import lax
from jax.experimental import pallas as pl
from jax.experimental.pallas import tpu as pltpu
from jax.sharding import PartitionSpec as P

ADAPTER_SCALE = 0.5
EPS = 1e-05

SIDE = 2
CORES = 2
CORNERS = SIDE * CORES
LANES = 128
CHUNK = 1024
SMALL = 16 << 20


def line_ring(places):
    odd = list(range(1, places, 2))
    even = list(range(0, places, 2))
    return [0] + odd + even[:0:-1]


def pairs(places, steps, flip):
    ring = line_ring(places)
    out = []
    for at, place in enumerate(ring):
        target = ring[(at + steps) % places]
        for corner in range(CORNERS):
            out.append((place * CORNERS + corner, target * CORNERS + (corner ^ flip)))
    return out


def ring_device(places, steps, flip):
    me = lax.axis_index("adapter")
    ring = line_ring(places)
    place, corner = me // CORNERS, me % CORNERS
    target = jnp.int32(0)
    for at, name in enumerate(ring):
        target = jnp.where(place == name, jnp.int32(ring[(at + steps) % places]), target)
    return target * CORNERS + (corner ^ flip)


def slots_kernel(index_ref, slot_ref, out_ref):
    index = index_ref[...]
    slot = jnp.zeros(index.shape, jnp.float32)
    for name in range(slot_ref.shape[0]):
        slot = jnp.where(index == name, slot_ref[name].astype(jnp.float32), slot)
    out_ref[...] = jnp.zeros(out_ref.shape, jnp.float32)
    out_ref[0:1, 0 : index.shape[1]] = slot


def own_slots(adapter_index, adapter_slot):
    rows = adapter_index.shape[0]
    vmem = pl.BlockSpec(memory_space=pltpu.VMEM)
    return pl.pallas_call(
        slots_kernel,
        out_shape=jax.ShapeDtypeStruct((8, LANES), jnp.float32),
        in_specs=[vmem, pl.BlockSpec(memory_space=pltpu.SMEM)],
        out_specs=vmem,
        compiler_params=pltpu.CompilerParams(vmem_limit_bytes=SMALL),
    )(adapter_index.reshape(1, rows), adapter_slot)


def slot_column(slots_ref, own_rows):
    across = lax.broadcasted_iota(jnp.int32, (own_rows, LANES), 1)
    down = lax.broadcasted_iota(jnp.int32, (own_rows, LANES), 0)
    columns = []
    for corner in range(CORNERS):
        row = slots_ref[corner : corner + 1, :]
        columns.append(jnp.sum(jnp.where(across == down, row, 0.0), axis=1, keepdims=True))
    return jnp.concatenate(columns, axis=0).astype(jnp.int32)


def prepare_kernel(*refs):
    blocks, refs = refs[:CORNERS], refs[CORNERS:]
    gain_ref, own_ref, other_ref, slots_ref, *before, rows_ref, part_ref = refs
    own_rows, width = blocks[0].shape
    rank = own_ref.shape[0]
    inverse = []
    for block in blocks:
        squares = jnp.zeros((own_rows, LANES), jnp.float32)
        for start in range(0, width, CHUNK):
            wide = block[:, start : start + CHUNK].astype(jnp.float32)
            wide = wide * wide
            for lane in range(0, CHUNK, LANES):
                squares = squares + wide[:, lane : lane + LANES]
        inverse.append(lax.rsqrt(jnp.sum(squares, axis=1, keepdims=True) / width + EPS))
    part = jnp.zeros((own_rows * CORNERS, 2 * rank), jnp.float32)
    for start in range(0, width, CHUNK):
        lanes = slice(start, start + CHUNK)
        gain = gain_ref[:, lanes]
        wide = [block[:, lanes].astype(jnp.float32) * inv * gain for block, inv in zip(blocks, inverse)]
        rows = jnp.concatenate(wide, axis=0).astype(jnp.bfloat16)
        rows_ref[:, lanes] = rows
        down = jnp.concatenate([own_ref[:, lanes], other_ref[:, lanes]], axis=0)
        part += lax.dot_general(
            rows, down, (((1,), (1,)), ((), ())), preferred_element_type=jnp.float32
        )
    slot = slot_column(slots_ref, own_rows)
    me = lax.axis_index("adapter")
    lanes = lax.broadcasted_iota(jnp.int32, part.shape, 1)
    holder = jnp.where(lanes < rank, me, me ^ 1)
    part = jnp.where(slot == holder, part, 0.0)
    part = part[:, :rank] + part[:, rank:]
    for ref in before:
        part = part + ref[...].astype(jnp.float32)
    part_ref[...] = part.astype(jnp.bfloat16)


def prepare(blocks, gain, own, other, slots, before):
    own_rows, width = blocks[0].shape
    rank = own.shape[0]
    rows = own_rows * CORNERS
    before = [] if before is None else [before]
    vmem = pl.BlockSpec(memory_space=pltpu.VMEM)
    return pl.pallas_call(
        prepare_kernel,
        out_shape=(
            jax.ShapeDtypeStruct((rows, width), jnp.bfloat16),
            jax.ShapeDtypeStruct((rows, rank), jnp.bfloat16),
        ),
        in_specs=[vmem] * (CORNERS + 4 + len(before)),
        out_specs=(vmem, vmem),
        compiler_params=pltpu.CompilerParams(vmem_limit_bytes=SMALL),
        cost_estimate=pl.CostEstimate(
            flops=2 * rows * width * 256, bytes_accessed=rows * width * 4, transcendentals=rows
        ),
    )(*blocks, gain, own, other, slots, *before)


def finish_kernel(places, devices, *refs):
    bases, shrinks, slots = refs[:places], refs[places : 2 * places], refs[2 * places : 3 * places]
    up_ref, out_ref = refs[3 * places :]
    rows, rank = shrinks[0].shape
    own_rows = rows // CORNERS
    lanes = lax.broadcasted_iota(jnp.int32, (rows, devices * rank), 1)
    for step in range(places):
        shrink = shrinks[step][...].astype(jnp.float32)
        wide = jnp.concatenate([shrink] * devices, axis=1)
        slot = slot_column(slots[step], own_rows)
        spread = jnp.where(lanes // rank == slot, wide, 0.0).astype(jnp.bfloat16)
        update = jnp.dot(spread, up_ref[...], preferred_element_type=jnp.float32)
        query = (bases[step][...] + ADAPTER_SCALE * update).astype(jnp.bfloat16)
        for corner in range(CORNERS):
            owner = ring_device(places, -step, corner)
            out_ref[owner] = query[corner * own_rows : (corner + 1) * own_rows]


def finish(bases, shrinks, slots, up):
    places, devices = len(bases), up.shape[0]
    rows, columns = bases[0].shape
    rank = up.shape[1]
    vmem = pl.BlockSpec(memory_space=pltpu.VMEM)
    return pl.pallas_call(
        lambda *refs: finish_kernel(places, devices, *refs),
        out_shape=jax.ShapeDtypeStruct((devices, rows // CORNERS, columns), jnp.bfloat16),
        in_specs=[vmem] * (3 * places + 1),
        out_specs=vmem,
        compiler_params=pltpu.CompilerParams(vmem_limit_bytes=SMALL),
    )(*bases, *shrinks, *slots, up.reshape(devices * rank, columns))


def shards(
    hidden, norm_weight, query_weight, down_weights, up_weights, adapter_index, adapter_slot
):
    devices = lax.axis_size("adapter")
    me = lax.axis_index("adapter")
    places = devices // CORNERS
    own_rows, width = hidden.shape
    rank = down_weights.shape[2]

    def move(x, steps, flip):
        return lax.ppermute(x, "adapter", pairs(places, steps, flip))

    def matmul(x, y):
        return jnp.dot(x, y, preferred_element_type=jnp.float32)

    slots = own_slots(adapter_index, adapter_slot)
    empty = jnp.zeros((8 - CORNERS, LANES), jnp.float32)
    pair = jnp.concatenate([slots[:1], move(slots, 0, 1)[:1], slots[2:]], axis=0)
    four = jnp.concatenate([pair[:2], move(pair, 0, 2)[:2], empty], axis=0)
    slots = [four] + [move(four, step, 0) for step in range(1, places)]

    chain = hidden
    gain = norm_weight.reshape(1, width)
    down = down_weights[0].T
    down_other = move(down, 0, 1)

    bases, travelling = [], None
    for step in range(places):
        if step:
            chain = move(chain, 1, 0)
        other_y = move(chain, 0, 2)
        blocks = [chain, move(chain, 0, 1), other_y, move(other_y, 0, 1)]
        before = None if travelling is None else move(travelling, 1, 0)
        rows, travelling = prepare(blocks, gain, down, down_other, slots[step], before)
        bases.append(matmul(rows, query_weight))

    blocks = move(travelling, 0, 2).reshape(CORNERS, own_rows, rank)
    blocks = jnp.concatenate([blocks[corner ^ 2] for corner in range(CORNERS)], axis=0)
    shrink = travelling + blocks
    shrinks = [move(shrink, step + 1, 0) for step in range(places - 1)] + [shrink]
    query = finish(bases, shrinks, slots, up_weights)
    query = query.reshape(devices * own_rows, query.shape[2])
    return lax.all_to_all(query, "adapter", split_axis=0, concat_axis=1, tiled=True)


def solution(mesh):
    in_specs = (
        P(("group", "adapter"), None),
        P(),
        P(None, "adapter"),
        P("adapter", None, None),
        P(None, None, "adapter"),
        P(("group", "adapter"), None),
        P(),
    )
    out_specs = P(("group", "adapter"), None)
    return jax.shard_map(shards, mesh=mesh, in_specs=in_specs, out_specs=out_specs, check_vma=False)
```

time: 172 us -> 97.2 us (0.57)
  blocking collectives: 88.8 us -> 16.5 us
  starting transfers between devices: 0.01 us -> 28.6 us
  waiting for transfers between devices: 47.6 us -> 30.2 us
  between operations: 14 us -> 0.14 us
  Pallas kernels: 0 us -> 6.82 us
  matrix products: 14.3 us -> 9.31 us
  other arithmetic: 3.95 us -> 0.1 us
  local copies, waits for them, and re-layouts: 2.78 us -> 5.17 us
    psum x1 -> x0, blocking collectives: 60.2 us -> none  [shards(): lax.psum(rounded.astype(jnp.float32), 'adapter').astype(jnp.bfloat16)]
    all_gather x1 -> x0, waiting for transfers between devices: 47.6 us -> none  [shards(): lax.all_gather(normalized_input, 'adapter', axis=0, tiled=True)]
    ppermute x0 -> x28, waiting for transfers between devices: none -> 30.2 us  [move(): return lax.ppermute(x, 'adapter', pairs(places, steps, flip))]
    ppermute x0 -> x28, starting transfers between devices: none -> 28.6 us  [move(): return lax.ppermute(x, 'adapter', pairs(places, steps, flip))]
    unnamed x1 -> x0, blocking collectives: 13.8 us -> none
    pallas_call x0 -> x6, Pallas kernels: none -> 6.82 us  [the longest x4 5.32 us: prepare(): pl.pallas_call(prepare_kernel, out_shape=(jax.ShapeDtypeStruct((rows, wid...]
    dot_general x3 -> x4, matrix products: 14.3 us -> 9.31 us  [matmul(): return jnp.dot(x, y, preferred_element_type=jnp.float32)]
    unnamed x5 -> x20, local copies, waits for them, and re-layouts: 2.01 us -> 4.31 us
  transfers between devices with their start and end apart: 1 -> 28, of which waited for: 1 -> 10; matrix products, arithmetic and copies ran while one was open for 2% -> 10% of each run, Pallas kernels for 0% -> 5%
where the time goes in v4:
time: 97.2 us; the launch traced here: 96.9 us
  waiting for transfers between devices  30.2 us (31%)
  starting transfers between devices  28.6 us (29%)
  blocking collectives  16.5 us (17%)
  matrix products  9.31 us (10%)
  Pallas kernels  6.82 us (7%)
  local copies, waits for them, and re-layouts  5.17 us (5%)
    ppermute x28, waiting for transfers between devices, move(): return lax.ppermute(x, 'adapter', pairs(places, steps, flip))  30.2 us
    ppermute x28, starting transfers between devices, move(): return lax.ppermute(x, 'adapter', pairs(places, steps, flip))  28.6 us
    all_to_all x1, blocking collectives, shards(): lax.all_to_all(query, 'adapter', split_axis=0, concat_axis=1, tiled=True)  16.5 us
    dot_general x4, matrix products, matmul(): return jnp.dot(x, y, preferred_element_type=jnp.float32)  9.31 us
    pallas_call x4, Pallas kernels, prepare(): pl.pallas_call(prepare_kernel, out_shape=(jax.ShapeDtypeStruct((rows, wid...  5.32 us
    unnamed x20, local copies, waits for them, and re-layouts  4.31 us
  transfers between devices with their start and end apart: 28, of which 10 were waited for; matrix products, arithmetic and copies ran while one was open for 10% of the time, Pallas kernels for 5%

profile of v4, /device:TPU:0, one launch (start us, length us, event | category | flops | bytes accessed | tf_op | source)
XLA Modules:
  0.0 96.9 jit_solution(11707264152922760410)
XLA Ops:
  0.0 3.0 %collective-permute-start.6 = (bf16[24,8192]{1,0:T(8,128)(2,1)}, bf16[24,8192]{1,0:T(8,128)(2,1)S(1)}, u32[]{:S(2)}, u32[]{:S(2)}) collective-permute-start(bf16[24,8192]{1,0:T(8,128)(2,1)} %refs_0_.1), channel_id=1, source_target_pairs={{0,4},{1,5},{2,6},{3,7},{4,12},{5,13},{6,14},{7,15},{12,8},{13,9},... | collective-permute-start | bytes 1179656 | tf_op jit(solution)/shard_map/ppermute | solution.py:175
  3.0 1.5 %collective-permute-start.1 = (bf16[24,8192]{1,0:T(8,128)(2,1)}, bf16[24,8192]{1,0:T(8,128)(2,1)S(1)}, u32[]{:S(2)}, u32[]{:S(2)}) collective-permute-start(bf16[24,8192]{1,0:T(8,128)(2,1)} %refs_0_.1), channel_id=1, source_target_pairs={{0,2},{1,3},{2,0},{3,1},{4,6},{5,7},{6,4},{7,5},{12,14},{13,15},{1... | collective-permute-start | bytes 1179656 | tf_op jit(solution)/shard_map/ppermute | solution.py:175
  7.8 5.5 %collective-permute-done.6.refs_0_ = bf16[24,8192]{1,0:T(8,128)(2,1)S(1)} collective-permute-done((bf16[24,8192]{1,0:T(8,128)(2,1)}, bf16[24,8192]{1,0:T(8,128)(2,1)S(1)}, u32[]{:S(2)}, u32[]{:S(2)}) %collective-permute-start.6) | collective-permute-done | bytes 393248 | tf_op jit(solution)/shard_map/ppermute | solution.py:175
  13.4 1.6 %collective-permute-start.8 = (bf16[24,8192]{1,0:T(8,128)(2,1)S(1)}, bf16[24,8192]{1,0:T(8,128)(2,1)S(1)}, u32[]{:S(2)}, u32[]{:S(2)}) collective-permute-start(bf16[24,8192]{1,0:T(8,128)(2,1)S(1)} %collective-permute-done.6.refs_0_), channel_id=1, source_target_pairs={{0,2},{1,3},{2,0},{3,1},{4,6},{5,7},{6,4},{7,5},{12,14},{13,15},{1... | collective-permute-start | bytes 1179656 | tf_op jit(solution)/shard_map/ppermute | solution.py:175
  15.5 8.3 %collective-permute-done.5 = f32[8,128]{1,0:T(8,128)S(1)} collective-permute-done((f32[8,128]{1,0:T(8,128)S(1)}, f32[8,128]{1,0:T(8,128)S(1)}, u32[]{:S(2)}, u32[]{:S(2)}) %collective-permute-start.5) | collective-permute-done | bytes 4128 | tf_op jit(solution)/shard_map/ppermute | solution.py:175
  23.7 1.2 %collective-permute-start.12 = (bf16[24,8192]{1,0:T(8,128)(2,1)S(1)}, bf16[24,8192]{1,0:T(8,128)(2,1)S(1)}, u32[]{:S(2)}, u32[]{:S(2)}) collective-permute-start(bf16[24,8192]{1,0:T(8,128)(2,1)S(1)} %collective-permute-done.6.refs_0_), channel_id=1, source_target_pairs={{0,4},{1,5},{2,6},{3,7},{4,12},{5,13},{6,14},{7,15},{12,8},{13,9},... | collective-permute-start | bytes 1179656 | tf_op jit(solution)/shard_map/ppermute | solution.py:175
  25.5 8.5 %collective-permute-done.12.refs_0_ = bf16[24,8192]{1,0:T(8,128)(2,1)S(1)} collective-permute-done((bf16[24,8192]{1,0:T(8,128)(2,1)S(1)}, bf16[24,8192]{1,0:T(8,128)(2,1)S(1)}, u32[]{:S(2)}, u32[]{:S(2)}) %collective-permute-start.12) | collective-permute-done | bytes 393248 | tf_op jit(solution)/shard_map/ppermute | solution.py:175
  36.2 3.1 %collective-permute-start.10 = (f32[8,128]{1,0:T(8,128)S(1)}, f32[8,128]{1,0:T(8,128)S(1)}, u32[]{:S(2)}, u32[]{:S(2)}) collective-permute-start(f32[8,128]{1,0:T(8,128)S(1)} %maximum_maximum_fusion.refs_7_.refs_8_), channel_id=1, source_target_pairs={{0,4},{1,5},{2,6},{3,7},{4,12},{5,13},{6,14},{7,15},{12,8},{13,9},... | collective-permute-start | bytes 12296 | tf_op jit(solution)/shard_map/ppermute | solution.py:175
  39.3 1.2 %copy-done = bf16[1,8192,64]{1,2,0:T(8,128)(2,1)S(1)} copy-done((bf16[1,8192,64]{1,2,0:T(8,128)(2,1)S(1)}, bf16[1,8192,64]{1,2,0:T(8,128)(2,1)}, u32[]{:S(2)}) %copy-start) | copy-done | bytes 1048600
  42.3 1.3 %shard_map.74 = (bf16[96,8192]{1,0:T(8,128)(2,1)S(1)}, bf16[96,64]{1,0:T(8,128)(2,1)S(1)}) custom-call(bf16[24,8192]{1,0:T(8,128)(2,1)S(1)} %copy-done.5, bf16[24,8192]{1,0:T(8,128)(2,1)S(1)} %collective-permute-done.refs_1_, bf16[24,8192]{1,0:T(8,128)(2,1)S(1)} %collective-permute-done.1.refs_2_, bf16[24,8192]{1,0:T(8,128)(2,1)S(1)} %collective-permute-done.2.refs_3_, ...), custom_call_target="tpu_custom_call" | custom-call | flops 402653184 | bytes 3145728 | tf_op jit(solution)/shard_map/pallas_call | solution.py:118
  44.9 2.8 %collective-permute-start.16 = (f32[8,128]{1,0:T(8,128)S(1)}, f32[8,128]{1,0:T(8,128)S(1)}, u32[]{:S(2)}, u32[]{:S(2)}) collective-permute-start(f32[8,128]{1,0:T(8,128)S(1)} %maximum_maximum_fusion.refs_7_.refs_8_), channel_id=1, source_target_pairs={{0,12},{1,13},{2,14},{3,15},{4,8},{5,9},{6,10},{7,11},{12,0},{13,1... | collective-permute-start | bytes 12296 | tf_op jit(solution)/shard_map/ppermute | solution.py:175
  48.8 1.3 %shard_map.75 = (bf16[96,8192]{1,0:T(8,128)(2,1)S(1)}, bf16[96,64]{1,0:T(8,128)(2,1)S(1)}) custom-call(bf16[24,8192]{1,0:T(8,128)(2,1)S(1)} %collective-permute-done.6.refs_0_, bf16[24,8192]{1,0:T(8,128)(2,1)S(1)} %collective-permute-done.7.refs_1_, bf16[24,8192]{1,0:T(8,128)(2,1)S(1)} %collective-permute-done.8.refs_2_, ...), custom_call_target="tpu_custom_call" | custom-call | flops 402653184 | bytes 3145728 | tf_op jit(solution)/shard_map/pallas_call | solution.py:118
  52.2 5.0 %fusion.1.refs_0_ = f32[96,512]{1,0:T(8,128)S(1)} fusion(bf16[96,8192]{1,0:T(8,128)(2,1)S(1)} %get-tuple-element.13, bf16[8192,512]{1,0:T(8,128)(2,1)} %param.9), kind=kOutput, calls=%fused_computation.5 | convolution fusion | flops 805306368 | bytes 10158080 | tf_op jit(solution)/shard_map/dot_general | solution.py:178
  57.2 2.6 %collective-permute-start.22 = (f32[8,128]{1,0:T(8,128)S(1)}, f32[8,128]{1,0:T(8,128)S(1)}, u32[]{:S(2)}, u32[]{:S(2)}) collective-permute-start(f32[8,128]{1,0:T(8,128)S(1)} %maximum_maximum_fusion.refs_7_.refs_8_), channel_id=1, source_target_pairs={{0,8},{1,9},{2,10},{3,11},{4,0},{5,1},{6,2},{7,3},{12,4},{13,5},{1... | collective-permute-start | bytes 12296 | tf_op jit(solution)/shard_map/ppermute | solution.py:175
  59.8 1.3 %shard_map.76 = (bf16[96,8192]{1,0:T(8,128)(2,1)S(1)}, bf16[96,64]{1,0:T(8,128)(2,1)S(1)}) custom-call(bf16[24,8192]{1,0:T(8,128)(2,1)S(1)} %collective-permute-done.12.refs_0_, bf16[24,8192]{1,0:T(8,128)(2,1)S(1)} %collective-permute-done.13.refs_1_, bf16[24,8192]{1,0:T(8,128)(2,1)S(1)} %collective-permute-done.14.refs_2_, ...), custom_call_target="tpu_custom_call" | custom-call | flops 402653184 | bytes 3145728 | tf_op jit(solution)/shard_map/pallas_call | solution.py:118
  62.8 1.4 %fusion.2.refs_1_ = f32[96,512]{1,0:T(8,128)S(1)} fusion(bf16[96,8192]{1,0:T(8,128)(2,1)S(1)} %get-tuple-element.15, bf16[8192,512]{1,0:T(8,128)(2,1)S(1)} %bitcast.29), kind=kOutput, calls=%fused_computation.6 | convolution fusion | flops 805306368 | bytes 10158080 | tf_op jit(solution)/shard_map/dot_general | solution.py:178
  64.2 1.7 %collective-permute-done.23.refs_8_ = bf16[96,64]{1,0:T(8,128)(2,1)S(1)} collective-permute-done((bf16[96,64]{1,0:T(8,128)(2,1)S(1)}, bf16[96,64]{1,0:T(8,128)(2,1)S(1)}, u32[]{:S(2)}, u32[]{:S(2)}) %collective-permute-start.23) | collective-permute-done | bytes 12320 | tf_op jit(solution)/shard_map/ppermute | solution.py:175
  65.9 1.3 %shard_map.77 = (bf16[96,8192]{1,0:T(8,128)(2,1)S(1)}, bf16[96,64]{1,0:T(8,128)(2,1)S(1)}) custom-call(bf16[24,8192]{1,0:T(8,128)(2,1)S(1)} %collective-permute-done.18.refs_0_, bf16[24,8192]{1,0:T(8,128)(2,1)S(1)} %collective-permute-done.19.refs_1_, bf16[24,8192]{1,0:T(8,128)(2,1)S(1)} %collective-permute-done.20.refs_2_, ...), custom_call_target="tpu_custom_call" | custom-call | flops 402653184 | bytes 3145728 | tf_op jit(solution)/shard_map/pallas_call | solution.py:118
  68.0 1.4 %fusion.3.refs_2_ = f32[96,512]{1,0:T(8,128)S(1)} fusion(bf16[96,8192]{1,0:T(8,128)(2,1)S(1)} %get-tuple-element.17, bf16[8192,512]{1,0:T(8,128)(2,1)S(1)} %bitcast.29), kind=kOutput, calls=%fused_computation.7 | convolution fusion | flops 805306368 | bytes 10158080 | tf_op jit(solution)/shard_map/dot_general | solution.py:178
  69.5 1.7 %collective-permute-done.24 = bf16[96,64]{1,0:T(8,128)(2,1)S(1)} collective-permute-done((bf16[96,64]{1,0:T(8,128)(2,1)S(1)}, bf16[96,64]{1,0:T(8,128)(2,1)S(1)}, u32[]{:S(2)}, u32[]{:S(2)}) %collective-permute-start.24) | collective-permute-done | bytes 12320 | tf_op jit(solution)/shard_map/ppermute | solution.py:175
  71.2 1.8 %collective-permute-start.25 = (bf16[96,64]{1,0:T(8,128)(2,1)S(1)}, bf16[96,64]{1,0:T(8,128)(2,1)S(1)}, u32[]{:S(2)}, u32[]{:S(2)}) collective-permute-start(bf16[96,64]{1,0:T(8,128)(2,1)S(1)} %maximum_add_fusion.refs_7_), channel_id=1, source_target_pairs={{0,4},{1,5},{2,6},{3,7},{4,12},{5,13},{6,14},{7,15},{12,8},{13,9},... | collective-permute-start | bytes 36872 | tf_op jit(solution)/shard_map/ppermute | solution.py:175
  74.1 1.9 %collective-permute-start.27 = (bf16[96,64]{1,0:T(8,128)(2,1)S(1)}, bf16[96,64]{1,0:T(8,128)(2,1)S(1)}, u32[]{:S(2)}, u32[]{:S(2)}) collective-permute-start(bf16[96,64]{1,0:T(8,128)(2,1)S(1)} %maximum_add_fusion.refs_7_), channel_id=1, source_target_pairs={{0,8},{1,9},{2,10},{3,11},{4,0},{5,1},{6,2},{7,3},{12,4},{13,5},{1... | collective-permute-start | bytes 36872 | tf_op jit(solution)/shard_map/ppermute | solution.py:175
  76.1 1.4 %fusion.4.refs_3_ = f32[96,512]{1,0:T(8,128)S(1)} fusion(bf16[96,8192]{1,0:T(8,128)(2,1)S(1)} %get-tuple-element.19, bf16[8192,512]{1,0:T(8,128)(2,1)S(1)} %bitcast.29), kind=kOutput, calls=%fused_computation.8 | convolution fusion | flops 805306368 | bytes 10158080 | tf_op jit(solution)/shard_map/dot_general | solution.py:178
  79.6 16.5 %all_to_all.16 = bf16[16,24,512]{2,1,0:T(8,128)(2,1)S(1)} all-to-all(bf16[16,24,512]{2,1,0:T(8,128)(2,1)S(1)} %shard_map.78), channel_id=1, replica_groups=mesh['group'=2,'adapter'=16] {'adapter'}, dimensions={0} | all-to-all | bytes 786432 | tf_op jit(solution)/shard_map/all_to_all | solution.py:207
  (75 shorter events, 19.1 us)
Async XLA Ops:
  0.0 13.4 %collective-permute-start.6 = (bf16[24,8192]{1,0:T(8,128)(2,1)}, bf16[24,8192]{1,0:T(8,128)(2,1)S(1)}, u32[]{:S(2)}, u32[]{:S(2)}) collective-permute-start(bf16[24,8192]{1,0:T(8,128)(2,1)} %refs_0_.1), channel_id=1, source_target_pairs={{0,4},{1,5},{2,6},{3,7},{4,12},{5,13},{6,14},{7,15},{12,8},{13,9},... | collective-permute-start | bytes 1179656 | tf_op jit(solution)/shard_map/ppermute | solution.py:175
  3.0 21.9 %collective-permute-start.1 = (bf16[24,8192]{1,0:T(8,128)(2,1)}, bf16[24,8192]{1,0:T(8,128)(2,1)S(1)}, u32[]{:S(2)}, u32[]{:S(2)}) collective-permute-start(bf16[24,8192]{1,0:T(8,128)(2,1)} %refs_0_.1), channel_id=1, source_target_pairs={{0,2},{1,3},{2,0},{3,1},{4,6},{5,7},{6,4},{7,5},{12,14},{13,15},{1... | collective-permute-start | bytes 1179656 | tf_op jit(solution)/shard_map/ppermute | solution.py:175
  4.5 31.6 %collective-permute-start.3 = (bf16[64,8192]{1,0:T(8,128)(2,1)}, bf16[64,8192]{1,0:T(8,128)(2,1)S(1)}, u32[]{:S(2)}, u32[]{:S(2)}) collective-permute-start(bf16[64,8192]{1,0:T(8,128)(2,1)} %bitcast.17), channel_id=1, source_target_pairs={{0,1},{1,0},{2,3},{3,2},{4,5},{5,4},{6,7},{7,6},{12,13},{13,12},{1... | collective-permute-start | bytes 3145736 | tf_op jit(solution)/shard_map/ppermute | solution.py:175
  7.0 17.9 %collective-permute-start = (bf16[24,8192]{1,0:T(8,128)(2,1)}, bf16[24,8192]{1,0:T(8,128)(2,1)S(1)}, u32[]{:S(2)}, u32[]{:S(2)}) collective-permute-start(bf16[24,8192]{1,0:T(8,128)(2,1)} %refs_0_.1), channel_id=1, source_target_pairs={{0,1},{1,0},{2,3},{3,2},{4,5},{5,4},{6,7},{7,6},{12,13},{13,12},{1... | collective-permute-start | bytes 1179656 | tf_op jit(solution)/shard_map/ppermute | solution.py:175
  13.4 12.1 %collective-permute-start.8 = (bf16[24,8192]{1,0:T(8,128)(2,1)S(1)}, bf16[24,8192]{1,0:T(8,128)(2,1)S(1)}, u32[]{:S(2)}, u32[]{:S(2)}) collective-permute-start(bf16[24,8192]{1,0:T(8,128)(2,1)S(1)} %collective-permute-done.6.refs_0_), channel_id=1, source_target_pairs={{0,2},{1,3},{2,0},{3,1},{4,6},{5,7},{6,4},{7,5},{12,14},{13,15},{1... | collective-permute-start | bytes 1179656 | tf_op jit(solution)/shard_map/ppermute | solution.py:175
  14.9 8.8 %collective-permute-start.5 = (f32[8,128]{1,0:T(8,128)S(1)}, f32[8,128]{1,0:T(8,128)S(1)}, u32[]{:S(2)}, u32[]{:S(2)}) collective-permute-start(f32[8,128]{1,0:T(8,128)S(1)} %pad_maximum_fusion), channel_id=1, source_target_pairs={{0,2},{1,3},{2,0},{3,1},{4,6},{5,7},{6,4},{7,5},{12,14},{13,15},{1... | collective-permute-start | bytes 12296 | tf_op jit(solution)/shard_map/ppermute | solution.py:175
  23.7 10.3 %collective-permute-start.12 = (bf16[24,8192]{1,0:T(8,128)(2,1)S(1)}, bf16[24,8192]{1,0:T(8,128)(2,1)S(1)}, u32[]{:S(2)}, u32[]{:S(2)}) collective-permute-start(bf16[24,8192]{1,0:T(8,128)(2,1)S(1)} %collective-permute-done.6.refs_0_), channel_id=1, source_target_pairs={{0,4},{1,5},{2,6},{3,7},{4,12},{5,13},{6,14},{7,15},{12,8},{13,9},... | collective-permute-start | bytes 1179656 | tf_op jit(solution)/shard_map/ppermute | solution.py:175
  24.9 10.1 %collective-permute-start.2 = (bf16[24,8192]{1,0:T(8,128)(2,1)S(1)}, bf16[24,8192]{1,0:T(8,128)(2,1)S(1)}, u32[]{:S(2)}, u32[]{:S(2)}) collective-permute-start(bf16[24,8192]{1,0:T(8,128)(2,1)S(1)} %collective-permute-done.1.refs_2_), channel_id=1, source_target_pairs={{0,1},{1,0},{2,3},{3,2},{4,5},{5,4},{6,7},{7,6},{12,13},{13,12},{1... | collective-permute-start | bytes 1179656 | tf_op jit(solution)/shard_map/ppermute | solution.py:175
  24.9 20.0 %collective-permute-start.7 = (bf16[24,8192]{1,0:T(8,128)(2,1)S(1)}, bf16[24,8192]{1,0:T(8,128)(2,1)S(1)}, u32[]{:S(2)}, u32[]{:S(2)}) collective-permute-start(bf16[24,8192]{1,0:T(8,128)(2,1)S(1)} %collective-permute-done.6.refs_0_), channel_id=1, source_target_pairs={{0,1},{1,0},{2,3},{3,2},{4,5},{5,4},{6,7},{7,6},{12,13},{13,12},{1... | collective-permute-start | bytes 1179656 | tf_op jit(solution)/shard_map/ppermute | solution.py:175
  25.4 23.4 %collective-permute-start.9 = (bf16[24,8192]{1,0:T(8,128)(2,1)S(1)}, bf16[24,8192]{1,0:T(8,128)(2,1)S(1)}, u32[]{:S(2)}, u32[]{:S(2)}) collective-permute-start(bf16[24,8192]{1,0:T(8,128)(2,1)S(1)} %collective-permute-done.8.refs_2_), channel_id=1, source_target_pairs={{0,1},{1,0},{2,3},{3,2},{4,5},{5,4},{6,7},{7,6},{12,13},{13,12},{1... | collective-permute-start | bytes 1179656 | tf_op jit(solution)/shard_map/ppermute | solution.py:175
  34.0 17.2 %collective-permute-start.14 = (bf16[24,8192]{1,0:T(8,128)(2,1)S(1)}, bf16[24,8192]{1,0:T(8,128)(2,1)S(1)}, u32[]{:S(2)}, u32[]{:S(2)}) collective-permute-start(bf16[24,8192]{1,0:T(8,128)(2,1)S(1)} %collective-permute-done.12.refs_0_), channel_id=1, source_target_pairs={{0,2},{1,3},{2,0},{3,1},{4,6},{5,7},{6,4},{7,5},{12,14},{13,15},{1... | collective-permute-start | bytes 1179656 | tf_op jit(solution)/shard_map/ppermute | solution.py:175
  35.0 16.5 %collective-permute-start.18 = (bf16[24,8192]{1,0:T(8,128)(2,1)S(1)}, bf16[24,8192]{1,0:T(8,128)(2,1)S(1)}, u32[]{:S(2)}, u32[]{:S(2)}) collective-permute-start(bf16[24,8192]{1,0:T(8,128)(2,1)S(1)} %collective-permute-done.12.refs_0_), channel_id=1, source_target_pairs={{0,4},{1,5},{2,6},{3,7},{4,12},{5,13},{6,14},{7,15},{12,8},{13,9},... | collective-permute-start | bytes 1179656 | tf_op jit(solution)/shard_map/ppermute | solution.py:175
  36.2 7.9 %collective-permute-start.10 = (f32[8,128]{1,0:T(8,128)S(1)}, f32[8,128]{1,0:T(8,128)S(1)}, u32[]{:S(2)}, u32[]{:S(2)}) collective-permute-start(f32[8,128]{1,0:T(8,128)S(1)} %maximum_maximum_fusion.refs_7_.refs_8_), channel_id=1, source_target_pairs={{0,4},{1,5},{2,6},{3,7},{4,12},{5,13},{6,14},{7,15},{12,8},{13,9},... | collective-permute-start | bytes 12296 | tf_op jit(solution)/shard_map/ppermute | solution.py:175
  44.1 4.7 %collective-permute-start.11 = (bf16[96,64]{1,0:T(8,128)(2,1)S(1)}, bf16[96,64]{1,0:T(8,128)(2,1)S(1)}, u32[]{:S(2)}, u32[]{:S(2)}) collective-permute-start(bf16[96,64]{1,0:T(8,128)(2,1)S(1)} %get-tuple-element.14), channel_id=1, source_target_pairs={{0,4},{1,5},{2,6},{3,7},{4,12},{5,13},{6,14},{7,15},{12,8},{13,9},... | collective-permute-start | bytes 36872 | tf_op jit(solution)/shard_map/ppermute | solution.py:175
  44.9 12.2 %collective-permute-start.16 = (f32[8,128]{1,0:T(8,128)S(1)}, f32[8,128]{1,0:T(8,128)S(1)}, u32[]{:S(2)}, u32[]{:S(2)}) collective-permute-start(f32[8,128]{1,0:T(8,128)S(1)} %maximum_maximum_fusion.refs_7_.refs_8_), channel_id=1, source_target_pairs={{0,12},{1,13},{2,14},{3,15},{4,8},{5,9},{6,10},{7,11},{12,0},{13,1... | collective-permute-start | bytes 12296 | tf_op jit(solution)/shard_map/ppermute | solution.py:175
  48.8 11.0 %collective-permute-start.13 = (bf16[24,8192]{1,0:T(8,128)(2,1)S(1)}, bf16[24,8192]{1,0:T(8,128)(2,1)S(1)}, u32[]{:S(2)}, u32[]{:S(2)}) collective-permute-start(bf16[24,8192]{1,0:T(8,128)(2,1)S(1)} %collective-permute-done.12.refs_0_), channel_id=1, source_target_pairs={{0,1},{1,0},{2,3},{3,2},{4,5},{5,4},{6,7},{7,6},{12,13},{13,12},{1... | collective-permute-start | bytes 1179656 | tf_op jit(solution)/shard_map/ppermute | solution.py:175
  50.2 9.6 %collective-permute-start.17 = (bf16[96,64]{1,0:T(8,128)(2,1)S(1)}, bf16[96,64]{1,0:T(8,128)(2,1)S(1)}, u32[]{:S(2)}, u32[]{:S(2)}) collective-permute-start(bf16[96,64]{1,0:T(8,128)(2,1)S(1)} %get-tuple-element.16), channel_id=1, source_target_pairs={{0,4},{1,5},{2,6},{3,7},{4,12},{5,13},{6,14},{7,15},{12,8},{13,9},... | collective-permute-start | bytes 36872 | tf_op jit(solution)/shard_map/ppermute | solution.py:175
  51.2 8.6 %collective-permute-start.15 = (bf16[24,8192]{1,0:T(8,128)(2,1)S(1)}, bf16[24,8192]{1,0:T(8,128)(2,1)S(1)}, u32[]{:S(2)}, u32[]{:S(2)}) collective-permute-start(bf16[24,8192]{1,0:T(8,128)(2,1)S(1)} %collective-permute-done.14.refs_2_), channel_id=1, source_target_pairs={{0,1},{1,0},{2,3},{3,2},{4,5},{5,4},{6,7},{7,6},{12,13},{13,12},{1... | collective-permute-start | bytes 1179656 | tf_op jit(solution)/shard_map/ppermute | solution.py:175
  51.4 11.3 %collective-permute-start.20 = (bf16[24,8192]{1,0:T(8,128)(2,1)S(1)}, bf16[24,8192]{1,0:T(8,128)(2,1)S(1)}, u32[]{:S(2)}, u32[]{:S(2)}) collective-permute-start(bf16[24,8192]{1,0:T(8,128)(2,1)S(1)} %collective-permute-done.18.refs_0_), channel_id=1, source_target_pairs={{0,2},{1,3},{2,0},{3,1},{4,6},{5,7},{6,4},{7,5},{12,14},{13,15},{1... | collective-permute-start | bytes 1179656 | tf_op jit(solution)/shard_map/ppermute | solution.py:175
  57.2 7.1 %collective-permute-start.22 = (f32[8,128]{1,0:T(8,128)S(1)}, f32[8,128]{1,0:T(8,128)S(1)}, u32[]{:S(2)}, u32[]{:S(2)}) collective-permute-start(f32[8,128]{1,0:T(8,128)S(1)} %maximum_maximum_fusion.refs_7_.refs_8_), channel_id=1, source_target_pairs={{0,8},{1,9},{2,10},{3,11},{4,0},{5,1},{6,2},{7,3},{12,4},{13,5},{1... | collective-permute-start | bytes 12296 | tf_op jit(solution)/shard_map/ppermute | solution.py:175
  61.1 4.8 %collective-permute-start.23 = (bf16[96,64]{1,0:T(8,128)(2,1)S(1)}, bf16[96,64]{1,0:T(8,128)(2,1)S(1)}, u32[]{:S(2)}, u32[]{:S(2)}) collective-permute-start(bf16[96,64]{1,0:T(8,128)(2,1)S(1)} %get-tuple-element.18), channel_id=1, source_target_pairs={{0,4},{1,5},{2,6},{3,7},{4,12},{5,13},{6,14},{7,15},{12,8},{13,9},... | collective-permute-start | bytes 36872 | tf_op jit(solution)/shard_map/ppermute | solution.py:175
  71.2 6.3 %collective-permute-start.25 = (bf16[96,64]{1,0:T(8,128)(2,1)S(1)}, bf16[96,64]{1,0:T(8,128)(2,1)S(1)}, u32[]{:S(2)}, u32[]{:S(2)}) collective-permute-start(bf16[96,64]{1,0:T(8,128)(2,1)S(1)} %maximum_add_fusion.refs_7_), channel_id=1, source_target_pairs={{0,4},{1,5},{2,6},{3,7},{4,12},{5,13},{6,14},{7,15},{12,8},{13,9},... | collective-permute-start | bytes 36872 | tf_op jit(solution)/shard_map/ppermute | solution.py:175
  73.0 5.6 %collective-permute-start.26 = (bf16[96,64]{1,0:T(8,128)(2,1)S(1)}, bf16[96,64]{1,0:T(8,128)(2,1)S(1)}, u32[]{:S(2)}, u32[]{:S(2)}) collective-permute-start(bf16[96,64]{1,0:T(8,128)(2,1)S(1)} %maximum_add_fusion.refs_7_), channel_id=1, source_target_pairs={{0,12},{1,13},{2,14},{3,15},{4,8},{5,9},{6,10},{7,11},{12,0},{13,1... | collective-permute-start | bytes 36872 | tf_op jit(solution)/shard_map/ppermute | solution.py:175
  74.1 4.5 %collective-permute-start.27 = (bf16[96,64]{1,0:T(8,128)(2,1)S(1)}, bf16[96,64]{1,0:T(8,128)(2,1)S(1)}, u32[]{:S(2)}, u32[]{:S(2)}) collective-permute-start(bf16[96,64]{1,0:T(8,128)(2,1)S(1)} %maximum_add_fusion.refs_7_), channel_id=1, source_target_pairs={{0,8},{1,9},{2,10},{3,11},{4,0},{5,1},{6,2},{7,3},{12,4},{13,5},{1... | collective-permute-start | bytes 36872 | tf_op jit(solution)/shard_map/ppermute | solution.py:175
  (14 other events, 55.1 us)

commit v5 on v4

--- a/solution.py
+++ b/solution.py
@@ -32,6 +32,13 @@
     return out
 
 
+def split_pairs(places):
+    flips, steps = pairs(places, 0, 2), pairs(places, 1, 0)
+    return [pair for pair in flips if pair[0] % CORES == 0] + [
+        pair for pair in steps if pair[0] % CORES
+    ]
+
+
 def ring_device(places, steps, flip):
     me = lax.axis_index("adapter")
     ring = line_ring(places)
@@ -42,63 +49,64 @@
     return target * CORNERS + (corner ^ flip)
 
 
-def slots_kernel(index_ref, slot_ref, out_ref):
+def slot_column(blocks, width):
+    return jnp.concatenate(
+        [block[:, width : width + 1].astype(jnp.float32) for block in blocks], axis=0
+    ).astype(jnp.int32)
+
+
+def norm_kernel(hidden_ref, gain_ref, index_ref, slot_ref, out_ref):
+    rows, width = hidden_ref.shape
+    squares = jnp.zeros((rows, LANES), jnp.float32)
+    for start in range(0, width, CHUNK):
+        wide = hidden_ref[:, start : start + CHUNK].astype(jnp.float32)
+        wide = wide * wide
+        for lane in range(0, CHUNK, LANES):
+            squares = squares + wide[:, lane : lane + LANES]
+    inv_rms = lax.rsqrt(jnp.sum(squares, axis=1, keepdims=True) / width + EPS)
+    for start in range(0, width, CHUNK):
+        lanes = slice(start, start + CHUNK)
+        wide = hidden_ref[:, lanes].astype(jnp.float32)
+        out_ref[:, lanes] = (wide * inv_rms * gain_ref[:, lanes]).astype(jnp.bfloat16)
     index = index_ref[...]
     slot = jnp.zeros(index.shape, jnp.float32)
     for name in range(slot_ref.shape[0]):
         slot = jnp.where(index == name, slot_ref[name].astype(jnp.float32), slot)
-    out_ref[...] = jnp.zeros(out_ref.shape, jnp.float32)
-    out_ref[0:1, 0 : index.shape[1]] = slot
-
-
-def own_slots(adapter_index, adapter_slot):
-    rows = adapter_index.shape[0]
+    across = lax.broadcasted_iota(jnp.int32, (rows, rows), 1)
+    down = lax.broadcasted_iota(jnp.int32, (rows, rows), 0)
+    column = jnp.sum(jnp.where(across == down, slot, 0.0), axis=1, keepdims=True)
+    out_ref[:, width:] = jnp.broadcast_to(column, (rows, LANES)).astype(jnp.bfloat16)
+
+
+def normalize(hidden, norm_weight, adapter_index, adapter_slot):
+    rows, width = hidden.shape
     vmem = pl.BlockSpec(memory_space=pltpu.VMEM)
     return pl.pallas_call(
-        slots_kernel,
-        out_shape=jax.ShapeDtypeStruct((8, LANES), jnp.float32),
-        in_specs=[vmem, pl.BlockSpec(memory_space=pltpu.SMEM)],
+        norm_kernel,
+        out_shape=jax.ShapeDtypeStruct((rows, width + LANES), jnp.bfloat16),
+        in_specs=[vmem, vmem, vmem, pl.BlockSpec(memory_space=pltpu.SMEM)],
         out_specs=vmem,
         compiler_params=pltpu.CompilerParams(vmem_limit_bytes=SMALL),
-    )(adapter_index.reshape(1, rows), adapter_slot)
-
-
-def slot_column(slots_ref, own_rows):
-    across = lax.broadcasted_iota(jnp.int32, (own_rows, LANES), 1)
-    down = lax.broadcasted_iota(jnp.int32, (own_rows, LANES), 0)
-    columns = []
-    for corner in range(CORNERS):
-        row = slots_ref[corner : corner + 1, :]
-        columns.append(jnp.sum(jnp.where(across == down, row, 0.0), axis=1, keepdims=True))
-    return jnp.concatenate(columns, axis=0).astype(jnp.int32)
+    )(hidden, norm_weight.reshape(1, width), adapter_index.reshape(1, rows), adapter_slot)
 
 
 def prepare_kernel(*refs):
     blocks, refs = refs[:CORNERS], refs[CORNERS:]
-    gain_ref, own_ref, other_ref, slots_ref, *before, rows_ref, part_ref = refs
-    own_rows, width = blocks[0].shape
-    rank = own_ref.shape[0]
-    inverse = []
-    for block in blocks:
-        squares = jnp.zeros((own_rows, LANES), jnp.float32)
-        for start in range(0, width, CHUNK):
-            wide = block[:, start : start + CHUNK].astype(jnp.float32)
-            wide = wide * wide
-            for lane in range(0, CHUNK, LANES):
-                squares = squares + wide[:, lane : lane + LANES]
-        inverse.append(lax.rsqrt(jnp.sum(squares, axis=1, keepdims=True) / width + EPS))
-    part = jnp.zeros((own_rows * CORNERS, 2 * rank), jnp.float32)
+    own_ref, other_ref, *before, rows_ref, part_ref, slot_ref = refs
+    rank, width = own_ref.shape
+    rows = rows_ref.shape[0]
+    part = jnp.zeros((rows, 2 * rank), jnp.float32)
     for start in range(0, width, CHUNK):
         lanes = slice(start, start + CHUNK)
-        gain = gain_ref[:, lanes]
-        wide = [block[:, lanes].astype(jnp.float32) * inv * gain for block, inv in zip(blocks, inverse)]
-        rows = jnp.concatenate(wide, axis=0).astype(jnp.bfloat16)
-        rows_ref[:, lanes] = rows
+        wide = [block[:, lanes].astype(jnp.float32) for block in blocks]
+        chunk = jnp.concatenate(wide, axis=0).astype(jnp.bfloat16)
+        rows_ref[:, lanes] = chunk
         down = jnp.concatenate([own_ref[:, lanes], other_ref[:, lanes]], axis=0)
         part += lax.dot_general(
-            rows, down, (((1,), (1,)), ((), ())), preferred_element_type=jnp.float32
+            chunk, down, (((1,), (1,)), ((), ())), preferred_element_type=jnp.float32
         )
-    slot = slot_column(slots_ref, own_rows)
+    slot = slot_column(blocks, width)
+    slot_ref[...] = jnp.broadcast_to(slot, slot_ref.shape)
     me = lax.axis_index("adapter")
     lanes = lax.broadcasted_iota(jnp.int32, part.shape, 1)
     holder = jnp.where(lanes < rank, me, me ^ 1)
@@ -109,10 +117,9 @@
     part_ref[...] = part.astype(jnp.bfloat16)
 
 
-def prepare(blocks, gain, own, other, slots, before):
-    own_rows, width = blocks[0].shape
-    rank = own.shape[0]
-    rows = own_rows * CORNERS
+def prepare(blocks, own, other, before):
+    rows = blocks[0].shape[0] * CORNERS
+    rank, width = own.shape
     before = [] if before is None else [before]
     vmem = pl.BlockSpec(memory_space=pltpu.VMEM)
     return pl.pallas_call(
@@ -120,14 +127,15 @@
         out_shape=(
             jax.ShapeDtypeStruct((rows, width), jnp.bfloat16),
             jax.ShapeDtypeStruct((rows, rank), jnp.bfloat16),
+            jax.ShapeDtypeStruct((rows, LANES), jnp.int32),
         ),
-        in_specs=[vmem] * (CORNERS + 4 + len(before)),
-        out_specs=(vmem, vmem),
+        in_specs=[vmem] * (CORNERS + 2 + len(before)),
+        out_specs=(vmem, vmem, vmem),
         compiler_params=pltpu.CompilerParams(vmem_limit_bytes=SMALL),
         cost_estimate=pl.CostEstimate(
-            flops=2 * rows * width * 256, bytes_accessed=rows * width * 4, transcendentals=rows
+            flops=2 * rows * width * 256, bytes_accessed=rows * width * 4, transcendentals=0
         ),
-    )(*blocks, gain, own, other, slots, *before)
+    )(*blocks, own, other, *before)
 
 
 def finish_kernel(places, devices, *refs):
@@ -139,7 +147,7 @@
     for step in range(places):
         shrink = shrinks[step][...].astype(jnp.float32)
         wide = jnp.concatenate([shrink] * devices, axis=1)
-        slot = slot_column(slots[step], own_rows)
+        slot = slots[step][:, 0:1]
         spread = jnp.where(lanes // rank == slot, wide, 0.0).astype(jnp.bfloat16)
         update = jnp.dot(spread, up_ref[...], preferred_element_type=jnp.float32)
         query = (bases[step][...] + ADAPTER_SCALE * update).astype(jnp.bfloat16)
@@ -177,25 +185,23 @@
     def matmul(x, y):
         return jnp.dot(x, y, preferred_element_type=jnp.float32)
 
-    slots = own_slots(adapter_index, adapter_slot)
-    empty = jnp.zeros((8 - CORNERS, LANES), jnp.float32)
-    pair = jnp.concatenate([slots[:1], move(slots, 0, 1)[:1], slots[2:]], axis=0)
-    four = jnp.concatenate([pair[:2], move(pair, 0, 2)[:2], empty], axis=0)
-    slots = [four] + [move(four, step, 0) for step in range(1, places)]
-
-    chain = hidden
-    gain = norm_weight.reshape(1, width)
+    chain = normalize(hidden, norm_weight, adapter_index, adapter_slot)
     down = down_weights[0].T
     down_other = move(down, 0, 1)
 
-    bases, travelling = [], None
+    bases, slots, travelling, other_y = [], [], None, None
     for step in range(places):
         if step:
             chain = move(chain, 1, 0)
-        other_y = move(chain, 0, 2)
+        if step < places - 1:
+            other_y = move(chain, 0, 2)
+        else:
+            source = jnp.where(me % CORES == 0, chain, other_y)
+            other_y = lax.ppermute(source, "adapter", split_pairs(places))
         blocks = [chain, move(chain, 0, 1), other_y, move(other_y, 0, 1)]
         before = None if travelling is None else move(travelling, 1, 0)
-        rows, travelling = prepare(blocks, gain, down, down_other, slots[step], before)
+        rows, travelling, slot = prepare(blocks, down, down_other, before)
+        slots.append(slot)
         bases.append(matmul(rows, query_weight))
 
     blocks = move(travelling, 0, 2).reshape(CORNERS, own_rows, rank)

time: 97.2 us -> 88.3 us (0.908)
  waiting for transfers between devices: 30.2 us -> 25.3 us
  starting transfers between devices: 28.6 us -> 24 us
  local copies, waits for them, and re-layouts: 5.17 us -> 6.27 us
    ppermute x28 -> x22, starting transfers between devices: 28.6 us -> 23.5 us  [move(): return lax.ppermute(x, 'adapter', pairs(places, steps, flip))]
    ppermute x28 -> x22, waiting for transfers between devices: 30.2 us -> 25.3 us  [move(): return lax.ppermute(x, 'adapter', pairs(places, steps, flip))]
    unnamed x20 -> x22, local copies, waits for them, and re-layouts: 4.31 us -> 5.49 us
  transfers between devices with their start and end apart: 28 -> 23, of which waited for: 10 -> 7; matrix products, arithmetic and copies ran while one was open for 10% -> 11% of each run, Pallas kernels for 5% -> 5%
where the time goes in v5:
time: 88.3 us; the launch traced here: 88 us
  waiting for transfers between devices  25.3 us (29%)
  starting transfers between devices  24 us (27%)
  blocking collectives  16.4 us (19%)
  matrix products  9.3 us (11%)
  Pallas kernels  6.48 us (7%)
  local copies, waits for them, and re-layouts  6.27 us (7%)
    ppermute x22, waiting for transfers between devices, move(): return lax.ppermute(x, 'adapter', pairs(places, steps, flip))  25.3 us
    ppermute x22, starting transfers between devices, move(): return lax.ppermute(x, 'adapter', pairs(places, steps, flip))  23.5 us
    all_to_all x1, blocking collectives, shards(): lax.all_to_all(query, 'adapter', split_axis=0, concat_axis=1, tiled=True)  16.4 us
    dot_general x4, matrix products, matmul(): return jnp.dot(x, y, preferred_element_type=jnp.float32)  9.3 us
    unnamed x22, local copies, waits for them, and re-layouts  5.49 us
    pallas_call x4, Pallas kernels, prepare(): pl.pallas_call(prepare_kernel, out_shape=(jax.ShapeDtypeStruct((rows, wid...  4.84 us
  transfers between devices with their start and end apart: 23, of which 7 were waited for; matrix products, arithmetic and copies ran while one was open for 11% of the time, Pallas kernels for 5%

profile of v5, /device:TPU:0, one launch (start us, length us, event | category | flops | bytes accessed | tf_op | source)
XLA Modules:
  0.0 88.0 jit_solution(16693736253293874348)
XLA Ops:
  0.0 1.0 %copy-done.5 = bf16[24,8192]{1,0:T(8,128)(2,1)S(1)} copy-done((bf16[24,8192]{1,0:T(8,128)(2,1)S(1)}, bf16[24,8192]{1,0:T(8,128)(2,1)}, u32[]{:S(2)}) %copy-start.5) | copy-done | bytes 393240
  3.9 3.1 %collective-permute-start.4 = (bf16[24,8320]{1,0:T(8,128)(2,1)S(1)}, bf16[24,8320]{1,0:T(8,128)(2,1)}, u32[]{:S(2)}, u32[]{:S(2)}) collective-permute-start(bf16[24,8320]{1,0:T(8,128)(2,1)S(1)} %shard_map.73.refs_0_), channel_id=1, source_target_pairs={{0,4},{1,5},{2,6},{3,7},{4,12},{5,13},{6,14},{7,15},{12,8},{13,9},... | collective-permute-start | bytes 1198088 | tf_op jit(solution)/shard_map/ppermute | solution.py:183
  6.9 1.5 %collective-permute-start.1 = (bf16[24,8320]{1,0:T(8,128)(2,1)S(1)}, bf16[24,8320]{1,0:T(8,128)(2,1)S(1)}, u32[]{:S(2)}, u32[]{:S(2)}) collective-permute-start(bf16[24,8320]{1,0:T(8,128)(2,1)S(1)} %shard_map.73.refs_0_), channel_id=1, source_target_pairs={{0,2},{1,3},{2,0},{3,1},{4,6},{5,7},{6,4},{7,5},{12,14},{13,15},{1... | collective-permute-start | bytes 1198088 | tf_op jit(solution)/shard_map/ppermute | solution.py:183
  9.0 8.3 %collective-permute-done.4.refs_0_ = bf16[24,8320]{1,0:T(8,128)(2,1)} collective-permute-done((bf16[24,8320]{1,0:T(8,128)(2,1)S(1)}, bf16[24,8320]{1,0:T(8,128)(2,1)}, u32[]{:S(2)}, u32[]{:S(2)}) %collective-permute-start.4) | collective-permute-done | bytes 399392 | tf_op jit(solution)/shard_map/ppermute | solution.py:183
  17.3 1.6 %collective-permute-start.6 = (bf16[24,8320]{1,0:T(8,128)(2,1)}, bf16[24,8320]{1,0:T(8,128)(2,1)}, u32[]{:S(2)}, u32[]{:S(2)}) collective-permute-start(bf16[24,8320]{1,0:T(8,128)(2,1)} %collective-permute-done.4.refs_0_), channel_id=1, source_target_pairs={{0,2},{1,3},{2,0},{3,1},{4,6},{5,7},{6,4},{7,5},{12,14},{13,15},{1... | collective-permute-start | bytes 1198088 | tf_op jit(solution)/shard_map/ppermute | solution.py:183
  20.1 8.0 %collective-permute-done.6.refs_2_ = bf16[24,8320]{1,0:T(8,128)(2,1)} collective-permute-done((bf16[24,8320]{1,0:T(8,128)(2,1)}, bf16[24,8320]{1,0:T(8,128)(2,1)}, u32[]{:S(2)}, u32[]{:S(2)}) %collective-permute-start.6) | collective-permute-done | bytes 399392 | tf_op jit(solution)/shard_map/ppermute | solution.py:183
  28.0 1.8 %collective-permute-done.9.refs_0_ = bf16[24,8320]{1,0:T(8,128)(2,1)S(1)} collective-permute-done((bf16[24,8320]{1,0:T(8,128)(2,1)}, bf16[24,8320]{1,0:T(8,128)(2,1)S(1)}, u32[]{:S(2)}, u32[]{:S(2)}) %collective-permute-start.9) | collective-permute-done | bytes 399392 | tf_op jit(solution)/shard_map/ppermute | solution.py:183
  31.2 1.2 %copy-done = bf16[1,8192,64]{1,2,0:T(8,128)(2,1)S(1)} copy-done((bf16[1,8192,64]{1,2,0:T(8,128)(2,1)S(1)}, bf16[1,8192,64]{1,2,0:T(8,128)(2,1)}, u32[]{:S(2)}) %copy-start) | copy-done | bytes 1048600
  32.4 0.9 shard_map.74
  33.3 1.2 %copy-done.2 = bf16[96,8192]{1,0:T(8,128)(2,1)} copy-done((bf16[96,8192]{1,0:T(8,128)(2,1)}, bf16[96,8192]{1,0:T(8,128)(2,1)S(1)}, u32[]{:S(2)}) %copy-start.2) | copy-done | bytes 1572888
  34.5 3.3 %collective-permute-start.8 = (bf16[96,64]{1,0:T(8,128)(2,1)S(1)}, bf16[96,64]{1,0:T(8,128)(2,1)S(1)}, u32[]{:S(2)}, u32[]{:S(2)}) collective-permute-start(bf16[96,64]{1,0:T(8,128)(2,1)S(1)} %get-tuple-element.18), channel_id=1, source_target_pairs={{0,4},{1,5},{2,6},{3,7},{4,12},{5,13},{6,14},{7,15},{12,8},{13,9},... | collective-permute-start | bytes 36872 | tf_op jit(solution)/shard_map/ppermute | solution.py:183
  37.8 4.3 %collective-permute-done.8.refs_6_ = bf16[96,64]{1,0:T(8,128)(2,1)S(1)} collective-permute-done((bf16[96,64]{1,0:T(8,128)(2,1)S(1)}, bf16[96,64]{1,0:T(8,128)(2,1)S(1)}, u32[]{:S(2)}, u32[]{:S(2)}) %collective-permute-start.8) | collective-permute-done | bytes 12320 | tf_op jit(solution)/shard_map/ppermute | solution.py:183
  42.1 2.2 %shard_map.75 = (bf16[96,8192]{1,0:T(8,128)(2,1)S(1)}, bf16[96,64]{1,0:T(8,128)(2,1)S(1)}, s32[96,128]{1,0:T(8,128)S(1)}) custom-call(bf16[24,8320]{1,0:T(8,128)(2,1)} %collective-permute-done.4.refs_0_, bf16[24,8320]{1,0:T(8,128)(2,1)} %collective-permute-done.5.refs_1_, bf16[24,8320]{1,0:T(8,128)(2,1)} %collective-permute-done.6.refs_2_, ...), custom_call_target="tpu_custom_call" | custom-call | flops 402653184 | bytes 3145728 | tf_op jit(solution)/shard_map/pallas_call | solution.py:125
  46.4 5.0 %fusion.1.refs_0_ = f32[96,512]{1,0:T(8,128)S(1)} fusion(bf16[96,8192]{1,0:T(8,128)(2,1)S(1)} %copy-done.3, bf16[8192,512]{1,0:T(8,128)(2,1)} %param.9), kind=kOutput, calls=%fused_computation.3 | convolution fusion | flops 805306368 | bytes 10158080 | tf_op jit(solution)/shard_map/dot_general | solution.py:186
  52.4 3.3 %collective-permute-start.18 = (bf16[96,64]{1,0:T(8,128)(2,1)S(1)}, bf16[96,64]{1,0:T(8,128)(2,1)S(1)}, u32[]{:S(2)}, u32[]{:S(2)}) collective-permute-start(bf16[96,64]{1,0:T(8,128)(2,1)S(1)} %get-tuple-element.22), channel_id=1, source_target_pairs={{0,4},{1,5},{2,6},{3,7},{4,12},{5,13},{6,14},{7,15},{12,8},{13,9},... | collective-permute-start | bytes 36872 | tf_op jit(solution)/shard_map/ppermute | solution.py:183
  55.7 1.4 %fusion.2.refs_1_ = f32[96,512]{1,0:T(8,128)S(1)} fusion(bf16[96,8192]{1,0:T(8,128)(2,1)S(1)} %get-tuple-element.19, bf16[8192,512]{1,0:T(8,128)(2,1)S(1)} %bitcast.26), kind=kOutput, calls=%fused_computation.4 | convolution fusion | flops 805306368 | bytes 10158080 | tf_op jit(solution)/shard_map/dot_general | solution.py:186
  57.4 0.9 shard_map.77
  58.3 1.6 %collective-permute-start.19 = (bf16[96,64]{1,0:T(8,128)(2,1)S(1)}, bf16[96,64]{1,0:T(8,128)(2,1)S(1)}, u32[]{:S(2)}, u32[]{:S(2)}) collective-permute-start(bf16[96,64]{1,0:T(8,128)(2,1)S(1)} %get-tuple-element.24), channel_id=1, source_target_pairs={{0,2},{1,3},{2,0},{3,1},{4,6},{5,7},{6,4},{7,5},{12,14},{13,15},{1... | collective-permute-start | bytes 36872 | tf_op jit(solution)/shard_map/ppermute | solution.py:183
  59.9 1.4 %fusion.3.refs_2_ = f32[96,512]{1,0:T(8,128)S(1)} fusion(bf16[96,8192]{1,0:T(8,128)(2,1)S(1)} %get-tuple-element.21, bf16[8192,512]{1,0:T(8,128)(2,1)S(1)} %bitcast.26), kind=kOutput, calls=%fused_computation.5 | convolution fusion | flops 805306368 | bytes 10158080 | tf_op jit(solution)/shard_map/dot_general | solution.py:186
  62.2 2.1 %collective-permute-start.20 = (bf16[96,64]{1,0:T(8,128)(2,1)S(1)}, bf16[96,64]{1,0:T(8,128)(2,1)S(1)}, u32[]{:S(2)}, u32[]{:S(2)}) collective-permute-start(bf16[96,64]{1,0:T(8,128)(2,1)S(1)} %maximum_add_fusion.refs_7_), channel_id=1, source_target_pairs={{0,4},{1,5},{2,6},{3,7},{4,12},{5,13},{6,14},{7,15},{12,8},{13,9},... | collective-permute-start | bytes 36872 | tf_op jit(solution)/shard_map/ppermute | solution.py:183
  64.8 1.9 %collective-permute-start.22 = (bf16[96,64]{1,0:T(8,128)(2,1)S(1)}, bf16[96,64]{1,0:T(8,128)(2,1)S(1)}, u32[]{:S(2)}, u32[]{:S(2)}) collective-permute-start(bf16[96,64]{1,0:T(8,128)(2,1)S(1)} %maximum_add_fusion.refs_7_), channel_id=1, source_target_pairs={{0,8},{1,9},{2,10},{3,11},{4,0},{5,1},{6,2},{7,3},{12,4},{13,5},{1... | collective-permute-start | bytes 36872 | tf_op jit(solution)/shard_map/ppermute | solution.py:183
  66.7 1.4 %fusion.4.refs_3_ = f32[96,512]{1,0:T(8,128)S(1)} fusion(bf16[96,8192]{1,0:T(8,128)(2,1)S(1)} %get-tuple-element.23, bf16[8192,512]{1,0:T(8,128)(2,1)S(1)} %bitcast.26), kind=kOutput, calls=%fused_computation.6 | convolution fusion | flops 805306368 | bytes 10158080 | tf_op jit(solution)/shard_map/dot_general | solution.py:186
  68.2 1.8 %collective-permute-done.21.refs_5_ = bf16[96,64]{1,0:T(8,128)(2,1)S(1)} collective-permute-done((bf16[96,64]{1,0:T(8,128)(2,1)S(1)}, bf16[96,64]{1,0:T(8,128)(2,1)S(1)}, u32[]{:S(2)}, u32[]{:S(2)}) %collective-permute-start.21) | collective-permute-done | bytes 12320 | tf_op jit(solution)/shard_map/ppermute | solution.py:183
  70.8 16.4 %all_to_all.16 = bf16[16,24,512]{2,1,0:T(8,128)(2,1)S(1)} all-to-all(bf16[16,24,512]{2,1,0:T(8,128)(2,1)S(1)} %shard_map.78), channel_id=1, replica_groups=mesh['group'=2,'adapter'=16] {'adapter'}, dimensions={0} | all-to-all | bytes 786432 | tf_op jit(solution)/shard_map/all_to_all | solution.py:213
  (60 shorter events, 12.3 us)
Async XLA Ops:
  3.9 13.4 %collective-permute-start.4 = (bf16[24,8320]{1,0:T(8,128)(2,1)S(1)}, bf16[24,8320]{1,0:T(8,128)(2,1)}, u32[]{:S(2)}, u32[]{:S(2)}) collective-permute-start(bf16[24,8320]{1,0:T(8,128)(2,1)S(1)} %shard_map.73.refs_0_), channel_id=1, source_target_pairs={{0,4},{1,5},{2,6},{3,7},{4,12},{5,13},{6,14},{7,15},{12,8},{13,9},... | collective-permute-start | bytes 1198088 | tf_op jit(solution)/shard_map/ppermute | solution.py:183
  6.9 12.6 %collective-permute-start.1 = (bf16[24,8320]{1,0:T(8,128)(2,1)S(1)}, bf16[24,8320]{1,0:T(8,128)(2,1)S(1)}, u32[]{:S(2)}, u32[]{:S(2)}) collective-permute-start(bf16[24,8320]{1,0:T(8,128)(2,1)S(1)} %shard_map.73.refs_0_), channel_id=1, source_target_pairs={{0,2},{1,3},{2,0},{3,1},{4,6},{5,7},{6,4},{7,5},{12,14},{13,15},{1... | collective-permute-start | bytes 1198088 | tf_op jit(solution)/shard_map/ppermute | solution.py:183
  8.4 22.8 %collective-permute-start.3 = (bf16[64,8192]{1,0:T(8,128)(2,1)}, bf16[64,8192]{1,0:T(8,128)(2,1)S(1)}, u32[]{:S(2)}, u32[]{:S(2)}) collective-permute-start(bf16[64,8192]{1,0:T(8,128)(2,1)} %bitcast.17), channel_id=1, source_target_pairs={{0,1},{1,0},{2,3},{3,2},{4,5},{5,4},{6,7},{7,6},{12,13},{13,12},{1... | collective-permute-start | bytes 3145736 | tf_op jit(solution)/shard_map/ppermute | solution.py:183
  8.5 11.1 %collective-permute-start = (bf16[24,8320]{1,0:T(8,128)(2,1)S(1)}, bf16[24,8320]{1,0:T(8,128)(2,1)S(1)}, u32[]{:S(2)}, u32[]{:S(2)}) collective-permute-start(bf16[24,8320]{1,0:T(8,128)(2,1)S(1)} %shard_map.73.refs_0_), channel_id=1, source_target_pairs={{0,1},{1,0},{2,3},{3,2},{4,5},{5,4},{6,7},{7,6},{12,13},{13,12},{1... | collective-permute-start | bytes 1198088 | tf_op jit(solution)/shard_map/ppermute | solution.py:183
  17.3 10.7 %collective-permute-start.6 = (bf16[24,8320]{1,0:T(8,128)(2,1)}, bf16[24,8320]{1,0:T(8,128)(2,1)}, u32[]{:S(2)}, u32[]{:S(2)}) collective-permute-start(bf16[24,8320]{1,0:T(8,128)(2,1)} %collective-permute-done.4.refs_0_), channel_id=1, source_target_pairs={{0,2},{1,3},{2,0},{3,1},{4,6},{5,7},{6,4},{7,5},{12,14},{13,15},{1... | collective-permute-start | bytes 1198088 | tf_op jit(solution)/shard_map/ppermute | solution.py:183
  18.9 10.9 %collective-permute-start.9 = (bf16[24,8320]{1,0:T(8,128)(2,1)}, bf16[24,8320]{1,0:T(8,128)(2,1)S(1)}, u32[]{:S(2)}, u32[]{:S(2)}) collective-permute-start(bf16[24,8320]{1,0:T(8,128)(2,1)} %collective-permute-done.4.refs_0_), channel_id=1, source_target_pairs={{0,4},{1,5},{2,6},{3,7},{4,12},{5,13},{6,14},{7,15},{12,8},{13,9},... | collective-permute-start | bytes 1198088 | tf_op jit(solution)/shard_map/ppermute | solution.py:183
  19.5 11.0 %collective-permute-start.2 = (bf16[24,8320]{1,0:T(8,128)(2,1)S(1)}, bf16[24,8320]{1,0:T(8,128)(2,1)S(1)}, u32[]{:S(2)}, u32[]{:S(2)}) collective-permute-start(bf16[24,8320]{1,0:T(8,128)(2,1)S(1)} %collective-permute-done.1.refs_2_), channel_id=1, source_target_pairs={{0,1},{1,0},{2,3},{3,2},{4,5},{5,4},{6,7},{7,6},{12,13},{13,12},{1... | collective-permute-start | bytes 1198088 | tf_op jit(solution)/shard_map/ppermute | solution.py:183
  19.6 18.2 %collective-permute-start.5 = (bf16[24,8320]{1,0:T(8,128)(2,1)}, bf16[24,8320]{1,0:T(8,128)(2,1)}, u32[]{:S(2)}, u32[]{:S(2)}) collective-permute-start(bf16[24,8320]{1,0:T(8,128)(2,1)} %collective-permute-done.4.refs_0_), channel_id=1, source_target_pairs={{0,1},{1,0},{2,3},{3,2},{4,5},{5,4},{6,7},{7,6},{12,13},{13,12},{1... | collective-permute-start | bytes 1198088 | tf_op jit(solution)/shard_map/ppermute | solution.py:183
  28.0 14.1 %collective-permute-start.7 = (bf16[24,8320]{1,0:T(8,128)(2,1)}, bf16[24,8320]{1,0:T(8,128)(2,1)}, u32[]{:S(2)}, u32[]{:S(2)}) collective-permute-start(bf16[24,8320]{1,0:T(8,128)(2,1)} %collective-permute-done.6.refs_2_), channel_id=1, source_target_pairs={{0,1},{1,0},{2,3},{3,2},{4,5},{5,4},{6,7},{7,6},{12,13},{13,12},{1... | collective-permute-start | bytes 1198088 | tf_op jit(solution)/shard_map/ppermute | solution.py:183
  29.8 15.4 %collective-permute-start.11 = (bf16[24,8320]{1,0:T(8,128)(2,1)S(1)}, bf16[24,8320]{1,0:T(8,128)(2,1)S(1)}, u32[]{:S(2)}, u32[]{:S(2)}) collective-permute-start(bf16[24,8320]{1,0:T(8,128)(2,1)S(1)} %collective-permute-done.9.refs_0_), channel_id=1, source_target_pairs={{0,2},{1,3},{2,0},{3,1},{4,6},{5,7},{6,4},{7,5},{12,14},{13,15},{1... | collective-permute-start | bytes 1198088 | tf_op jit(solution)/shard_map/ppermute | solution.py:183
  30.6 14.6 %collective-permute-start.14 = (bf16[24,8320]{1,0:T(8,128)(2,1)S(1)}, bf16[24,8320]{1,0:T(8,128)(2,1)S(1)}, u32[]{:S(2)}, u32[]{:S(2)}) collective-permute-start(bf16[24,8320]{1,0:T(8,128)(2,1)S(1)} %collective-permute-done.9.refs_0_), channel_id=1, source_target_pairs={{0,4},{1,5},{2,6},{3,7},{4,12},{5,13},{6,14},{7,15},{12,8},{13,9},... | collective-permute-start | bytes 1198088 | tf_op jit(solution)/shard_map/ppermute | solution.py:183
  32.4 9.7 %copy-start.1 = (bf16[1,8192,64]{1,2,0:T(8,128)(2,1)S(1)}, bf16[1,8192,64]{1,2,0:T(8,128)(2,1)}, u32[]{:S(2)}) copy-start(bf16[1,8192,64]{1,2,0:T(8,128)(2,1)} %param.10) | copy-start | bytes 3145732
  34.5 7.6 %collective-permute-start.8 = (bf16[96,64]{1,0:T(8,128)(2,1)S(1)}, bf16[96,64]{1,0:T(8,128)(2,1)S(1)}, u32[]{:S(2)}, u32[]{:S(2)}) collective-permute-start(bf16[96,64]{1,0:T(8,128)(2,1)S(1)} %get-tuple-element.18), channel_id=1, source_target_pairs={{0,4},{1,5},{2,6},{3,7},{4,12},{5,13},{6,14},{7,15},{12,8},{13,9},... | collective-permute-start | bytes 36872 | tf_op jit(solution)/shard_map/ppermute | solution.py:183
  37.8 13.7 %collective-permute-start.10 = (bf16[24,8320]{1,0:T(8,128)(2,1)S(1)}, bf16[24,8320]{1,0:T(8,128)(2,1)S(1)}, u32[]{:S(2)}, u32[]{:S(2)}) collective-permute-start(bf16[24,8320]{1,0:T(8,128)(2,1)S(1)} %collective-permute-done.9.refs_0_), channel_id=1, source_target_pairs={{0,1},{1,0},{2,3},{3,2},{4,5},{5,4},{6,7},{7,6},{12,13},{13,12},{1... | collective-permute-start | bytes 1198088 | tf_op jit(solution)/shard_map/ppermute | solution.py:183
  44.3 7.1 %collective-permute-start.13 = (bf16[96,64]{1,0:T(8,128)(2,1)S(1)}, bf16[96,64]{1,0:T(8,128)(2,1)S(1)}, u32[]{:S(2)}, u32[]{:S(2)}) collective-permute-start(bf16[96,64]{1,0:T(8,128)(2,1)S(1)} %get-tuple-element.20), channel_id=1, source_target_pairs={{0,4},{1,5},{2,6},{3,7},{4,12},{5,13},{6,14},{7,15},{12,8},{13,9},... | collective-permute-start | bytes 36872 | tf_op jit(solution)/shard_map/ppermute | solution.py:183
  45.2 10.4 %collective-permute-start.16 = (bf16[24,8320]{1,0:T(8,128)(2,1)S(1)}, bf16[24,8320]{1,0:T(8,128)(2,1)S(1)}, u32[]{:S(2)}, u32[]{:S(2)}) collective-permute-start(bf16[24,8320]{1,0:T(8,128)(2,1)S(1)} %broadcast_select_fusion), channel_id=1, source_target_pairs={{0,2},{2,0},{4,6},{6,4},{12,14},{14,12},{8,10},{10,8},{1,5},{3,7},... | collective-permute-start | bytes 1198088 | tf_op jit(solution)/shard_map/ppermute | solution.py:200
  45.8 5.7 %collective-permute-start.12 = (bf16[24,8320]{1,0:T(8,128)(2,1)S(1)}, bf16[24,8320]{1,0:T(8,128)(2,1)S(1)}, u32[]{:S(2)}, u32[]{:S(2)}) collective-permute-start(bf16[24,8320]{1,0:T(8,128)(2,1)S(1)} %collective-permute-done.11.refs_2_), channel_id=1, source_target_pairs={{0,1},{1,0},{2,3},{3,2},{4,5},{5,4},{6,7},{7,6},{12,13},{13,12},{1... | collective-permute-start | bytes 1198088 | tf_op jit(solution)/shard_map/ppermute | solution.py:183
  51.4 5.8 %collective-permute-start.15 = (bf16[24,8320]{1,0:T(8,128)(2,1)S(1)}, bf16[24,8320]{1,0:T(8,128)(2,1)S(1)}, u32[]{:S(2)}, u32[]{:S(2)}) collective-permute-start(bf16[24,8320]{1,0:T(8,128)(2,1)S(1)} %collective-permute-done.14.refs_0_), channel_id=1, source_target_pairs={{0,1},{1,0},{2,3},{3,2},{4,5},{5,4},{6,7},{7,6},{12,13},{13,12},{1... | collective-permute-start | bytes 1198088 | tf_op jit(solution)/shard_map/ppermute | solution.py:183
  52.4 4.8 %collective-permute-start.18 = (bf16[96,64]{1,0:T(8,128)(2,1)S(1)}, bf16[96,64]{1,0:T(8,128)(2,1)S(1)}, u32[]{:S(2)}, u32[]{:S(2)}) collective-permute-start(bf16[96,64]{1,0:T(8,128)(2,1)S(1)} %get-tuple-element.22), channel_id=1, source_target_pairs={{0,4},{1,5},{2,6},{3,7},{4,12},{5,13},{6,14},{7,15},{12,8},{13,9},... | collective-permute-start | bytes 36872 | tf_op jit(solution)/shard_map/ppermute | solution.py:183
  55.7 1.7 %collective-permute-start.17 = (bf16[24,8320]{1,0:T(8,128)(2,1)S(1)}, bf16[24,8320]{1,0:T(8,128)(2,1)S(1)}, u32[]{:S(2)}, u32[]{:S(2)}) collective-permute-start(bf16[24,8320]{1,0:T(8,128)(2,1)S(1)} %collective-permute-done.16.refs_2_), channel_id=1, source_target_pairs={{0,1},{1,0},{2,3},{3,2},{4,5},{5,4},{6,7},{7,6},{12,13},{13,12},{1... | collective-permute-start | bytes 1198088 | tf_op jit(solution)/shard_map/ppermute | solution.py:183
  58.3 3.9 %collective-permute-start.19 = (bf16[96,64]{1,0:T(8,128)(2,1)S(1)}, bf16[96,64]{1,0:T(8,128)(2,1)S(1)}, u32[]{:S(2)}, u32[]{:S(2)}) collective-permute-start(bf16[96,64]{1,0:T(8,128)(2,1)S(1)} %get-tuple-element.24), channel_id=1, source_target_pairs={{0,2},{1,3},{2,0},{3,1},{4,6},{5,7},{6,4},{7,5},{12,14},{13,15},{1... | collective-permute-start | bytes 36872 | tf_op jit(solution)/shard_map/ppermute | solution.py:183
  62.2 6.0 %collective-permute-start.20 = (bf16[96,64]{1,0:T(8,128)(2,1)S(1)}, bf16[96,64]{1,0:T(8,128)(2,1)S(1)}, u32[]{:S(2)}, u32[]{:S(2)}) collective-permute-start(bf16[96,64]{1,0:T(8,128)(2,1)S(1)} %maximum_add_fusion.refs_7_), channel_id=1, source_target_pairs={{0,4},{1,5},{2,6},{3,7},{4,12},{5,13},{6,14},{7,15},{12,8},{13,9},... | collective-permute-start | bytes 36872 | tf_op jit(solution)/shard_map/ppermute | solution.py:183
  64.3 5.6 %collective-permute-start.21 = (bf16[96,64]{1,0:T(8,128)(2,1)S(1)}, bf16[96,64]{1,0:T(8,128)(2,1)S(1)}, u32[]{:S(2)}, u32[]{:S(2)}) collective-permute-start(bf16[96,64]{1,0:T(8,128)(2,1)S(1)} %maximum_add_fusion.refs_7_), channel_id=1, source_target_pairs={{0,12},{1,13},{2,14},{3,15},{4,8},{5,9},{6,10},{7,11},{12,0},{13,1... | collective-permute-start | bytes 36872 | tf_op jit(solution)/shard_map/ppermute | solution.py:183
  64.8 5.1 %collective-permute-start.22 = (bf16[96,64]{1,0:T(8,128)(2,1)S(1)}, bf16[96,64]{1,0:T(8,128)(2,1)S(1)}, u32[]{:S(2)}, u32[]{:S(2)}) collective-permute-start(bf16[96,64]{1,0:T(8,128)(2,1)S(1)} %maximum_add_fusion.refs_7_), channel_id=1, source_target_pairs={{0,8},{1,9},{2,10},{3,11},{4,0},{5,1},{6,2},{7,3},{12,4},{13,5},{1... | collective-permute-start | bytes 36872 | tf_op jit(solution)/shard_map/ppermute | solution.py:183
  (10 other events, 35.9 us)

commit v6 on v5

--- a/solution.py
+++ b/solution.py
@@ -55,7 +55,17 @@
     ).astype(jnp.int32)
 
 
-def norm_kernel(hidden_ref, gain_ref, index_ref, slot_ref, out_ref):
+def norm_kernel(*refs):
+    sources, (out_ref, *buffers, sems) = refs[:4], refs[4:]
+    copies = [
+        pltpu.make_async_copy(source, buffer, sems.at[number])
+        for number, (source, buffer) in enumerate(zip(sources, buffers))
+    ]
+    for copy in copies:
+        copy.start()
+    for copy in copies:
+        copy.wait()
+    hidden_ref, gain_ref, index_ref, slot_ref = buffers
     rows, width = hidden_ref.shape
     squares = jnp.zeros((rows, LANES), jnp.float32)
     for start in range(0, width, CHUNK):
@@ -70,8 +80,8 @@
         out_ref[:, lanes] = (wide * inv_rms * gain_ref[:, lanes]).astype(jnp.bfloat16)
     index = index_ref[...]
     slot = jnp.zeros(index.shape, jnp.float32)
-    for name in range(slot_ref.shape[0]):
-        slot = jnp.where(index == name, slot_ref[name].astype(jnp.float32), slot)
+    for name in range(slot_ref.shape[1]):
+        slot = jnp.where(index == name, slot_ref[0, name].astype(jnp.float32), slot)
     across = lax.broadcasted_iota(jnp.int32, (rows, rows), 1)
     down = lax.broadcasted_iota(jnp.int32, (rows, rows), 0)
     column = jnp.sum(jnp.where(across == down, slot, 0.0), axis=1, keepdims=True)
@@ -80,31 +90,49 @@
 
 def normalize(hidden, norm_weight, adapter_index, adapter_slot):
     rows, width = hidden.shape
-    vmem = pl.BlockSpec(memory_space=pltpu.VMEM)
+    sources = (
+        hidden,
+        norm_weight.reshape(1, width),
+        adapter_index.reshape(1, rows),
+        adapter_slot.reshape(1, -1),
+    )
+    spaces = (pltpu.VMEM, pltpu.VMEM, pltpu.VMEM, pltpu.SMEM)
     return pl.pallas_call(
         norm_kernel,
         out_shape=jax.ShapeDtypeStruct((rows, width + LANES), jnp.bfloat16),
-        in_specs=[vmem, vmem, vmem, pl.BlockSpec(memory_space=pltpu.SMEM)],
-        out_specs=vmem,
-        compiler_params=pltpu.CompilerParams(vmem_limit_bytes=SMALL),
-    )(hidden, norm_weight.reshape(1, width), adapter_index.reshape(1, rows), adapter_slot)
-
-
-def prepare_kernel(*refs):
+        in_specs=[pl.BlockSpec(memory_space=pltpu.HBM)] * len(sources),
+        out_specs=pl.BlockSpec(memory_space=pltpu.VMEM),
+        scratch_shapes=[space(x.shape, x.dtype) for space, x in zip(spaces, sources)]
+        + [pltpu.SemaphoreType.DMA((len(sources),))],
+    )(*sources)
+
+
+def step_kernel(with_base, *refs):
     blocks, refs = refs[:CORNERS], refs[CORNERS:]
-    own_ref, other_ref, *before, rows_ref, part_ref, slot_ref = refs
+    own_ref, other_ref, *refs = refs
+    if with_base:
+        weight_ref, *before, part_ref, slot_ref, base_ref = refs
+    else:
+        *before, part_ref, slot_ref, rows_ref = refs
     rank, width = own_ref.shape
-    rows = rows_ref.shape[0]
+    rows = part_ref.shape[0]
     part = jnp.zeros((rows, 2 * rank), jnp.float32)
+    if with_base:
+        base_ref[...] = jnp.zeros(base_ref.shape, jnp.float32)
     for start in range(0, width, CHUNK):
         lanes = slice(start, start + CHUNK)
         wide = [block[:, lanes].astype(jnp.float32) for block in blocks]
         chunk = jnp.concatenate(wide, axis=0).astype(jnp.bfloat16)
-        rows_ref[:, lanes] = chunk
         down = jnp.concatenate([own_ref[:, lanes], other_ref[:, lanes]], axis=0)
         part += lax.dot_general(
             chunk, down, (((1,), (1,)), ((), ())), preferred_element_type=jnp.float32
         )
+        if with_base:
+            base_ref[...] += jnp.dot(
+                chunk, weight_ref[lanes, :], preferred_element_type=jnp.float32
+            )
+        else:
+            rows_ref[:, lanes] = chunk
     slot = slot_column(blocks, width)
     slot_ref[...] = jnp.broadcast_to(slot, slot_ref.shape)
     me = lax.axis_index("adapter")
@@ -117,34 +145,43 @@
     part_ref[...] = part.astype(jnp.bfloat16)
 
 
-def prepare(blocks, own, other, before):
+def step_rows(blocks, own, other, weight, before):
     rows = blocks[0].shape[0] * CORNERS
     rank, width = own.shape
-    before = [] if before is None else [before]
+    with_base = weight is not None
+    third = (
+        jax.ShapeDtypeStruct((rows, weight.shape[1]), jnp.float32)
+        if with_base
+        else jax.ShapeDtypeStruct((rows, width), jnp.bfloat16)
+    )
+    operands = [*blocks, own, other, *([weight] if with_base else []), *before]
     vmem = pl.BlockSpec(memory_space=pltpu.VMEM)
     return pl.pallas_call(
-        prepare_kernel,
+        lambda *refs: step_kernel(with_base, *refs),
         out_shape=(
-            jax.ShapeDtypeStruct((rows, width), jnp.bfloat16),
             jax.ShapeDtypeStruct((rows, rank), jnp.bfloat16),
             jax.ShapeDtypeStruct((rows, LANES), jnp.int32),
+            third,
         ),
-        in_specs=[vmem] * (CORNERS + 2 + len(before)),
+        in_specs=[vmem] * len(operands),
         out_specs=(vmem, vmem, vmem),
         compiler_params=pltpu.CompilerParams(vmem_limit_bytes=SMALL),
-        cost_estimate=pl.CostEstimate(
-            flops=2 * rows * width * 256, bytes_accessed=rows * width * 4, transcendentals=0
-        ),
-    )(*blocks, own, other, *before)
-
-
-def finish_kernel(places, devices, *refs):
+        cost_estimate=pl.CostEstimate(flops=1, bytes_accessed=1, transcendentals=0),
+    )(*operands)
+
+
+def after(x, *others):
+    return lax.optimization_barrier((x, *others))[0]
+
+
+def finish_kernel(offsets, devices, *refs):
+    places = len(offsets)
     bases, shrinks, slots = refs[:places], refs[places : 2 * places], refs[2 * places : 3 * places]
     up_ref, out_ref = refs[3 * places :]
     rows, rank = shrinks[0].shape
     own_rows = rows // CORNERS
     lanes = lax.broadcasted_iota(jnp.int32, (rows, devices * rank), 1)
-    for step in range(places):
+    for step, offset in enumerate(offsets):
         shrink = shrinks[step][...].astype(jnp.float32)
         wide = jnp.concatenate([shrink] * devices, axis=1)
         slot = slots[step][:, 0:1]
@@ -152,17 +189,17 @@
         update = jnp.dot(spread, up_ref[...], preferred_element_type=jnp.float32)
         query = (bases[step][...] + ADAPTER_SCALE * update).astype(jnp.bfloat16)
         for corner in range(CORNERS):
-            owner = ring_device(places, -step, corner)
+            owner = ring_device(places, -offset, corner)
             out_ref[owner] = query[corner * own_rows : (corner + 1) * own_rows]
 
 
-def finish(bases, shrinks, slots, up):
+def finish(offsets, bases, shrinks, slots, up):
     places, devices = len(bases), up.shape[0]
     rows, columns = bases[0].shape
     rank = up.shape[1]
     vmem = pl.BlockSpec(memory_space=pltpu.VMEM)
     return pl.pallas_call(
-        lambda *refs: finish_kernel(places, devices, *refs),
+        lambda *refs: finish_kernel(offsets, devices, *refs),
         out_shape=jax.ShapeDtypeStruct((devices, rows // CORNERS, columns), jnp.bfloat16),
         in_specs=[vmem] * (3 * places + 1),
         out_specs=vmem,
@@ -182,33 +219,44 @@
     def move(x, steps, flip):
         return lax.ppermute(x, "adapter", pairs(places, steps, flip))
 
-    def matmul(x, y):
-        return jnp.dot(x, y, preferred_element_type=jnp.float32)
-
     chain = normalize(hidden, norm_weight, adapter_index, adapter_slot)
     down = down_weights[0].T
     down_other = move(down, 0, 1)
 
-    bases, slots, travelling, other_y = [], [], None, None
-    for step in range(places):
-        if step:
-            chain = move(chain, 1, 0)
-        if step < places - 1:
-            other_y = move(chain, 0, 2)
+    far = places // 2
+    offsets = [0] + [sign * near for near in range(1, far) for sign in (1, -1)] + [far]
+    block = {0: chain}
+    for near in range(1, far):
+        block[near] = move(block[near - 1], 1, 0)
+        block[-near] = move(block[1 - near], -1, 0)
+    block[far] = move(block[far - 1], 1, 0)
+    other, crossed = {}, None
+    parts, slots, bases, done, before = {}, {}, {}, [], []
+    for offset in offsets:
+        here = after(block[offset], *done[:-1])
+        if offset != far:
+            other[offset] = move(here, 0, 2)
         else:
-            source = jnp.where(me % CORES == 0, chain, other_y)
-            other_y = lax.ppermute(source, "adapter", split_pairs(places))
-        blocks = [chain, move(chain, 0, 1), other_y, move(other_y, 0, 1)]
-        before = None if travelling is None else move(travelling, 1, 0)
-        rows, travelling, slot = prepare(blocks, down, down_other, before)
-        slots.append(slot)
-        bases.append(matmul(rows, query_weight))
-
-    blocks = move(travelling, 0, 2).reshape(CORNERS, own_rows, rank)
+            source = jnp.where((me & 1) == 0, after(here, *before[:-1]), other[far - 1])
+            other[far] = lax.ppermute(source, "adapter", split_pairs(places))
+        there = after(other[offset], *done)
+        rows = [here, move(here, 0, 1), there, move(there, 0, 1)]
+        if offset != far:
+            parts[offset], slots[offset], bases[offset] = step_rows(
+                rows, down, down_other, query_weight, []
+            )
+            done.append(parts[offset])
+            before.append(move(parts[offset], far - offset, 0))
+    part, slots[far], rows = step_rows(rows, down, down_other, None, before)
+    bases[far] = jnp.dot(rows, query_weight, preferred_element_type=jnp.float32)
+
+    blocks = move(part, 0, 2).reshape(CORNERS, own_rows, rank)
     blocks = jnp.concatenate([blocks[corner ^ 2] for corner in range(CORNERS)], axis=0)
-    shrink = travelling + blocks
-    shrinks = [move(shrink, step + 1, 0) for step in range(places - 1)] + [shrink]
-    query = finish(bases, shrinks, slots, up_weights)
+    part = part + blocks
+    shrinks = [part if offset == far else move(part, offset - far, 0) for offset in offsets]
+    bases = [bases[offset] for offset in offsets]
+    slots = [slots[offset] for offset in offsets]
+    query = finish(offsets, bases, shrinks, slots, up_weights)
     query = query.reshape(devices * own_rows, query.shape[2])
     return lax.all_to_all(query, "adapter", split_axis=0, concat_axis=1, tiled=True)
 

time: 88.3 us -> 89.3 us (1.011)
  Pallas kernels: 6.48 us -> 13.8 us
  local copies, waits for them, and re-layouts: 6.27 us -> 11.1 us
  matrix products: 9.3 us -> 4.92 us
  waiting for transfers between devices: 25.3 us -> 22.3 us
  starting transfers between devices: 24 us -> 21.2 us
  blocking collectives: 16.4 us -> 15.4 us
    pallas_call x5, Pallas kernels: 5.7 us -> 11.7 us  [the longest x4 10.9 us: step_rows(): pl.pallas_call(lambda *refs: step_kernel(with_base, *refs), out_shape=(ja...]
    unnamed x22 -> x20, local copies, waits for them, and re-layouts: 5.49 us -> 10.3 us
    dot_general x4 -> x1, matrix products: 9.3 us -> 4.92 us  [shards(): bases[far] = jnp.dot(rows, query_weight, preferred_element_type=jnp.float32)]
    ppermute x22, waiting for transfers between devices: 25.3 us -> 21.5 us  [move(): return lax.ppermute(x, 'adapter', pairs(places, steps, flip))]
    ppermute x22, starting transfers between devices: 23.5 us -> 20.5 us  [move(): return lax.ppermute(x, 'adapter', pairs(places, steps, flip))]
    pallas_call x1, Pallas kernels: 0.78 us -> 2.01 us  [normalize(): pl.pallas_call(norm_kernel, out_shape=jax.ShapeDtypeStruct((rows, width +...]
    all_to_all x1, blocking collectives: 16.4 us -> 15.4 us  [shards(): lax.all_to_all(query, 'adapter', split_axis=0, concat_axis=1, tiled=True)]
  transfers between devices with their start and end apart: 23 -> 23, of which waited for: 7 -> 9; matrix products, arithmetic and copies ran while one was open for 11% -> 6% of each run, Pallas kernels for 5% -> 13%
where the time goes in v6:
time: 89.3 us; the launch traced here: 88.8 us
  waiting for transfers between devices  22.3 us (25%)
  starting transfers between devices  21.2 us (24%)
  blocking collectives  15.4 us (17%)
  Pallas kernels  13.8 us (15%)
  local copies, waits for them, and re-layouts  11.1 us (12%)
  matrix products  4.92 us (6%)
    ppermute x22, waiting for transfers between devices, move(): return lax.ppermute(x, 'adapter', pairs(places, steps, flip))  21.5 us
    ppermute x22, starting transfers between devices, move(): return lax.ppermute(x, 'adapter', pairs(places, steps, flip))  20.5 us
    all_to_all x1, blocking collectives, shards(): lax.all_to_all(query, 'adapter', split_axis=0, concat_axis=1, tiled=True)  15.4 us
    pallas_call x4, Pallas kernels, step_rows(): pl.pallas_call(lambda *refs: step_kernel(with_base, *refs), out_shape=(ja...  10.9 us
    unnamed x20, local copies, waits for them, and re-layouts  10.3 us
    dot_general x1, matrix products, shards(): bases[far] = jnp.dot(rows, query_weight, preferred_element_type=jnp.float32)  4.92 us
    pallas_call x1, Pallas kernels, normalize(): pl.pallas_call(norm_kernel, out_shape=jax.ShapeDtypeStruct((rows, width +...  2.01 us
  transfers between devices with their start and end apart: 23, of which 9 were waited for; matrix products, arithmetic and copies ran while one was open for 6% of the time, Pallas kernels for 13%

profile of v6, /device:TPU:0, one launch (start us, length us, event | category | flops | bytes accessed | tf_op | source)
XLA Modules:
  0.0 88.8 jit_solution(3845332532784381703)
XLA Ops:
  0.5 2.0 %shard_map.73.refs_0_ = bf16[24,8320]{1,0:T(8,128)(2,1)} custom-call(bf16[24,8192]{1,0:T(8,128)(2,1)} %refs_0_.1, f32[1,8192]{1,0:T(1,128)} %bitcast.19, s32[1,24]{1,0:T(1,128)} %bitcast.20, s32[1,16]{1,0:T(1,128)} %bitcast.21), custom_call_target="tpu_custom_call" | custom-call | tf_op jit(solution)/shard_map/pallas_call | solution.py:100
  2.5 2.6 %collective-permute-start.1 = (bf16[24,8320]{1,0:T(8,128)(2,1)}, bf16[24,8320]{1,0:T(8,128)(2,1)S(1)}, u32[]{:S(2)}, u32[]{:S(2)}) collective-permute-start(bf16[24,8320]{1,0:T(8,128)(2,1)} %shard_map.73.refs_0_), channel_id=1, source_target_pairs={{0,2},{1,3},{2,0},{3,1},{4,6},{5,7},{6,4},{7,5},{12,14},{13,15},{1... | collective-permute-start | bytes 1198088 | tf_op jit(solution)/shard_map/ppermute | solution.py:220
  5.1 1.6 %collective-permute-start.4 = (bf16[24,8320]{1,0:T(8,128)(2,1)}, bf16[24,8320]{1,0:T(8,128)(2,1)}, u32[]{:S(2)}, u32[]{:S(2)}) collective-permute-start(bf16[24,8320]{1,0:T(8,128)(2,1)} %shard_map.73.refs_0_), channel_id=1, source_target_pairs={{0,4},{1,5},{2,6},{3,7},{4,12},{5,13},{6,14},{7,15},{12,8},{13,9},... | collective-permute-start | bytes 1198088 | tf_op jit(solution)/shard_map/ppermute | solution.py:220
  6.6 8.5 %collective-permute-done.1.refs_2_ = bf16[24,8320]{1,0:T(8,128)(2,1)S(1)} collective-permute-done((bf16[24,8320]{1,0:T(8,128)(2,1)}, bf16[24,8320]{1,0:T(8,128)(2,1)S(1)}, u32[]{:S(2)}, u32[]{:S(2)}) %collective-permute-start.1) | collective-permute-done | bytes 399392 | tf_op jit(solution)/shard_map/ppermute | solution.py:220
  15.2 2.4 %collective-permute-done.4.refs_0_ = bf16[24,8320]{1,0:T(8,128)(2,1)} collective-permute-done((bf16[24,8320]{1,0:T(8,128)(2,1)}, bf16[24,8320]{1,0:T(8,128)(2,1)}, u32[]{:S(2)}, u32[]{:S(2)}) %collective-permute-start.4) | collective-permute-done | bytes 399392 | tf_op jit(solution)/shard_map/ppermute | solution.py:220
  18.1 1.7 %collective-permute-start.8 = (bf16[24,8320]{1,0:T(8,128)(2,1)}, bf16[24,8320]{1,0:T(8,128)(2,1)S(1)}, u32[]{:S(2)}, u32[]{:S(2)}) collective-permute-start(bf16[24,8320]{1,0:T(8,128)(2,1)} %shard_map.73.refs_0_), channel_id=1, source_target_pairs={{0,8},{1,9},{2,10},{3,11},{4,0},{5,1},{6,2},{7,3},{12,4},{13,5},{1... | collective-permute-start | bytes 1198088 | tf_op jit(solution)/shard_map/ppermute | solution.py:220
  19.9 3.4 %copy-done = bf16[8192,512]{1,0:T(8,128)(2,1)S(1)} copy-done((bf16[8192,512]{1,0:T(8,128)(2,1)S(1)}, bf16[8192,512]{1,0:T(8,128)(2,1)}, u32[]{:S(2)}) %copy-start) | copy-done | bytes 8388632
  25.5 2.6 %shard_map.74 = (bf16[96,64]{1,0:T(8,128)(2,1)}, s32[96,128]{1,0:T(8,128)S(1)}, f32[96,512]{1,0:T(8,128)S(1)}) custom-call(bf16[24,8320]{1,0:T(8,128)(2,1)S(1)} %copy-done.4, bf16[24,8320]{1,0:T(8,128)(2,1)S(1)} %collective-permute-done.refs_1_, bf16[24,8320]{1,0:T(8,128)(2,1)S(1)} %collective-permute-done.1.refs_2_, ...), custom_call_target="tpu_custom_call" | custom-call | flops 1 | bytes 1 | tf_op jit(solution)/shard_map/pallas_call | solution.py:159
  29.2 1.2 %collective-permute-start.10 = (bf16[24,8320]{1,0:T(8,128)(2,1)S(1)}, bf16[24,8320]{1,0:T(8,128)(2,1)}, u32[]{:S(2)}, u32[]{:S(2)}) collective-permute-start(bf16[24,8320]{1,0:T(8,128)(2,1)S(1)} %collective-permute-done.8.refs_0_), channel_id=1, source_target_pairs={{0,2},{1,3},{2,0},{3,1},{4,6},{5,7},{6,4},{7,5},{12,14},{13,15},{1... | collective-permute-start | bytes 1198088 | tf_op jit(solution)/shard_map/ppermute | solution.py:220
  30.5 3.6 %collective-permute-start.14 = (bf16[96,64]{1,0:T(8,128)(2,1)}, bf16[96,64]{1,0:T(8,128)(2,1)}, u32[]{:S(2)}, u32[]{:S(2)}) collective-permute-start(bf16[96,64]{1,0:T(8,128)(2,1)} %get-tuple-element.24), channel_id=1, source_target_pairs={{0,12},{1,13},{2,14},{3,15},{4,8},{5,9},{6,10},{7,11},{12,0},{13,1... | collective-permute-start | bytes 36872 | tf_op jit(solution)/shard_map/ppermute | solution.py:220
  34.1 3.6 %shard_map.75 = (bf16[96,64]{1,0:T(8,128)(2,1)}, s32[96,128]{1,0:T(8,128)S(1)}, f32[96,512]{1,0:T(8,128)S(1)}) custom-call(bf16[24,8320]{1,0:T(8,128)(2,1)} %collective-permute-done.4.refs_0_, bf16[24,8320]{1,0:T(8,128)(2,1)S(1)} %collective-permute-done.5.refs_1_, bf16[24,8320]{1,0:T(8,128)(2,1)S(1)} %collective-permute-done.6.refs_2_, ...), custom_call_target="tpu_custom_call" | custom-call | flops 1 | bytes 1 | tf_op jit(solution)/shard_map/pallas_call | solution.py:159
  38.9 2.5 %collective-permute-done.12.refs_0_ = bf16[24,8320]{1,0:T(8,128)(2,1)S(1)} collective-permute-done((bf16[24,8320]{1,0:T(8,128)(2,1)}, bf16[24,8320]{1,0:T(8,128)(2,1)S(1)}, u32[]{:S(2)}, u32[]{:S(2)}) %collective-permute-start.12) | collective-permute-done | bytes 399392 | tf_op jit(solution)/shard_map/ppermute | solution.py:220
  41.5 1.6 %collective-permute-done.14.refs_6_ = bf16[96,64]{1,0:T(8,128)(2,1)} collective-permute-done((bf16[96,64]{1,0:T(8,128)(2,1)}, bf16[96,64]{1,0:T(8,128)(2,1)}, u32[]{:S(2)}, u32[]{:S(2)}) %collective-permute-start.14) | collective-permute-done | bytes 12320 | tf_op jit(solution)/shard_map/ppermute | solution.py:220
  44.7 3.4 %copy-done.1 = bf16[8192,512]{1,0:T(8,128)(2,1)S(1)} copy-done((bf16[8192,512]{1,0:T(8,128)(2,1)S(1)}, bf16[8192,512]{1,0:T(8,128)(2,1)}, u32[]{:S(2)}) %copy-start.1) | copy-done | bytes 8388632
  48.1 3.0 %shard_map.76 = (bf16[96,64]{1,0:T(8,128)(2,1)S(1)}, s32[96,128]{1,0:T(8,128)S(1)}, f32[96,512]{1,0:T(8,128)S(1)}) custom-call(bf16[24,8320]{1,0:T(8,128)(2,1)S(1)} %collective-permute-done.8.refs_0_, bf16[24,8320]{1,0:T(8,128)(2,1)S(1)} %collective-permute-done.9.refs_1_, bf16[24,8320]{1,0:T(8,128)(2,1)} %collective-permute-done.10.refs_2_, ...), custom_call_target="tpu_custom_call" | custom-call | flops 1 | bytes 1 | tf_op jit(solution)/shard_map/pallas_call | solution.py:159
  51.9 1.3 %collective-permute-start.18 = (bf16[96,64]{1,0:T(8,128)(2,1)S(1)}, bf16[96,64]{1,0:T(8,128)(2,1)S(1)}, u32[]{:S(2)}, u32[]{:S(2)}) collective-permute-start(bf16[96,64]{1,0:T(8,128)(2,1)S(1)} %get-tuple-element.33), channel_id=1, source_target_pairs={{0,8},{1,9},{2,10},{3,11},{4,0},{5,1},{6,2},{7,3},{12,4},{13,5},{1... | collective-permute-start | bytes 36872 | tf_op jit(solution)/shard_map/ppermute | solution.py:220
  53.3 2.5 %collective-permute-done.18.refs_8_ = bf16[96,64]{1,0:T(8,128)(2,1)S(1)} collective-permute-done((bf16[96,64]{1,0:T(8,128)(2,1)S(1)}, bf16[96,64]{1,0:T(8,128)(2,1)S(1)}, u32[]{:S(2)}, u32[]{:S(2)}) %collective-permute-start.18) | collective-permute-done | bytes 12320 | tf_op jit(solution)/shard_map/ppermute | solution.py:220
  55.8 1.6 %shard_map.77 = (bf16[96,64]{1,0:T(8,128)(2,1)S(1)}, s32[96,128]{1,0:T(8,128)S(1)}, bf16[96,8192]{1,0:T(8,128)(2,1)S(1)}) custom-call(bf16[24,8320]{1,0:T(8,128)(2,1)S(1)} %collective-permute-done.12.refs_0_, bf16[24,8320]{1,0:T(8,128)(2,1)S(1)} %collective-permute-done.13.refs_1_, bf16[24,8320]{1,0:T(8,128)(2,1)S(1)} %collective-permute-done.16.refs_2_, ...), custom_call_target="tpu_custom_call" | custom-call | flops 1 | bytes 1 | tf_op jit(solution)/shard_map/pallas_call | solution.py:159
  57.4 1.3 %collective-permute-start.19 = (bf16[96,64]{1,0:T(8,128)(2,1)S(1)}, bf16[96,64]{1,0:T(8,128)(2,1)S(1)}, u32[]{:S(2)}, u32[]{:S(2)}) collective-permute-start(bf16[96,64]{1,0:T(8,128)(2,1)S(1)} %get-tuple-element.36), channel_id=1, source_target_pairs={{0,2},{1,3},{2,0},{3,1},{4,6},{5,7},{6,4},{7,5},{12,14},{13,15},{1... | collective-permute-start | bytes 36872 | tf_op jit(solution)/shard_map/ppermute | solution.py:220
  58.7 2.6 %collective-permute-done.19 = bf16[96,64]{1,0:T(8,128)(2,1)S(1)} collective-permute-done((bf16[96,64]{1,0:T(8,128)(2,1)S(1)}, bf16[96,64]{1,0:T(8,128)(2,1)S(1)}, u32[]{:S(2)}, u32[]{:S(2)}) %collective-permute-start.19) | collective-permute-done | bytes 12320 | tf_op jit(solution)/shard_map/ppermute | solution.py:220
  61.3 2.2 %collective-permute-start.22 = (bf16[96,64]{1,0:T(8,128)(2,1)S(1)}, bf16[96,64]{1,0:T(8,128)(2,1)S(1)}, u32[]{:S(2)}, u32[]{:S(2)}) collective-permute-start(bf16[96,64]{1,0:T(8,128)(2,1)S(1)} %maximum_add_fusion.refs_7_), channel_id=1, source_target_pairs={{0,4},{1,5},{2,6},{3,7},{4,12},{5,13},{6,14},{7,15},{12,8},{13,9},... | collective-permute-start | bytes 36872 | tf_op jit(solution)/shard_map/ppermute | solution.py:220
  64.3 2.5 %collective-permute-start.20 = (bf16[96,64]{1,0:T(8,128)(2,1)S(1)}, bf16[96,64]{1,0:T(8,128)(2,1)S(1)}, u32[]{:S(2)}, u32[]{:S(2)}) collective-permute-start(bf16[96,64]{1,0:T(8,128)(2,1)S(1)} %maximum_add_fusion.refs_7_), channel_id=1, source_target_pairs={{0,12},{1,13},{2,14},{3,15},{4,8},{5,9},{6,10},{7,11},{12,0},{13,1... | collective-permute-start | bytes 36872 | tf_op jit(solution)/shard_map/ppermute | solution.py:220
  66.8 4.9 %fusion.1.refs_3_ = f32[96,512]{1,0:T(8,128)S(1)} fusion(bf16[96,8192]{1,0:T(8,128)(2,1)S(1)} %get-tuple-element.35, bf16[8192,512]{1,0:T(8,128)(2,1)} %refs_6_.5), kind=kOutput, calls=%fused_computation.3 | convolution fusion | flops 805306368 | bytes 10158080 | tf_op jit(solution)/shard_map/dot_general | solution.py:251
  72.7 15.4 %all_to_all.16 = bf16[16,24,512]{2,1,0:T(8,128)(2,1)S(1)} all-to-all(bf16[16,24,512]{2,1,0:T(8,128)(2,1)S(1)} %shard_map.78), channel_id=1, replica_groups=mesh['group'=2,'adapter'=16] {'adapter'}, dimensions={0} | all-to-all | bytes 786432 | tf_op jit(solution)/shard_map/all_to_all | solution.py:261
  (54 shorter events, 10.5 us)
Async XLA Ops:
  0.0 19.9 %collective-permute-start.3 = (bf16[64,8192]{1,0:T(8,128)(2,1)}, bf16[64,8192]{1,0:T(8,128)(2,1)S(1)}, u32[]{:S(2)}, u32[]{:S(2)}) collective-permute-start(bf16[64,8192]{1,0:T(8,128)(2,1)} %bitcast.12), channel_id=1, source_target_pairs={{0,1},{1,0},{2,3},{3,2},{4,5},{5,4},{6,7},{7,6},{12,13},{13,12},{1... | collective-permute-start | bytes 3145736 | tf_op jit(solution)/shard_map/ppermute | solution.py:220
  2.5 12.7 %collective-permute-start.1 = (bf16[24,8320]{1,0:T(8,128)(2,1)}, bf16[24,8320]{1,0:T(8,128)(2,1)S(1)}, u32[]{:S(2)}, u32[]{:S(2)}) collective-permute-start(bf16[24,8320]{1,0:T(8,128)(2,1)} %shard_map.73.refs_0_), channel_id=1, source_target_pairs={{0,2},{1,3},{2,0},{3,1},{4,6},{5,7},{6,4},{7,5},{12,14},{13,15},{1... | collective-permute-start | bytes 1198088 | tf_op jit(solution)/shard_map/ppermute | solution.py:220
  5.1 12.6 %collective-permute-start.4 = (bf16[24,8320]{1,0:T(8,128)(2,1)}, bf16[24,8320]{1,0:T(8,128)(2,1)}, u32[]{:S(2)}, u32[]{:S(2)}) collective-permute-start(bf16[24,8320]{1,0:T(8,128)(2,1)} %shard_map.73.refs_0_), channel_id=1, source_target_pairs={{0,4},{1,5},{2,6},{3,7},{4,12},{5,13},{6,14},{7,15},{12,8},{13,9},... | collective-permute-start | bytes 1198088 | tf_op jit(solution)/shard_map/ppermute | solution.py:220
  6.6 13.2 %collective-permute-start = (bf16[24,8320]{1,0:T(8,128)(2,1)}, bf16[24,8320]{1,0:T(8,128)(2,1)S(1)}, u32[]{:S(2)}, u32[]{:S(2)}) collective-permute-start(bf16[24,8320]{1,0:T(8,128)(2,1)} %shard_map.73.refs_0_), channel_id=1, source_target_pairs={{0,1},{1,0},{2,3},{3,2},{4,5},{5,4},{6,7},{7,6},{12,13},{13,12},{1... | collective-permute-start | bytes 1198088 | tf_op jit(solution)/shard_map/ppermute | solution.py:220
  15.2 4.7 %collective-permute-start.2 = (bf16[24,8320]{1,0:T(8,128)(2,1)S(1)}, bf16[24,8320]{1,0:T(8,128)(2,1)S(1)}, u32[]{:S(2)}, u32[]{:S(2)}) collective-permute-start(bf16[24,8320]{1,0:T(8,128)(2,1)S(1)} %collective-permute-done.1.refs_2_), channel_id=1, source_target_pairs={{0,1},{1,0},{2,3},{3,2},{4,5},{5,4},{6,7},{7,6},{12,13},{13,12},{1... | collective-permute-start | bytes 1198088 | tf_op jit(solution)/shard_map/ppermute | solution.py:220
  17.7 10.8 %collective-permute-start.6 = (bf16[24,8320]{1,0:T(8,128)(2,1)}, bf16[24,8320]{1,0:T(8,128)(2,1)S(1)}, u32[]{:S(2)}, u32[]{:S(2)}) collective-permute-start(bf16[24,8320]{1,0:T(8,128)(2,1)} %collective-permute-done.4.refs_0_), channel_id=1, source_target_pairs={{0,2},{1,3},{2,0},{3,1},{4,6},{5,7},{6,4},{7,5},{12,14},{13,15},{1... | collective-permute-start | bytes 1198088 | tf_op jit(solution)/shard_map/ppermute | solution.py:220
  18.1 11.1 %collective-permute-start.8 = (bf16[24,8320]{1,0:T(8,128)(2,1)}, bf16[24,8320]{1,0:T(8,128)(2,1)S(1)}, u32[]{:S(2)}, u32[]{:S(2)}) collective-permute-start(bf16[24,8320]{1,0:T(8,128)(2,1)} %shard_map.73.refs_0_), channel_id=1, source_target_pairs={{0,8},{1,9},{2,10},{3,11},{4,0},{5,1},{6,2},{7,3},{12,4},{13,5},{1... | collective-permute-start | bytes 1198088 | tf_op jit(solution)/shard_map/ppermute | solution.py:220
  19.9 14.2 %collective-permute-start.5 = (bf16[24,8320]{1,0:T(8,128)(2,1)}, bf16[24,8320]{1,0:T(8,128)(2,1)S(1)}, u32[]{:S(2)}, u32[]{:S(2)}) collective-permute-start(bf16[24,8320]{1,0:T(8,128)(2,1)} %collective-permute-done.4.refs_0_), channel_id=1, source_target_pairs={{0,1},{1,0},{2,3},{3,2},{4,5},{5,4},{6,7},{7,6},{12,13},{13,12},{1... | collective-permute-start | bytes 1198088 | tf_op jit(solution)/shard_map/ppermute | solution.py:220
  28.1 16.6 %copy-start.3 = (bf16[1,8192,64]{1,2,0:T(8,128)(2,1)S(1)}, bf16[1,8192,64]{1,2,0:T(8,128)(2,1)}, u32[]{:S(2)}) copy-start(bf16[1,8192,64]{1,2,0:T(8,128)(2,1)} %param.10) | copy-start | bytes 3145732
  28.5 5.6 %collective-permute-start.7 = (bf16[24,8320]{1,0:T(8,128)(2,1)S(1)}, bf16[24,8320]{1,0:T(8,128)(2,1)S(1)}, u32[]{:S(2)}, u32[]{:S(2)}) collective-permute-start(bf16[24,8320]{1,0:T(8,128)(2,1)S(1)} %collective-permute-done.6.refs_2_), channel_id=1, source_target_pairs={{0,1},{1,0},{2,3},{3,2},{4,5},{5,4},{6,7},{7,6},{12,13},{13,12},{1... | collective-permute-start | bytes 1198088 | tf_op jit(solution)/shard_map/ppermute | solution.py:220
  28.6 12.9 %collective-permute-start.12 = (bf16[24,8320]{1,0:T(8,128)(2,1)}, bf16[24,8320]{1,0:T(8,128)(2,1)S(1)}, u32[]{:S(2)}, u32[]{:S(2)}) collective-permute-start(bf16[24,8320]{1,0:T(8,128)(2,1)} %collective-permute-done.4.refs_0_), channel_id=1, source_target_pairs={{0,4},{1,5},{2,6},{3,7},{4,12},{5,13},{6,14},{7,15},{12,8},{13,9},... | collective-permute-start | bytes 1198088 | tf_op jit(solution)/shard_map/ppermute | solution.py:220
  29.2 12.3 %collective-permute-start.10 = (bf16[24,8320]{1,0:T(8,128)(2,1)S(1)}, bf16[24,8320]{1,0:T(8,128)(2,1)}, u32[]{:S(2)}, u32[]{:S(2)}) collective-permute-start(bf16[24,8320]{1,0:T(8,128)(2,1)S(1)} %collective-permute-done.8.refs_0_), channel_id=1, source_target_pairs={{0,2},{1,3},{2,0},{3,1},{4,6},{5,7},{6,4},{7,5},{12,14},{13,15},{1... | collective-permute-start | bytes 1198088 | tf_op jit(solution)/shard_map/ppermute | solution.py:220
  30.5 12.6 %collective-permute-start.14 = (bf16[96,64]{1,0:T(8,128)(2,1)}, bf16[96,64]{1,0:T(8,128)(2,1)}, u32[]{:S(2)}, u32[]{:S(2)}) collective-permute-start(bf16[96,64]{1,0:T(8,128)(2,1)} %get-tuple-element.24), channel_id=1, source_target_pairs={{0,12},{1,13},{2,14},{3,15},{4,8},{5,9},{6,10},{7,11},{12,0},{13,1... | collective-permute-start | bytes 36872 | tf_op jit(solution)/shard_map/ppermute | solution.py:220
  38.9 5.0 %collective-permute-start.15 = (bf16[96,64]{1,0:T(8,128)(2,1)}, bf16[96,64]{1,0:T(8,128)(2,1)}, u32[]{:S(2)}, u32[]{:S(2)}) collective-permute-start(bf16[96,64]{1,0:T(8,128)(2,1)} %get-tuple-element.28), channel_id=1, source_target_pairs={{0,4},{1,5},{2,6},{3,7},{4,12},{5,13},{6,14},{7,15},{12,8},{13,9},... | collective-permute-start | bytes 36872 | tf_op jit(solution)/shard_map/ppermute | solution.py:220
  38.9 5.8 %collective-permute-start.9 = (bf16[24,8320]{1,0:T(8,128)(2,1)S(1)}, bf16[24,8320]{1,0:T(8,128)(2,1)S(1)}, u32[]{:S(2)}, u32[]{:S(2)}) collective-permute-start(bf16[24,8320]{1,0:T(8,128)(2,1)S(1)} %collective-permute-done.8.refs_0_), channel_id=1, source_target_pairs={{0,1},{1,0},{2,3},{3,2},{4,5},{5,4},{6,7},{7,6},{12,13},{13,12},{1... | collective-permute-start | bytes 1198088 | tf_op jit(solution)/shard_map/ppermute | solution.py:220
  41.5 3.2 %collective-permute-start.11 = (bf16[24,8320]{1,0:T(8,128)(2,1)}, bf16[24,8320]{1,0:T(8,128)(2,1)S(1)}, u32[]{:S(2)}, u32[]{:S(2)}) collective-permute-start(bf16[24,8320]{1,0:T(8,128)(2,1)} %collective-permute-done.10.refs_2_), channel_id=1, source_target_pairs={{0,1},{1,0},{2,3},{3,2},{4,5},{5,4},{6,7},{7,6},{12,13},{13,12},{1... | collective-permute-start | bytes 1198088 | tf_op jit(solution)/shard_map/ppermute | solution.py:220
  44.0 7.9 %collective-permute-start.16 = (bf16[24,8320]{1,0:T(8,128)(2,1)S(1)}, bf16[24,8320]{1,0:T(8,128)(2,1)S(1)}, u32[]{:S(2)}, u32[]{:S(2)}) collective-permute-start(bf16[24,8320]{1,0:T(8,128)(2,1)S(1)} %broadcast_select_fusion), channel_id=1, source_target_pairs={{0,2},{2,0},{4,6},{6,4},{12,14},{14,12},{8,10},{10,8},{1,5},{3,7},... | collective-permute-start | bytes 1198088 | tf_op jit(solution)/shard_map/ppermute | solution.py:241
  44.7 8.6 %collective-permute-start.13 = (bf16[24,8320]{1,0:T(8,128)(2,1)S(1)}, bf16[24,8320]{1,0:T(8,128)(2,1)S(1)}, u32[]{:S(2)}, u32[]{:S(2)}) collective-permute-start(bf16[24,8320]{1,0:T(8,128)(2,1)S(1)} %collective-permute-done.12.refs_0_), channel_id=1, source_target_pairs={{0,1},{1,0},{2,3},{3,2},{4,5},{5,4},{6,7},{7,6},{12,13},{13,12},{1... | collective-permute-start | bytes 1198088 | tf_op jit(solution)/shard_map/ppermute | solution.py:220
  51.9 3.8 %collective-permute-start.17 = (bf16[24,8320]{1,0:T(8,128)(2,1)S(1)}, bf16[24,8320]{1,0:T(8,128)(2,1)S(1)}, u32[]{:S(2)}, u32[]{:S(2)}) collective-permute-start(bf16[24,8320]{1,0:T(8,128)(2,1)S(1)} %collective-permute-done.16.refs_2_), channel_id=1, source_target_pairs={{0,1},{1,0},{2,3},{3,2},{4,5},{5,4},{6,7},{7,6},{12,13},{13,12},{1... | collective-permute-start | bytes 1198088 | tf_op jit(solution)/shard_map/ppermute | solution.py:220
  51.9 3.8 %collective-permute-start.18 = (bf16[96,64]{1,0:T(8,128)(2,1)S(1)}, bf16[96,64]{1,0:T(8,128)(2,1)S(1)}, u32[]{:S(2)}, u32[]{:S(2)}) collective-permute-start(bf16[96,64]{1,0:T(8,128)(2,1)S(1)} %get-tuple-element.33), channel_id=1, source_target_pairs={{0,8},{1,9},{2,10},{3,11},{4,0},{5,1},{6,2},{7,3},{12,4},{13,5},{1... | collective-permute-start | bytes 36872 | tf_op jit(solution)/shard_map/ppermute | solution.py:220
  57.4 3.9 %collective-permute-start.19 = (bf16[96,64]{1,0:T(8,128)(2,1)S(1)}, bf16[96,64]{1,0:T(8,128)(2,1)S(1)}, u32[]{:S(2)}, u32[]{:S(2)}) collective-permute-start(bf16[96,64]{1,0:T(8,128)(2,1)S(1)} %get-tuple-element.36), channel_id=1, source_target_pairs={{0,2},{1,3},{2,0},{3,1},{4,6},{5,7},{6,4},{7,5},{12,14},{13,15},{1... | collective-permute-start | bytes 36872 | tf_op jit(solution)/shard_map/ppermute | solution.py:220
  61.3 10.4 %collective-permute-start.22 = (bf16[96,64]{1,0:T(8,128)(2,1)S(1)}, bf16[96,64]{1,0:T(8,128)(2,1)S(1)}, u32[]{:S(2)}, u32[]{:S(2)}) collective-permute-start(bf16[96,64]{1,0:T(8,128)(2,1)S(1)} %maximum_add_fusion.refs_7_), channel_id=1, source_target_pairs={{0,4},{1,5},{2,6},{3,7},{4,12},{5,13},{6,14},{7,15},{12,8},{13,9},... | collective-permute-start | bytes 36872 | tf_op jit(solution)/shard_map/ppermute | solution.py:220
  63.5 8.2 %collective-permute-start.21 = (bf16[96,64]{1,0:T(8,128)(2,1)S(1)}, bf16[96,64]{1,0:T(8,128)(2,1)S(1)}, u32[]{:S(2)}, u32[]{:S(2)}) collective-permute-start(bf16[96,64]{1,0:T(8,128)(2,1)S(1)} %maximum_add_fusion.refs_7_), channel_id=1, source_target_pairs={{0,8},{1,9},{2,10},{3,11},{4,0},{5,1},{6,2},{7,3},{12,4},{13,5},{1... | collective-permute-start | bytes 36872 | tf_op jit(solution)/shard_map/ppermute | solution.py:220
  64.3 7.5 %collective-permute-start.20 = (bf16[96,64]{1,0:T(8,128)(2,1)S(1)}, bf16[96,64]{1,0:T(8,128)(2,1)S(1)}, u32[]{:S(2)}, u32[]{:S(2)}) collective-permute-start(bf16[96,64]{1,0:T(8,128)(2,1)S(1)} %maximum_add_fusion.refs_7_), channel_id=1, source_target_pairs={{0,12},{1,13},{2,14},{3,15},{4,8},{5,9},{6,10},{7,11},{12,0},{13,1... | collective-permute-start | bytes 36872 | tf_op jit(solution)/shard_map/ppermute | solution.py:220
  (9 other events, 25.2 us)

commit v7 on v6

v7 whole, which is shorter than its diff:
```python
import jax
import jax.numpy as jnp
from jax import lax
from jax.experimental import pallas as pl
from jax.experimental.pallas import tpu as pltpu
from jax.sharding import PartitionSpec as P

ADAPTER_SCALE = 0.5
EPS = 1e-05

SIDE = 2
CORES = 2
CORNERS = SIDE * CORES
LANES = 128
CHUNK = 1024
VMEM_LIMIT = 24 << 20
VMEM = pl.BlockSpec(memory_space=pltpu.VMEM)


def line_ring(places):
    odd = list(range(1, places, 2))
    even = list(range(0, places, 2))
    return [0] + odd + even[:0:-1]


def pairs(places, steps, flip):
    ring = line_ring(places)
    out = []
    for at, place in enumerate(ring):
        target = ring[(at + steps) % places]
        for corner in range(CORNERS):
            out.append((place * CORNERS + corner, target * CORNERS + (corner ^ flip)))
    return out


def split_pairs(places):
    flips, steps = pairs(places, 0, 2), pairs(places, 1, 0)
    return [pair for pair in flips if pair[0] % CORES == 0] + [
        pair for pair in steps if pair[0] % CORES
    ]


def ring_chip(places, steps, side):
    chip = lax.axis_index("adapter") // CORES
    ring = line_ring(places)
    target = jnp.int32(0)
    for at, name in enumerate(ring):
        target = jnp.where(chip // SIDE == name, jnp.int32(ring[(at + steps) % places]), target)
    return target * SIDE + ((chip % SIDE) ^ side)


def after(x, *others):
    return lax.optimization_barrier((x, *others))[0]


def call(kernel, out_shape, operands, specs=None, scratch=(), limit=VMEM_LIMIT):
    return pl.pallas_call(
        kernel,
        out_shape=out_shape,
        in_specs=[VMEM] * len(operands) if specs is None else specs,
        out_specs=jax.tree.map(lambda _: VMEM, out_shape),
        scratch_shapes=list(scratch),
        compiler_params=pltpu.CompilerParams(vmem_limit_bytes=limit),
        cost_estimate=pl.CostEstimate(flops=1, bytes_accessed=1, transcendentals=0),
    )(*operands)


def norm_kernel(*refs):
    sources, (out_ref, *buffers, sems) = refs[:4], refs[4:]
    copies = [
        pltpu.make_async_copy(source, buffer, sems.at[number])
        for number, (source, buffer) in enumerate(zip(sources, buffers))
    ]
    for copy in copies:
        copy.start()
    for copy in copies:
        copy.wait()
    hidden_ref, gain_ref, index_ref, slot_ref = buffers
    rows, width = hidden_ref.shape
    squares = jnp.zeros((rows, LANES), jnp.float32)
    for start in range(0, width, CHUNK):
        wide = hidden_ref[:, start : start + CHUNK].astype(jnp.float32)
        wide = wide * wide
        for lane in range(0, CHUNK, LANES):
            squares = squares + wide[:, lane : lane + LANES]
    inv_rms = lax.rsqrt(jnp.sum(squares, axis=1, keepdims=True) / width + EPS)
    for start in range(0, width, CHUNK):
        lanes = slice(start, start + CHUNK)
        wide = hidden_ref[:, lanes].astype(jnp.float32)
        out_ref[:, lanes] = (wide * inv_rms * gain_ref[:, lanes]).astype(jnp.bfloat16)
    index = index_ref[...]
    slot = jnp.zeros(index.shape, jnp.float32)
    for name in range(slot_ref.shape[1]):
        slot = jnp.where(index == name, slot_ref[0, name].astype(jnp.float32), slot)
    across = lax.broadcasted_iota(jnp.int32, (rows, rows), 1)
    down = lax.broadcasted_iota(jnp.int32, (rows, rows), 0)
    column = jnp.sum(jnp.where(across == down, slot, 0.0), axis=1, keepdims=True)
    out_ref[:, width:] = jnp.broadcast_to(column, (rows, LANES)).astype(jnp.bfloat16)


def normalize(hidden, norm_weight, adapter_index, adapter_slot):
    rows, width = hidden.shape
    sources = (
        hidden,
        norm_weight.reshape(1, width),
        adapter_index.reshape(1, rows),
        adapter_slot.reshape(1, -1),
    )
    spaces = (pltpu.VMEM, pltpu.VMEM, pltpu.VMEM, pltpu.SMEM)
    return pl.pallas_call(
        norm_kernel,
        out_shape=jax.ShapeDtypeStruct((rows, width + LANES), jnp.bfloat16),
        in_specs=[pl.BlockSpec(memory_space=pltpu.HBM)] * len(sources),
        out_specs=VMEM,
        scratch_shapes=[space(x.shape, x.dtype) for space, x in zip(spaces, sources)]
        + [pltpu.SemaphoreType.DMA((len(sources),))],
    )(*sources)


def stacked(blocks, lanes):
    wide = [block[:, lanes].astype(jnp.float32) for block in blocks]
    return jnp.concatenate(wide, axis=0).astype(jnp.bfloat16)


def shrink_kernel(*refs):
    blocks, (own_ref, other_ref, *before, part_ref, slot_ref) = refs[:SIDE], refs[SIDE:]
    rank, width = own_ref.shape
    rows = part_ref.shape[0]
    part = jnp.zeros((rows, 2 * rank), jnp.float32)
    for start in range(0, width, CHUNK):
        lanes = slice(start, start + CHUNK)
        down = jnp.concatenate([own_ref[:, lanes], other_ref[:, lanes]], axis=0)
        part += lax.dot_general(
            stacked(blocks, lanes), down, (((1,), (1,)), ((), ())), preferred_element_type=jnp.float32
        )
    slot = jnp.concatenate(
        [block[:, width : width + 1].astype(jnp.float32) for block in blocks], axis=0
    ).astype(jnp.int32)
    slot_ref[...] = jnp.broadcast_to(slot, slot_ref.shape)
    me = lax.axis_index("adapter")
    lanes = lax.broadcasted_iota(jnp.int32, part.shape, 1)
    part = jnp.where(slot == jnp.where(lanes < rank, me, me ^ 1), part, 0.0)
    part = part[:, :rank] + part[:, rank:]
    for ref in before:
        part = part + ref[...].astype(jnp.float32)
    part_ref[...] = part.astype(jnp.bfloat16)


def shrink_rows(blocks, own, other, before):
    rows = blocks[0].shape[0] * SIDE
    out_shape = (
        jax.ShapeDtypeStruct((rows, own.shape[0]), jnp.bfloat16),
        jax.ShapeDtypeStruct((rows, LANES), jnp.int32),
    )
    return call(shrink_kernel, out_shape, (*blocks, own, other, *before))


def base_kernel(*refs):
    *blocks, weight_ref, out_ref, buffer, sems = refs
    width = weight_ref.shape[0]
    copies = []
    for number, start in enumerate(range(0, width, CHUNK)):
        rows = pl.ds(start, CHUNK)
        copies.append(
            pltpu.make_async_copy(weight_ref.at[rows], buffer.at[rows], sems.at[number])
        )
        copies[-1].start()
    out_ref[...] = jnp.zeros(out_ref.shape, jnp.float32)
    for number, start in enumerate(range(0, width, CHUNK)):
        lanes = slice(start, start + CHUNK)
        rows = stacked(blocks, lanes)
        copies[number].wait()
        out_ref[...] += jnp.dot(rows, buffer[lanes, :], preferred_element_type=jnp.float32)


def base_rows(blocks, weight):
    rows = blocks[0].shape[0] * len(blocks)
    specs = [VMEM] * len(blocks) + [pl.BlockSpec(memory_space=pltpu.HBM)]
    return call(
        base_kernel,
        jax.ShapeDtypeStruct((rows, weight.shape[1]), jnp.float32),
        (*blocks, weight),
        specs,
        (
            pltpu.VMEM(weight.shape, weight.dtype),
            pltpu.SemaphoreType.DMA((weight.shape[0] // CHUNK,)),
        ),
        48 << 20,
    )


def finish_kernel(steps, per_base, *refs):
    bases, refs = refs[: 2 * (steps // per_base)], refs[2 * (steps // per_base) :]
    shrinks, slots, (own_ref, other_ref, *outs) = refs[:steps], refs[steps : 2 * steps], refs[2 * steps :]
    rows, rank = shrinks[0].shape
    own_rows = rows // SIDE
    columns = own_ref.shape[1]
    depth = own_ref.shape[0]
    core = lax.axis_index("adapter") % CORES
    lanes = lax.broadcasted_iota(jnp.int32, (rows, depth), 1)
    for step in range(steps):
        wide = jnp.concatenate([shrinks[step][...].astype(jnp.float32)] * (depth // rank), axis=1)
        spread = jnp.where(lanes // rank == slots[step][:, 0:1], wide, 0.0).astype(jnp.bfloat16)
        first = step % per_base * rows
        for which, up_ref in enumerate((own_ref, other_ref)):
            update = jnp.dot(spread, up_ref[...], preferred_element_type=jnp.float32)
            base = bases[2 * (step // per_base) + which][first : first + rows, :]
            query = (base + ADAPTER_SCALE * update).astype(jnp.bfloat16)
            at = pl.multiple_of((core ^ which) * columns, columns)
            for side in range(SIDE):
                outs[step * SIDE + side][:, pl.ds(at, columns)] = query[
                    side * own_rows : (side + 1) * own_rows
                ]


def finish(bases, shrinks, slots, own, other):
    steps, per_base = len(shrinks), 2 * len(shrinks) // len(bases)
    rows = shrinks[0].shape[0] // SIDE
    block = jax.ShapeDtypeStruct((rows, CORES * own.shape[1]), jnp.bfloat16)
    return call(
        lambda *refs: finish_kernel(steps, per_base, *refs),
        [block] * (steps * SIDE),
        (*bases, *shrinks, *slots, own, other),
    )


def assemble_kernel(places, offsets, *refs):
    *blocks, out_ref = refs
    columns = blocks[0].shape[1]
    for step, offset in enumerate(offsets):
        for side in range(SIDE):
            at = pl.multiple_of(ring_chip(places, offset, side) * columns, columns)
            out_ref[:, pl.ds(at, columns)] = blocks[step * SIDE + side][...]


def assemble(places, offsets, blocks):
    rows, columns = blocks[0].shape
    return call(
        lambda *refs: assemble_kernel(places, offsets, *refs),
        jax.ShapeDtypeStruct((rows, columns * len(blocks)), jnp.bfloat16),
        blocks,
    )


def shards(
    hidden, norm_weight, query_weight, down_weights, up_weights, adapter_index, adapter_slot
):
    devices = lax.axis_size("adapter")
    me = lax.axis_index("adapter")
    places = devices // CORNERS
    own_rows, width = hidden.shape
    columns = query_weight.shape[1]
    rank = down_weights.shape[2]

    def move(x, steps, flip):
        return lax.ppermute(x, "adapter", pairs(places, steps, flip))

    chain = normalize(hidden, norm_weight, adapter_index, adapter_slot)
    down = down_weights[0].T
    up = up_weights.reshape(devices * rank, columns)
    down_other = move(down, 0, 1)
    weight_other = move(query_weight, 0, 1)

    far = places // 2
    offsets = [0] + [sign * near for near in range(1, far) for sign in (1, -1)] + [far]
    block = {0: chain}
    for near in range(1, far):
        block[near] = move(block[near - 1], 1, 0)
        block[-near] = move(block[1 - near], -1, 0)
    block[far] = move(block[far - 1], 1, 0)
    other, parts, slots, before, bases, queue = {}, [], [], [], [], []
    for number, offset in enumerate(offsets):
        here = after(block[offset], *parts[:-1])
        if offset != far:
            other[offset] = move(here, 0, 2)
        else:
            here = after(here, other[offsets[-2]], *before[:-1], *bases)
            source = jnp.where((me & 1) == 0, here, other[far - 1])
            other[far] = lax.ppermute(source, "adapter", split_pairs(places))
            bases.append(base_rows(after(queue, source), weight_other))
            up_other = move(after(up, source), 0, 1)
            other[far] = after(other[far], bases[-1])
        rows = [here, after(other[offset], *parts)]
        if 0 < offset < far:
            rows = after(rows, block[-offset])
        part, slot = shrink_rows(rows, down, down_other, before if offset == far else [])
        parts.append(part)
        slots.append(slot)
        if offset != far:
            before.append(move(part, far - offset, 0))
        if number % 2 == 0:
            waiting = rows
        else:
            if queue and offset != far:
                bases.append(base_rows(queue, weight_other))
            queue = waiting + rows
            if offset != far:
                bases.append(base_rows(queue, query_weight))

    across = move(part, 0, 2)
    base_own = base_rows(queue, query_weight)
    across = after(across, base_own)
    part = part + jnp.concatenate([across[own_rows:], across[:own_rows]], axis=0)
    shrinks = [part if offset == far else move(part, offset - far, 0) for offset in offsets]
    bases += [base_own, base_rows(queue, weight_other)]
    blocks = finish(bases, shrinks, slots, up, up_other)
    parts = []
    for number, offset in enumerate(offsets):
        for side in range(SIDE):
            piece = blocks[number * SIDE + side]
            parts.append(move(piece, -offset, 2 * side) if offset or side else piece)
    return assemble(places, offsets, parts)


def solution(mesh):
    in_specs = (
        P(("group", "adapter"), None),
        P(),
        P(None, "adapter"),
        P("adapter", None, None),
        P(None, None, "adapter"),
        P(("group", "adapter"), None),
        P(),
    )
    out_specs = P(("group", "adapter"), None)
    return jax.shard_map(shards, mesh=mesh, in_specs=in_specs, out_specs=out_specs, check_vma=False)
```

time: 89.3 us -> 92 us (1.030)
  starting transfers between devices: 21.2 us -> 44.9 us
  blocking collectives: 15.4 us -> 0 us
  Pallas kernels: 13.8 us -> 29.2 us
  waiting for transfers between devices: 22.3 us -> 12.9 us
  local copies, waits for them, and re-layouts: 11.1 us -> 4.23 us
  matrix products: 4.92 us -> 0 us
    ppermute x22 -> x23, starting transfers between devices: 20.5 us -> 43.3 us  [move(): return lax.ppermute(x, 'adapter', pairs(places, steps, flip))]
    pallas_call x5 -> x10, Pallas kernels: 11.7 us -> 27.2 us  [call(): pl.pallas_call(kernel, out_shape=out_shape, in_specs=[VMEM] * len(operand...]
    all_to_all x1 -> x0, blocking collectives: 15.4 us -> none  [shards(): lax.all_to_all(query, 'adapter', split_axis=0, concat_axis=1, tiled=True)]
    ppermute x22 -> x23, waiting for transfers between devices: 21.5 us -> 12.9 us  [move(): return lax.ppermute(x, 'adapter', pairs(places, steps, flip))]
    unnamed x20 -> x14, local copies, waits for them, and re-layouts: 10.3 us -> 4.23 us
    dot_general x1 -> x0, matrix products: 4.92 us -> none  [shards(): bases[far] = jnp.dot(rows, query_weight, preferred_element_type=jnp.float32)]
  transfers between devices with their start and end apart: 23 -> 24, of which waited for: 9 -> 5; matrix products, arithmetic and copies ran while one was open for 6% -> 0% of each run, Pallas kernels for 13% -> 29%
where the time goes in v7:
time: 92 us; the launch traced here: 91.5 us
  starting transfers between devices  44.9 us (49%)
  Pallas kernels  29.2 us (32%)
  waiting for transfers between devices  12.9 us (14%)
  local copies, waits for them, and re-layouts  4.23 us (5%)
    ppermute x23, starting transfers between devices, move(): return lax.ppermute(x, 'adapter', pairs(places, steps, flip))  43.3 us
    pallas_call x10, Pallas kernels, call(): pl.pallas_call(kernel, out_shape=out_shape, in_specs=[VMEM] * len(operand...  27.2 us
    ppermute x23, waiting for transfers between devices, move(): return lax.ppermute(x, 'adapter', pairs(places, steps, flip))  12.9 us
    unnamed x14, local copies, waits for them, and re-layouts  4.23 us
    pallas_call x1, Pallas kernels, normalize(): pl.pallas_call(norm_kernel, out_shape=jax.ShapeDtypeStruct((rows, width +...  2.02 us
  transfers between devices with their start and end apart: 24, of which 5 were waited for; matrix products, arithmetic and copies ran while one was open for 0% of the time, Pallas kernels for 29%

profile of v7, /device:TPU:0, one launch (start us, length us, event | category | flops | bytes accessed | tf_op | source)
XLA Modules:
  0.0 91.5 jit_solution(14073259245576248207)
XLA Ops:
  0.5 2.0 %shard_map.73.refs_0_ = bf16[24,8320]{1,0:T(8,128)(2,1)} custom-call(bf16[24,8192]{1,0:T(8,128)(2,1)} %refs_0_.1, f32[1,8192]{1,0:T(1,128)} %bitcast.14, s32[1,24]{1,0:T(1,128)} %bitcast.15, s32[1,16]{1,0:T(1,128)} %bitcast.16), custom_call_target="tpu_custom_call" | custom-call | tf_op jit(solution)/shard_map/pallas_call | solution.py:110
  2.5 3.1 %collective-permute-start.1 = (bf16[24,8320]{1,0:T(8,128)(2,1)}, bf16[24,8320]{1,0:T(8,128)(2,1)}, u32[]{:S(2)}, u32[]{:S(2)}) collective-permute-start(bf16[24,8320]{1,0:T(8,128)(2,1)} %shard_map.73.refs_0_), channel_id=1, source_target_pairs={{0,4},{1,5},{2,6},{3,7},{4,12},{5,13},{6,14},{7,15},{12,8},{13,9},... | collective-permute-start | bytes 1198088 | tf_op jit(solution)/shard_map/ppermute | solution.py:256
  5.6 1.5 %collective-permute-start = (bf16[24,8320]{1,0:T(8,128)(2,1)}, bf16[24,8320]{1,0:T(8,128)(2,1)S(1)}, u32[]{:S(2)}, u32[]{:S(2)}) collective-permute-start(bf16[24,8320]{1,0:T(8,128)(2,1)} %shard_map.73.refs_0_), channel_id=1, source_target_pairs={{0,2},{1,3},{2,0},{3,1},{4,6},{5,7},{6,4},{7,5},{12,14},{13,15},{1... | collective-permute-start | bytes 1198088 | tf_op jit(solution)/shard_map/ppermute | solution.py:256
  8.5 8.0 %collective-permute-done.1.refs_2_.refs_0_ = bf16[24,8320]{1,0:T(8,128)(2,1)} collective-permute-done((bf16[24,8320]{1,0:T(8,128)(2,1)}, bf16[24,8320]{1,0:T(8,128)(2,1)}, u32[]{:S(2)}, u32[]{:S(2)}) %collective-permute-start.1) | collective-permute-done | bytes 399392 | tf_op jit(solution)/shard_map/ppermute | solution.py:256
  16.5 1.6 %collective-permute-start.2 = (bf16[24,8320]{1,0:T(8,128)(2,1)}, bf16[24,8320]{1,0:T(8,128)(2,1)S(1)}, u32[]{:S(2)}, u32[]{:S(2)}) collective-permute-start(bf16[24,8320]{1,0:T(8,128)(2,1)} %collective-permute-done.1.refs_2_.refs_0_), channel_id=1, source_target_pairs={{0,2},{1,3},{2,0},{3,1},{4,6},{5,7},{6,4},{7,5},{12,14},{13,15},{1... | collective-permute-start | bytes 1198088 | tf_op jit(solution)/shard_map/ppermute | solution.py:256
  18.0 9.3 %collective-permute-start.5 = (bf16[24,8320]{1,0:T(8,128)(2,1)}, bf16[24,8320]{1,0:T(8,128)(2,1)S(1)}, u32[]{:S(2)}, u32[]{:S(2)}) collective-permute-start(bf16[24,8320]{1,0:T(8,128)(2,1)} %collective-permute-done.1.refs_2_.refs_0_), channel_id=1, source_target_pairs={{0,4},{1,5},{2,6},{3,7},{4,12},{5,13},{6,14},{7,15},{12,8},{13,9},... | collective-permute-start | bytes 1198088 | tf_op jit(solution)/shard_map/ppermute | solution.py:256
  31.0 3.0 %collective-permute-start.7 = (bf16[48,64]{1,0:T(8,128)(2,1)S(1)}, bf16[48,64]{1,0:T(8,128)(2,1)S(1)}, u32[]{:S(2)}, u32[]{:S(2)}) collective-permute-start(bf16[48,64]{1,0:T(8,128)(2,1)S(1)} %get-tuple-element.36), channel_id=1, source_target_pairs={{0,12},{1,13},{2,14},{3,15},{4,8},{5,9},{6,10},{7,11},{12,0},{13,1... | collective-permute-start | bytes 18440 | tf_op jit(solution)/shard_map/ppermute | solution.py:256
  34.0 1.9 %shard_map.76 = (bf16[48,64]{1,0:T(8,128)(2,1)S(1)}, s32[48,128]{1,0:T(8,128)S(1)}) custom-call(bf16[24,8320]{1,0:T(8,128)(2,1)} %collective-permute-done.1.refs_2_.refs_0_, bf16[24,8320]{1,0:T(8,128)(2,1)S(1)} %collective-permute-done.2.refs_3_.refs_1_, bf16[64,8192]{1,0:T(8,128)(2,1)S(1)} %bitcast.9, bf16[64,8192]{1,0:T(8,128)(2,1)S(1)} %collective-permute-done.3.refs_3_), custom_call_target="tpu_custom_call" | custom-call | flops 1 | bytes 1 | tf_op jit(solution)/shard_map/pallas_call | solution.py:57
  38.4 4.9 %shard_map.75.refs_0_ = f32[96,512]{1,0:T(8,128)S(1)} custom-call(bf16[24,8320]{1,0:T(8,128)(2,1)S(1)} %copy-done.3, bf16[24,8320]{1,0:T(8,128)(2,1)S(1)} %copy-done.5, bf16[24,8320]{1,0:T(8,128)(2,1)} %collective-permute-done.1.refs_2_.refs_0_, bf16[24,8320]{1,0:T(8,128)(2,1)S(1)} %collective-permute-done.2.refs_3_.refs_1_, bf16[8192,512]{1,0:T(8,128)(2,1)} %refs_4_.3), custom_call_target="tpu_custom_call" | custom-call | flops 1 | bytes 1 | tf_op jit(solution)/shard_map/pallas_call | solution.py:57
  43.5 1.6 %collective-permute-start.10 = (bf16[24,8320]{1,0:T(8,128)(2,1)S(1)}, bf16[24,8320]{1,0:T(8,128)(2,1)S(1)}, u32[]{:S(2)}, u32[]{:S(2)}) collective-permute-start(bf16[24,8320]{1,0:T(8,128)(2,1)S(1)} %broadcast_select_fusion), channel_id=1, source_target_pairs={{0,2},{2,0},{4,6},{6,4},{12,14},{14,12},{8,10},{10,8},{1,5},{3,7},... | collective-permute-start | bytes 1198088 | tf_op jit(solution)/shard_map/ppermute | solution.py:279
  45.0 1.9 %shard_map.78 = (bf16[48,64]{1,0:T(8,128)(2,1)S(1)}, s32[48,128]{1,0:T(8,128)S(1)}) custom-call(bf16[24,8320]{1,0:T(8,128)(2,1)S(1)} %collective-permute-done.4.refs_0_, bf16[24,8320]{1,0:T(8,128)(2,1)} %collective-permute-done.6.refs_1_, bf16[64,8192]{1,0:T(8,128)(2,1)S(1)} %bitcast.10, bf16[64,8192]{1,0:T(8,128)(2,1)S(1)} %collective-permute-done.3.refs_3_), custom_call_target="tpu_custom_call" | custom-call | flops 1 | bytes 1 | tf_op jit(solution)/shard_map/pallas_call | solution.py:57
  46.9 2.6 %collective-permute-start.11 = (bf16[48,64]{1,0:T(8,128)(2,1)S(1)}, bf16[48,64]{1,0:T(8,128)(2,1)S(1)}, u32[]{:S(2)}, u32[]{:S(2)}) collective-permute-start(bf16[48,64]{1,0:T(8,128)(2,1)S(1)} %get-tuple-element.50), channel_id=1, source_target_pairs={{0,8},{1,9},{2,10},{3,11},{4,0},{5,1},{6,2},{7,3},{12,4},{13,5},{1... | collective-permute-start | bytes 18440 | tf_op jit(solution)/shard_map/ppermute | solution.py:256
  49.5 4.8 %shard_map.77.refs_1_ = f32[96,512]{1,0:T(8,128)S(1)} custom-call(bf16[24,8320]{1,0:T(8,128)(2,1)S(1)} %copy-done.3, bf16[24,8320]{1,0:T(8,128)(2,1)S(1)} %copy-done.5, bf16[24,8320]{1,0:T(8,128)(2,1)} %collective-permute-done.1.refs_2_.refs_0_, bf16[24,8320]{1,0:T(8,128)(2,1)S(1)} %collective-permute-done.2.refs_3_.refs_1_, ...), custom_call_target="tpu_custom_call" | custom-call | flops 1 | bytes 1 | tf_op jit(solution)/shard_map/pallas_call | solution.py:57
  54.3 1.5 %collective-permute-done.11.refs_6_ = bf16[48,64]{1,0:T(8,128)(2,1)S(1)} collective-permute-done((bf16[48,64]{1,0:T(8,128)(2,1)S(1)}, bf16[48,64]{1,0:T(8,128)(2,1)S(1)}, u32[]{:S(2)}, u32[]{:S(2)}) %collective-permute-start.11) | collective-permute-done | bytes 6176 | tf_op jit(solution)/shard_map/ppermute | solution.py:256
  57.3 4.8 %shard_map.79.refs_2_ = f32[96,512]{1,0:T(8,128)S(1)} custom-call(bf16[24,8320]{1,0:T(8,128)(2,1)S(1)} %collective-permute-done.4.refs_0_, bf16[24,8320]{1,0:T(8,128)(2,1)} %collective-permute-done.6.refs_1_, bf16[24,8320]{1,0:T(8,128)(2,1)S(1)} %collective-permute-done.5.refs_2_.refs_0_, bf16[24,8320]{1,0:T(8,128)(2,1)S(1)} %collective-permute-done.10.refs_3_.refs_1_, ...), custom_call_target="tpu_custom_call" | custom-call | flops 1 | bytes 1 | tf_op jit(solution)/shard_map/pallas_call | solution.py:57
  62.1 5.6 %collective-permute-start.13 = (bf16[48,64]{1,0:T(8,128)(2,1)S(1)}, bf16[48,64]{1,0:T(8,128)(2,1)S(1)}, u32[]{:S(2)}, u32[]{:S(2)}) collective-permute-start(bf16[48,64]{1,0:T(8,128)(2,1)S(1)} %maximum_add_fusion.refs_7_), channel_id=1, source_target_pairs={{0,12},{1,13},{2,14},{3,15},{4,8},{5,9},{6,10},{7,11},{12,0},{13,1... | collective-permute-start | bytes 18440 | tf_op jit(solution)/shard_map/ppermute | solution.py:256
  67.7 2.0 %collective-permute-start.15 = (bf16[48,64]{1,0:T(8,128)(2,1)S(1)}, bf16[48,64]{1,0:T(8,128)(2,1)S(1)}, u32[]{:S(2)}, u32[]{:S(2)}) collective-permute-start(bf16[48,64]{1,0:T(8,128)(2,1)S(1)} %maximum_add_fusion.refs_7_), channel_id=1, source_target_pairs={{0,4},{1,5},{2,6},{3,7},{4,12},{5,13},{6,14},{7,15},{12,8},{13,9},... | collective-permute-start | bytes 18440 | tf_op jit(solution)/shard_map/ppermute | solution.py:256
  69.7 4.8 %shard_map.80.refs_3_ = f32[96,512]{1,0:T(8,128)S(1)} custom-call(bf16[24,8320]{1,0:T(8,128)(2,1)S(1)} %collective-permute-done.4.refs_0_, bf16[24,8320]{1,0:T(8,128)(2,1)} %collective-permute-done.6.refs_1_, bf16[24,8320]{1,0:T(8,128)(2,1)S(1)} %collective-permute-done.5.refs_2_.refs_0_, bf16[24,8320]{1,0:T(8,128)(2,1)S(1)} %collective-permute-done.10.refs_3_.refs_1_, ...), custom_call_target="tpu_custom_call" | custom-call | flops 1 | bytes 1 | tf_op jit(solution)/shard_map/pallas_call | solution.py:57
  74.5 1.6 %shard_map.82 = (bf16[24,1024]{1,0:T(8,128)(2,1)S(1)}, bf16[24,1024]{1,0:T(8,128)(2,1)S(1)}, bf16[24,1024]{1,0:T(8,128)(2,1)S(1)}, bf16[24,1024]{1,0:T(8,128)(2,...) custom-call(f32[96,512]{1,0:T(8,128)S(1)} %shard_map.75.refs_0_, ...), custom_call_target="tpu_custom_call" | custom-call | flops 1 | bytes 1 | tf_op jit(solution)/shard_map/pallas_call | solution.py:57
  76.2 1.6 %collective-permute-start.17 = (bf16[24,1024]{1,0:T(8,128)(2,1)S(1)}, bf16[24,1024]{1,0:T(8,128)(2,1)S(1)}, u32[]{:S(2)}, u32[]{:S(2)}) collective-permute-start(bf16[24,1024]{1,0:T(8,128)(2,1)S(1)} %get-tuple-element.60), channel_id=1, source_target_pairs={{0,2},{1,3},{2,0},{3,1},{4,6},{5,7},{6,4},{7,5},{12,14},{13,15},{1... | collective-permute-start | bytes 147464 | tf_op jit(solution)/shard_map/ppermute | solution.py:256
  78.6 2.0 %collective-permute-start.20 = (bf16[24,1024]{1,0:T(8,128)(2,1)S(1)}, bf16[24,1024]{1,0:T(8,128)(2,1)S(1)}, u32[]{:S(2)}, u32[]{:S(2)}) collective-permute-start(bf16[24,1024]{1,0:T(8,128)(2,1)S(1)} %get-tuple-element.63), channel_id=1, source_target_pairs={{0,4},{1,5},{2,6},{3,7},{4,12},{5,13},{6,14},{7,15},{12,8},{13,9},... | collective-permute-start | bytes 147464 | tf_op jit(solution)/shard_map/ppermute | solution.py:256
  80.6 3.0 %collective-permute-start.21 = (bf16[24,1024]{1,0:T(8,128)(2,1)S(1)}, bf16[24,1024]{1,0:T(8,128)(2,1)S(1)}, u32[]{:S(2)}, u32[]{:S(2)}) collective-permute-start(bf16[24,1024]{1,0:T(8,128)(2,1)S(1)} %get-tuple-element.64), channel_id=1, source_target_pairs={{0,6},{1,7},{2,4},{3,5},{4,14},{5,15},{6,12},{7,13},{12,10},{13,11... | collective-permute-start | bytes 147464 | tf_op jit(solution)/shard_map/ppermute | solution.py:256
  83.9 3.4 %collective-permute-start.23 = (bf16[24,1024]{1,0:T(8,128)(2,1)S(1)}, bf16[24,1024]{1,0:T(8,128)(2,1)S(1)}, u32[]{:S(2)}, u32[]{:S(2)}) collective-permute-start(bf16[24,1024]{1,0:T(8,128)(2,1)S(1)} %get-tuple-element.66), channel_id=1, source_target_pairs={{0,14},{1,15},{2,12},{3,13},{4,10},{5,11},{6,8},{7,9},{12,2},{13,3... | collective-permute-start | bytes 147464 | tf_op jit(solution)/shard_map/ppermute | solution.py:256
  87.5 2.0 %collective-permute-done.22.refs_6_ = bf16[24,1024]{1,0:T(8,128)(2,1)S(1)} collective-permute-done((bf16[24,1024]{1,0:T(8,128)(2,1)S(1)}, bf16[24,1024]{1,0:T(8,128)(2,1)S(1)}, u32[]{:S(2)}, u32[]{:S(2)}) %collective-permute-start.22) | collective-permute-done | bytes 49184 | tf_op jit(solution)/shard_map/ppermute | solution.py:256
  (52 shorter events, 13.1 us)
Async XLA Ops:
  0.0 49.5 %collective-permute-start.9 = (bf16[8192,512]{1,0:T(8,128)(2,1)}, bf16[8192,512]{1,0:T(8,128)(2,1)}, u32[]{:S(2)}, u32[]{:S(2)}) collective-permute-start(bf16[8192,512]{1,0:T(8,128)(2,1)} %refs_4_.3), channel_id=1, source_target_pairs={{0,1},{1,0},{2,3},{3,2},{4,5},{5,4},{6,7},{7,6},{12,13},{13,12},{1... | collective-permute-start | bytes 25165832 | tf_op jit(solution)/shard_map/ppermute | solution.py:256
  0.5 26.9 %collective-permute-start.3 = (bf16[64,8192]{1,0:T(8,128)(2,1)}, bf16[64,8192]{1,0:T(8,128)(2,1)S(1)}, u32[]{:S(2)}, u32[]{:S(2)}) collective-permute-start(bf16[64,8192]{1,0:T(8,128)(2,1)} %bitcast.7), channel_id=1, source_target_pairs={{0,1},{1,0},{2,3},{3,2},{4,5},{5,4},{6,7},{7,6},{12,13},{13,12},{1... | collective-permute-start | bytes 3145736 | tf_op jit(solution)/shard_map/ppermute | solution.py:256
  2.5 13.9 %collective-permute-start.1 = (bf16[24,8320]{1,0:T(8,128)(2,1)}, bf16[24,8320]{1,0:T(8,128)(2,1)}, u32[]{:S(2)}, u32[]{:S(2)}) collective-permute-start(bf16[24,8320]{1,0:T(8,128)(2,1)} %shard_map.73.refs_0_), channel_id=1, source_target_pairs={{0,4},{1,5},{2,6},{3,7},{4,12},{5,13},{6,14},{7,15},{12,8},{13,9},... | collective-permute-start | bytes 1198088 | tf_op jit(solution)/shard_map/ppermute | solution.py:256
  5.6 12.4 %collective-permute-start = (bf16[24,8320]{1,0:T(8,128)(2,1)}, bf16[24,8320]{1,0:T(8,128)(2,1)S(1)}, u32[]{:S(2)}, u32[]{:S(2)}) collective-permute-start(bf16[24,8320]{1,0:T(8,128)(2,1)} %shard_map.73.refs_0_), channel_id=1, source_target_pairs={{0,2},{1,3},{2,0},{3,1},{4,6},{5,7},{6,4},{7,5},{12,14},{13,15},{1... | collective-permute-start | bytes 1198088 | tf_op jit(solution)/shard_map/ppermute | solution.py:256
  7.1 23.3 %collective-permute-start.4 = (bf16[24,8320]{1,0:T(8,128)(2,1)}, bf16[24,8320]{1,0:T(8,128)(2,1)S(1)}, u32[]{:S(2)}, u32[]{:S(2)}) collective-permute-start(bf16[24,8320]{1,0:T(8,128)(2,1)} %shard_map.73.refs_0_), channel_id=1, source_target_pairs={{0,8},{1,9},{2,10},{3,11},{4,0},{5,1},{6,2},{7,3},{12,4},{13,5},{1... | collective-permute-start | bytes 1198088 | tf_op jit(solution)/shard_map/ppermute | solution.py:256
  16.5 17.6 %collective-permute-start.2 = (bf16[24,8320]{1,0:T(8,128)(2,1)}, bf16[24,8320]{1,0:T(8,128)(2,1)S(1)}, u32[]{:S(2)}, u32[]{:S(2)}) collective-permute-start(bf16[24,8320]{1,0:T(8,128)(2,1)} %collective-permute-done.1.refs_2_.refs_0_), channel_id=1, source_target_pairs={{0,2},{1,3},{2,0},{3,1},{4,6},{5,7},{6,4},{7,5},{12,14},{13,15},{1... | collective-permute-start | bytes 1198088 | tf_op jit(solution)/shard_map/ppermute | solution.py:256
  18.0 25.2 %collective-permute-start.5 = (bf16[24,8320]{1,0:T(8,128)(2,1)}, bf16[24,8320]{1,0:T(8,128)(2,1)S(1)}, u32[]{:S(2)}, u32[]{:S(2)}) collective-permute-start(bf16[24,8320]{1,0:T(8,128)(2,1)} %collective-permute-done.1.refs_2_.refs_0_), channel_id=1, source_target_pairs={{0,4},{1,5},{2,6},{3,7},{4,12},{5,13},{6,14},{7,15},{12,8},{13,9},... | collective-permute-start | bytes 1198088 | tf_op jit(solution)/shard_map/ppermute | solution.py:256
  30.5 12.8 %collective-permute-start.6 = (bf16[24,8320]{1,0:T(8,128)(2,1)S(1)}, bf16[24,8320]{1,0:T(8,128)(2,1)}, u32[]{:S(2)}, u32[]{:S(2)}) collective-permute-start(bf16[24,8320]{1,0:T(8,128)(2,1)S(1)} %collective-permute-done.4.refs_0_), channel_id=1, source_target_pairs={{0,2},{1,3},{2,0},{3,1},{4,6},{5,7},{6,4},{7,5},{12,14},{13,15},{1... | collective-permute-start | bytes 1198088 | tf_op jit(solution)/shard_map/ppermute | solution.py:256
  31.0 12.2 %collective-permute-start.7 = (bf16[48,64]{1,0:T(8,128)(2,1)S(1)}, bf16[48,64]{1,0:T(8,128)(2,1)S(1)}, u32[]{:S(2)}, u32[]{:S(2)}) collective-permute-start(bf16[48,64]{1,0:T(8,128)(2,1)S(1)} %get-tuple-element.36), channel_id=1, source_target_pairs={{0,12},{1,13},{2,14},{3,15},{4,8},{5,9},{6,10},{7,11},{12,0},{13,1... | collective-permute-start | bytes 18440 | tf_op jit(solution)/shard_map/ppermute | solution.py:256
  35.9 7.4 %collective-permute-start.8 = (bf16[48,64]{1,0:T(8,128)(2,1)S(1)}, bf16[48,64]{1,0:T(8,128)(2,1)S(1)}, u32[]{:S(2)}, u32[]{:S(2)}) collective-permute-start(bf16[48,64]{1,0:T(8,128)(2,1)S(1)} %get-tuple-element.40), channel_id=1, source_target_pairs={{0,4},{1,5},{2,6},{3,7},{4,12},{5,13},{6,14},{7,15},{12,8},{13,9},... | collective-permute-start | bytes 18440 | tf_op jit(solution)/shard_map/ppermute | solution.py:256
  43.4 31.1 %collective-permute-start.16 = (bf16[1024,512]{1,0:T(8,128)(2,1)S(1)}, bf16[1024,512]{1,0:T(8,128)(2,1)S(1)}, u32[]{:S(2)}, u32[]{:S(2)}) collective-permute-start(bf16[1024,512]{1,0:T(8,128)(2,1)S(1)} %bitcast.12), channel_id=1, source_target_pairs={{0,1},{1,0},{2,3},{3,2},{4,5},{5,4},{6,7},{7,6},{12,13},{13,12},{1... | collective-permute-start | bytes 3145736 | tf_op jit(solution)/shard_map/ppermute | solution.py:256
  43.5 10.8 %collective-permute-start.10 = (bf16[24,8320]{1,0:T(8,128)(2,1)S(1)}, bf16[24,8320]{1,0:T(8,128)(2,1)S(1)}, u32[]{:S(2)}, u32[]{:S(2)}) collective-permute-start(bf16[24,8320]{1,0:T(8,128)(2,1)S(1)} %broadcast_select_fusion), channel_id=1, source_target_pairs={{0,2},{2,0},{4,6},{6,4},{12,14},{14,12},{8,10},{10,8},{1,5},{3,7},... | collective-permute-start | bytes 1198088 | tf_op jit(solution)/shard_map/ppermute | solution.py:279
  46.9 8.9 %collective-permute-start.11 = (bf16[48,64]{1,0:T(8,128)(2,1)S(1)}, bf16[48,64]{1,0:T(8,128)(2,1)S(1)}, u32[]{:S(2)}, u32[]{:S(2)}) collective-permute-start(bf16[48,64]{1,0:T(8,128)(2,1)S(1)} %get-tuple-element.50), channel_id=1, source_target_pairs={{0,8},{1,9},{2,10},{3,11},{4,0},{5,1},{6,2},{7,3},{12,4},{13,5},{1... | collective-permute-start | bytes 18440 | tf_op jit(solution)/shard_map/ppermute | solution.py:256
  56.7 5.4 %collective-permute-start.12 = (bf16[48,64]{1,0:T(8,128)(2,1)S(1)}, bf16[48,64]{1,0:T(8,128)(2,1)S(1)}, u32[]{:S(2)}, u32[]{:S(2)}) collective-permute-start(bf16[48,64]{1,0:T(8,128)(2,1)S(1)} %get-tuple-element.52), channel_id=1, source_target_pairs={{0,2},{1,3},{2,0},{3,1},{4,6},{5,7},{6,4},{7,5},{12,14},{13,15},{1... | collective-permute-start | bytes 18440 | tf_op jit(solution)/shard_map/ppermute | solution.py:256
  62.1 12.4 %collective-permute-start.13 = (bf16[48,64]{1,0:T(8,128)(2,1)S(1)}, bf16[48,64]{1,0:T(8,128)(2,1)S(1)}, u32[]{:S(2)}, u32[]{:S(2)}) collective-permute-start(bf16[48,64]{1,0:T(8,128)(2,1)S(1)} %maximum_add_fusion.refs_7_), channel_id=1, source_target_pairs={{0,12},{1,13},{2,14},{3,15},{4,8},{5,9},{6,10},{7,11},{12,0},{13,1... | collective-permute-start | bytes 18440 | tf_op jit(solution)/shard_map/ppermute | solution.py:256
  67.7 6.8 %collective-permute-start.14 = (bf16[48,64]{1,0:T(8,128)(2,1)S(1)}, bf16[48,64]{1,0:T(8,128)(2,1)S(1)}, u32[]{:S(2)}, u32[]{:S(2)}) collective-permute-start(bf16[48,64]{1,0:T(8,128)(2,1)S(1)} %maximum_add_fusion.refs_7_), channel_id=1, source_target_pairs={{0,8},{1,9},{2,10},{3,11},{4,0},{5,1},{6,2},{7,3},{12,4},{13,5},{1... | collective-permute-start | bytes 18440 | tf_op jit(solution)/shard_map/ppermute | solution.py:256
  67.7 6.8 %collective-permute-start.15 = (bf16[48,64]{1,0:T(8,128)(2,1)S(1)}, bf16[48,64]{1,0:T(8,128)(2,1)S(1)}, u32[]{:S(2)}, u32[]{:S(2)}) collective-permute-start(bf16[48,64]{1,0:T(8,128)(2,1)S(1)} %maximum_add_fusion.refs_7_), channel_id=1, source_target_pairs={{0,4},{1,5},{2,6},{3,7},{4,12},{5,13},{6,14},{7,15},{12,8},{13,9},... | collective-permute-start | bytes 18440 | tf_op jit(solution)/shard_map/ppermute | solution.py:256
  76.2 7.4 %collective-permute-start.17 = (bf16[24,1024]{1,0:T(8,128)(2,1)S(1)}, bf16[24,1024]{1,0:T(8,128)(2,1)S(1)}, u32[]{:S(2)}, u32[]{:S(2)}) collective-permute-start(bf16[24,1024]{1,0:T(8,128)(2,1)S(1)} %get-tuple-element.60), channel_id=1, source_target_pairs={{0,2},{1,3},{2,0},{3,1},{4,6},{5,7},{6,4},{7,5},{12,14},{13,15},{1... | collective-permute-start | bytes 147464 | tf_op jit(solution)/shard_map/ppermute | solution.py:256
  77.7 6.2 %collective-permute-start.18 = (bf16[24,1024]{1,0:T(8,128)(2,1)S(1)}, bf16[24,1024]{1,0:T(8,128)(2,1)S(1)}, u32[]{:S(2)}, u32[]{:S(2)}) collective-permute-start(bf16[24,1024]{1,0:T(8,128)(2,1)S(1)} %get-tuple-element.61), channel_id=1, source_target_pairs={{0,8},{1,9},{2,10},{3,11},{4,0},{5,1},{6,2},{7,3},{12,4},{13,5},{1... | collective-permute-start | bytes 147464 | tf_op jit(solution)/shard_map/ppermute | solution.py:256
  78.6 8.7 %collective-permute-start.19 = (bf16[24,1024]{1,0:T(8,128)(2,1)S(1)}, bf16[24,1024]{1,0:T(8,128)(2,1)S(1)}, u32[]{:S(2)}, u32[]{:S(2)}) collective-permute-start(bf16[24,1024]{1,0:T(8,128)(2,1)S(1)} %get-tuple-element.62), channel_id=1, source_target_pairs={{0,10},{1,11},{2,8},{3,9},{4,2},{5,3},{6,0},{7,1},{12,6},{13,7},{1... | collective-permute-start | bytes 147464 | tf_op jit(solution)/shard_map/ppermute | solution.py:256
  78.6 8.7 %collective-permute-start.20 = (bf16[24,1024]{1,0:T(8,128)(2,1)S(1)}, bf16[24,1024]{1,0:T(8,128)(2,1)S(1)}, u32[]{:S(2)}, u32[]{:S(2)}) collective-permute-start(bf16[24,1024]{1,0:T(8,128)(2,1)S(1)} %get-tuple-element.63), channel_id=1, source_target_pairs={{0,4},{1,5},{2,6},{3,7},{4,12},{5,13},{6,14},{7,15},{12,8},{13,9},... | collective-permute-start | bytes 147464 | tf_op jit(solution)/shard_map/ppermute | solution.py:256
  80.6 6.9 %collective-permute-start.21 = (bf16[24,1024]{1,0:T(8,128)(2,1)S(1)}, bf16[24,1024]{1,0:T(8,128)(2,1)S(1)}, u32[]{:S(2)}, u32[]{:S(2)}) collective-permute-start(bf16[24,1024]{1,0:T(8,128)(2,1)S(1)} %get-tuple-element.64), channel_id=1, source_target_pairs={{0,6},{1,7},{2,4},{3,5},{4,14},{5,15},{6,12},{7,13},{12,10},{13,11... | collective-permute-start | bytes 147464 | tf_op jit(solution)/shard_map/ppermute | solution.py:256
  83.6 5.9 %collective-permute-start.22 = (bf16[24,1024]{1,0:T(8,128)(2,1)S(1)}, bf16[24,1024]{1,0:T(8,128)(2,1)S(1)}, u32[]{:S(2)}, u32[]{:S(2)}) collective-permute-start(bf16[24,1024]{1,0:T(8,128)(2,1)S(1)} %get-tuple-element.65), channel_id=1, source_target_pairs={{0,12},{1,13},{2,14},{3,15},{4,8},{5,9},{6,10},{7,11},{12,0},{13,1... | collective-permute-start | bytes 147464 | tf_op jit(solution)/shard_map/ppermute | solution.py:256
  83.9 6.8 %collective-permute-start.23 = (bf16[24,1024]{1,0:T(8,128)(2,1)S(1)}, bf16[24,1024]{1,0:T(8,128)(2,1)S(1)}, u32[]{:S(2)}, u32[]{:S(2)}) collective-permute-start(bf16[24,1024]{1,0:T(8,128)(2,1)S(1)} %get-tuple-element.66), channel_id=1, source_target_pairs={{0,14},{1,15},{2,12},{3,13},{4,10},{5,11},{6,8},{7,9},{12,2},{13,3... | collective-permute-start | bytes 147464 | tf_op jit(solution)/shard_map/ppermute | solution.py:256
  (7 other events, 42.6 us)

commit v8 on v7

--- a/solution.py
+++ b/solution.py
@@ -14,6 +14,7 @@
 LANES = 128
 CHUNK = 1024
 VMEM_LIMIT = 24 << 20
+AHEAD = 2
 VMEM = pl.BlockSpec(memory_space=pltpu.VMEM)
 
 
@@ -122,10 +123,10 @@
     return jnp.concatenate(wide, axis=0).astype(jnp.bfloat16)
 
 
-def shrink_kernel(*refs):
-    blocks, (own_ref, other_ref, *before, part_ref, slot_ref) = refs[:SIDE], refs[SIDE:]
+def shrink_kernel(count, *refs):
+    blocks, (own_ref, other_ref, *before, part_ref, slot_ref) = refs[:count], refs[count:]
     rank, width = own_ref.shape
-    rows = part_ref.shape[0]
+    rows = slot_ref.shape[0]
     part = jnp.zeros((rows, 2 * rank), jnp.float32)
     for start in range(0, width, CHUNK):
         lanes = slice(start, start + CHUNK)
@@ -141,18 +142,41 @@
     lanes = lax.broadcasted_iota(jnp.int32, part.shape, 1)
     part = jnp.where(slot == jnp.where(lanes < rank, me, me ^ 1), part, 0.0)
     part = part[:, :rank] + part[:, rank:]
+    first = 0
     for ref in before:
-        part = part + ref[...].astype(jnp.float32)
-    part_ref[...] = part.astype(jnp.bfloat16)
-
-
-def shrink_rows(blocks, own, other, before):
-    rows = blocks[0].shape[0] * SIDE
+        part_ref[first : first + ref.shape[0], :] = ref[...]
+        first += ref.shape[0]
+    part_ref[first:, :] = part.astype(jnp.bfloat16)
+
+
+def shrink_rows(blocks, own, other, before=()):
+    rows = blocks[0].shape[0] * len(blocks)
+    total = rows + sum(part.shape[0] for part in before)
     out_shape = (
-        jax.ShapeDtypeStruct((rows, own.shape[0]), jnp.bfloat16),
+        jax.ShapeDtypeStruct((total, own.shape[0]), jnp.bfloat16),
         jax.ShapeDtypeStruct((rows, LANES), jnp.int32),
     )
-    return call(shrink_kernel, out_shape, (*blocks, own, other, *before))
+    return call(
+        lambda *refs: shrink_kernel(len(blocks), *refs), out_shape, (*blocks, own, other, *before)
+    )
+
+
+def pack_kernel(own_rows, part_ref, across_ref, out_ref):
+    rows, rank = part_ref.shape
+    part = part_ref[...].astype(jnp.float32)
+    across = across_ref[...].astype(jnp.float32)
+    swapped = []
+    for first in range(0, rows, SIDE * own_rows):
+        middle, last = first + own_rows, first + SIDE * own_rows
+        swapped += [across[middle:last], across[first:middle]]
+    total = part + jnp.concatenate(swapped, axis=0)
+    out_ref[...] = jnp.concatenate([total[: rows // 2], total[rows // 2 :]], axis=1).astype(jnp.bfloat16)
+
+
+def pack(part, across, own_rows):
+    rows, rank = part.shape
+    out_shape = jax.ShapeDtypeStruct((rows // 2, 2 * rank), part.dtype)
+    return call(lambda *refs: pack_kernel(own_rows, *refs), out_shape, (part, across))
 
 
 def base_kernel(*refs):
@@ -164,12 +188,15 @@
         copies.append(
             pltpu.make_async_copy(weight_ref.at[rows], buffer.at[rows], sems.at[number])
         )
-        copies[-1].start()
+    for copy in copies[:AHEAD]:
+        copy.start()
     out_ref[...] = jnp.zeros(out_ref.shape, jnp.float32)
     for number, start in enumerate(range(0, width, CHUNK)):
         lanes = slice(start, start + CHUNK)
         rows = stacked(blocks, lanes)
         copies[number].wait()
+        if number + AHEAD < len(copies):
+            copies[number + AHEAD].start()
         out_ref[...] += jnp.dot(rows, buffer[lanes, :], preferred_element_type=jnp.float32)
 
 
@@ -189,56 +216,41 @@
     )
 
 
-def finish_kernel(steps, per_base, *refs):
-    bases, refs = refs[: 2 * (steps // per_base)], refs[2 * (steps // per_base) :]
-    shrinks, slots, (own_ref, other_ref, *outs) = refs[:steps], refs[steps : 2 * steps], refs[2 * steps :]
-    rows, rank = shrinks[0].shape
-    own_rows = rows // SIDE
-    columns = own_ref.shape[1]
-    depth = own_ref.shape[0]
+def finish_kernel(places, rank, *refs):
+    moved, refs = refs[:places], refs[places:]
+    slot_count = len(refs) - places - 3
+    bases, slots = refs[:places], refs[places : places + slot_count]
+    own_ref, other_ref, out_ref = refs[places + slot_count :]
+    depth, columns = own_ref.shape
+    rows = SIDE * out_ref.shape[1]
     core = lax.axis_index("adapter") % CORES
     lanes = lax.broadcasted_iota(jnp.int32, (rows, depth), 1)
-    for step in range(steps):
-        wide = jnp.concatenate([shrinks[step][...].astype(jnp.float32)] * (depth // rank), axis=1)
-        spread = jnp.where(lanes // rank == slots[step][:, 0:1], wide, 0.0).astype(jnp.bfloat16)
-        first = step % per_base * rows
+    slot = jnp.concatenate([ref[:, 0:1] for ref in slots], axis=0)
+    for step in range(places):
+        shrink = jnp.zeros((rows, rank), jnp.float32)
+        for back in range(places):
+            half, first = divmod((step - back) % places, places // 2)
+            part = moved[back][first * rows : (first + 1) * rows, half * rank : (half + 1) * rank]
+            shrink += part.astype(jnp.float32)
+        wide = jnp.concatenate([shrink] * (depth // rank), axis=1)
+        here = slot[step * rows : (step + 1) * rows]
+        spread = jnp.where(lanes // rank == here, wide, 0.0).astype(jnp.bfloat16)
         for which, up_ref in enumerate((own_ref, other_ref)):
             update = jnp.dot(spread, up_ref[...], preferred_element_type=jnp.float32)
-            base = bases[2 * (step // per_base) + which][first : first + rows, :]
+            base = bases[step // 2 * 2 + which][step % 2 * rows : (step % 2 + 1) * rows, :]
             query = (base + ADAPTER_SCALE * update).astype(jnp.bfloat16)
             at = pl.multiple_of((core ^ which) * columns, columns)
             for side in range(SIDE):
-                outs[step * SIDE + side][:, pl.ds(at, columns)] = query[
-                    side * own_rows : (side + 1) * own_rows
-                ]
-
-
-def finish(bases, shrinks, slots, own, other):
-    steps, per_base = len(shrinks), 2 * len(shrinks) // len(bases)
-    rows = shrinks[0].shape[0] // SIDE
-    block = jax.ShapeDtypeStruct((rows, CORES * own.shape[1]), jnp.bfloat16)
+                chip = ring_chip(places, -step, side)
+                out_ref[chip, :, pl.ds(at, columns)] = query[side * rows // SIDE : (side + 1) * rows // SIDE]
+
+
+def finish(moved, bases, slots, own, other, own_rows):
+    places, rank = len(moved), moved[0].shape[1] // 2
     return call(
-        lambda *refs: finish_kernel(steps, per_base, *refs),
-        [block] * (steps * SIDE),
-        (*bases, *shrinks, *slots, own, other),
-    )
-
-
-def assemble_kernel(places, offsets, *refs):
-    *blocks, out_ref = refs
-    columns = blocks[0].shape[1]
-    for step, offset in enumerate(offsets):
-        for side in range(SIDE):
-            at = pl.multiple_of(ring_chip(places, offset, side) * columns, columns)
-            out_ref[:, pl.ds(at, columns)] = blocks[step * SIDE + side][...]
-
-
-def assemble(places, offsets, blocks):
-    rows, columns = blocks[0].shape
-    return call(
-        lambda *refs: assemble_kernel(places, offsets, *refs),
-        jax.ShapeDtypeStruct((rows, columns * len(blocks)), jnp.bfloat16),
-        blocks,
+        lambda *refs: finish_kernel(places, rank, *refs),
+        jax.ShapeDtypeStruct((places * SIDE, own_rows, CORES * own.shape[1]), jnp.bfloat16),
+        (*moved, *bases, *slots, own, other),
     )
 
 
@@ -255,61 +267,47 @@
     def move(x, steps, flip):
         return lax.ppermute(x, "adapter", pairs(places, steps, flip))
 
-    chain = normalize(hidden, norm_weight, adapter_index, adapter_slot)
     down = down_weights[0].T
     up = up_weights.reshape(devices * rank, columns)
     down_other = move(down, 0, 1)
+    up_other = move(up, 0, 1)
     weight_other = move(query_weight, 0, 1)
 
-    far = places // 2
-    offsets = [0] + [sign * near for near in range(1, far) for sign in (1, -1)] + [far]
-    block = {0: chain}
-    for near in range(1, far):
-        block[near] = move(block[near - 1], 1, 0)
-        block[-near] = move(block[1 - near], -1, 0)
-    block[far] = move(block[far - 1], 1, 0)
-    other, parts, slots, before, bases, queue = {}, [], [], [], [], []
-    for number, offset in enumerate(offsets):
-        here = after(block[offset], *parts[:-1])
-        if offset != far:
-            other[offset] = move(here, 0, 2)
-        else:
-            here = after(here, other[offsets[-2]], *before[:-1], *bases)
-            source = jnp.where((me & 1) == 0, here, other[far - 1])
-            other[far] = lax.ppermute(source, "adapter", split_pairs(places))
-            bases.append(base_rows(after(queue, source), weight_other))
-            up_other = move(after(up, source), 0, 1)
-            other[far] = after(other[far], bases[-1])
-        rows = [here, after(other[offset], *parts)]
-        if 0 < offset < far:
-            rows = after(rows, block[-offset])
-        part, slot = shrink_rows(rows, down, down_other, before if offset == far else [])
-        parts.append(part)
-        slots.append(slot)
-        if offset != far:
-            before.append(move(part, far - offset, 0))
-        if number % 2 == 0:
-            waiting = rows
-        else:
-            if queue and offset != far:
-                bases.append(base_rows(queue, weight_other))
-            queue = waiting + rows
-            if offset != far:
-                bases.append(base_rows(queue, query_weight))
+    block, other = [normalize(hidden, norm_weight, adapter_index, adapter_slot)], []
+    parts, slots, bases = [], [], []
+    last = places - 1
+    for step in range(last):
+        block.append(move(block[step], 1, 0))
+        other.append(move(after(block[step], *other[-1:]), 0, 2))
+        if step % 2 == 0 and step:
+            rows = [block[step - 2], other[step - 2], block[step - 1], other[step - 1]]
+            rows = after(rows, block[step])
+            part, slot = shrink_rows(rows, down, down_other)
+            parts.append(part)
+            slots.append(slot)
+            bases.append(base_rows(after(rows, part), query_weight))
+            if step < last - 1:
+                bases.append(base_rows(rows, weight_other))
+    source = jnp.where((me & 1) == 0, after(block[last], *bases, other[-1]), other[-1])
+    crossed = lax.ppermute(source, "adapter", split_pairs(places))
+    part, slot = shrink_rows(after([block[last - 1], other[-1]], source), down, down_other)
+    parts.append(part)
+    slots.append(slot)
+    bases.append(base_rows(after(rows, part), weight_other))
+    crossed = after(crossed, *bases)
+    part, slot = shrink_rows([block[last], crossed], down, down_other, parts)
+    slots.append(slot)
 
     across = move(part, 0, 2)
-    base_own = base_rows(queue, query_weight)
-    across = after(across, base_own)
-    part = part + jnp.concatenate([across[own_rows:], across[:own_rows]], axis=0)
-    shrinks = [part if offset == far else move(part, offset - far, 0) for offset in offsets]
-    bases += [base_own, base_rows(queue, weight_other)]
-    blocks = finish(bases, shrinks, slots, up, up_other)
-    parts = []
-    for number, offset in enumerate(offsets):
-        for side in range(SIDE):
-            piece = blocks[number * SIDE + side]
-            parts.append(move(piece, -offset, 2 * side) if offset or side else piece)
-    return assemble(places, offsets, parts)
+    rows = [block[last - 1], other[-1], block[last], crossed]
+    bases.append(base_rows(rows, query_weight))
+    part = pack(part, after(across, bases[-1]), own_rows)
+    moved = [part] + [move(part, steps, 0) for steps in range(1, places)]
+    bases.append(base_rows(rows, weight_other))
+    query = finish(moved, bases, slots, up, up_other, own_rows)
+    groups = [list(range(core, devices, CORES)) for core in range(CORES)]
+    query = lax.all_to_all(query, "adapter", 0, 0, axis_index_groups=groups, tiled=True)
+    return query.transpose(1, 0, 2).reshape(own_rows, devices * columns)
 
 
 def solution(mesh):

time: 92 us -> 86.5 us (0.940)
  starting transfers between devices: 44.9 us -> 17.6 us
  blocking collectives: 0 us -> 14.6 us
  waiting for transfers between devices: 12.9 us -> 19.5 us
  Pallas kernels: 29.2 us -> 30.9 us
  local copies, waits for them, and re-layouts: 4.23 us -> 3 us
    ppermute x23 -> x13, starting transfers between devices: 43.3 us -> 17 us  [move(): return lax.ppermute(x, 'adapter', pairs(places, steps, flip))]
    all_to_all x0 -> x1, blocking collectives: none -> 14.6 us  [shards(): lax.all_to_all(query, 'adapter', 0, 0, axis_index_groups=groups, tiled=True)]
    ppermute x23 -> x13, waiting for transfers between devices: 12.9 us -> 18.8 us  [move(): return lax.ppermute(x, 'adapter', pairs(places, steps, flip))]
    unnamed x14 -> x8, local copies, waits for them, and re-layouts: 4.23 us -> 2.23 us
    pallas_call x10 -> x9, Pallas kernels: 27.2 us -> 28.9 us  [call(): pl.pallas_call(kernel, out_shape=out_shape, in_specs=[VMEM] * len(operand...]
    ppermute x1, starting transfers between devices: 1.57 us -> 0.56 us  [shards(): crossed = lax.ppermute(source, 'adapter', split_pairs(places))]
  transfers between devices with their start and end apart: 24 -> 14, of which waited for: 5 -> 5; matrix products, arithmetic and copies ran while one was open for 0% -> 0% of each run, Pallas kernels for 29% -> 33%
where the time goes in v8:
time: 86.5 us; the launch traced here: 85.8 us
  Pallas kernels  30.9 us (36%)
  waiting for transfers between devices  19.5 us (23%)
  starting transfers between devices  17.6 us (20%)
  blocking collectives  14.6 us (17%)
  local copies, waits for them, and re-layouts  3 us (3%)
    pallas_call x9, Pallas kernels, call(): pl.pallas_call(kernel, out_shape=out_shape, in_specs=[VMEM] * len(operand...  28.9 us
    ppermute x13, waiting for transfers between devices, move(): return lax.ppermute(x, 'adapter', pairs(places, steps, flip))  18.8 us
    ppermute x13, starting transfers between devices, move(): return lax.ppermute(x, 'adapter', pairs(places, steps, flip))  17 us
    all_to_all x1, blocking collectives, shards(): lax.all_to_all(query, 'adapter', 0, 0, axis_index_groups=groups, tiled=True)  14.6 us
    unnamed x8, local copies, waits for them, and re-layouts  2.23 us
    pallas_call x1, Pallas kernels, normalize(): pl.pallas_call(norm_kernel, out_shape=jax.ShapeDtypeStruct((rows, width +...  2.04 us
  transfers between devices with their start and end apart: 14, of which 5 were waited for; matrix products, arithmetic and copies ran while one was open for 0% of the time, Pallas kernels for 33%

profile of v8, /device:TPU:0, one launch (start us, length us, event | category | flops | bytes accessed | tf_op | source)
XLA Modules:
  0.0 85.8 jit_solution(4095212000314150795)
XLA Ops:
  0.5 2.0 %shard_map.73.refs_0_ = bf16[24,8320]{1,0:T(8,128)(2,1)} custom-call(bf16[24,8192]{1,0:T(8,128)(2,1)} %refs_0_.1, f32[1,8192]{1,0:T(1,128)} %bitcast.17, s32[1,24]{1,0:T(1,128)} %bitcast.18, s32[1,16]{1,0:T(1,128)} %bitcast.19), custom_call_target="tpu_custom_call" | custom-call | tf_op jit(solution)/shard_map/pallas_call | solution.py:111
  2.5 2.6 %collective-permute-start = (bf16[24,8320]{1,0:T(8,128)(2,1)}, bf16[24,8320]{1,0:T(8,128)(2,1)S(1)}, u32[]{:S(2)}, u32[]{:S(2)}) collective-permute-start(bf16[24,8320]{1,0:T(8,128)(2,1)} %shard_map.73.refs_0_), channel_id=1, source_target_pairs={{0,4},{1,5},{2,6},{3,7},{4,12},{5,13},{6,14},{7,15},{12,8},{13,9},... | collective-permute-start | bytes 1198088 | tf_op jit(solution)/shard_map/ppermute | solution.py:268
  5.1 1.5 %collective-permute-start.3 = (bf16[24,8320]{1,0:T(8,128)(2,1)}, bf16[24,8320]{1,0:T(8,128)(2,1)S(1)}, u32[]{:S(2)}, u32[]{:S(2)}) collective-permute-start(bf16[24,8320]{1,0:T(8,128)(2,1)} %shard_map.73.refs_0_), channel_id=1, source_target_pairs={{0,2},{1,3},{2,0},{3,1},{4,6},{5,7},{6,4},{7,5},{12,14},{13,15},{1... | collective-permute-start | bytes 1198088 | tf_op jit(solution)/shard_map/ppermute | solution.py:268
  6.6 9.6 %collective-permute-done.refs_2_ = bf16[24,8320]{1,0:T(8,128)(2,1)S(1)} collective-permute-done((bf16[24,8320]{1,0:T(8,128)(2,1)}, bf16[24,8320]{1,0:T(8,128)(2,1)S(1)}, u32[]{:S(2)}, u32[]{:S(2)}) %collective-permute-start) | collective-permute-done | bytes 399392 | tf_op jit(solution)/shard_map/ppermute | solution.py:268
  16.7 2.6 %collective-permute-start.1 = (bf16[24,8320]{1,0:T(8,128)(2,1)S(1)}, bf16[24,8320]{1,0:T(8,128)(2,1)S(1)}, u32[]{:S(2)}, u32[]{:S(2)}) collective-permute-start(bf16[24,8320]{1,0:T(8,128)(2,1)S(1)} %collective-permute-done.refs_2_), channel_id=1, source_target_pairs={{0,4},{1,5},{2,6},{3,7},{4,12},{5,13},{6,14},{7,15},{12,8},{13,9},... | collective-permute-start | bytes 1198088 | tf_op jit(solution)/shard_map/ppermute | solution.py:268
  19.3 1.5 %collective-permute-start.4 = (bf16[24,8320]{1,0:T(8,128)(2,1)S(1)}, bf16[24,8320]{1,0:T(8,128)(2,1)S(1)}, u32[]{:S(2)}, u32[]{:S(2)}) collective-permute-start(bf16[24,8320]{1,0:T(8,128)(2,1)S(1)} %collective-permute-done.refs_2_), channel_id=1, source_target_pairs={{0,2},{1,3},{2,0},{3,1},{4,6},{5,7},{6,4},{7,5},{12,14},{13,15},{1... | collective-permute-start | bytes 1198088 | tf_op jit(solution)/shard_map/ppermute | solution.py:268
  20.8 7.4 %collective-permute-done.1.refs_0_ = bf16[24,8320]{1,0:T(8,128)(2,1)S(1)} collective-permute-done((bf16[24,8320]{1,0:T(8,128)(2,1)S(1)}, bf16[24,8320]{1,0:T(8,128)(2,1)S(1)}, u32[]{:S(2)}, u32[]{:S(2)}) %collective-permute-start.1) | collective-permute-done | bytes 399392 | tf_op jit(solution)/shard_map/ppermute | solution.py:268
  28.2 1.3 %collective-permute-done.4.refs_3_ = bf16[24,8320]{1,0:T(8,128)(2,1)S(1)} collective-permute-done((bf16[24,8320]{1,0:T(8,128)(2,1)S(1)}, bf16[24,8320]{1,0:T(8,128)(2,1)S(1)}, u32[]{:S(2)}, u32[]{:S(2)}) %collective-permute-start.4) | collective-permute-done | bytes 399392 | tf_op jit(solution)/shard_map/ppermute | solution.py:268
  29.6 1.5 %collective-permute-start.6 = (bf16[24,8320]{1,0:T(8,128)(2,1)S(1)}, bf16[24,8320]{1,0:T(8,128)(2,1)S(1)}, u32[]{:S(2)}, u32[]{:S(2)}) collective-permute-start(bf16[24,8320]{1,0:T(8,128)(2,1)S(1)} %collective-permute-done.1.refs_0_), channel_id=1, source_target_pairs={{0,2},{1,3},{2,0},{3,1},{4,6},{5,7},{6,4},{7,5},{12,14},{13,15},{1... | collective-permute-start | bytes 1198088 | tf_op jit(solution)/shard_map/ppermute | solution.py:268
  31.1 1.5 %collective-permute-start.2 = (bf16[24,8320]{1,0:T(8,128)(2,1)S(1)}, bf16[24,8320]{1,0:T(8,128)(2,1)S(1)}, u32[]{:S(2)}, u32[]{:S(2)}) collective-permute-start(bf16[24,8320]{1,0:T(8,128)(2,1)S(1)} %collective-permute-done.1.refs_0_), channel_id=1, source_target_pairs={{0,4},{1,5},{2,6},{3,7},{4,12},{5,13},{6,14},{7,15},{12,8},{13,9},... | collective-permute-start | bytes 1198088 | tf_op jit(solution)/shard_map/ppermute | solution.py:268
  32.6 1.2 %copy-done = bf16[1,8192,64]{1,2,0:T(8,128)(2,1)S(1)} copy-done((bf16[1,8192,64]{1,2,0:T(8,128)(2,1)S(1)}, bf16[1,8192,64]{1,2,0:T(8,128)(2,1)}, u32[]{:S(2)}) %copy-start) | copy-done | bytes 1048600
  33.8 1.0 %copy-done.2 = bf16[24,8320]{1,0:T(8,128)(2,1)S(1)} copy-done((bf16[24,8320]{1,0:T(8,128)(2,1)S(1)}, bf16[24,8320]{1,0:T(8,128)(2,1)}, u32[]{:S(2)}) %copy-start.2) | copy-done | bytes 399384
  35.7 5.8 %shard_map.75.refs_4_ = f32[96,512]{1,0:T(8,128)S(1)} custom-call(bf16[24,8320]{1,0:T(8,128)(2,1)S(1)} %copy-done.2, bf16[24,8320]{1,0:T(8,128)(2,1)S(1)} %collective-permute-done.3.refs_1_, bf16[24,8320]{1,0:T(8,128)(2,1)S(1)} %collective-permute-done.refs_2_, bf16[24,8320]{1,0:T(8,128)(2,1)S(1)} %collective-permute-done.4.refs_3_, bf16[8192,512]{1,0:T(8,128)(2,1)} %refs_4_.3), custom_call_target="tpu_custom_call" | custom-call | flops 1 | bytes 1 | tf_op jit(solution)/shard_map/pallas_call | solution.py:58
  42.2 0.9 %shard_map.76 = (bf16[48,64]{1,0:T(8,128)(2,1)S(1)}, s32[48,128]{1,0:T(8,128)S(1)}) custom-call(bf16[24,8320]{1,0:T(8,128)(2,1)S(1)} %collective-permute-done.1.refs_0_, bf16[24,8320]{1,0:T(8,128)(2,1)S(1)} %collective-permute-done.6.refs_1_, bf16[64,8192]{1,0:T(8,128)(2,1)S(1)} %bitcast.12, bf16[64,8192]{1,0:T(8,128)(2,1)S(1)} %collective-permute-done.5.refs_5_.refs_3_), custom_call_target="tpu_custom_call" | custom-call | flops 1 | bytes 1 | tf_op jit(solution)/shard_map/pallas_call | solution.py:58
  43.1 5.8 %shard_map.77.refs_5_ = f32[96,512]{1,0:T(8,128)S(1)} custom-call(bf16[24,8320]{1,0:T(8,128)(2,1)S(1)} %copy-done.2, bf16[24,8320]{1,0:T(8,128)(2,1)S(1)} %collective-permute-done.3.refs_1_, bf16[24,8320]{1,0:T(8,128)(2,1)S(1)} %collective-permute-done.refs_2_, bf16[24,8320]{1,0:T(8,128)(2,1)S(1)} %collective-permute-done.4.refs_3_, ...), custom_call_target="tpu_custom_call" | custom-call | flops 1 | bytes 1 | tf_op jit(solution)/shard_map/pallas_call | solution.py:58
  49.5 0.9 %shard_map.78 = (bf16[192,64]{1,0:T(8,128)(2,1)S(1)}, s32[48,128]{1,0:T(8,128)S(1)}) custom-call(bf16[24,8320]{1,0:T(8,128)(2,1)S(1)} %collective-permute-done.2.refs_0_.refs_2_, bf16[24,8320]{1,0:T(8,128)(2,1)S(1)} %collective-permute-done.7.refs_1_.refs_3_, bf16[64,8192]{1,0:T(8,128)(2,1)S(1)} %bitcast.13, ...), custom_call_target="tpu_custom_call" | custom-call | flops 1 | bytes 1 | tf_op jit(solution)/shard_map/pallas_call | solution.py:58
  50.4 1.0 %collective-permute-start.9 = (bf16[192,64]{1,0:T(8,128)(2,1)S(1)}, bf16[192,64]{1,0:T(8,128)(2,1)S(1)}, u32[]{:S(2)}, u32[]{:S(2)}) collective-permute-start(bf16[192,64]{1,0:T(8,128)(2,1)S(1)} %get-tuple-element.50.refs_0_), channel_id=1, source_target_pairs={{0,2},{1,3},{2,0},{3,1},{4,6},{5,7},{6,4},{7,5},{12,14},{13,15},{1... | collective-permute-start | bytes 73736 | tf_op jit(solution)/shard_map/ppermute | solution.py:268
  51.4 5.8 %shard_map.79.refs_6_ = f32[96,512]{1,0:T(8,128)S(1)} custom-call(bf16[24,8320]{1,0:T(8,128)(2,1)S(1)} %collective-permute-done.1.refs_0_, bf16[24,8320]{1,0:T(8,128)(2,1)S(1)} %collective-permute-done.6.refs_1_, bf16[24,8320]{1,0:T(8,128)(2,1)S(1)} %collective-permute-done.2.refs_0_.refs_2_, bf16[24,8320]{1,0:T(8,128)(2,1)S(1)} %collective-permute-done.7.refs_1_.refs_3_, ...), custom_call_target="tpu_custom_call" | custom-call | flops 1 | bytes 1 | tf_op jit(solution)/shard_map/pallas_call | solution.py:58
  57.3 1.2 %collective-permute-start.10 = (bf16[96,128]{1,0:T(8,128)(2,1)S(1)}, bf16[96,128]{1,0:T(8,128)(2,1)S(1)}, u32[]{:S(2)}, u32[]{:S(2)}) collective-permute-start(bf16[96,128]{1,0:T(8,128)(2,1)S(1)} %shard_map.80.refs_0_), channel_id=1, source_target_pairs={{0,4},{1,5},{2,6},{3,7},{4,12},{5,13},{6,14},{7,15},{12,8},{13,9},... | collective-permute-start | bytes 73736 | tf_op jit(solution)/shard_map/ppermute | solution.py:268
  58.5 1.7 %collective-permute-start.11 = (bf16[96,128]{1,0:T(8,128)(2,1)S(1)}, bf16[96,128]{1,0:T(8,128)(2,1)S(1)}, u32[]{:S(2)}, u32[]{:S(2)}) collective-permute-start(bf16[96,128]{1,0:T(8,128)(2,1)S(1)} %shard_map.80.refs_0_), channel_id=1, source_target_pairs={{0,12},{1,13},{2,14},{3,15},{4,8},{5,9},{6,10},{7,11},{12,0},{13,1... | collective-permute-start | bytes 73736 | tf_op jit(solution)/shard_map/ppermute | solution.py:268
  60.2 1.4 %collective-permute-start.12 = (bf16[96,128]{1,0:T(8,128)(2,1)S(1)}, bf16[96,128]{1,0:T(8,128)(2,1)S(1)}, u32[]{:S(2)}, u32[]{:S(2)}) collective-permute-start(bf16[96,128]{1,0:T(8,128)(2,1)S(1)} %shard_map.80.refs_0_), channel_id=1, source_target_pairs={{0,8},{1,9},{2,10},{3,11},{4,0},{5,1},{6,2},{7,3},{12,4},{13,5},{1... | collective-permute-start | bytes 73736 | tf_op jit(solution)/shard_map/ppermute | solution.py:268
  61.6 5.8 %shard_map.81.refs_7_ = f32[96,512]{1,0:T(8,128)S(1)} custom-call(bf16[24,8320]{1,0:T(8,128)(2,1)S(1)} %collective-permute-done.1.refs_0_, bf16[24,8320]{1,0:T(8,128)(2,1)S(1)} %collective-permute-done.6.refs_1_, bf16[24,8320]{1,0:T(8,128)(2,1)S(1)} %collective-permute-done.2.refs_0_.refs_2_, bf16[24,8320]{1,0:T(8,128)(2,1)S(1)} %collective-permute-done.7.refs_1_.refs_3_, ...), custom_call_target="tpu_custom_call" | custom-call | flops 1 | bytes 1 | tf_op jit(solution)/shard_map/pallas_call | solution.py:58
  67.5 2.9 %shard_map.82 = bf16[8,24,1024]{2,1,0:T(8,128)(2,1)S(1)} custom-call(bf16[96,128]{1,0:T(8,128)(2,1)S(1)} %shard_map.80.refs_0_, bf16[96,128]{1,0:T(8,128)(2,1)S(1)} %collective-permute-done.10.refs_1_, bf16[96,128]{1,0:T(8,128)(2,1)S(1)} %collective-permute-done.11.refs_2_, bf16[96,128]{1,0:T(8,128)(2,1)S(1)} %collective-permute-done.12.refs_3_, ...), custom_call_target="tpu_custom_call" | custom-call | flops 1 | bytes 1 | tf_op jit(solution)/shard_map/pallas_call | solution.py:58
  70.4 14.6 %all_to_all.5 = bf16[8,24,1024]{2,1,0:T(8,128)(2,1)S(1)} all-to-all(bf16[8,24,1024]{2,1,0:T(8,128)(2,1)S(1)} %shard_map.82), channel_id=1, replica_groups={{0,2,4,6,8,10,12,14},{1,3,5,7,9,11,13,15},{16,18,20,22,24,26,28,30},{17..., dimensions={0} | all-to-all | bytes 786432 | tf_op jit(solution)/shard_map/all_to_all | solution.py:309
  (25 shorter events, 3.9 us)
Async XLA Ops:
  0.0 43.1 %collective-permute-start.8 = (bf16[8192,512]{1,0:T(8,128)(2,1)}, bf16[8192,512]{1,0:T(8,128)(2,1)}, u32[]{:S(2)}, u32[]{:S(2)}) collective-permute-start(bf16[8192,512]{1,0:T(8,128)(2,1)} %refs_4_.3), channel_id=1, source_target_pairs={{0,1},{1,0},{2,3},{3,2},{4,5},{5,4},{6,7},{7,6},{12,13},{13,12},{1... | collective-permute-start | bytes 25165832 | tf_op jit(solution)/shard_map/ppermute | solution.py:268
  2.5 13.8 %collective-permute-start = (bf16[24,8320]{1,0:T(8,128)(2,1)}, bf16[24,8320]{1,0:T(8,128)(2,1)S(1)}, u32[]{:S(2)}, u32[]{:S(2)}) collective-permute-start(bf16[24,8320]{1,0:T(8,128)(2,1)} %shard_map.73.refs_0_), channel_id=1, source_target_pairs={{0,4},{1,5},{2,6},{3,7},{4,12},{5,13},{6,14},{7,15},{12,8},{13,9},... | collective-permute-start | bytes 1198088 | tf_op jit(solution)/shard_map/ppermute | solution.py:268
  5.1 11.6 %collective-permute-start.3 = (bf16[24,8320]{1,0:T(8,128)(2,1)}, bf16[24,8320]{1,0:T(8,128)(2,1)S(1)}, u32[]{:S(2)}, u32[]{:S(2)}) collective-permute-start(bf16[24,8320]{1,0:T(8,128)(2,1)} %shard_map.73.refs_0_), channel_id=1, source_target_pairs={{0,2},{1,3},{2,0},{3,1},{4,6},{5,7},{6,4},{7,5},{12,14},{13,15},{1... | collective-permute-start | bytes 1198088 | tf_op jit(solution)/shard_map/ppermute | solution.py:268
  6.6 26.0 %collective-permute-start.5 = (bf16[64,8192]{1,0:T(8,128)(2,1)}, bf16[64,8192]{1,0:T(8,128)(2,1)S(1)}, u32[]{:S(2)}, u32[]{:S(2)}) collective-permute-start(bf16[64,8192]{1,0:T(8,128)(2,1)} %bitcast.10), channel_id=1, source_target_pairs={{0,1},{1,0},{2,3},{3,2},{4,5},{5,4},{6,7},{7,6},{12,13},{13,12},{1... | collective-permute-start | bytes 3145736 | tf_op jit(solution)/shard_map/ppermute | solution.py:268
  16.7 11.5 %collective-permute-start.1 = (bf16[24,8320]{1,0:T(8,128)(2,1)S(1)}, bf16[24,8320]{1,0:T(8,128)(2,1)S(1)}, u32[]{:S(2)}, u32[]{:S(2)}) collective-permute-start(bf16[24,8320]{1,0:T(8,128)(2,1)S(1)} %collective-permute-done.refs_2_), channel_id=1, source_target_pairs={{0,4},{1,5},{2,6},{3,7},{4,12},{5,13},{6,14},{7,15},{12,8},{13,9},... | collective-permute-start | bytes 1198088 | tf_op jit(solution)/shard_map/ppermute | solution.py:268
  19.3 10.3 %collective-permute-start.4 = (bf16[24,8320]{1,0:T(8,128)(2,1)S(1)}, bf16[24,8320]{1,0:T(8,128)(2,1)S(1)}, u32[]{:S(2)}, u32[]{:S(2)}) collective-permute-start(bf16[24,8320]{1,0:T(8,128)(2,1)S(1)} %collective-permute-done.refs_2_), channel_id=1, source_target_pairs={{0,2},{1,3},{2,0},{3,1},{4,6},{5,7},{6,4},{7,5},{12,14},{13,15},{1... | collective-permute-start | bytes 1198088 | tf_op jit(solution)/shard_map/ppermute | solution.py:268
  29.6 11.9 %collective-permute-start.6 = (bf16[24,8320]{1,0:T(8,128)(2,1)S(1)}, bf16[24,8320]{1,0:T(8,128)(2,1)S(1)}, u32[]{:S(2)}, u32[]{:S(2)}) collective-permute-start(bf16[24,8320]{1,0:T(8,128)(2,1)S(1)} %collective-permute-done.1.refs_0_), channel_id=1, source_target_pairs={{0,2},{1,3},{2,0},{3,1},{4,6},{5,7},{6,4},{7,5},{12,14},{13,15},{1... | collective-permute-start | bytes 1198088 | tf_op jit(solution)/shard_map/ppermute | solution.py:268
  31.1 10.4 %collective-permute-start.2 = (bf16[24,8320]{1,0:T(8,128)(2,1)S(1)}, bf16[24,8320]{1,0:T(8,128)(2,1)S(1)}, u32[]{:S(2)}, u32[]{:S(2)}) collective-permute-start(bf16[24,8320]{1,0:T(8,128)(2,1)S(1)} %collective-permute-done.1.refs_0_), channel_id=1, source_target_pairs={{0,4},{1,5},{2,6},{3,7},{4,12},{5,13},{6,14},{7,15},{12,8},{13,9},... | collective-permute-start | bytes 1198088 | tf_op jit(solution)/shard_map/ppermute | solution.py:268
  32.6 34.8 %collective-permute-start.13 = (bf16[1024,512]{1,0:T(8,128)(2,1)}, bf16[1024,512]{1,0:T(8,128)(2,1)}, u32[]{:S(2)}, u32[]{:S(2)}) collective-permute-start(bf16[1024,512]{1,0:T(8,128)(2,1)} %bitcast.14), channel_id=1, source_target_pairs={{0,1},{1,0},{2,3},{3,2},{4,5},{5,4},{6,7},{7,6},{12,13},{13,12},{1... | collective-permute-start | bytes 3145736 | tf_op jit(solution)/shard_map/ppermute | solution.py:268
  32.6 1.2 %copy-start = (bf16[1,8192,64]{1,2,0:T(8,128)(2,1)S(1)}, bf16[1,8192,64]{1,2,0:T(8,128)(2,1)}, u32[]{:S(2)}) copy-start(bf16[1,8192,64]{1,2,0:T(8,128)(2,1)} %param.10) | copy-start | bytes 3145732
  33.8 1.0 %copy-start.2 = (bf16[24,8320]{1,0:T(8,128)(2,1)S(1)}, bf16[24,8320]{1,0:T(8,128)(2,1)}, u32[]{:S(2)}) copy-start(bf16[24,8320]{1,0:T(8,128)(2,1)} %shard_map.73.refs_0_) | copy-start | bytes 1198084
  34.8 7.3 %copy-start.1 = (bf16[1,8192,64]{1,2,0:T(8,128)(2,1)S(1)}, bf16[1,8192,64]{1,2,0:T(8,128)(2,1)}, u32[]{:S(2)}) copy-start(bf16[1,8192,64]{1,2,0:T(8,128)(2,1)} %param.10) | copy-start | bytes 3145732
  41.6 7.9 %collective-permute-start.7 = (bf16[24,8320]{1,0:T(8,128)(2,1)S(1)}, bf16[24,8320]{1,0:T(8,128)(2,1)S(1)}, u32[]{:S(2)}, u32[]{:S(2)}) collective-permute-start(bf16[24,8320]{1,0:T(8,128)(2,1)S(1)} %broadcast_select_fusion), channel_id=1, source_target_pairs={{0,2},{2,0},{4,6},{6,4},{12,14},{14,12},{8,10},{10,8},{1,5},{3,7},... | collective-permute-start | bytes 1198088 | tf_op jit(solution)/shard_map/ppermute | solution.py:292
  50.4 17.1 %copy-start.3 = (bf16[16,64,512]{2,1,0:T(8,128)(2,1)S(1)}, bf16[16,64,512]{2,1,0:T(8,128)(2,1)}, u32[]{:S(2)}) copy-start(bf16[16,64,512]{2,1,0:T(8,128)(2,1)} %param.11) | copy-start | bytes 3145732
  50.4 6.8 %collective-permute-start.9 = (bf16[192,64]{1,0:T(8,128)(2,1)S(1)}, bf16[192,64]{1,0:T(8,128)(2,1)S(1)}, u32[]{:S(2)}, u32[]{:S(2)}) collective-permute-start(bf16[192,64]{1,0:T(8,128)(2,1)S(1)} %get-tuple-element.50.refs_0_), channel_id=1, source_target_pairs={{0,2},{1,3},{2,0},{3,1},{4,6},{5,7},{6,4},{7,5},{12,14},{13,15},{1... | collective-permute-start | bytes 73736 | tf_op jit(solution)/shard_map/ppermute | solution.py:268
  57.3 10.1 %collective-permute-start.10 = (bf16[96,128]{1,0:T(8,128)(2,1)S(1)}, bf16[96,128]{1,0:T(8,128)(2,1)S(1)}, u32[]{:S(2)}, u32[]{:S(2)}) collective-permute-start(bf16[96,128]{1,0:T(8,128)(2,1)S(1)} %shard_map.80.refs_0_), channel_id=1, source_target_pairs={{0,4},{1,5},{2,6},{3,7},{4,12},{5,13},{6,14},{7,15},{12,8},{13,9},... | collective-permute-start | bytes 73736 | tf_op jit(solution)/shard_map/ppermute | solution.py:268
  58.5 9.0 %collective-permute-start.11 = (bf16[96,128]{1,0:T(8,128)(2,1)S(1)}, bf16[96,128]{1,0:T(8,128)(2,1)S(1)}, u32[]{:S(2)}, u32[]{:S(2)}) collective-permute-start(bf16[96,128]{1,0:T(8,128)(2,1)S(1)} %shard_map.80.refs_0_), channel_id=1, source_target_pairs={{0,12},{1,13},{2,14},{3,15},{4,8},{5,9},{6,10},{7,11},{12,0},{13,1... | collective-permute-start | bytes 73736 | tf_op jit(solution)/shard_map/ppermute | solution.py:268
  60.2 7.3 %collective-permute-start.12 = (bf16[96,128]{1,0:T(8,128)(2,1)S(1)}, bf16[96,128]{1,0:T(8,128)(2,1)S(1)}, u32[]{:S(2)}, u32[]{:S(2)}) collective-permute-start(bf16[96,128]{1,0:T(8,128)(2,1)S(1)} %shard_map.80.refs_0_), channel_id=1, source_target_pairs={{0,8},{1,9},{2,10},{3,11},{4,0},{5,1},{6,2},{7,3},{12,4},{13,5},{1... | collective-permute-start | bytes 73736 | tf_op jit(solution)/shard_map/ppermute | solution.py:268

commit v9 on v8

--- a/solution.py
+++ b/solution.py
@@ -14,7 +14,6 @@
 LANES = 128
 CHUNK = 1024
 VMEM_LIMIT = 24 << 20
-AHEAD = 2
 VMEM = pl.BlockSpec(memory_space=pltpu.VMEM)
 
 
@@ -54,14 +53,13 @@
     return lax.optimization_barrier((x, *others))[0]
 
 
-def call(kernel, out_shape, operands, specs=None, scratch=(), limit=VMEM_LIMIT):
+def call(kernel, out_shape, operands):
     return pl.pallas_call(
         kernel,
         out_shape=out_shape,
-        in_specs=[VMEM] * len(operands) if specs is None else specs,
+        in_specs=[VMEM] * len(operands),
         out_specs=jax.tree.map(lambda _: VMEM, out_shape),
-        scratch_shapes=list(scratch),
-        compiler_params=pltpu.CompilerParams(vmem_limit_bytes=limit),
+        compiler_params=pltpu.CompilerParams(vmem_limit_bytes=VMEM_LIMIT),
         cost_estimate=pl.CostEstimate(flops=1, bytes_accessed=1, transcendentals=0),
     )(*operands)
 
@@ -124,15 +122,17 @@
 
 
 def shrink_kernel(count, *refs):
-    blocks, (own_ref, other_ref, *before, part_ref, slot_ref) = refs[:count], refs[count:]
+    blocks, (own_ref, other_ref, *before, part_ref, slot_ref, rows_ref) = refs[:count], refs[count:]
     rank, width = own_ref.shape
     rows = slot_ref.shape[0]
     part = jnp.zeros((rows, 2 * rank), jnp.float32)
     for start in range(0, width, CHUNK):
         lanes = slice(start, start + CHUNK)
         down = jnp.concatenate([own_ref[:, lanes], other_ref[:, lanes]], axis=0)
+        chunk = stacked(blocks, lanes)
+        rows_ref[:, lanes] = chunk
         part += lax.dot_general(
-            stacked(blocks, lanes), down, (((1,), (1,)), ((), ())), preferred_element_type=jnp.float32
+            chunk, down, (((1,), (1,)), ((), ())), preferred_element_type=jnp.float32
         )
     slot = jnp.concatenate(
         [block[:, width : width + 1].astype(jnp.float32) for block in blocks], axis=0
@@ -155,6 +155,7 @@
     out_shape = (
         jax.ShapeDtypeStruct((total, own.shape[0]), jnp.bfloat16),
         jax.ShapeDtypeStruct((rows, LANES), jnp.int32),
+        jax.ShapeDtypeStruct((rows, own.shape[1]), jnp.bfloat16),
     )
     return call(
         lambda *refs: shrink_kernel(len(blocks), *refs), out_shape, (*blocks, own, other, *before)
@@ -179,43 +180,6 @@
     return call(lambda *refs: pack_kernel(own_rows, *refs), out_shape, (part, across))
 
 
-def base_kernel(*refs):
-    *blocks, weight_ref, out_ref, buffer, sems = refs
-    width = weight_ref.shape[0]
-    copies = []
-    for number, start in enumerate(range(0, width, CHUNK)):
-        rows = pl.ds(start, CHUNK)
-        copies.append(
-            pltpu.make_async_copy(weight_ref.at[rows], buffer.at[rows], sems.at[number])
-        )
-    for copy in copies[:AHEAD]:
-        copy.start()
-    out_ref[...] = jnp.zeros(out_ref.shape, jnp.float32)
-    for number, start in enumerate(range(0, width, CHUNK)):
-        lanes = slice(start, start + CHUNK)
-        rows = stacked(blocks, lanes)
-        copies[number].wait()
-        if number + AHEAD < len(copies):
-            copies[number + AHEAD].start()
-        out_ref[...] += jnp.dot(rows, buffer[lanes, :], preferred_element_type=jnp.float32)
-
-
-def base_rows(blocks, weight):
-    rows = blocks[0].shape[0] * len(blocks)
-    specs = [VMEM] * len(blocks) + [pl.BlockSpec(memory_space=pltpu.HBM)]
-    return call(
-        base_kernel,
-        jax.ShapeDtypeStruct((rows, weight.shape[1]), jnp.float32),
-        (*blocks, weight),
-        specs,
-        (
-            pltpu.VMEM(weight.shape, weight.dtype),
-            pltpu.SemaphoreType.DMA((weight.shape[0] // CHUNK,)),
-        ),
-        48 << 20,
-    )
-
-
 def finish_kernel(places, rank, *refs):
     moved, refs = refs[:places], refs[places:]
     slot_count = len(refs) - places - 3
@@ -224,22 +188,26 @@
     depth, columns = own_ref.shape
     rows = SIDE * out_ref.shape[1]
     core = lax.axis_index("adapter") % CORES
-    lanes = lax.broadcasted_iota(jnp.int32, (rows, depth), 1)
-    slot = jnp.concatenate([ref[:, 0:1] for ref in slots], axis=0)
+    shrinks = []
     for step in range(places):
         shrink = jnp.zeros((rows, rank), jnp.float32)
         for back in range(places):
             half, first = divmod((step - back) % places, places // 2)
             part = moved[back][first * rows : (first + 1) * rows, half * rank : (half + 1) * rank]
             shrink += part.astype(jnp.float32)
-        wide = jnp.concatenate([shrink] * (depth // rank), axis=1)
-        here = slot[step * rows : (step + 1) * rows]
-        spread = jnp.where(lanes // rank == here, wide, 0.0).astype(jnp.bfloat16)
-        for which, up_ref in enumerate((own_ref, other_ref)):
-            update = jnp.dot(spread, up_ref[...], preferred_element_type=jnp.float32)
+        shrinks.append(shrink)
+    shrink = jnp.concatenate(shrinks, axis=0)
+    slot = jnp.concatenate([ref[:, 0:1] for ref in slots], axis=0)
+    wide = jnp.concatenate([shrink] * (depth // rank), axis=1)
+    lanes = lax.broadcasted_iota(jnp.int32, wide.shape, 1)
+    spread = jnp.where(lanes // rank == slot, wide, 0.0).astype(jnp.bfloat16)
+    for which, up_ref in enumerate((own_ref, other_ref)):
+        update = jnp.dot(spread, up_ref[...], preferred_element_type=jnp.float32)
+        at = pl.multiple_of((core ^ which) * columns, columns)
+        for step in range(places):
+            here = slice(step * rows, (step + 1) * rows)
             base = bases[step // 2 * 2 + which][step % 2 * rows : (step % 2 + 1) * rows, :]
-            query = (base + ADAPTER_SCALE * update).astype(jnp.bfloat16)
-            at = pl.multiple_of((core ^ which) * columns, columns)
+            query = (base + ADAPTER_SCALE * update[here]).astype(jnp.bfloat16)
             for side in range(SIDE):
                 chip = ring_chip(places, -step, side)
                 out_ref[chip, :, pl.ds(at, columns)] = query[side * rows // SIDE : (side + 1) * rows // SIDE]
@@ -267,6 +235,9 @@
     def move(x, steps, flip):
         return lax.ppermute(x, "adapter", pairs(places, steps, flip))
 
+    def base_rows(rows, weight):
+        return jnp.dot(rows, weight, preferred_element_type=jnp.float32)
+
     down = down_weights[0].T
     up = up_weights.reshape(devices * rank, columns)
     down_other = move(down, 0, 1)
@@ -282,24 +253,21 @@
         if step % 2 == 0 and step:
             rows = [block[step - 2], other[step - 2], block[step - 1], other[step - 1]]
             rows = after(rows, block[step])
-            part, slot = shrink_rows(rows, down, down_other)
+            part, slot, rows = shrink_rows(rows, down, down_other)
             parts.append(part)
             slots.append(slot)
-            bases.append(base_rows(after(rows, part), query_weight))
+            bases.append(base_rows(rows, query_weight))
             if step < last - 1:
                 bases.append(base_rows(rows, weight_other))
     source = jnp.where((me & 1) == 0, after(block[last], *bases, other[-1]), other[-1])
     crossed = lax.ppermute(source, "adapter", split_pairs(places))
-    part, slot = shrink_rows(after([block[last - 1], other[-1]], source), down, down_other)
-    parts.append(part)
+    bases.append(base_rows(after(rows, source), weight_other))
+    crossed = after(crossed, *bases)
+    rows = [block[last - 1], other[-1], block[last], crossed]
+    part, slot, rows = shrink_rows(rows, down, down_other, parts)
     slots.append(slot)
-    bases.append(base_rows(after(rows, part), weight_other))
-    crossed = after(crossed, *bases)
-    part, slot = shrink_rows([block[last], crossed], down, down_other, parts)
-    slots.append(slot)
 
     across = move(part, 0, 2)
-    rows = [block[last - 1], other[-1], block[last], crossed]
     bases.append(base_rows(rows, query_weight))
     part = pack(part, after(across, bases[-1]), own_rows)
     moved = [part] + [move(part, steps, 0) for steps in range(1, places)]

time: 86.5 us -> 78.2 us (0.904)
  Pallas kernels: 30.9 us -> 5.62 us
  matrix products: 0 us -> 16.7 us
  starting transfers between devices: 17.6 us -> 19.2 us
  blocking collectives: 14.6 us -> 13.7 us
    pallas_call x9 -> x4, Pallas kernels: 28.9 us -> 3.58 us  [call(): pl.pallas_call(kernel, out_shape=out_shape, in_specs=[VMEM] * len(operand...]
    dot_general x0 -> x4, matrix products: none -> 16.7 us  [base_rows(): return jnp.dot(rows, weight, preferred_element_type=jnp.float32)]
    ppermute x1, starting transfers between devices: 0.56 us -> 1.57 us  [shards(): crossed = lax.ppermute(source, 'adapter', split_pairs(places))]
    all_to_all x1, blocking collectives: 14.6 us -> 13.7 us  [shards(): lax.all_to_all(query, 'adapter', 0, 0, axis_index_groups=groups, tiled=True)]
    unnamed x8 -> x12, local copies, waits for them, and re-layouts: 2.23 us -> 2.25 us
  transfers between devices with their start and end apart: 14 -> 14, of which waited for: 5 -> 6; matrix products, arithmetic and copies ran while one was open for 0% -> 21% of each run, Pallas kernels for 33% -> 6%
where the time goes in v9:
time: 78.2 us; the launch traced here: 77.8 us
  waiting for transfers between devices  19.5 us (25%)
  starting transfers between devices  19.2 us (25%)
  matrix products  16.7 us (21%)
  blocking collectives  13.7 us (18%)
  Pallas kernels  5.62 us (7%)
  local copies, waits for them, and re-layouts  3.02 us (4%)
    ppermute x13, waiting for transfers between devices, move(): return lax.ppermute(x, 'adapter', pairs(places, steps, flip))  18.7 us
    ppermute x13, starting transfers between devices, move(): return lax.ppermute(x, 'adapter', pairs(places, steps, flip))  17.7 us
    dot_general x4, matrix products, base_rows(): return jnp.dot(rows, weight, preferred_element_type=jnp.float32)  16.7 us
    all_to_all x1, blocking collectives, shards(): lax.all_to_all(query, 'adapter', 0, 0, axis_index_groups=groups, tiled=True)  13.7 us
    pallas_call x4, Pallas kernels, call(): pl.pallas_call(kernel, out_shape=out_shape, in_specs=[VMEM] * len(operand...  3.58 us
    unnamed x12, local copies, waits for them, and re-layouts  2.25 us
    pallas_call x1, Pallas kernels, normalize(): pl.pallas_call(norm_kernel, out_shape=jax.ShapeDtypeStruct((rows, width +...  2.04 us
    ppermute x1, starting transfers between devices, shards(): crossed = lax.ppermute(source, 'adapter', split_pairs(places))  1.57 us
  transfers between devices with their start and end apart: 14, of which 6 were waited for; matrix products, arithmetic and copies ran while one was open for 21% of the time, Pallas kernels for 6%

profile of v9, /device:TPU:0, one launch (start us, length us, event | category | flops | bytes accessed | tf_op | source)
XLA Modules:
  0.0 77.8 jit_solution(10006214477676594282)
XLA Ops:
  0.5 2.0 %shard_map.73.refs_0_ = bf16[24,8320]{1,0:T(8,128)(2,1)} custom-call(bf16[24,8192]{1,0:T(8,128)(2,1)} %refs_0_.1, f32[1,8192]{1,0:T(1,128)} %bitcast.26, s32[1,24]{1,0:T(1,128)} %bitcast.27, s32[1,16]{1,0:T(1,128)} %bitcast.28), custom_call_target="tpu_custom_call" | custom-call | tf_op jit(solution)/shard_map/pallas_call | solution.py:109
  2.6 3.1 %collective-permute-start = (bf16[24,8320]{1,0:T(8,128)(2,1)}, bf16[24,8320]{1,0:T(8,128)(2,1)S(1)}, u32[]{:S(2)}, u32[]{:S(2)}) collective-permute-start(bf16[24,8320]{1,0:T(8,128)(2,1)} %shard_map.73.refs_0_), channel_id=1, source_target_pairs={{0,4},{1,5},{2,6},{3,7},{4,12},{5,13},{6,14},{7,15},{12,8},{13,9},... | collective-permute-start | bytes 1198088 | tf_op jit(solution)/shard_map/ppermute | solution.py:236
  5.6 1.5 %collective-permute-start.2 = (bf16[24,8320]{1,0:T(8,128)(2,1)}, bf16[24,8320]{1,0:T(8,128)(2,1)S(1)}, u32[]{:S(2)}, u32[]{:S(2)}) collective-permute-start(bf16[24,8320]{1,0:T(8,128)(2,1)} %shard_map.73.refs_0_), channel_id=1, source_target_pairs={{0,2},{1,3},{2,0},{3,1},{4,6},{5,7},{6,4},{7,5},{12,14},{13,15},{1... | collective-permute-start | bytes 1198088 | tf_op jit(solution)/shard_map/ppermute | solution.py:236
  7.2 9.1 %collective-permute-done.refs_2_ = bf16[24,8320]{1,0:T(8,128)(2,1)S(1)} collective-permute-done((bf16[24,8320]{1,0:T(8,128)(2,1)}, bf16[24,8320]{1,0:T(8,128)(2,1)S(1)}, u32[]{:S(2)}, u32[]{:S(2)}) %collective-permute-start) | collective-permute-done | bytes 399392 | tf_op jit(solution)/shard_map/ppermute | solution.py:236
  16.7 1.5 %collective-permute-start.3 = (bf16[24,8320]{1,0:T(8,128)(2,1)S(1)}, bf16[24,8320]{1,0:T(8,128)(2,1)}, u32[]{:S(2)}, u32[]{:S(2)}) collective-permute-start(bf16[24,8320]{1,0:T(8,128)(2,1)S(1)} %collective-permute-done.refs_2_), channel_id=1, source_target_pairs={{0,2},{1,3},{2,0},{3,1},{4,6},{5,7},{6,4},{7,5},{12,14},{13,15},{1... | collective-permute-start | bytes 1198088 | tf_op jit(solution)/shard_map/ppermute | solution.py:236
  18.2 2.6 %collective-permute-start.1 = (bf16[24,8320]{1,0:T(8,128)(2,1)S(1)}, bf16[24,8320]{1,0:T(8,128)(2,1)S(1)}, u32[]{:S(2)}, u32[]{:S(2)}) collective-permute-start(bf16[24,8320]{1,0:T(8,128)(2,1)S(1)} %collective-permute-done.refs_2_), channel_id=1, source_target_pairs={{0,4},{1,5},{2,6},{3,7},{4,12},{5,13},{6,14},{7,15},{12,8},{13,9},... | collective-permute-start | bytes 1198088 | tf_op jit(solution)/shard_map/ppermute | solution.py:236
  20.8 6.2 %collective-permute-done.3.refs_3_ = bf16[24,8320]{1,0:T(8,128)(2,1)} collective-permute-done((bf16[24,8320]{1,0:T(8,128)(2,1)S(1)}, bf16[24,8320]{1,0:T(8,128)(2,1)}, u32[]{:S(2)}, u32[]{:S(2)}) %collective-permute-start.3) | collective-permute-done | bytes 399392 | tf_op jit(solution)/shard_map/ppermute | solution.py:236
  27.0 1.8 %collective-permute-done.1.refs_0_ = bf16[24,8320]{1,0:T(8,128)(2,1)S(1)} collective-permute-done((bf16[24,8320]{1,0:T(8,128)(2,1)S(1)}, bf16[24,8320]{1,0:T(8,128)(2,1)S(1)}, u32[]{:S(2)}, u32[]{:S(2)}) %collective-permute-start.1) | collective-permute-done | bytes 399392 | tf_op jit(solution)/shard_map/ppermute | solution.py:236
  29.5 1.5 %collective-permute-start.5 = (bf16[24,8320]{1,0:T(8,128)(2,1)S(1)}, bf16[24,8320]{1,0:T(8,128)(2,1)S(1)}, u32[]{:S(2)}, u32[]{:S(2)}) collective-permute-start(bf16[24,8320]{1,0:T(8,128)(2,1)S(1)} %collective-permute-done.1.refs_0_), channel_id=1, source_target_pairs={{0,4},{1,5},{2,6},{3,7},{4,12},{5,13},{6,14},{7,15},{12,8},{13,9},... | collective-permute-start | bytes 1198088 | tf_op jit(solution)/shard_map/ppermute | solution.py:236
  31.1 1.2 %copy-done = bf16[1,8192,64]{1,2,0:T(8,128)(2,1)S(1)} copy-done((bf16[1,8192,64]{1,2,0:T(8,128)(2,1)S(1)}, bf16[1,8192,64]{1,2,0:T(8,128)(2,1)}, u32[]{:S(2)}) %copy-start) | copy-done | bytes 1048600
  32.3 1.0 %copy-done.2 = bf16[24,8320]{1,0:T(8,128)(2,1)S(1)} copy-done((bf16[24,8320]{1,0:T(8,128)(2,1)S(1)}, bf16[24,8320]{1,0:T(8,128)(2,1)}, u32[]{:S(2)}) %copy-start.2) | copy-done | bytes 399384
  33.3 1.9 %shard_map.74 = (bf16[96,64]{1,0:T(8,128)(2,1)S(1)}, s32[96,128]{1,0:T(8,128)S(1)}, bf16[96,8192]{1,0:T(8,128)(2,1)S(1)}) custom-call(bf16[24,8320]{1,0:T(8,128)(2,1)S(1)} %copy-done.2, bf16[24,8320]{1,0:T(8,128)(2,1)S(1)} %collective-permute-done.2.refs_1_, bf16[24,8320]{1,0:T(8,128)(2,1)S(1)} %collective-permute-done.refs_2_, ...), custom_call_target="tpu_custom_call" | custom-call | flops 1 | bytes 1 | tf_op jit(solution)/shard_map/pallas_call | solution.py:57
  35.1 4.8 %fusion.refs_4_ = f32[96,512]{1,0:T(8,128)S(1)} fusion(bf16[96,8192]{1,0:T(8,128)(2,1)S(1)} %get-tuple-element.29, bf16[8192,512]{1,0:T(8,128)(2,1)} %param.9), kind=kOutput, calls=%fused_computation.1 | convolution fusion | flops 805306368 | bytes 10158080 | tf_op jit(solution)/shard_map/dot_general | solution.py:239
  40.1 1.6 %collective-permute-start.7 = (bf16[24,8320]{1,0:T(8,128)(2,1)S(1)}, bf16[24,8320]{1,0:T(8,128)(2,1)S(1)}, u32[]{:S(2)}, u32[]{:S(2)}) collective-permute-start(bf16[24,8320]{1,0:T(8,128)(2,1)S(1)} %broadcast_select_fusion), channel_id=1, source_target_pairs={{0,2},{2,0},{4,6},{6,4},{12,14},{14,12},{8,10},{10,8},{1,5},{3,7},... | collective-permute-start | bytes 1198088 | tf_op jit(solution)/shard_map/ppermute | solution.py:263
  41.7 5.6 %fusion.1.refs_5_ = f32[96,512]{1,0:T(8,128)S(1)} fusion(bf16[96,8192]{1,0:T(8,128)(2,1)S(1)} %get-tuple-element.29, bf16[8192,512]{1,0:T(8,128)(2,1)} %collective-permute-done.8), kind=kOutput, calls=%fused_computation.2 | convolution fusion | flops 805306368 | bytes 10158080 | tf_op jit(solution)/shard_map/dot_general | solution.py:239
  48.0 0.9 %shard_map.75 = (bf16[192,64]{1,0:T(8,128)(2,1)S(1)}, s32[96,128]{1,0:T(8,128)S(1)}, bf16[96,8192]{1,0:T(8,128)(2,1)S(1)}) custom-call(bf16[24,8320]{1,0:T(8,128)(2,1)S(1)} %collective-permute-done.1.refs_0_, bf16[24,8320]{1,0:T(8,128)(2,1)S(1)} %collective-permute-done.4.refs_1_, bf16[24,8320]{1,0:T(8,128)(2,1)S(1)} %collective-permute-done.5.refs_2_, ...), custom_call_target="tpu_custom_call" | custom-call | flops 1 | bytes 1 | tf_op jit(solution)/shard_map/pallas_call | solution.py:57
  48.9 1.6 %collective-permute-start.9 = (bf16[192,64]{1,0:T(8,128)(2,1)S(1)}, bf16[192,64]{1,0:T(8,128)(2,1)S(1)}, u32[]{:S(2)}, u32[]{:S(2)}) collective-permute-start(bf16[192,64]{1,0:T(8,128)(2,1)S(1)} %get-tuple-element.32.refs_0_), channel_id=1, source_target_pairs={{0,2},{1,3},{2,0},{3,1},{4,6},{5,7},{6,4},{7,5},{12,14},{13,15},{1... | collective-permute-start | bytes 73736 | tf_op jit(solution)/shard_map/ppermute | solution.py:236
  50.5 1.4 %fusion.2.refs_6_ = f32[96,512]{1,0:T(8,128)S(1)} fusion(bf16[96,8192]{1,0:T(8,128)(2,1)S(1)} %get-tuple-element.33, bf16[8192,512]{1,0:T(8,128)(2,1)S(1)} %bitcast.24), kind=kOutput, calls=%fused_computation.3 | convolution fusion | flops 805306368 | bytes 10158080 | tf_op jit(solution)/shard_map/dot_general | solution.py:239
  51.9 1.1 %collective-permute-done.9.refs_1_ = bf16[192,64]{1,0:T(8,128)(2,1)S(1)} collective-permute-done((bf16[192,64]{1,0:T(8,128)(2,1)S(1)}, bf16[192,64]{1,0:T(8,128)(2,1)S(1)}, u32[]{:S(2)}, u32[]{:S(2)}) %collective-permute-start.9) | collective-permute-done | bytes 24608 | tf_op jit(solution)/shard_map/ppermute | solution.py:236
  53.1 2.4 %collective-permute-start.10 = (bf16[96,128]{1,0:T(8,128)(2,1)S(1)}, bf16[96,128]{1,0:T(8,128)(2,1)S(1)}, u32[]{:S(2)}, u32[]{:S(2)}) collective-permute-start(bf16[96,128]{1,0:T(8,128)(2,1)S(1)} %shard_map.76.refs_0_), channel_id=1, source_target_pairs={{0,4},{1,5},{2,6},{3,7},{4,12},{5,13},{6,14},{7,15},{12,8},{13,9},... | collective-permute-start | bytes 73736 | tf_op jit(solution)/shard_map/ppermute | solution.py:236
  56.1 1.7 %collective-permute-start.12 = (bf16[96,128]{1,0:T(8,128)(2,1)S(1)}, bf16[96,128]{1,0:T(8,128)(2,1)S(1)}, u32[]{:S(2)}, u32[]{:S(2)}) collective-permute-start(bf16[96,128]{1,0:T(8,128)(2,1)S(1)} %shard_map.76.refs_0_), channel_id=1, source_target_pairs={{0,8},{1,9},{2,10},{3,11},{4,0},{5,1},{6,2},{7,3},{12,4},{13,5},{1... | collective-permute-start | bytes 73736 | tf_op jit(solution)/shard_map/ppermute | solution.py:236
  57.8 4.8 %fusion.3.refs_7_ = f32[96,512]{1,0:T(8,128)S(1)} fusion(bf16[96,8192]{1,0:T(8,128)(2,1)S(1)} %get-tuple-element.33, bf16[8192,512]{1,0:T(8,128)(2,1)} %collective-permute-done.8), kind=kOutput, calls=%fused_computation.4 | convolution fusion | flops 805306368 | bytes 10158080 | tf_op jit(solution)/shard_map/dot_general | solution.py:239
  63.4 13.7 %all_to_all.5 = bf16[8,24,1024]{2,1,0:T(8,128)(2,1)S(1)} all-to-all(bf16[8,24,1024]{2,1,0:T(8,128)(2,1)S(1)} %shard_map.77), channel_id=1, replica_groups={{0,2,4,6,8,10,12,14},{1,3,5,7,9,11,13,15},{16,18,20,22,24,26,28,30},{17..., dimensions={0} | all-to-all | bytes 786432 | tf_op jit(solution)/shard_map/all_to_all | solution.py:277
  77.1 0.8 copy.9
  (29 shorter events, 3.8 us)
Async XLA Ops:
  0.0 41.7 %collective-permute-start.8 = (bf16[8192,512]{1,0:T(8,128)(2,1)}, bf16[8192,512]{1,0:T(8,128)(2,1)}, u32[]{:S(2)}, u32[]{:S(2)}) collective-permute-start(bf16[8192,512]{1,0:T(8,128)(2,1)} %param.9), channel_id=1, source_target_pairs={{0,1},{1,0},{2,3},{3,2},{4,5},{5,4},{6,7},{7,6},{12,13},{13,12},{1... | collective-permute-start | bytes 25165832 | tf_op jit(solution)/shard_map/ppermute | solution.py:236
  0.5 30.6 %collective-permute-start.6 = (bf16[64,8192]{1,0:T(8,128)(2,1)}, bf16[64,8192]{1,0:T(8,128)(2,1)S(1)}, u32[]{:S(2)}, u32[]{:S(2)}) collective-permute-start(bf16[64,8192]{1,0:T(8,128)(2,1)} %bitcast.18), channel_id=1, source_target_pairs={{0,1},{1,0},{2,3},{3,2},{4,5},{5,4},{6,7},{7,6},{12,13},{13,12},{1... | collective-permute-start | bytes 3145736 | tf_op jit(solution)/shard_map/ppermute | solution.py:236
  2.6 13.7 %collective-permute-start = (bf16[24,8320]{1,0:T(8,128)(2,1)}, bf16[24,8320]{1,0:T(8,128)(2,1)S(1)}, u32[]{:S(2)}, u32[]{:S(2)}) collective-permute-start(bf16[24,8320]{1,0:T(8,128)(2,1)} %shard_map.73.refs_0_), channel_id=1, source_target_pairs={{0,4},{1,5},{2,6},{3,7},{4,12},{5,13},{6,14},{7,15},{12,8},{13,9},... | collective-permute-start | bytes 1198088 | tf_op jit(solution)/shard_map/ppermute | solution.py:236
  5.6 11.1 %collective-permute-start.2 = (bf16[24,8320]{1,0:T(8,128)(2,1)}, bf16[24,8320]{1,0:T(8,128)(2,1)S(1)}, u32[]{:S(2)}, u32[]{:S(2)}) collective-permute-start(bf16[24,8320]{1,0:T(8,128)(2,1)} %shard_map.73.refs_0_), channel_id=1, source_target_pairs={{0,2},{1,3},{2,0},{3,1},{4,6},{5,7},{6,4},{7,5},{12,14},{13,15},{1... | collective-permute-start | bytes 1198088 | tf_op jit(solution)/shard_map/ppermute | solution.py:236
  16.7 10.3 %collective-permute-start.3 = (bf16[24,8320]{1,0:T(8,128)(2,1)S(1)}, bf16[24,8320]{1,0:T(8,128)(2,1)}, u32[]{:S(2)}, u32[]{:S(2)}) collective-permute-start(bf16[24,8320]{1,0:T(8,128)(2,1)S(1)} %collective-permute-done.refs_2_), channel_id=1, source_target_pairs={{0,2},{1,3},{2,0},{3,1},{4,6},{5,7},{6,4},{7,5},{12,14},{13,15},{1... | collective-permute-start | bytes 1198088 | tf_op jit(solution)/shard_map/ppermute | solution.py:236
  18.2 10.6 %collective-permute-start.1 = (bf16[24,8320]{1,0:T(8,128)(2,1)S(1)}, bf16[24,8320]{1,0:T(8,128)(2,1)S(1)}, u32[]{:S(2)}, u32[]{:S(2)}) collective-permute-start(bf16[24,8320]{1,0:T(8,128)(2,1)S(1)} %collective-permute-done.refs_2_), channel_id=1, source_target_pairs={{0,4},{1,5},{2,6},{3,7},{4,12},{5,13},{6,14},{7,15},{12,8},{13,9},... | collective-permute-start | bytes 1198088 | tf_op jit(solution)/shard_map/ppermute | solution.py:236
  20.8 41.8 %collective-permute-start.13 = (bf16[1024,512]{1,0:T(8,128)(2,1)}, bf16[1024,512]{1,0:T(8,128)(2,1)S(1)}, u32[]{:S(2)}, u32[]{:S(2)}) collective-permute-start(bf16[1024,512]{1,0:T(8,128)(2,1)} %bitcast.21), channel_id=1, source_target_pairs={{0,1},{1,0},{2,3},{3,2},{4,5},{5,4},{6,7},{7,6},{12,13},{13,12},{1... | collective-permute-start | bytes 3145736 | tf_op jit(solution)/shard_map/ppermute | solution.py:236
  28.8 11.1 %collective-permute-start.4 = (bf16[24,8320]{1,0:T(8,128)(2,1)S(1)}, bf16[24,8320]{1,0:T(8,128)(2,1)S(1)}, u32[]{:S(2)}, u32[]{:S(2)}) collective-permute-start(bf16[24,8320]{1,0:T(8,128)(2,1)S(1)} %collective-permute-done.1.refs_0_), channel_id=1, source_target_pairs={{0,2},{1,3},{2,0},{3,1},{4,6},{5,7},{6,4},{7,5},{12,14},{13,15},{1... | collective-permute-start | bytes 1198088 | tf_op jit(solution)/shard_map/ppermute | solution.py:236
  29.5 10.4 %collective-permute-start.5 = (bf16[24,8320]{1,0:T(8,128)(2,1)S(1)}, bf16[24,8320]{1,0:T(8,128)(2,1)S(1)}, u32[]{:S(2)}, u32[]{:S(2)}) collective-permute-start(bf16[24,8320]{1,0:T(8,128)(2,1)S(1)} %collective-permute-done.1.refs_0_), channel_id=1, source_target_pairs={{0,4},{1,5},{2,6},{3,7},{4,12},{5,13},{6,14},{7,15},{12,8},{13,9},... | collective-permute-start | bytes 1198088 | tf_op jit(solution)/shard_map/ppermute | solution.py:236
  31.0 1.2 %copy-start = (bf16[1,8192,64]{1,2,0:T(8,128)(2,1)S(1)}, bf16[1,8192,64]{1,2,0:T(8,128)(2,1)}, u32[]{:S(2)}) copy-start(bf16[1,8192,64]{1,2,0:T(8,128)(2,1)} %param.10) | copy-start | bytes 3145732
  32.3 1.0 %copy-start.2 = (bf16[24,8320]{1,0:T(8,128)(2,1)S(1)}, bf16[24,8320]{1,0:T(8,128)(2,1)}, u32[]{:S(2)}) copy-start(bf16[24,8320]{1,0:T(8,128)(2,1)} %shard_map.73.refs_0_) | copy-start | bytes 1198084
  40.0 10.5 %slice-start = ((s8[8388608]{0:T(1024)(128)(4,1)}), s8[4194304]{0:T(1024)(128)(4,1)S(1)}, s32[]{:S(2)}) async-start(s8[8388608]{0:T(1024)(128)(4,1)} %bitcast.23), calls=%async_computation.1 | async-start | bytes 8388608
  40.1 7.9 %copy-start.1 = (bf16[1,8192,64]{1,2,0:T(8,128)(2,1)S(1)}, bf16[1,8192,64]{1,2,0:T(8,128)(2,1)}, u32[]{:S(2)}) copy-start(bf16[1,8192,64]{1,2,0:T(8,128)(2,1)} %param.10) | copy-start | bytes 3145732
  40.1 10.4 %slice-start.1 = ((s8[8388608]{0:T(1024)(128)(4,1)}), s8[4194304]{0:T(1024)(128)(4,1)S(1)}, s32[]{:S(2)}) async-start(s8[8388608]{0:T(1024)(128)(4,1)} %bitcast.23), calls=%async_computation.2 | async-start | bytes 8388608
  40.1 7.9 %collective-permute-start.7 = (bf16[24,8320]{1,0:T(8,128)(2,1)S(1)}, bf16[24,8320]{1,0:T(8,128)(2,1)S(1)}, u32[]{:S(2)}, u32[]{:S(2)}) collective-permute-start(bf16[24,8320]{1,0:T(8,128)(2,1)S(1)} %broadcast_select_fusion), channel_id=1, source_target_pairs={{0,2},{2,0},{4,6},{6,4},{12,14},{14,12},{8,10},{10,8},{1,5},{3,7},... | collective-permute-start | bytes 1198088 | tf_op jit(solution)/shard_map/ppermute | solution.py:263
  48.9 4.2 %collective-permute-start.9 = (bf16[192,64]{1,0:T(8,128)(2,1)S(1)}, bf16[192,64]{1,0:T(8,128)(2,1)S(1)}, u32[]{:S(2)}, u32[]{:S(2)}) collective-permute-start(bf16[192,64]{1,0:T(8,128)(2,1)S(1)} %get-tuple-element.32.refs_0_), channel_id=1, source_target_pairs={{0,2},{1,3},{2,0},{3,1},{4,6},{5,7},{6,4},{7,5},{12,14},{13,15},{1... | collective-permute-start | bytes 73736 | tf_op jit(solution)/shard_map/ppermute | solution.py:236
  53.1 9.5 %copy-start.3 = (bf16[16,64,512]{2,1,0:T(8,128)(2,1)S(1)}, bf16[16,64,512]{2,1,0:T(8,128)(2,1)}, u32[]{:S(2)}) copy-start(bf16[16,64,512]{2,1,0:T(8,128)(2,1)} %param.11) | copy-start | bytes 3145732
  53.1 9.5 %collective-permute-start.10 = (bf16[96,128]{1,0:T(8,128)(2,1)S(1)}, bf16[96,128]{1,0:T(8,128)(2,1)S(1)}, u32[]{:S(2)}, u32[]{:S(2)}) collective-permute-start(bf16[96,128]{1,0:T(8,128)(2,1)S(1)} %shard_map.76.refs_0_), channel_id=1, source_target_pairs={{0,4},{1,5},{2,6},{3,7},{4,12},{5,13},{6,14},{7,15},{12,8},{13,9},... | collective-permute-start | bytes 73736 | tf_op jit(solution)/shard_map/ppermute | solution.py:236
  55.6 7.1 %collective-permute-start.11 = (bf16[96,128]{1,0:T(8,128)(2,1)S(1)}, bf16[96,128]{1,0:T(8,128)(2,1)S(1)}, u32[]{:S(2)}, u32[]{:S(2)}) collective-permute-start(bf16[96,128]{1,0:T(8,128)(2,1)S(1)} %shard_map.76.refs_0_), channel_id=1, source_target_pairs={{0,12},{1,13},{2,14},{3,15},{4,8},{5,9},{6,10},{7,11},{12,0},{13,1... | collective-permute-start | bytes 73736 | tf_op jit(solution)/shard_map/ppermute | solution.py:236
  56.1 6.6 %collective-permute-start.12 = (bf16[96,128]{1,0:T(8,128)(2,1)S(1)}, bf16[96,128]{1,0:T(8,128)(2,1)S(1)}, u32[]{:S(2)}, u32[]{:S(2)}) collective-permute-start(bf16[96,128]{1,0:T(8,128)(2,1)S(1)} %shard_map.76.refs_0_), channel_id=1, source_target_pairs={{0,8},{1,9},{2,10},{3,11},{4,0},{5,1},{6,2},{7,3},{12,4},{13,5},{1... | collective-permute-start | bytes 73736 | tf_op jit(solution)/shard_map/ppermute | solution.py:236

commit v10 on v9

--- a/solution.py
+++ b/solution.py
@@ -149,7 +149,7 @@
     part_ref[first:, :] = part.astype(jnp.bfloat16)
 
 
-def shrink_rows(blocks, own, other, before=()):
+def shrink_rows(blocks, own, other, before=(), tokens=()):
     rows = blocks[0].shape[0] * len(blocks)
     total = rows + sum(part.shape[0] for part in before)
     out_shape = (
@@ -158,7 +158,9 @@
         jax.ShapeDtypeStruct((rows, own.shape[1]), jnp.bfloat16),
     )
     return call(
-        lambda *refs: shrink_kernel(len(blocks), *refs), out_shape, (*blocks, own, other, *before)
+        lambda *refs: shrink_kernel(len(blocks), *refs[len(tokens) :]),
+        out_shape,
+        (*tokens, *blocks, own, other, *before),
     )
 
 
@@ -178,6 +180,55 @@
     rows, rank = part.shape
     out_shape = jax.ShapeDtypeStruct((rows // 2, 2 * rank), part.dtype)
     return call(lambda *refs: pack_kernel(own_rows, *refs), out_shape, (part, across))
+
+
+def base_kernel(*refs):
+    *blocks, weight_ref, out_ref, kept_ref, sems = refs
+    width = weight_ref.shape[0]
+    copies = []
+    for number, start in enumerate(range(0, width, CHUNK)):
+        rows = pl.ds(start, CHUNK)
+        copies.append(
+            pltpu.make_async_copy(weight_ref.at[rows], kept_ref.at[rows], sems.at[number])
+        )
+        copies[-1].start()
+    out_ref[...] = jnp.zeros(out_ref.shape, jnp.float32)
+    for number, start in enumerate(range(0, width, CHUNK)):
+        lanes = slice(start, start + CHUNK)
+        rows = stacked(blocks, lanes)
+        copies[number].wait()
+        out_ref[...] += jnp.dot(rows, kept_ref[lanes, :], preferred_element_type=jnp.float32)
+
+
+def base_and_weight(blocks, weight):
+    rows = blocks[0].shape[0] * len(blocks)
+    return pl.pallas_call(
+        base_kernel,
+        out_shape=(
+            jax.ShapeDtypeStruct((rows, weight.shape[1]), jnp.float32),
+            jax.ShapeDtypeStruct(weight.shape, weight.dtype),
+        ),
+        in_specs=[VMEM] * len(blocks) + [pl.BlockSpec(memory_space=pltpu.HBM)],
+        out_specs=(VMEM, VMEM),
+        scratch_shapes=[pltpu.SemaphoreType.DMA((weight.shape[0] // CHUNK,))],
+        compiler_params=pltpu.CompilerParams(vmem_limit_bytes=VMEM_LIMIT),
+        cost_estimate=pl.CostEstimate(flops=1, bytes_accessed=1, transcendentals=0),
+    )(*blocks, weight)
+
+
+def token_kernel(block_ref, out_ref):
+    out_ref[...] = jnp.zeros(out_ref.shape, out_ref.dtype)
+
+
+def token(block):
+    return pl.pallas_call(
+        token_kernel,
+        out_shape=jax.ShapeDtypeStruct((8, LANES), jnp.float32),
+        in_specs=[pl.BlockSpec(memory_space=pl.ANY)],
+        out_specs=VMEM,
+        compiler_params=pltpu.CompilerParams(vmem_limit_bytes=VMEM_LIMIT),
+        cost_estimate=pl.CostEstimate(flops=1000000, bytes_accessed=1, transcendentals=0),
+    )(block)
 
 
 def finish_kernel(places, rank, *refs):
@@ -245,26 +296,30 @@
     weight_other = move(query_weight, 0, 1)
 
     block, other = [normalize(hidden, norm_weight, adapter_index, adapter_slot)], []
-    parts, slots, bases = [], [], []
+    parts, slots, bases, tokens = [], [], [], []
     last = places - 1
     for step in range(last):
-        block.append(move(block[step], 1, 0))
+        if step:
+            tokens.append(token(block[step]))
+        block.append(move(after(block[step], *tokens[-1:]), 1, 0))
         other.append(move(after(block[step], *other[-1:]), 0, 2))
         if step % 2 == 0 and step:
             rows = [block[step - 2], other[step - 2], block[step - 1], other[step - 1]]
-            rows = after(rows, block[step])
-            part, slot, rows = shrink_rows(rows, down, down_other)
+            blocks = after(rows, block[step])
+            part, slot, rows = shrink_rows(blocks, down, down_other)
             parts.append(part)
             slots.append(slot)
             bases.append(base_rows(rows, query_weight))
             if step < last - 1:
                 bases.append(base_rows(rows, weight_other))
-    source = jnp.where((me & 1) == 0, after(block[last], *bases, other[-1]), other[-1])
+    tokens.append(token(block[last]))
+    source = jnp.where((me & 1) == 0, after(block[last], *bases, other[-1], tokens[-1]), other[-1])
     crossed = lax.ppermute(source, "adapter", split_pairs(places))
-    bases.append(base_rows(after(rows, source), weight_other))
+    base, weight_other = base_and_weight(after(blocks, source), weight_other)
+    bases.append(base)
     crossed = after(crossed, *bases)
     rows = [block[last - 1], other[-1], block[last], crossed]
-    part, slot, rows = shrink_rows(rows, down, down_other, parts)
+    part, slot, rows = shrink_rows(rows, down, down_other, parts, tokens)
     slots.append(slot)
 
     across = move(part, 0, 2)

time: 78.2 us -> 74.8 us (0.957)
  matrix products: 16.7 us -> 7.86 us
  waiting for transfers between devices: 19.5 us -> 25.7 us
  Pallas kernels: 5.62 us -> 8.43 us
  starting transfers between devices: 19.2 us -> 16.4 us
  blocking collectives: 13.7 us -> 12.9 us
    dot_general x4 -> x3, matrix products: 16.7 us -> 7.86 us  [base_rows(): return jnp.dot(rows, weight, preferred_element_type=jnp.float32)]
    pallas_call x0 -> x4, Pallas kernels: none -> 3.79 us  [the longest x1 3.79 us: base_and_weight(): pl.pallas_call(base_kernel, out_shape=(jax.ShapeDtypeStruct((rows, weight...]
    ppermute x13, waiting for transfers between devices: 18.7 us -> 22.3 us  [move(): return lax.ppermute(x, 'adapter', pairs(places, steps, flip))]
    ppermute x1, waiting for transfers between devices: 0.75 us -> 3.38 us  [shards(): crossed = lax.ppermute(source, 'adapter', split_pairs(places))]
    ppermute x13, starting transfers between devices: 17.7 us -> 15.8 us  [move(): return lax.ppermute(x, 'adapter', pairs(places, steps, flip))]
    pallas_call x4, Pallas kernels: 3.58 us -> 2.58 us  [call(): pl.pallas_call(kernel, out_shape=out_shape, in_specs=[VMEM] * len(operand...]
    ppermute x1, starting transfers between devices: 1.57 us -> 0.69 us  [shards(): crossed = lax.ppermute(source, 'adapter', split_pairs(places))]
    unnamed x12 -> x14, local copies, waits for them, and re-layouts: 2.25 us -> 2.25 us
  transfers between devices with their start and end apart: 14 -> 14, of which waited for: 6 -> 6; matrix products, arithmetic and copies ran while one was open for 21% -> 11% of each run, Pallas kernels for 6% -> 10%
where the time goes in v10:
time: 74.8 us; the launch traced here: 74.6 us
  waiting for transfers between devices  25.7 us (34%)
  starting transfers between devices  16.4 us (22%)
  blocking collectives  12.9 us (17%)
  Pallas kernels  8.43 us (11%)
  matrix products  7.86 us (11%)
  local copies, waits for them, and re-layouts  3.02 us (4%)
    ppermute x13, waiting for transfers between devices, move(): return lax.ppermute(x, 'adapter', pairs(places, steps, flip))  22.3 us
    ppermute x13, starting transfers between devices, move(): return lax.ppermute(x, 'adapter', pairs(places, steps, flip))  15.8 us
    all_to_all x1, blocking collectives, shards(): lax.all_to_all(query, 'adapter', 0, 0, axis_index_groups=groups, tiled=True)  12.9 us
    dot_general x3, matrix products, base_rows(): return jnp.dot(rows, weight, preferred_element_type=jnp.float32)  7.86 us
    pallas_call x1, Pallas kernels, base_and_weight(): pl.pallas_call(base_kernel, out_shape=(jax.ShapeDtypeStruct((rows, weight...  3.79 us
    ppermute x1, waiting for transfers between devices, shards(): crossed = lax.ppermute(source, 'adapter', split_pairs(places))  3.38 us
    pallas_call x4, Pallas kernels, call(): pl.pallas_call(kernel, out_shape=out_shape, in_specs=[VMEM] * len(operand...  2.58 us
    unnamed x14, local copies, waits for them, and re-layouts  2.25 us
  transfers between devices with their start and end apart: 14, of which 6 were waited for; matrix products, arithmetic and copies ran while one was open for 11% of the time, Pallas kernels for 10%

profile of v10, /device:TPU:0, one launch (start us, length us, event | category | flops | bytes accessed | tf_op | source)
XLA Modules:
  0.0 74.6 jit_solution(8603452098201843652)
XLA Ops:
  0.5 2.1 %shard_map.73.refs_0_ = bf16[24,8320]{1,0:T(8,128)(2,1)} custom-call(bf16[24,8192]{1,0:T(8,128)(2,1)} %refs_0_.1, f32[1,8192]{1,0:T(1,128)} %bitcast.24, s32[1,24]{1,0:T(1,128)} %bitcast.25, s32[1,16]{1,0:T(1,128)} %bitcast.26), custom_call_target="tpu_custom_call" | custom-call | tf_op jit(solution)/shard_map/pallas_call | solution.py:109
  2.6 3.1 %collective-permute-start = (bf16[24,8320]{1,0:T(8,128)(2,1)}, bf16[24,8320]{1,0:T(8,128)(2,1)S(1)}, u32[]{:S(2)}, u32[]{:S(2)}) collective-permute-start(bf16[24,8320]{1,0:T(8,128)(2,1)} %shard_map.73.refs_0_), channel_id=1, source_target_pairs={{0,4},{1,5},{2,6},{3,7},{4,12},{5,13},{6,14},{7,15},{12,8},{13,9},... | collective-permute-start | bytes 1198088 | tf_op jit(solution)/shard_map/ppermute | solution.py:287
  5.6 1.5 %collective-permute-start.3 = (bf16[24,8320]{1,0:T(8,128)(2,1)}, bf16[24,8320]{1,0:T(8,128)(2,1)S(1)}, u32[]{:S(2)}, u32[]{:S(2)}) collective-permute-start(bf16[24,8320]{1,0:T(8,128)(2,1)} %shard_map.73.refs_0_), channel_id=1, source_target_pairs={{0,2},{1,3},{2,0},{3,1},{4,6},{5,7},{6,4},{7,5},{12,14},{13,15},{1... | collective-permute-start | bytes 1198088 | tf_op jit(solution)/shard_map/ppermute | solution.py:287
  7.2 9.1 %collective-permute-done.block_ref.refs_2_ = bf16[24,8320]{1,0:T(8,128)(2,1)S(1)} collective-permute-done((bf16[24,8320]{1,0:T(8,128)(2,1)}, bf16[24,8320]{1,0:T(8,128)(2,1)S(1)}, u32[]{:S(2)}, u32[]{:S(2)}) %collective-permute-start) | collective-permute-done | bytes 399392 | tf_op jit(solution)/shard_map/ppermute | solution.py:287
  16.3 0.9 %collective-permute-start.1 = (bf16[24,8320]{1,0:T(8,128)(2,1)S(1)}, bf16[24,8320]{1,0:T(8,128)(2,1)S(1)}, u32[]{:S(2)}, u32[]{:S(2)}) collective-permute-start(bf16[24,8320]{1,0:T(8,128)(2,1)S(1)} %collective-permute-done.block_ref.refs_2_), channel_id=1, source_target_pairs={{0,4},{1,5},{2,6},{3,7},{4,12},{5,13},{6,14},{7,15},{12,8},{13,9},... | collective-permute-start | bytes 1198088 | tf_op jit(solution)/shard_map/ppermute | solution.py:287
  17.2 1.5 %collective-permute-start.4 = (bf16[24,8320]{1,0:T(8,128)(2,1)S(1)}, bf16[24,8320]{1,0:T(8,128)(2,1)S(1)}, u32[]{:S(2)}, u32[]{:S(2)}) collective-permute-start(bf16[24,8320]{1,0:T(8,128)(2,1)S(1)} %collective-permute-done.block_ref.refs_2_), channel_id=1, source_target_pairs={{0,2},{1,3},{2,0},{3,1},{4,6},{5,7},{6,4},{7,5},{12,14},{13,15},{1... | collective-permute-start | bytes 1198088 | tf_op jit(solution)/shard_map/ppermute | solution.py:287
  18.8 9.1 %collective-permute-done.1.block_ref.refs_3_ = bf16[24,8320]{1,0:T(8,128)(2,1)S(1)} collective-permute-done((bf16[24,8320]{1,0:T(8,128)(2,1)S(1)}, bf16[24,8320]{1,0:T(8,128)(2,1)S(1)}, u32[]{:S(2)}, u32[]{:S(2)}) %collective-permute-start.1) | collective-permute-done | bytes 399392 | tf_op jit(solution)/shard_map/ppermute | solution.py:287
  27.8 2.7 %collective-permute-start.2 = (bf16[24,8320]{1,0:T(8,128)(2,1)S(1)}, bf16[24,8320]{1,0:T(8,128)(2,1)S(1)}, u32[]{:S(2)}, u32[]{:S(2)}) collective-permute-start(bf16[24,8320]{1,0:T(8,128)(2,1)S(1)} %collective-permute-done.1.block_ref.refs_3_), channel_id=1, source_target_pairs={{0,4},{1,5},{2,6},{3,7},{4,12},{5,13},{6,14},{7,15},{12,8},{13,9},... | collective-permute-start | bytes 1198088 | tf_op jit(solution)/shard_map/ppermute | solution.py:287
  30.5 1.5 %collective-permute-start.5 = (bf16[24,8320]{1,0:T(8,128)(2,1)S(1)}, bf16[24,8320]{1,0:T(8,128)(2,1)S(1)}, u32[]{:S(2)}, u32[]{:S(2)}) collective-permute-start(bf16[24,8320]{1,0:T(8,128)(2,1)S(1)} %collective-permute-done.1.block_ref.refs_3_), channel_id=1, source_target_pairs={{0,2},{1,3},{2,0},{3,1},{4,6},{5,7},{6,4},{7,5},{12,14},{13,15},{1... | collective-permute-start | bytes 1198088 | tf_op jit(solution)/shard_map/ppermute | solution.py:287
  32.1 1.2 %copy-done = bf16[1,8192,64]{1,2,0:T(8,128)(2,1)S(1)} copy-done((bf16[1,8192,64]{1,2,0:T(8,128)(2,1)S(1)}, bf16[1,8192,64]{1,2,0:T(8,128)(2,1)}, u32[]{:S(2)}) %copy-start) | copy-done | bytes 1048600
  33.3 1.0 %copy-done.2 = bf16[24,8320]{1,0:T(8,128)(2,1)S(1)} copy-done((bf16[24,8320]{1,0:T(8,128)(2,1)S(1)}, bf16[24,8320]{1,0:T(8,128)(2,1)}, u32[]{:S(2)}) %copy-start.2) | copy-done | bytes 399384
  34.3 0.9 %shard_map.77 = (bf16[96,64]{1,0:T(8,128)(2,1)S(1)}, s32[96,128]{1,0:T(8,128)S(1)}, bf16[96,8192]{1,0:T(8,128)(2,1)S(1)}) custom-call(bf16[24,8320]{1,0:T(8,128)(2,1)S(1)} %copy-done.2, bf16[24,8320]{1,0:T(8,128)(2,1)S(1)} %collective-permute-done.3.refs_1_, bf16[24,8320]{1,0:T(8,128)(2,1)S(1)} %collective-permute-done.block_ref.refs_2_, ...), custom_call_target="tpu_custom_call" | custom-call | flops 1 | bytes 1 | tf_op jit(solution)/shard_map/pallas_call | solution.py:57
  35.2 5.0 %fusion.refs_4_ = f32[96,512]{1,0:T(8,128)S(1)} fusion(bf16[96,8192]{1,0:T(8,128)(2,1)S(1)} %get-tuple-element.36, bf16[8192,512]{1,0:T(8,128)(2,1)} %param.9), kind=kOutput, calls=%fused_computation.1 | convolution fusion | flops 805306368 | bytes 10158080 | tf_op jit(solution)/shard_map/dot_general | solution.py:290
  41.0 3.8 %shard_map.78 = (f32[96,512]{1,0:T(8,128)S(1)}, bf16[8192,512]{1,0:T(8,128)(2,1)S(1)}) custom-call(bf16[24,8320]{1,0:T(8,128)(2,1)S(1)} %copy-done.3, bf16[24,8320]{1,0:T(8,128)(2,1)S(1)} %collective-permute-done.3.refs_1_, bf16[24,8320]{1,0:T(8,128)(2,1)S(1)} %collective-permute-done.block_ref.refs_2_, bf16[24,8320]{1,0:T(8,128)(2,1)S(1)} %collective-permute-done.4.refs_3_, ...), custom_call_target="tpu_custom_call" | custom-call | flops 1 | bytes 1 | tf_op jit(solution)/shard_map/pallas_call | solution.py:205
  44.8 3.4 %collective-permute-done.7.refs_6_ = bf16[24,8320]{1,0:T(8,128)(2,1)S(1)} collective-permute-done((bf16[24,8320]{1,0:T(8,128)(2,1)S(1)}, bf16[24,8320]{1,0:T(8,128)(2,1)S(1)}, u32[]{:S(2)}, u32[]{:S(2)}) %collective-permute-start.7) | collective-permute-done | bytes 399392 | tf_op jit(solution)/shard_map/ppermute | solution.py:317
  48.2 0.9 %shard_map.79 = (bf16[192,64]{1,0:T(8,128)(2,1)S(1)}, s32[96,128]{1,0:T(8,128)S(1)}, bf16[96,8192]{1,0:T(8,128)(2,1)S(1)}) custom-call(f32[8,128]{1,0:T(8,128)S(1)} %shard_map.74.refs_0_, f32[8,128]{1,0:T(8,128)S(1)} %shard_map.75.refs_1_, f32[8,128]{1,0:T(8,128)S(1)} %shard_map.76.refs_2_, bf16[24,8320]{1,0:T(8,128)(2,1)S(1)} %collective-permute-done.1.block_ref.refs_3_, ...), custom_call_target="tpu_custom_call" | custom-call | flops 1 | bytes 1 | tf_op jit(solution)/shard_map/pallas_call | solution.py:57
  49.8 1.4 %fusion.1.refs_6_ = f32[96,512]{1,0:T(8,128)S(1)} fusion(bf16[96,8192]{1,0:T(8,128)(2,1)S(1)} %get-tuple-element.46, bf16[8192,512]{1,0:T(8,128)(2,1)S(1)} %bitcast.22), kind=kOutput, calls=%fused_computation.2 | convolution fusion | flops 805306368 | bytes 10158080 | tf_op jit(solution)/shard_map/dot_general | solution.py:290
  51.2 2.0 %collective-permute-done.9.refs_1_ = bf16[192,64]{1,0:T(8,128)(2,1)S(1)} collective-permute-done((bf16[192,64]{1,0:T(8,128)(2,1)S(1)}, bf16[192,64]{1,0:T(8,128)(2,1)S(1)}, u32[]{:S(2)}, u32[]{:S(2)}) %collective-permute-start.9) | collective-permute-done | bytes 24608 | tf_op jit(solution)/shard_map/ppermute | solution.py:287
  53.3 1.2 %collective-permute-start.10 = (bf16[96,128]{1,0:T(8,128)(2,1)S(1)}, bf16[96,128]{1,0:T(8,128)(2,1)S(1)}, u32[]{:S(2)}, u32[]{:S(2)}) collective-permute-start(bf16[96,128]{1,0:T(8,128)(2,1)S(1)} %shard_map.80.refs_0_), channel_id=1, source_target_pairs={{0,4},{1,5},{2,6},{3,7},{4,12},{5,13},{6,14},{7,15},{12,8},{13,9},... | collective-permute-start | bytes 73736 | tf_op jit(solution)/shard_map/ppermute | solution.py:287
  54.7 1.8 %collective-permute-start.12 = (bf16[96,128]{1,0:T(8,128)(2,1)S(1)}, bf16[96,128]{1,0:T(8,128)(2,1)S(1)}, u32[]{:S(2)}, u32[]{:S(2)}) collective-permute-start(bf16[96,128]{1,0:T(8,128)(2,1)S(1)} %shard_map.80.refs_0_), channel_id=1, source_target_pairs={{0,8},{1,9},{2,10},{3,11},{4,0},{5,1},{6,2},{7,3},{12,4},{13,5},{1... | collective-permute-start | bytes 73736 | tf_op jit(solution)/shard_map/ppermute | solution.py:287
  56.5 1.4 %fusion.2.refs_7_ = f32[96,512]{1,0:T(8,128)S(1)} fusion(bf16[96,8192]{1,0:T(8,128)(2,1)S(1)} %get-tuple-element.46, bf16[8192,512]{1,0:T(8,128)(2,1)S(1)} %get-tuple-element.48), kind=kOutput, calls=%fused_computation.3 | convolution fusion | flops 805306368 | bytes 10158080 | tf_op jit(solution)/shard_map/dot_general | solution.py:290
  58.0 2.1 %collective-permute-done.11.refs_2_ = bf16[96,128]{1,0:T(8,128)(2,1)S(1)} collective-permute-done((bf16[96,128]{1,0:T(8,128)(2,1)S(1)}, bf16[96,128]{1,0:T(8,128)(2,1)S(1)}, u32[]{:S(2)}, u32[]{:S(2)}) %collective-permute-start.11) | collective-permute-done | bytes 24608 | tf_op jit(solution)/shard_map/ppermute | solution.py:287
  60.9 12.9 %all_to_all.5 = bf16[8,24,1024]{2,1,0:T(8,128)(2,1)S(1)} all-to-all(bf16[8,24,1024]{2,1,0:T(8,128)(2,1)S(1)} %shard_map.81), channel_id=1, replica_groups={{0,2,4,6,8,10,12,14},{1,3,5,7,9,11,13,15},{16,18,20,22,24,26,28,30},{17..., dimensions={0} | all-to-all | bytes 786432 | tf_op jit(solution)/shard_map/all_to_all | solution.py:332
  73.8 0.8 %copy.9 = bf16[8,3,8,1024]{3,2,0,1:T(8,128)(2,1)} copy(bf16[8,3,8,1024]{3,2,1,0:T(8,128)(2,1)S(1)} %bitcast.23) | data formatting | bytes 786432 | tf_op jit(solution)/shard_map/reshape | solution.py:333
  (34 shorter events, 3.1 us)
Async XLA Ops:
  0.0 41.0 %collective-permute-start.8 = (bf16[8192,512]{1,0:T(8,128)(2,1)}, bf16[8192,512]{1,0:T(8,128)(2,1)}, u32[]{:S(2)}, u32[]{:S(2)}) collective-permute-start(bf16[8192,512]{1,0:T(8,128)(2,1)} %param.9), channel_id=1, source_target_pairs={{0,1},{1,0},{2,3},{3,2},{4,5},{5,4},{6,7},{7,6},{12,13},{13,12},{1... | collective-permute-start | bytes 25165832 | tf_op jit(solution)/shard_map/ppermute | solution.py:287
  0.5 31.6 %collective-permute-start.6 = (bf16[64,8192]{1,0:T(8,128)(2,1)}, bf16[64,8192]{1,0:T(8,128)(2,1)S(1)}, u32[]{:S(2)}, u32[]{:S(2)}) collective-permute-start(bf16[64,8192]{1,0:T(8,128)(2,1)} %bitcast.16), channel_id=1, source_target_pairs={{0,1},{1,0},{2,3},{3,2},{4,5},{5,4},{6,7},{7,6},{12,13},{13,12},{1... | collective-permute-start | bytes 3145736 | tf_op jit(solution)/shard_map/ppermute | solution.py:287
  2.6 13.7 %collective-permute-start = (bf16[24,8320]{1,0:T(8,128)(2,1)}, bf16[24,8320]{1,0:T(8,128)(2,1)S(1)}, u32[]{:S(2)}, u32[]{:S(2)}) collective-permute-start(bf16[24,8320]{1,0:T(8,128)(2,1)} %shard_map.73.refs_0_), channel_id=1, source_target_pairs={{0,4},{1,5},{2,6},{3,7},{4,12},{5,13},{6,14},{7,15},{12,8},{13,9},... | collective-permute-start | bytes 1198088 | tf_op jit(solution)/shard_map/ppermute | solution.py:287
  5.6 11.6 %collective-permute-start.3 = (bf16[24,8320]{1,0:T(8,128)(2,1)}, bf16[24,8320]{1,0:T(8,128)(2,1)S(1)}, u32[]{:S(2)}, u32[]{:S(2)}) collective-permute-start(bf16[24,8320]{1,0:T(8,128)(2,1)} %shard_map.73.refs_0_), channel_id=1, source_target_pairs={{0,2},{1,3},{2,0},{3,1},{4,6},{5,7},{6,4},{7,5},{12,14},{13,15},{1... | collective-permute-start | bytes 1198088 | tf_op jit(solution)/shard_map/ppermute | solution.py:287
  16.3 11.5 %collective-permute-start.1 = (bf16[24,8320]{1,0:T(8,128)(2,1)S(1)}, bf16[24,8320]{1,0:T(8,128)(2,1)S(1)}, u32[]{:S(2)}, u32[]{:S(2)}) collective-permute-start(bf16[24,8320]{1,0:T(8,128)(2,1)S(1)} %collective-permute-done.block_ref.refs_2_), channel_id=1, source_target_pairs={{0,4},{1,5},{2,6},{3,7},{4,12},{5,13},{6,14},{7,15},{12,8},{13,9},... | collective-permute-start | bytes 1198088 | tf_op jit(solution)/shard_map/ppermute | solution.py:287
  17.2 10.6 %collective-permute-start.4 = (bf16[24,8320]{1,0:T(8,128)(2,1)S(1)}, bf16[24,8320]{1,0:T(8,128)(2,1)S(1)}, u32[]{:S(2)}, u32[]{:S(2)}) collective-permute-start(bf16[24,8320]{1,0:T(8,128)(2,1)S(1)} %collective-permute-done.block_ref.refs_2_), channel_id=1, source_target_pairs={{0,2},{1,3},{2,0},{3,1},{4,6},{5,7},{6,4},{7,5},{12,14},{13,15},{1... | collective-permute-start | bytes 1198088 | tf_op jit(solution)/shard_map/ppermute | solution.py:287
  27.8 12.4 %collective-permute-start.2 = (bf16[24,8320]{1,0:T(8,128)(2,1)S(1)}, bf16[24,8320]{1,0:T(8,128)(2,1)S(1)}, u32[]{:S(2)}, u32[]{:S(2)}) collective-permute-start(bf16[24,8320]{1,0:T(8,128)(2,1)S(1)} %collective-permute-done.1.block_ref.refs_3_), channel_id=1, source_target_pairs={{0,4},{1,5},{2,6},{3,7},{4,12},{5,13},{6,14},{7,15},{12,8},{13,9},... | collective-permute-start | bytes 1198088 | tf_op jit(solution)/shard_map/ppermute | solution.py:287
  30.5 9.7 %collective-permute-start.5 = (bf16[24,8320]{1,0:T(8,128)(2,1)S(1)}, bf16[24,8320]{1,0:T(8,128)(2,1)S(1)}, u32[]{:S(2)}, u32[]{:S(2)}) collective-permute-start(bf16[24,8320]{1,0:T(8,128)(2,1)S(1)} %collective-permute-done.1.block_ref.refs_3_), channel_id=1, source_target_pairs={{0,2},{1,3},{2,0},{3,1},{4,6},{5,7},{6,4},{7,5},{12,14},{13,15},{1... | collective-permute-start | bytes 1198088 | tf_op jit(solution)/shard_map/ppermute | solution.py:287
  32.1 1.2 %copy-start = (bf16[1,8192,64]{1,2,0:T(8,128)(2,1)S(1)}, bf16[1,8192,64]{1,2,0:T(8,128)(2,1)}, u32[]{:S(2)}) copy-start(bf16[1,8192,64]{1,2,0:T(8,128)(2,1)} %param.10) | copy-start | bytes 3145732
  33.3 1.0 %copy-start.2 = (bf16[24,8320]{1,0:T(8,128)(2,1)S(1)}, bf16[24,8320]{1,0:T(8,128)(2,1)}, u32[]{:S(2)}) copy-start(bf16[24,8320]{1,0:T(8,128)(2,1)} %shard_map.73.refs_0_) | copy-start | bytes 1198084
  35.2 14.6 %slice-start = ((s8[8388608]{0:T(1024)(128)(4,1)}), s8[4194304]{0:T(1024)(128)(4,1)S(1)}, s32[]{:S(2)}) async-start(s8[8388608]{0:T(1024)(128)(4,1)} %bitcast.21), calls=%async_computation.1 | async-start | bytes 8388608
  35.2 5.8 %copy-start.4 = (bf16[16,64,512]{2,1,0:T(8,128)(2,1)S(1)}, bf16[16,64,512]{2,1,0:T(8,128)(2,1)}, u32[]{:S(2)}) copy-start(bf16[16,64,512]{2,1,0:T(8,128)(2,1)} %param.11) | copy-start | bytes 3145732
  35.2 5.8 %copy-start.3 = (bf16[24,8320]{1,0:T(8,128)(2,1)S(1)}, bf16[24,8320]{1,0:T(8,128)(2,1)}, u32[]{:S(2)}) copy-start(bf16[24,8320]{1,0:T(8,128)(2,1)} %shard_map.73.refs_0_) | copy-start | bytes 1198084
  35.2 14.6 %slice-start.1 = ((s8[8388608]{0:T(1024)(128)(4,1)}), s8[4194304]{0:T(1024)(128)(4,1)S(1)}, s32[]{:S(2)}) async-start(s8[8388608]{0:T(1024)(128)(4,1)} %bitcast.21), calls=%async_computation.2 | async-start | bytes 8388608
  40.2 8.0 %copy-start.1 = (bf16[1,8192,64]{1,2,0:T(8,128)(2,1)S(1)}, bf16[1,8192,64]{1,2,0:T(8,128)(2,1)}, u32[]{:S(2)}) copy-start(bf16[1,8192,64]{1,2,0:T(8,128)(2,1)} %param.10) | copy-start | bytes 3145732
  40.3 7.9 %collective-permute-start.7 = (bf16[24,8320]{1,0:T(8,128)(2,1)S(1)}, bf16[24,8320]{1,0:T(8,128)(2,1)S(1)}, u32[]{:S(2)}, u32[]{:S(2)}) collective-permute-start(bf16[24,8320]{1,0:T(8,128)(2,1)S(1)} %broadcast_select_fusion), channel_id=1, source_target_pairs={{0,2},{2,0},{4,6},{6,4},{12,14},{14,12},{8,10},{10,8},{1,5},{3,7},... | collective-permute-start | bytes 1198088 | tf_op jit(solution)/shard_map/ppermute | solution.py:317
  41.0 17.0 %collective-permute-start.13 = (bf16[1024,512]{1,0:T(8,128)(2,1)S(1)}, bf16[1024,512]{1,0:T(8,128)(2,1)S(1)}, u32[]{:S(2)}, u32[]{:S(2)}) collective-permute-start(bf16[1024,512]{1,0:T(8,128)(2,1)S(1)} %bitcast.19), channel_id=1, source_target_pairs={{0,1},{1,0},{2,3},{3,2},{4,5},{5,4},{6,7},{7,6},{12,13},{13,12},{1... | collective-permute-start | bytes 3145736 | tf_op jit(solution)/shard_map/ppermute | solution.py:287
  49.1 4.2 %collective-permute-start.9 = (bf16[192,64]{1,0:T(8,128)(2,1)S(1)}, bf16[192,64]{1,0:T(8,128)(2,1)S(1)}, u32[]{:S(2)}, u32[]{:S(2)}) collective-permute-start(bf16[192,64]{1,0:T(8,128)(2,1)S(1)} %get-tuple-element.45.refs_0_), channel_id=1, source_target_pairs={{0,2},{1,3},{2,0},{3,1},{4,6},{5,7},{6,4},{7,5},{12,14},{13,15},{1... | collective-permute-start | bytes 73736 | tf_op jit(solution)/shard_map/ppermute | solution.py:287
  53.3 4.7 %collective-permute-start.10 = (bf16[96,128]{1,0:T(8,128)(2,1)S(1)}, bf16[96,128]{1,0:T(8,128)(2,1)S(1)}, u32[]{:S(2)}, u32[]{:S(2)}) collective-permute-start(bf16[96,128]{1,0:T(8,128)(2,1)S(1)} %shard_map.80.refs_0_), channel_id=1, source_target_pairs={{0,4},{1,5},{2,6},{3,7},{4,12},{5,13},{6,14},{7,15},{12,8},{13,9},... | collective-permute-start | bytes 73736 | tf_op jit(solution)/shard_map/ppermute | solution.py:287
  54.5 5.6 %collective-permute-start.11 = (bf16[96,128]{1,0:T(8,128)(2,1)S(1)}, bf16[96,128]{1,0:T(8,128)(2,1)S(1)}, u32[]{:S(2)}, u32[]{:S(2)}) collective-permute-start(bf16[96,128]{1,0:T(8,128)(2,1)S(1)} %shard_map.80.refs_0_), channel_id=1, source_target_pairs={{0,12},{1,13},{2,14},{3,15},{4,8},{5,9},{6,10},{7,11},{12,0},{13,1... | collective-permute-start | bytes 73736 | tf_op jit(solution)/shard_map/ppermute | solution.py:287
  54.7 5.4 %collective-permute-start.12 = (bf16[96,128]{1,0:T(8,128)(2,1)S(1)}, bf16[96,128]{1,0:T(8,128)(2,1)S(1)}, u32[]{:S(2)}, u32[]{:S(2)}) collective-permute-start(bf16[96,128]{1,0:T(8,128)(2,1)S(1)} %shard_map.80.refs_0_), channel_id=1, source_target_pairs={{0,8},{1,9},{2,10},{3,11},{4,0},{5,1},{6,2},{7,3},{12,4},{13,5},{1... | collective-permute-start | bytes 73736 | tf_op jit(solution)/shard_map/ppermute | solution.py:287

commit v11 on v10

--- a/solution.py
+++ b/solution.py
@@ -35,8 +35,8 @@
 
 def split_pairs(places):
     flips, steps = pairs(places, 0, 2), pairs(places, 1, 0)
-    return [pair for pair in flips if pair[0] % CORES == 0] + [
-        pair for pair in steps if pair[0] % CORES
+    return [pair for pair in flips if pair[0] % CORES] + [
+        pair for pair in steps if pair[0] % CORES == 0
     ]
 
 
@@ -183,34 +183,34 @@
 
 
 def base_kernel(*refs):
-    *blocks, weight_ref, out_ref, kept_ref, sems = refs
+    *blocks, weight_ref, out_ref, buffer, sems = refs
     width = weight_ref.shape[0]
     copies = []
     for number, start in enumerate(range(0, width, CHUNK)):
-        rows = pl.ds(start, CHUNK)
+        here = pl.ds(start, CHUNK)
         copies.append(
-            pltpu.make_async_copy(weight_ref.at[rows], kept_ref.at[rows], sems.at[number])
+            pltpu.make_async_copy(weight_ref.at[here], buffer.at[here], sems.at[number])
         )
         copies[-1].start()
     out_ref[...] = jnp.zeros(out_ref.shape, jnp.float32)
     for number, start in enumerate(range(0, width, CHUNK)):
         lanes = slice(start, start + CHUNK)
-        rows = stacked(blocks, lanes)
+        rows = jnp.concatenate([block[:, lanes] for block in blocks], axis=0)
         copies[number].wait()
-        out_ref[...] += jnp.dot(rows, kept_ref[lanes, :], preferred_element_type=jnp.float32)
-
-
-def base_and_weight(blocks, weight):
+        out_ref[...] += jnp.dot(rows, buffer[lanes, :], preferred_element_type=jnp.float32)
+
+
+def base_other(blocks, weight):
     rows = blocks[0].shape[0] * len(blocks)
     return pl.pallas_call(
         base_kernel,
-        out_shape=(
-            jax.ShapeDtypeStruct((rows, weight.shape[1]), jnp.float32),
-            jax.ShapeDtypeStruct(weight.shape, weight.dtype),
-        ),
+        out_shape=jax.ShapeDtypeStruct((rows, weight.shape[1]), jnp.float32),
         in_specs=[VMEM] * len(blocks) + [pl.BlockSpec(memory_space=pltpu.HBM)],
-        out_specs=(VMEM, VMEM),
-        scratch_shapes=[pltpu.SemaphoreType.DMA((weight.shape[0] // CHUNK,))],
+        out_specs=VMEM,
+        scratch_shapes=[
+            pltpu.VMEM(weight.shape, weight.dtype),
+            pltpu.SemaphoreType.DMA((weight.shape[0] // CHUNK,)),
+        ],
         compiler_params=pltpu.CompilerParams(vmem_limit_bytes=VMEM_LIMIT),
         cost_estimate=pl.CostEstimate(flops=1, bytes_accessed=1, transcendentals=0),
     )(*blocks, weight)
@@ -233,9 +233,8 @@
 
 def finish_kernel(places, rank, *refs):
     moved, refs = refs[:places], refs[places:]
-    slot_count = len(refs) - places - 3
-    bases, slots = refs[:places], refs[places : places + slot_count]
-    own_ref, other_ref, out_ref = refs[places + slot_count :]
+    bases, slots = refs[: places + 1], refs[places + 1 : 2 * places + 1]
+    own_ref, other_ref, out_ref = refs[2 * places + 1 :]
     depth, columns = own_ref.shape
     rows = SIDE * out_ref.shape[1]
     core = lax.axis_index("adapter") % CORES
@@ -257,7 +256,7 @@
         at = pl.multiple_of((core ^ which) * columns, columns)
         for step in range(places):
             here = slice(step * rows, (step + 1) * rows)
-            base = bases[step // 2 * 2 + which][step % 2 * rows : (step % 2 + 1) * rows, :]
+            base = bases[places][here, :] if which else bases[step][...]
             query = (base + ADAPTER_SCALE * update[here]).astype(jnp.bfloat16)
             for side in range(SIDE):
                 chip = ring_chip(places, -step, side)
@@ -296,37 +295,38 @@
     weight_other = move(query_weight, 0, 1)
 
     block, other = [normalize(hidden, norm_weight, adapter_index, adapter_slot)], []
-    parts, slots, bases, tokens = [], [], [], []
+    parts, slots, rows, bases, tokens = [], [], [], [], []
     last = places - 1
+
+    def meet(blocks, before=()):
+        part, slot, here = shrink_rows(blocks, down, down_other, before, tokens if before else ())
+        parts.append(part)
+        slots.append(slot)
+        rows.append(here)
+
     for step in range(last):
         if step:
+            block[step] = after(block[step], *bases[-1:])
             tokens.append(token(block[step]))
         block.append(move(after(block[step], *tokens[-1:]), 1, 0))
         other.append(move(after(block[step], *other[-1:]), 0, 2))
-        if step % 2 == 0 and step:
-            rows = [block[step - 2], other[step - 2], block[step - 1], other[step - 1]]
-            blocks = after(rows, block[step])
-            part, slot, rows = shrink_rows(blocks, down, down_other)
-            parts.append(part)
-            slots.append(slot)
-            bases.append(base_rows(rows, query_weight))
-            if step < last - 1:
-                bases.append(base_rows(rows, weight_other))
+        if step:
+            meet(after([block[step - 1], other[step - 1]], block[step]))
+            bases.append(base_rows(rows[-1], query_weight))
+    block[last] = after(block[last], bases[-1])
     tokens.append(token(block[last]))
-    source = jnp.where((me & 1) == 0, after(block[last], *bases, other[-1], tokens[-1]), other[-1])
+    source = after(block[last], other[-1], tokens[-1])
+    source = jnp.where((me & 1) == 1, source, other[-1])
     crossed = lax.ppermute(source, "adapter", split_pairs(places))
-    base, weight_other = base_and_weight(after(blocks, source), weight_other)
-    bases.append(base)
-    crossed = after(crossed, *bases)
-    rows = [block[last - 1], other[-1], block[last], crossed]
-    part, slot, rows = shrink_rows(rows, down, down_other, parts, tokens)
-    slots.append(slot)
-
-    across = move(part, 0, 2)
-    bases.append(base_rows(rows, query_weight))
-    part = pack(part, after(across, bases[-1]), own_rows)
+    meet(after([block[last - 1], other[-1]], source))
+    bases.append(base_rows(rows[-1], query_weight))
+    meet([block[last], after(crossed, bases[-1])], parts)
+
+    across = move(parts[-1], 0, 2)
+    bases.append(base_rows(rows[-1], query_weight))
+    part = pack(parts[-1], after(across, bases[-1]), own_rows)
     moved = [part] + [move(part, steps, 0) for steps in range(1, places)]
-    bases.append(base_rows(rows, weight_other))
+    bases.append(base_other(rows, weight_other))
     query = finish(moved, bases, slots, up, up_other, own_rows)
     groups = [list(range(core, devices, CORES)) for core in range(CORES)]
     query = lax.all_to_all(query, "adapter", 0, 0, axis_index_groups=groups, tiled=True)

time: 74.8 us -> 76.7 us (1.025)
  waiting for transfers between devices: 25.7 us -> 22.5 us
  matrix products: 7.86 us -> 9.98 us
  Pallas kernels: 8.43 us -> 10.4 us
    ppermute x13, waiting for transfers between devices: 22.3 us -> 16.8 us  [move(): return lax.ppermute(x, 'adapter', pairs(places, steps, flip))]
    ppermute x1, waiting for transfers between devices: 3.38 us -> 5.65 us  [shards(): crossed = lax.ppermute(source, 'adapter', split_pairs(places))]
    dot_general x3 -> x4, matrix products: 7.86 us -> 9.98 us  [base_rows(): return jnp.dot(rows, weight, preferred_element_type=jnp.float32)]
    pallas_call x4 -> x6, Pallas kernels: 2.58 us -> 4.46 us  [call(): pl.pallas_call(kernel, out_shape=out_shape, in_specs=[VMEM] * len(operand...]
    unnamed x14 -> x12, local copies, waits for them, and re-layouts: 2.25 us -> 2.25 us
  transfers between devices with their start and end apart: 14 -> 14, of which waited for: 6 -> 6; matrix products, arithmetic and copies ran while one was open for 11% -> 13% of each run, Pallas kernels for 10% -> 13%
where the time goes in v11:
time: 76.7 us; the launch traced here: 76.4 us
  waiting for transfers between devices  22.5 us (29%)
  starting transfers between devices  16.9 us (22%)
  blocking collectives  13.5 us (18%)
  Pallas kernels  10.4 us (14%)
  matrix products  9.98 us (13%)
  local copies, waits for them, and re-layouts  3.02 us (4%)
    ppermute x13, waiting for transfers between devices, move(): return lax.ppermute(x, 'adapter', pairs(places, steps, flip))  16.8 us
    ppermute x13, starting transfers between devices, move(): return lax.ppermute(x, 'adapter', pairs(places, steps, flip))  16.2 us
    all_to_all x1, blocking collectives, shards(): lax.all_to_all(query, 'adapter', 0, 0, axis_index_groups=groups, tiled=True)  13.5 us
    dot_general x4, matrix products, base_rows(): return jnp.dot(rows, weight, preferred_element_type=jnp.float32)  9.98 us
    ppermute x1, waiting for transfers between devices, shards(): crossed = lax.ppermute(source, 'adapter', split_pairs(places))  5.65 us
    pallas_call x6, Pallas kernels, call(): pl.pallas_call(kernel, out_shape=out_shape, in_specs=[VMEM] * len(operand...  4.46 us
    pallas_call x1, Pallas kernels, base_other(): pl.pallas_call(base_kernel, out_shape=jax.ShapeDtypeStruct((rows, weight....  3.85 us
    unnamed x12, local copies, waits for them, and re-layouts  2.25 us
  transfers between devices with their start and end apart: 14, of which 6 were waited for; matrix products, arithmetic and copies ran while one was open for 13% of the time, Pallas kernels for 13%

profile of v11, /device:TPU:0, one launch (start us, length us, event | category | flops | bytes accessed | tf_op | source)
XLA Modules:
  0.0 76.4 jit_solution(2769316097418457885)
XLA Ops:
  0.5 2.1 %shard_map.73.refs_0_ = bf16[24,8320]{1,0:T(8,128)(2,1)} custom-call(bf16[24,8192]{1,0:T(8,128)(2,1)} %refs_0_.1, f32[1,8192]{1,0:T(1,128)} %bitcast.28, s32[1,24]{1,0:T(1,128)} %bitcast.29, s32[1,16]{1,0:T(1,128)} %bitcast.30), custom_call_target="tpu_custom_call" | custom-call | tf_op jit(solution)/shard_map/pallas_call | solution.py:109
  2.6 3.1 %collective-permute-start = (bf16[24,8320]{1,0:T(8,128)(2,1)}, bf16[24,8320]{1,0:T(8,128)(2,1)S(1)}, u32[]{:S(2)}, u32[]{:S(2)}) collective-permute-start(bf16[24,8320]{1,0:T(8,128)(2,1)} %shard_map.73.refs_0_), channel_id=1, source_target_pairs={{0,4},{1,5},{2,6},{3,7},{4,12},{5,13},{6,14},{7,15},{12,8},{13,9},... | collective-permute-start | bytes 1198088 | tf_op jit(solution)/shard_map/ppermute | solution.py:286
  5.6 1.5 %collective-permute-start.2 = (bf16[24,8320]{1,0:T(8,128)(2,1)}, bf16[24,8320]{1,0:T(8,128)(2,1)S(1)}, u32[]{:S(2)}, u32[]{:S(2)}) collective-permute-start(bf16[24,8320]{1,0:T(8,128)(2,1)} %shard_map.73.refs_0_), channel_id=1, source_target_pairs={{0,2},{1,3},{2,0},{3,1},{4,6},{5,7},{6,4},{7,5},{12,14},{13,15},{1... | collective-permute-start | bytes 1198088 | tf_op jit(solution)/shard_map/ppermute | solution.py:286
  7.2 9.1 %collective-permute-done.block_ref.refs_0_ = bf16[24,8320]{1,0:T(8,128)(2,1)S(1)} collective-permute-done((bf16[24,8320]{1,0:T(8,128)(2,1)}, bf16[24,8320]{1,0:T(8,128)(2,1)S(1)}, u32[]{:S(2)}, u32[]{:S(2)}) %collective-permute-start) | collective-permute-done | bytes 399392 | tf_op jit(solution)/shard_map/ppermute | solution.py:286
  16.7 2.6 %collective-permute-start.1 = (bf16[24,8320]{1,0:T(8,128)(2,1)S(1)}, bf16[24,8320]{1,0:T(8,128)(2,1)S(1)}, u32[]{:S(2)}, u32[]{:S(2)}) collective-permute-start(bf16[24,8320]{1,0:T(8,128)(2,1)S(1)} %collective-permute-done.block_ref.refs_0_), channel_id=1, source_target_pairs={{0,4},{1,5},{2,6},{3,7},{4,12},{5,13},{6,14},{7,15},{12,8},{13,9},... | collective-permute-start | bytes 1198088 | tf_op jit(solution)/shard_map/ppermute | solution.py:286
  19.3 1.5 %collective-permute-start.5 = (bf16[24,8320]{1,0:T(8,128)(2,1)S(1)}, bf16[24,8320]{1,0:T(8,128)(2,1)S(1)}, u32[]{:S(2)}, u32[]{:S(2)}) collective-permute-start(bf16[24,8320]{1,0:T(8,128)(2,1)S(1)} %collective-permute-done.block_ref.refs_0_), channel_id=1, source_target_pairs={{0,2},{1,3},{2,0},{3,1},{4,6},{5,7},{6,4},{7,5},{12,14},{13,15},{1... | collective-permute-start | bytes 1198088 | tf_op jit(solution)/shard_map/ppermute | solution.py:286
  20.9 1.2 %copy-done = bf16[1,8192,64]{1,2,0:T(8,128)(2,1)S(1)} copy-done((bf16[1,8192,64]{1,2,0:T(8,128)(2,1)S(1)}, bf16[1,8192,64]{1,2,0:T(8,128)(2,1)}, u32[]{:S(2)}) %copy-start) | copy-done | bytes 1048600
  22.1 1.0 %copy-done.2 = bf16[24,8320]{1,0:T(8,128)(2,1)S(1)} copy-done((bf16[24,8320]{1,0:T(8,128)(2,1)S(1)}, bf16[24,8320]{1,0:T(8,128)(2,1)}, u32[]{:S(2)}) %copy-start.2) | copy-done | bytes 399384
  24.0 5.4 %fusion.refs_4_ = f32[48,512]{1,0:T(8,128)S(1)} fusion(bf16[48,8192]{1,0:T(8,128)(2,1)S(1)} %get-tuple-element.35.refs_0_, bf16[8192,512]{1,0:T(8,128)(2,1)} %param.9), kind=kOutput, calls=%fused_computation.1 | convolution fusion | flops 402653184 | bytes 9273344 | tf_op jit(solution)/shard_map/dot_general | solution.py:289
  29.5 1.2 %collective-permute-start.4 = (bf16[24,8320]{1,0:T(8,128)(2,1)S(1)}, bf16[24,8320]{1,0:T(8,128)(2,1)S(1)}, u32[]{:S(2)}, u32[]{:S(2)}) collective-permute-start(bf16[24,8320]{1,0:T(8,128)(2,1)S(1)} %collective-permute-done.1.block_ref.refs_0_), channel_id=1, source_target_pairs={{0,4},{1,5},{2,6},{3,7},{4,12},{5,13},{6,14},{7,15},{12,8},{13,9},... | collective-permute-start | bytes 1198088 | tf_op jit(solution)/shard_map/ppermute | solution.py:286
  30.7 1.4 %collective-permute-start.6 = (bf16[24,8320]{1,0:T(8,128)(2,1)S(1)}, bf16[24,8320]{1,0:T(8,128)(2,1)S(1)}, u32[]{:S(2)}, u32[]{:S(2)}) collective-permute-start(bf16[24,8320]{1,0:T(8,128)(2,1)S(1)} %collective-permute-done.1.block_ref.refs_0_), channel_id=1, source_target_pairs={{0,2},{1,3},{2,0},{3,1},{4,6},{5,7},{6,4},{7,5},{12,14},{13,15},{1... | collective-permute-start | bytes 1198088 | tf_op jit(solution)/shard_map/ppermute | solution.py:286
  33.0 1.5 %fusion.1.refs_5_ = f32[48,512]{1,0:T(8,128)S(1)} fusion(bf16[48,8192]{1,0:T(8,128)(2,1)S(1)} %get-tuple-element.41.refs_1_, bf16[8192,512]{1,0:T(8,128)(2,1)S(1)} %bitcast.26), kind=kOutput, calls=%fused_computation.2 | convolution fusion | flops 402653184 | bytes 9273344 | tf_op jit(solution)/shard_map/dot_general | solution.py:289
  34.5 5.3 %collective-permute-done.4.block_ref.refs_3_ = bf16[24,8320]{1,0:T(8,128)(2,1)S(1)} collective-permute-done((bf16[24,8320]{1,0:T(8,128)(2,1)S(1)}, bf16[24,8320]{1,0:T(8,128)(2,1)S(1)}, u32[]{:S(2)}, u32[]{:S(2)}) %collective-permute-start.4) | collective-permute-done | bytes 399392 | tf_op jit(solution)/shard_map/ppermute | solution.py:286
  40.9 0.9 %shard_map.79 = (bf16[48,64]{1,0:T(8,128)(2,1)S(1)}, s32[48,128]{1,0:T(8,128)S(1)}, bf16[48,8192]{1,0:T(8,128)(2,1)S(1)}) custom-call(bf16[24,8320]{1,0:T(8,128)(2,1)S(1)} %collective-permute-done.1.block_ref.refs_0_, bf16[24,8320]{1,0:T(8,128)(2,1)S(1)} %collective-permute-done.6.refs_1_, bf16[64,8192]{1,0:T(8,128)(2,1)S(1)} %bitcast.21, ...), custom_call_target="tpu_custom_call" | custom-call | flops 1 | bytes 1 | tf_op jit(solution)/shard_map/pallas_call | solution.py:57
  41.8 1.5 %fusion.2.refs_6_ = f32[48,512]{1,0:T(8,128)S(1)} fusion(bf16[48,8192]{1,0:T(8,128)(2,1)S(1)} %get-tuple-element.47.refs_2_, bf16[8192,512]{1,0:T(8,128)(2,1)S(1)} %bitcast.26), kind=kOutput, calls=%fused_computation.3 | convolution fusion | flops 402653184 | bytes 9273344 | tf_op jit(solution)/shard_map/dot_general | solution.py:289
  43.4 5.6 %collective-permute-done.7.refs_4_ = bf16[24,8320]{1,0:T(8,128)(2,1)S(1)} collective-permute-done((bf16[24,8320]{1,0:T(8,128)(2,1)S(1)}, bf16[24,8320]{1,0:T(8,128)(2,1)S(1)}, u32[]{:S(2)}, u32[]{:S(2)}) %collective-permute-start.7) | collective-permute-done | bytes 399392 | tf_op jit(solution)/shard_map/ppermute | solution.py:320
  49.0 0.9 %shard_map.80 = (bf16[192,64]{1,0:T(8,128)(2,1)S(1)}, s32[48,128]{1,0:T(8,128)S(1)}, bf16[48,8192]{1,0:T(8,128)(2,1)S(1)}) custom-call(f32[8,128]{1,0:T(8,128)S(1)} %shard_map.74.refs_0_, f32[8,128]{1,0:T(8,128)S(1)} %shard_map.76.refs_1_, f32[8,128]{1,0:T(8,128)S(1)} %shard_map.78.refs_2_, bf16[24,8320]{1,0:T(8,128)(2,1)S(1)} %collective-permute-done.4.block_ref.refs_3_, ...), custom_call_target="tpu_custom_call" | custom-call | flops 1 | bytes 1 | tf_op jit(solution)/shard_map/pallas_call | solution.py:57
  49.9 1.0 %collective-permute-start.8 = (bf16[192,64]{1,0:T(8,128)(2,1)S(1)}, bf16[192,64]{1,0:T(8,128)(2,1)S(1)}, u32[]{:S(2)}, u32[]{:S(2)}) collective-permute-start(bf16[192,64]{1,0:T(8,128)(2,1)S(1)} %get-tuple-element.52.refs_0_), channel_id=1, source_target_pairs={{0,2},{1,3},{2,0},{3,1},{4,6},{5,7},{6,4},{7,5},{12,14},{13,15},{1... | collective-permute-start | bytes 73736 | tf_op jit(solution)/shard_map/ppermute | solution.py:286
  51.0 1.5 %fusion.3.refs_7_ = f32[48,512]{1,0:T(8,128)S(1)} fusion(bf16[48,8192]{1,0:T(8,128)(2,1)S(1)} %get-tuple-element.53.refs_3_, bf16[8192,512]{1,0:T(8,128)(2,1)S(1)} %bitcast.26), kind=kOutput, calls=%fused_computation.4 | convolution fusion | flops 402653184 | bytes 9273344 | tf_op jit(solution)/shard_map/dot_general | solution.py:289
  52.5 1.6 %collective-permute-done.8.refs_1_ = bf16[192,64]{1,0:T(8,128)(2,1)S(1)} collective-permute-done((bf16[192,64]{1,0:T(8,128)(2,1)S(1)}, bf16[192,64]{1,0:T(8,128)(2,1)S(1)}, u32[]{:S(2)}, u32[]{:S(2)}) %collective-permute-start.8) | collective-permute-done | bytes 24608 | tf_op jit(solution)/shard_map/ppermute | solution.py:286
  54.2 1.3 %collective-permute-start.10 = (bf16[96,128]{1,0:T(8,128)(2,1)S(1)}, bf16[96,128]{1,0:T(8,128)(2,1)S(1)}, u32[]{:S(2)}, u32[]{:S(2)}) collective-permute-start(bf16[96,128]{1,0:T(8,128)(2,1)S(1)} %shard_map.81.refs_0_), channel_id=1, source_target_pairs={{0,12},{1,13},{2,14},{3,15},{4,8},{5,9},{6,10},{7,11},{12,0},{13,1... | collective-permute-start | bytes 73736 | tf_op jit(solution)/shard_map/ppermute | solution.py:286
  55.5 2.0 %collective-permute-start.9 = (bf16[96,128]{1,0:T(8,128)(2,1)S(1)}, bf16[96,128]{1,0:T(8,128)(2,1)S(1)}, u32[]{:S(2)}, u32[]{:S(2)}) collective-permute-start(bf16[96,128]{1,0:T(8,128)(2,1)S(1)} %shard_map.81.refs_0_), channel_id=1, source_target_pairs={{0,4},{1,5},{2,6},{3,7},{4,12},{5,13},{6,14},{7,15},{12,8},{13,9},... | collective-permute-start | bytes 73736 | tf_op jit(solution)/shard_map/ppermute | solution.py:286
  57.5 3.8 %shard_map.82.refs_8_ = f32[192,512]{1,0:T(8,128)S(1)} custom-call(bf16[48,8192]{1,0:T(8,128)(2,1)S(1)} %get-tuple-element.35.refs_0_, bf16[48,8192]{1,0:T(8,128)(2,1)S(1)} %get-tuple-element.41.refs_1_, bf16[48,8192]{1,0:T(8,128)(2,1)S(1)} %get-tuple-element.47.refs_2_, bf16[48,8192]{1,0:T(8,128)(2,1)S(1)} %get-tuple-element.53.refs_3_, ...), custom_call_target="tpu_custom_call" | custom-call | flops 1 | bytes 1 | tf_op jit(solution)/shard_map/pallas_call | solution.py:205
  62.2 13.5 %all_to_all.5 = bf16[8,24,1024]{2,1,0:T(8,128)(2,1)S(1)} all-to-all(bf16[8,24,1024]{2,1,0:T(8,128)(2,1)S(1)} %shard_map.83), channel_id=1, replica_groups={{0,2,4,6,8,10,12,14},{1,3,5,7,9,11,13,15},{16,18,20,22,24,26,28,30},{17..., dimensions={0} | all-to-all | bytes 786432 | tf_op jit(solution)/shard_map/all_to_all | solution.py:332
  (35 shorter events, 5.5 us)
Async XLA Ops:
  0.0 57.5 %collective-permute-start.12 = (bf16[8192,512]{1,0:T(8,128)(2,1)}, bf16[8192,512]{1,0:T(8,128)(2,1)}, u32[]{:S(2)}, u32[]{:S(2)}) collective-permute-start(bf16[8192,512]{1,0:T(8,128)(2,1)} %param.9), channel_id=1, source_target_pairs={{0,1},{1,0},{2,3},{3,2},{4,5},{5,4},{6,7},{7,6},{12,13},{13,12},{1... | collective-permute-start | bytes 25165832 | tf_op jit(solution)/shard_map/ppermute | solution.py:286
  0.5 20.4 %collective-permute-start.3 = (bf16[64,8192]{1,0:T(8,128)(2,1)}, bf16[64,8192]{1,0:T(8,128)(2,1)S(1)}, u32[]{:S(2)}, u32[]{:S(2)}) collective-permute-start(bf16[64,8192]{1,0:T(8,128)(2,1)} %bitcast.18), channel_id=1, source_target_pairs={{0,1},{1,0},{2,3},{3,2},{4,5},{5,4},{6,7},{7,6},{12,13},{13,12},{1... | collective-permute-start | bytes 3145736 | tf_op jit(solution)/shard_map/ppermute | solution.py:286
  2.6 13.7 %collective-permute-start = (bf16[24,8320]{1,0:T(8,128)(2,1)}, bf16[24,8320]{1,0:T(8,128)(2,1)S(1)}, u32[]{:S(2)}, u32[]{:S(2)}) collective-permute-start(bf16[24,8320]{1,0:T(8,128)(2,1)} %shard_map.73.refs_0_), channel_id=1, source_target_pairs={{0,4},{1,5},{2,6},{3,7},{4,12},{5,13},{6,14},{7,15},{12,8},{13,9},... | collective-permute-start | bytes 1198088 | tf_op jit(solution)/shard_map/ppermute | solution.py:286
  5.6 11.1 %collective-permute-start.2 = (bf16[24,8320]{1,0:T(8,128)(2,1)}, bf16[24,8320]{1,0:T(8,128)(2,1)S(1)}, u32[]{:S(2)}, u32[]{:S(2)}) collective-permute-start(bf16[24,8320]{1,0:T(8,128)(2,1)} %shard_map.73.refs_0_), channel_id=1, source_target_pairs={{0,2},{1,3},{2,0},{3,1},{4,6},{5,7},{6,4},{7,5},{12,14},{13,15},{1... | collective-permute-start | bytes 1198088 | tf_op jit(solution)/shard_map/ppermute | solution.py:286
  7.2 54.2 %collective-permute-start.13 = (bf16[1024,512]{1,0:T(8,128)(2,1)}, bf16[1024,512]{1,0:T(8,128)(2,1)S(1)}, u32[]{:S(2)}, u32[]{:S(2)}) collective-permute-start(bf16[1024,512]{1,0:T(8,128)(2,1)} %bitcast.23), channel_id=1, source_target_pairs={{0,1},{1,0},{2,3},{3,2},{4,5},{5,4},{6,7},{7,6},{12,13},{13,12},{1... | collective-permute-start | bytes 3145736 | tf_op jit(solution)/shard_map/ppermute | solution.py:286
  16.7 12.7 %collective-permute-start.1 = (bf16[24,8320]{1,0:T(8,128)(2,1)S(1)}, bf16[24,8320]{1,0:T(8,128)(2,1)S(1)}, u32[]{:S(2)}, u32[]{:S(2)}) collective-permute-start(bf16[24,8320]{1,0:T(8,128)(2,1)S(1)} %collective-permute-done.block_ref.refs_0_), channel_id=1, source_target_pairs={{0,4},{1,5},{2,6},{3,7},{4,12},{5,13},{6,14},{7,15},{12,8},{13,9},... | collective-permute-start | bytes 1198088 | tf_op jit(solution)/shard_map/ppermute | solution.py:286
  19.3 10.1 %collective-permute-start.5 = (bf16[24,8320]{1,0:T(8,128)(2,1)S(1)}, bf16[24,8320]{1,0:T(8,128)(2,1)S(1)}, u32[]{:S(2)}, u32[]{:S(2)}) collective-permute-start(bf16[24,8320]{1,0:T(8,128)(2,1)S(1)} %collective-permute-done.block_ref.refs_0_), channel_id=1, source_target_pairs={{0,2},{1,3},{2,0},{3,1},{4,6},{5,7},{6,4},{7,5},{12,14},{13,15},{1... | collective-permute-start | bytes 1198088 | tf_op jit(solution)/shard_map/ppermute | solution.py:286
  20.8 1.2 %copy-start = (bf16[1,8192,64]{1,2,0:T(8,128)(2,1)S(1)}, bf16[1,8192,64]{1,2,0:T(8,128)(2,1)}, u32[]{:S(2)}) copy-start(bf16[1,8192,64]{1,2,0:T(8,128)(2,1)} %param.10) | copy-start | bytes 3145732
  22.1 1.0 %copy-start.2 = (bf16[24,8320]{1,0:T(8,128)(2,1)S(1)}, bf16[24,8320]{1,0:T(8,128)(2,1)}, u32[]{:S(2)}) copy-start(bf16[24,8320]{1,0:T(8,128)(2,1)} %shard_map.73.refs_0_) | copy-start | bytes 1198084
  23.1 9.9 %slice-start = ((s8[8388608]{0:T(1024)(128)(4,1)}), s8[4194304]{0:T(1024)(128)(4,1)S(1)}, s32[]{:S(2)}) async-start(s8[8388608]{0:T(1024)(128)(4,1)} %bitcast.25), calls=%async_computation.1 | async-start | bytes 8388608
  24.0 8.1 %copy-start.1 = (bf16[1,8192,64]{1,2,0:T(8,128)(2,1)S(1)}, bf16[1,8192,64]{1,2,0:T(8,128)(2,1)}, u32[]{:S(2)}) copy-start(bf16[1,8192,64]{1,2,0:T(8,128)(2,1)} %param.10) | copy-start | bytes 3145732
  24.0 9.0 %slice-start.1 = ((s8[8388608]{0:T(1024)(128)(4,1)}), s8[4194304]{0:T(1024)(128)(4,1)S(1)}, s32[]{:S(2)}) async-start(s8[8388608]{0:T(1024)(128)(4,1)} %bitcast.25), calls=%async_computation.2 | async-start | bytes 8388608
  29.5 10.4 %collective-permute-start.4 = (bf16[24,8320]{1,0:T(8,128)(2,1)S(1)}, bf16[24,8320]{1,0:T(8,128)(2,1)S(1)}, u32[]{:S(2)}, u32[]{:S(2)}) collective-permute-start(bf16[24,8320]{1,0:T(8,128)(2,1)S(1)} %collective-permute-done.1.block_ref.refs_0_), channel_id=1, source_target_pairs={{0,4},{1,5},{2,6},{3,7},{4,12},{5,13},{6,14},{7,15},{12,8},{13,9},... | collective-permute-start | bytes 1198088 | tf_op jit(solution)/shard_map/ppermute | solution.py:286
  30.7 9.5 %collective-permute-start.6 = (bf16[24,8320]{1,0:T(8,128)(2,1)S(1)}, bf16[24,8320]{1,0:T(8,128)(2,1)S(1)}, u32[]{:S(2)}, u32[]{:S(2)}) collective-permute-start(bf16[24,8320]{1,0:T(8,128)(2,1)S(1)} %collective-permute-done.1.block_ref.refs_0_), channel_id=1, source_target_pairs={{0,2},{1,3},{2,0},{3,1},{4,6},{5,7},{6,4},{7,5},{12,14},{13,15},{1... | collective-permute-start | bytes 1198088 | tf_op jit(solution)/shard_map/ppermute | solution.py:286
  40.2 8.8 %collective-permute-start.7 = (bf16[24,8320]{1,0:T(8,128)(2,1)S(1)}, bf16[24,8320]{1,0:T(8,128)(2,1)S(1)}, u32[]{:S(2)}, u32[]{:S(2)}) collective-permute-start(bf16[24,8320]{1,0:T(8,128)(2,1)S(1)} %broadcast_select_fusion), channel_id=1, source_target_pairs={{1,3},{3,1},{5,7},{7,5},{13,15},{15,13},{9,11},{11,9},{0,4},{2,6},... | collective-permute-start | bytes 1198088 | tf_op jit(solution)/shard_map/ppermute | solution.py:320
  49.9 4.2 %collective-permute-start.8 = (bf16[192,64]{1,0:T(8,128)(2,1)S(1)}, bf16[192,64]{1,0:T(8,128)(2,1)S(1)}, u32[]{:S(2)}, u32[]{:S(2)}) collective-permute-start(bf16[192,64]{1,0:T(8,128)(2,1)S(1)} %get-tuple-element.52.refs_0_), channel_id=1, source_target_pairs={{0,2},{1,3},{2,0},{3,1},{4,6},{5,7},{6,4},{7,5},{12,14},{13,15},{1... | collective-permute-start | bytes 73736 | tf_op jit(solution)/shard_map/ppermute | solution.py:286
  52.5 8.9 %copy-start.3 = (bf16[16,64,512]{2,1,0:T(8,128)(2,1)S(1)}, bf16[16,64,512]{2,1,0:T(8,128)(2,1)}, u32[]{:S(2)}) copy-start(bf16[16,64,512]{2,1,0:T(8,128)(2,1)} %param.11) | copy-start | bytes 3145732
  54.2 7.2 %collective-permute-start.10 = (bf16[96,128]{1,0:T(8,128)(2,1)S(1)}, bf16[96,128]{1,0:T(8,128)(2,1)S(1)}, u32[]{:S(2)}, u32[]{:S(2)}) collective-permute-start(bf16[96,128]{1,0:T(8,128)(2,1)S(1)} %shard_map.81.refs_0_), channel_id=1, source_target_pairs={{0,12},{1,13},{2,14},{3,15},{4,8},{5,9},{6,10},{7,11},{12,0},{13,1... | collective-permute-start | bytes 73736 | tf_op jit(solution)/shard_map/ppermute | solution.py:286
  55.5 5.9 %collective-permute-start.11 = (bf16[96,128]{1,0:T(8,128)(2,1)S(1)}, bf16[96,128]{1,0:T(8,128)(2,1)S(1)}, u32[]{:S(2)}, u32[]{:S(2)}) collective-permute-start(bf16[96,128]{1,0:T(8,128)(2,1)S(1)} %shard_map.81.refs_0_), channel_id=1, source_target_pairs={{0,8},{1,9},{2,10},{3,11},{4,0},{5,1},{6,2},{7,3},{12,4},{13,5},{1... | collective-permute-start | bytes 73736 | tf_op jit(solution)/shard_map/ppermute | solution.py:286
  55.5 5.9 %collective-permute-start.9 = (bf16[96,128]{1,0:T(8,128)(2,1)S(1)}, bf16[96,128]{1,0:T(8,128)(2,1)S(1)}, u32[]{:S(2)}, u32[]{:S(2)}) collective-permute-start(bf16[96,128]{1,0:T(8,128)(2,1)S(1)} %shard_map.81.refs_0_), channel_id=1, source_target_pairs={{0,4},{1,5},{2,6},{3,7},{4,12},{5,13},{6,14},{7,15},{12,8},{13,9},... | collective-permute-start | bytes 73736 | tf_op jit(solution)/shard_map/ppermute | solution.py:286

commit v12 on v11

--- a/solution.py
+++ b/solution.py
@@ -31,13 +31,6 @@
         for corner in range(CORNERS):
             out.append((place * CORNERS + corner, target * CORNERS + (corner ^ flip)))
     return out
-
-
-def split_pairs(places):
-    flips, steps = pairs(places, 0, 2), pairs(places, 1, 0)
-    return [pair for pair in flips if pair[0] % CORES] + [
-        pair for pair in steps if pair[0] % CORES == 0
-    ]
 
 
 def ring_chip(places, steps, side):
@@ -116,80 +109,105 @@
     )(*sources)
 
 
-def stacked(blocks, lanes):
-    wide = [block[:, lanes].astype(jnp.float32) for block in blocks]
-    return jnp.concatenate(wide, axis=0).astype(jnp.bfloat16)
-
-
-def shrink_kernel(count, *refs):
-    blocks, (own_ref, other_ref, *before, part_ref, slot_ref, rows_ref) = refs[:count], refs[count:]
+def columns_of(pieces, start):
+    for piece in pieces:
+        if start < piece.shape[1]:
+            return piece[:, start : start + CHUNK].astype(jnp.float32)
+        start -= piece.shape[1]
+
+
+def shrink_kernel(counts, halves, *refs):
+    blocks, refs = [], list(refs)
+    for count in counts:
+        blocks.append(refs[:count])
+        refs = refs[count:]
+    own_ref, other_ref, *before, part_ref, slot_ref, rows_ref = refs
     rank, width = own_ref.shape
     rows = slot_ref.shape[0]
     part = jnp.zeros((rows, 2 * rank), jnp.float32)
     for start in range(0, width, CHUNK):
         lanes = slice(start, start + CHUNK)
+        wide = [columns_of(block, start) for block in blocks]
+        chunk = jnp.concatenate(wide, axis=0).astype(jnp.bfloat16)
+        rows_ref[:, lanes] = chunk
         down = jnp.concatenate([own_ref[:, lanes], other_ref[:, lanes]], axis=0)
-        chunk = stacked(blocks, lanes)
-        rows_ref[:, lanes] = chunk
         part += lax.dot_general(
             chunk, down, (((1,), (1,)), ((), ())), preferred_element_type=jnp.float32
         )
-    slot = jnp.concatenate(
-        [block[:, width : width + 1].astype(jnp.float32) for block in blocks], axis=0
-    ).astype(jnp.int32)
+    slot = [block[-1][:, block[-1].shape[1] - LANES :].astype(jnp.float32) for block in blocks]
+    slot = jnp.concatenate(slot, axis=0)[:, 0:1].astype(jnp.int32)
     slot_ref[...] = jnp.broadcast_to(slot, slot_ref.shape)
     me = lax.axis_index("adapter")
     lanes = lax.broadcasted_iota(jnp.int32, part.shape, 1)
     part = jnp.where(slot == jnp.where(lanes < rank, me, me ^ 1), part, 0.0)
     part = part[:, :rank] + part[:, rank:]
-    first = 0
-    for ref in before:
-        part_ref[first : first + ref.shape[0], :] = ref[...]
-        first += ref.shape[0]
-    part_ref[first:, :] = part.astype(jnp.bfloat16)
+    if halves:
+        steps = [ref[...].astype(jnp.float32) for ref in before] + [part]
+        middle = len(steps) // 2
+        halves = [jnp.concatenate(steps[:middle], axis=0), jnp.concatenate(steps[middle:], axis=0)]
+        part = jnp.concatenate(halves, axis=1)
+    part_ref[...] = part.astype(jnp.bfloat16)
 
 
 def shrink_rows(blocks, own, other, before=(), tokens=()):
-    rows = blocks[0].shape[0] * len(blocks)
-    total = rows + sum(part.shape[0] for part in before)
+    rows = blocks[0][0].shape[0] * len(blocks)
+    rank, width = own.shape
+    packed = (rows * (len(before) + 1) // 2, 2 * rank) if before else (rows, rank)
     out_shape = (
-        jax.ShapeDtypeStruct((total, own.shape[0]), jnp.bfloat16),
+        jax.ShapeDtypeStruct(packed, jnp.bfloat16),
         jax.ShapeDtypeStruct((rows, LANES), jnp.int32),
-        jax.ShapeDtypeStruct((rows, own.shape[1]), jnp.bfloat16),
-    )
+        jax.ShapeDtypeStruct((rows, width), jnp.bfloat16),
+    )
+    counts = [len(block) for block in blocks]
+    pieces = [piece for block in blocks for piece in block]
     return call(
-        lambda *refs: shrink_kernel(len(blocks), *refs[len(tokens) :]),
+        lambda *refs: shrink_kernel(counts, bool(before), *refs[len(tokens) :]),
         out_shape,
-        (*tokens, *blocks, own, other, *before),
-    )
-
-
-def pack_kernel(own_rows, part_ref, across_ref, out_ref):
-    rows, rank = part_ref.shape
-    part = part_ref[...].astype(jnp.float32)
-    across = across_ref[...].astype(jnp.float32)
-    swapped = []
-    for first in range(0, rows, SIDE * own_rows):
-        middle, last = first + own_rows, first + SIDE * own_rows
-        swapped += [across[middle:last], across[first:middle]]
-    total = part + jnp.concatenate(swapped, axis=0)
-    out_ref[...] = jnp.concatenate([total[: rows // 2], total[rows // 2 :]], axis=1).astype(jnp.bfloat16)
-
-
-def pack(part, across, own_rows):
-    rows, rank = part.shape
-    out_shape = jax.ShapeDtypeStruct((rows // 2, 2 * rank), part.dtype)
-    return call(lambda *refs: pack_kernel(own_rows, *refs), out_shape, (part, across))
+        (*tokens, *pieces, own, other, *before),
+    )
+
+
+def sum_kernel(places, *refs):
+    *moved, out_ref = refs
+    half, rank = moved[0].shape[0], moved[0].shape[1] // 2
+    rows = half // (places // 2)
+    for step in range(places):
+        shrink = jnp.zeros((rows, rank), jnp.float32)
+        for back in range(places):
+            shrink += packed_step(moved[back], (step - back) % places, places)
+        side, first = divmod(step, places // 2)
+        out_ref[first * rows : (first + 1) * rows, side * rank : (side + 1) * rank] = shrink.astype(
+            jnp.bfloat16
+        )
+
+
+def packed_step(ref, step, places):
+    rank = ref.shape[1] // 2
+    rows = ref.shape[0] // (places // 2)
+    side, first = divmod(step, places // 2)
+    return ref[first * rows : (first + 1) * rows, side * rank : (side + 1) * rank].astype(jnp.float32)
+
+
+def cut_kernel(first, block_ref, out_ref):
+    out_ref[...] = block_ref[:, first : first + out_ref.shape[1]]
+
+
+def cut(block, first, last):
+    return call(
+        lambda *refs: cut_kernel(first, *refs),
+        jax.ShapeDtypeStruct((block.shape[0], last - first), block.dtype),
+        (block,),
+    )
 
 
 def base_kernel(*refs):
-    *blocks, weight_ref, out_ref, buffer, sems = refs
+    *blocks, weight_ref, out_ref, kept_ref, sems = refs
     width = weight_ref.shape[0]
     copies = []
     for number, start in enumerate(range(0, width, CHUNK)):
         here = pl.ds(start, CHUNK)
         copies.append(
-            pltpu.make_async_copy(weight_ref.at[here], buffer.at[here], sems.at[number])
+            pltpu.make_async_copy(weight_ref.at[here], kept_ref.at[here], sems.at[number])
         )
         copies[-1].start()
     out_ref[...] = jnp.zeros(out_ref.shape, jnp.float32)
@@ -197,20 +215,20 @@
         lanes = slice(start, start + CHUNK)
         rows = jnp.concatenate([block[:, lanes] for block in blocks], axis=0)
         copies[number].wait()
-        out_ref[...] += jnp.dot(rows, buffer[lanes, :], preferred_element_type=jnp.float32)
-
-
-def base_other(blocks, weight):
+        out_ref[...] += jnp.dot(rows, kept_ref[lanes, :], preferred_element_type=jnp.float32)
+
+
+def base_and_weight(blocks, weight):
     rows = blocks[0].shape[0] * len(blocks)
     return pl.pallas_call(
         base_kernel,
-        out_shape=jax.ShapeDtypeStruct((rows, weight.shape[1]), jnp.float32),
+        out_shape=(
+            jax.ShapeDtypeStruct((rows, weight.shape[1]), jnp.float32),
+            jax.ShapeDtypeStruct(weight.shape, weight.dtype),
+        ),
         in_specs=[VMEM] * len(blocks) + [pl.BlockSpec(memory_space=pltpu.HBM)],
-        out_specs=VMEM,
-        scratch_shapes=[
-            pltpu.VMEM(weight.shape, weight.dtype),
-            pltpu.SemaphoreType.DMA((weight.shape[0] // CHUNK,)),
-        ],
+        out_specs=(VMEM, VMEM),
+        scratch_shapes=[pltpu.SemaphoreType.DMA((weight.shape[0] // CHUNK,))],
         compiler_params=pltpu.CompilerParams(vmem_limit_bytes=VMEM_LIMIT),
         cost_estimate=pl.CostEstimate(flops=1, bytes_accessed=1, transcendentals=0),
     )(*blocks, weight)
@@ -231,44 +249,47 @@
     )(block)
 
 
-def finish_kernel(places, rank, *refs):
-    moved, refs = refs[:places], refs[places:]
-    bases, slots = refs[: places + 1], refs[places + 1 : 2 * places + 1]
-    own_ref, other_ref, out_ref = refs[2 * places + 1 :]
+def finish_kernel(places, *refs):
+    shrink_ref, across_ref, *refs = refs
+    bases, slots = refs[: places + 2], refs[places + 2 : 2 * places + 2]
+    own_ref, other_ref, out_ref = refs[2 * places + 2 :]
     depth, columns = own_ref.shape
-    rows = SIDE * out_ref.shape[1]
+    own_rows = out_ref.shape[1]
+    rows = SIDE * own_rows
     core = lax.axis_index("adapter") % CORES
     shrinks = []
     for step in range(places):
-        shrink = jnp.zeros((rows, rank), jnp.float32)
-        for back in range(places):
-            half, first = divmod((step - back) % places, places // 2)
-            part = moved[back][first * rows : (first + 1) * rows, half * rank : (half + 1) * rank]
-            shrink += part.astype(jnp.float32)
-        shrinks.append(shrink)
+        across = packed_step(across_ref, step, places)
+        swapped = jnp.concatenate([across[own_rows:], across[:own_rows]], axis=0)
+        shrinks.append(packed_step(shrink_ref, step, places) + swapped)
     shrink = jnp.concatenate(shrinks, axis=0)
     slot = jnp.concatenate([ref[:, 0:1] for ref in slots], axis=0)
-    wide = jnp.concatenate([shrink] * (depth // rank), axis=1)
+    wide = jnp.concatenate([shrink] * (depth // shrink.shape[1]), axis=1)
     lanes = lax.broadcasted_iota(jnp.int32, wide.shape, 1)
-    spread = jnp.where(lanes // rank == slot, wide, 0.0).astype(jnp.bfloat16)
+    spread = jnp.where(lanes // shrink.shape[1] == slot, wide, 0.0).astype(jnp.bfloat16)
     for which, up_ref in enumerate((own_ref, other_ref)):
         update = jnp.dot(spread, up_ref[...], preferred_element_type=jnp.float32)
         at = pl.multiple_of((core ^ which) * columns, columns)
         for step in range(places):
             here = slice(step * rows, (step + 1) * rows)
-            base = bases[places][here, :] if which else bases[step][...]
+            if which == 0:
+                base = bases[step][...]
+            elif step == places - 1:
+                base = bases[places + 1][...]
+            else:
+                base = bases[places][here, :]
             query = (base + ADAPTER_SCALE * update[here]).astype(jnp.bfloat16)
             for side in range(SIDE):
                 chip = ring_chip(places, -step, side)
-                out_ref[chip, :, pl.ds(at, columns)] = query[side * rows // SIDE : (side + 1) * rows // SIDE]
-
-
-def finish(moved, bases, slots, own, other, own_rows):
-    places, rank = len(moved), moved[0].shape[1] // 2
+                out_ref[chip, :, pl.ds(at, columns)] = query[side * own_rows : (side + 1) * own_rows]
+
+
+def finish(shrink, across, bases, slots, own, other, own_rows):
+    places = len(slots)
     return call(
-        lambda *refs: finish_kernel(places, rank, *refs),
+        lambda *refs: finish_kernel(places, *refs),
         jax.ShapeDtypeStruct((places * SIDE, own_rows, CORES * own.shape[1]), jnp.bfloat16),
-        (*moved, *bases, *slots, own, other),
+        (shrink, across, *bases, *slots, own, other),
     )
 
 
@@ -276,9 +297,9 @@
     hidden, norm_weight, query_weight, down_weights, up_weights, adapter_index, adapter_slot
 ):
     devices = lax.axis_size("adapter")
-    me = lax.axis_index("adapter")
     places = devices // CORNERS
     own_rows, width = hidden.shape
+    half = width // 2
     columns = query_weight.shape[1]
     rank = down_weights.shape[2]
 
@@ -311,23 +332,28 @@
         block.append(move(after(block[step], *tokens[-1:]), 1, 0))
         other.append(move(after(block[step], *other[-1:]), 0, 2))
         if step:
-            meet(after([block[step - 1], other[step - 1]], block[step]))
+            meet(after([[block[step - 1]], [other[step - 1]]], block[step]))
             bases.append(base_rows(rows[-1], query_weight))
     block[last] = after(block[last], bases[-1])
     tokens.append(token(block[last]))
-    source = after(block[last], other[-1], tokens[-1])
-    source = jnp.where((me & 1) == 1, source, other[-1])
-    crossed = lax.ppermute(source, "adapter", split_pairs(places))
-    meet(after([block[last - 1], other[-1]], source))
+    low = move(cut(after(other[-1], tokens[-1]), 0, half), 1, 0)
+    high = move(cut(after(block[last], tokens[-1]), half, block[last].shape[1]), 0, 2)
+    meet(after([[block[last - 1]], [other[-1]]], block[last]))
+    base, weight_other = base_and_weight(after(rows, block[last]), weight_other)
+    low, high = after(low, base), after(high, base)
+    meet([[block[last]], [low, high]], parts)
+
+    part = parts[-1]
+    moved = [part] + [move(part, steps, 0) for steps in range(1, places)]
     bases.append(base_rows(rows[-1], query_weight))
-    meet([block[last], after(crossed, bases[-1])], parts)
-
-    across = move(parts[-1], 0, 2)
-    bases.append(base_rows(rows[-1], query_weight))
-    part = pack(parts[-1], after(across, bases[-1]), own_rows)
-    moved = [part] + [move(part, steps, 0) for steps in range(1, places)]
-    bases.append(base_other(rows, weight_other))
-    query = finish(moved, bases, slots, up, up_other, own_rows)
+    moved = after(moved, bases[-1])
+    shrink = call(
+        lambda *refs: sum_kernel(places, *refs), jax.ShapeDtypeStruct(part.shape, part.dtype), moved
+    )
+    across = move(shrink, 0, 2)
+    bases.insert(last - 1, base_rows(after(rows[last - 1], shrink), query_weight))
+    bases += [base, base_rows(after(rows[-1], shrink), weight_other)]
+    query = finish(shrink, across, bases, slots, up, up_other, own_rows)
     groups = [list(range(core, devices, CORES)) for core in range(CORES)]
     query = lax.all_to_all(query, "adapter", 0, 0, axis_index_groups=groups, tiled=True)
     return query.transpose(1, 0, 2).reshape(own_rows, devices * columns)

time: 76.7 us -> 75.9 us (0.990)
  waiting for transfers between devices: 22.5 us -> 19.8 us
  matrix products: 9.98 us -> 11.5 us
  blocking collectives: 13.5 us -> 14.6 us
    ppermute x1 -> x0, waiting for transfers between devices: 5.65 us -> none  [shards(): crossed = lax.ppermute(source, 'adapter', split_pairs(places))]
    ppermute x13 -> x15, waiting for transfers between devices: 16.8 us -> 19.8 us  [move(): return lax.ppermute(x, 'adapter', pairs(places, steps, flip))]
    dot_general x4 -> x5, matrix products: 9.98 us -> 11.5 us  [base_rows(): return jnp.dot(rows, weight, preferred_element_type=jnp.float32)]
    all_to_all x1, blocking collectives: 13.5 us -> 14.6 us  [shards(): lax.all_to_all(query, 'adapter', 0, 0, axis_index_groups=groups, tiled=True)]
    pallas_call x6 -> x8, Pallas kernels: 4.46 us -> 4.51 us  [call(): pl.pallas_call(kernel, out_shape=out_shape, in_specs=[VMEM] * len(operand...]
    ppermute x13 -> x15, starting transfers between devices: 16.2 us -> 16.2 us  [move(): return lax.ppermute(x, 'adapter', pairs(places, steps, flip))]
  transfers between devices with their start and end apart: 14 -> 15, of which waited for: 6 -> 8; matrix products, arithmetic and copies ran while one was open for 13% -> 15% of each run, Pallas kernels for 13% -> 13%
where the time goes in v12:
time: 75.9 us; the launch traced here: 75.7 us
  waiting for transfers between devices  19.8 us (26%)
  starting transfers between devices  16.2 us (21%)
  blocking collectives  14.6 us (19%)
  matrix products  11.5 us (15%)
  Pallas kernels  10.4 us (14%)
  local copies, waits for them, and re-layouts  3.02 us (4%)
    ppermute x15, waiting for transfers between devices, move(): return lax.ppermute(x, 'adapter', pairs(places, steps, flip))  19.8 us
    ppermute x15, starting transfers between devices, move(): return lax.ppermute(x, 'adapter', pairs(places, steps, flip))  16.2 us
    all_to_all x1, blocking collectives, shards(): lax.all_to_all(query, 'adapter', 0, 0, axis_index_groups=groups, tiled=True)  14.6 us
    dot_general x5, matrix products, base_rows(): return jnp.dot(rows, weight, preferred_element_type=jnp.float32)  11.5 us
    pallas_call x8, Pallas kernels, call(): pl.pallas_call(kernel, out_shape=out_shape, in_specs=[VMEM] * len(operand...  4.51 us
    pallas_call x1, Pallas kernels, base_and_weight(): pl.pallas_call(base_kernel, out_shape=(jax.ShapeDtypeStruct((rows, weight...  3.8 us
    unnamed x12, local copies, waits for them, and re-layouts  2.24 us
    pallas_call x1, Pallas kernels, normalize(): pl.pallas_call(norm_kernel, out_shape=jax.ShapeDtypeStruct((rows, width +...  2.06 us
  transfers between devices with their start and end apart: 15, of which 8 were waited for; matrix products, arithmetic and copies ran while one was open for 15% of the time, Pallas kernels for 13%

profile of v12, /device:TPU:0, one launch (start us, length us, event | category | flops | bytes accessed | tf_op | source)
XLA Modules:
  0.0 75.7 jit_solution(1703136155314738144)
XLA Ops:
  0.5 2.1 %shard_map.73.refs_0_ = bf16[24,8320]{1,0:T(8,128)(2,1)} custom-call(bf16[24,8192]{1,0:T(8,128)(2,1)} %refs_0_.1, f32[1,8192]{1,0:T(1,128)} %bitcast.30, s32[1,24]{1,0:T(1,128)} %bitcast.31, s32[1,16]{1,0:T(1,128)} %bitcast.32), custom_call_target="tpu_custom_call" | custom-call | tf_op jit(solution)/shard_map/pallas_call | solution.py:102
  2.6 3.1 %collective-permute-start = (bf16[24,8320]{1,0:T(8,128)(2,1)}, bf16[24,8320]{1,0:T(8,128)(2,1)S(1)}, u32[]{:S(2)}, u32[]{:S(2)}) collective-permute-start(bf16[24,8320]{1,0:T(8,128)(2,1)} %shard_map.73.refs_0_), channel_id=1, source_target_pairs={{0,4},{1,5},{2,6},{3,7},{4,12},{5,13},{6,14},{7,15},{12,8},{13,9},... | collective-permute-start | bytes 1198088 | tf_op jit(solution)/shard_map/ppermute | solution.py:307
  5.7 1.5 %collective-permute-start.2 = (bf16[24,8320]{1,0:T(8,128)(2,1)}, bf16[24,8320]{1,0:T(8,128)(2,1)S(1)}, u32[]{:S(2)}, u32[]{:S(2)}) collective-permute-start(bf16[24,8320]{1,0:T(8,128)(2,1)} %shard_map.73.refs_0_), channel_id=1, source_target_pairs={{0,2},{1,3},{2,0},{3,1},{4,6},{5,7},{6,4},{7,5},{12,14},{13,15},{1... | collective-permute-start | bytes 1198088 | tf_op jit(solution)/shard_map/ppermute | solution.py:307
  7.2 9.1 %collective-permute-done.block_ref.refs_0_ = bf16[24,8320]{1,0:T(8,128)(2,1)S(1)} collective-permute-done((bf16[24,8320]{1,0:T(8,128)(2,1)}, bf16[24,8320]{1,0:T(8,128)(2,1)S(1)}, u32[]{:S(2)}, u32[]{:S(2)}) %collective-permute-start) | collective-permute-done | bytes 399392 | tf_op jit(solution)/shard_map/ppermute | solution.py:307
  16.3 0.9 %collective-permute-start.1 = (bf16[24,8320]{1,0:T(8,128)(2,1)S(1)}, bf16[24,8320]{1,0:T(8,128)(2,1)S(1)}, u32[]{:S(2)}, u32[]{:S(2)}) collective-permute-start(bf16[24,8320]{1,0:T(8,128)(2,1)S(1)} %collective-permute-done.block_ref.refs_0_), channel_id=1, source_target_pairs={{0,4},{1,5},{2,6},{3,7},{4,12},{5,13},{6,14},{7,15},{12,8},{13,9},... | collective-permute-start | bytes 1198088 | tf_op jit(solution)/shard_map/ppermute | solution.py:307
  17.2 1.5 %collective-permute-start.5 = (bf16[24,8320]{1,0:T(8,128)(2,1)S(1)}, bf16[24,8320]{1,0:T(8,128)(2,1)S(1)}, u32[]{:S(2)}, u32[]{:S(2)}) collective-permute-start(bf16[24,8320]{1,0:T(8,128)(2,1)S(1)} %collective-permute-done.block_ref.refs_0_), channel_id=1, source_target_pairs={{0,2},{1,3},{2,0},{3,1},{4,6},{5,7},{6,4},{7,5},{12,14},{13,15},{1... | collective-permute-start | bytes 1198088 | tf_op jit(solution)/shard_map/ppermute | solution.py:307
  18.8 1.2 %copy-done = bf16[1,8192,64]{1,2,0:T(8,128)(2,1)S(1)} copy-done((bf16[1,8192,64]{1,2,0:T(8,128)(2,1)S(1)}, bf16[1,8192,64]{1,2,0:T(8,128)(2,1)}, u32[]{:S(2)}) %copy-start) | copy-done | bytes 1048600
  20.0 1.0 %copy-done.2 = bf16[24,8320]{1,0:T(8,128)(2,1)S(1)} copy-done((bf16[24,8320]{1,0:T(8,128)(2,1)S(1)}, bf16[24,8320]{1,0:T(8,128)(2,1)}, u32[]{:S(2)}) %copy-start.2) | copy-done | bytes 399384
  21.9 5.4 %fusion.refs_2_ = f32[48,512]{1,0:T(8,128)S(1)} fusion(bf16[48,8192]{1,0:T(8,128)(2,1)S(1)} %get-tuple-element.60.refs_0_, bf16[8192,512]{1,0:T(8,128)(2,1)} %param.9), kind=kOutput, calls=%fused_computation | convolution fusion | flops 402653184 | bytes 9273344 | tf_op jit(solution)/shard_map/dot_general | solution.py:310
  27.8 2.9 %collective-permute-start.4 = (bf16[24,8320]{1,0:T(8,128)(2,1)S(1)}, bf16[24,8320]{1,0:T(8,128)(2,1)S(1)}, u32[]{:S(2)}, u32[]{:S(2)}) collective-permute-start(bf16[24,8320]{1,0:T(8,128)(2,1)S(1)} %collective-permute-done.1.block_ref.refs_0_), channel_id=1, source_target_pairs={{0,4},{1,5},{2,6},{3,7},{4,12},{5,13},{6,14},{7,15},{12,8},{13,9},... | collective-permute-start | bytes 1198088 | tf_op jit(solution)/shard_map/ppermute | solution.py:307
  31.2 0.9 %shard_map.77 = (bf16[48,64]{1,0:T(8,128)(2,1)S(1)}, s32[48,128]{1,0:T(8,128)S(1)}, bf16[48,8192]{1,0:T(8,128)(2,1)S(1)}) custom-call(bf16[24,8320]{1,0:T(8,128)(2,1)S(1)} %collective-permute-done.block_ref.refs_0_, bf16[24,8320]{1,0:T(8,128)(2,1)S(1)} %collective-permute-done.5.refs_1_, bf16[64,8192]{1,0:T(8,128)(2,1)S(1)} %bitcast.22, ...), custom_call_target="tpu_custom_call" | custom-call | flops 1 | bytes 1 | tf_op jit(solution)/shard_map/pallas_call | solution.py:50
  32.2 1.5 %fusion.1.refs_3_ = f32[48,512]{1,0:T(8,128)S(1)} fusion(bf16[48,8192]{1,0:T(8,128)(2,1)S(1)} %get-tuple-element.61.refs_1_, bf16[8192,512]{1,0:T(8,128)(2,1)S(1)} %bitcast.28), kind=kOutput, calls=%fused_computation.1 | convolution fusion | flops 402653184 | bytes 9273344 | tf_op jit(solution)/shard_map/dot_general | solution.py:310
  33.7 4.7 %collective-permute-done.4.block_ref.refs_0_.refs_3_ = bf16[24,8320]{1,0:T(8,128)(2,1)S(1)} collective-permute-done((bf16[24,8320]{1,0:T(8,128)(2,1)S(1)}, bf16[24,8320]{1,0:T(8,128)(2,1)S(1)}, u32[]{:S(2)}, u32[]{:S(2)}) %collective-permute-start.4) | collective-permute-done | bytes 399392 | tf_op jit(solution)/shard_map/ppermute | solution.py:307
  38.4 1.0 %collective-permute-start.9 = (bf16[24,4224]{1,0:T(8,128)(2,1)S(1)}, bf16[24,4224]{1,0:T(8,128)(2,1)S(1)}, u32[]{:S(2)}, u32[]{:S(2)}) collective-permute-start(bf16[24,4224]{1,0:T(8,128)(2,1)S(1)} %shard_map.82), channel_id=1, source_target_pairs={{0,2},{1,3},{2,0},{3,1},{4,6},{5,7},{6,4},{7,5},{12,14},{13,15},{1... | collective-permute-start | bytes 608264 | tf_op jit(solution)/shard_map/ppermute | solution.py:307
  39.4 2.1 %collective-permute-done.6.refs_0_.refs_1_ = bf16[24,8320]{1,0:T(8,128)(2,1)S(1)} collective-permute-done((bf16[24,8320]{1,0:T(8,128)(2,1)S(1)}, bf16[24,8320]{1,0:T(8,128)(2,1)S(1)}, u32[]{:S(2)}, u32[]{:S(2)}) %collective-permute-start.6) | collective-permute-done | bytes 399392 | tf_op jit(solution)/shard_map/ppermute | solution.py:307
  42.6 3.8 %shard_map.81 = (f32[144,512]{1,0:T(8,128)S(1)}, bf16[8192,512]{1,0:T(8,128)(2,1)S(1)}) custom-call(bf16[48,8192]{1,0:T(8,128)(2,1)S(1)} %get-tuple-element.60.refs_0_, bf16[48,8192]{1,0:T(8,128)(2,1)S(1)} %get-tuple-element.61.refs_1_, bf16[48,8192]{1,0:T(8,128)(2,1)S(1)} %get-tuple-element.76.refs_2_, bf16[8192,512]{1,0:T(8,128)(2,1)} %collective-permute-done.8.refs_3_), custom_call_target="tpu_custom_call" | custom-call | flops 1 | bytes 1 | tf_op jit(solution)/shard_map/pallas_call | solution.py:223
  46.4 1.7 %collective-permute-done.7.refs_4_ = bf16[24,4096]{1,0:T(8,128)(2,1)S(1)} collective-permute-done((bf16[24,4096]{1,0:T(8,128)(2,1)S(1)}, bf16[24,4096]{1,0:T(8,128)(2,1)S(1)}, u32[]{:S(2)}, u32[]{:S(2)}) %collective-permute-start.7) | collective-permute-done | bytes 196640 | tf_op jit(solution)/shard_map/ppermute | solution.py:307
  48.2 1.0 %shard_map.83 = (bf16[96,128]{1,0:T(8,128)(2,1)S(1)}, s32[48,128]{1,0:T(8,128)S(1)}, bf16[48,8192]{1,0:T(8,128)(2,1)S(1)}) custom-call(f32[8,128]{1,0:T(8,128)S(1)} %shard_map.74.refs_0_, f32[8,128]{1,0:T(8,128)S(1)} %shard_map.76.refs_1_, f32[8,128]{1,0:T(8,128)S(1)} %shard_map.78.refs_2_, ...), custom_call_target="tpu_custom_call" | custom-call | flops 1 | bytes 1 | tf_op jit(solution)/shard_map/pallas_call | solution.py:50
  49.4 2.3 %collective-permute-start.11 = (bf16[96,128]{1,0:T(8,128)(2,1)S(1)}, bf16[96,128]{1,0:T(8,128)(2,1)S(1)}, u32[]{:S(2)}, u32[]{:S(2)}) collective-permute-start(bf16[96,128]{1,0:T(8,128)(2,1)S(1)} %get-tuple-element.72.refs_0_), channel_id=1, source_target_pairs={{0,12},{1,13},{2,14},{3,15},{4,8},{5,9},{6,10},{7,11},{12,0},{13,1... | collective-permute-start | bytes 73736 | tf_op jit(solution)/shard_map/ppermute | solution.py:307
  51.7 1.0 %collective-permute-start.12 = (bf16[96,128]{1,0:T(8,128)(2,1)S(1)}, bf16[96,128]{1,0:T(8,128)(2,1)S(1)}, u32[]{:S(2)}, u32[]{:S(2)}) collective-permute-start(bf16[96,128]{1,0:T(8,128)(2,1)S(1)} %get-tuple-element.72.refs_0_), channel_id=1, source_target_pairs={{0,8},{1,9},{2,10},{3,11},{4,0},{5,1},{6,2},{7,3},{12,4},{13,5},{1... | collective-permute-start | bytes 73736 | tf_op jit(solution)/shard_map/ppermute | solution.py:307
  52.7 1.5 %fusion.2.refs_5_ = f32[48,512]{1,0:T(8,128)S(1)} fusion(bf16[48,8192]{1,0:T(8,128)(2,1)S(1)} %get-tuple-element.77, bf16[8192,512]{1,0:T(8,128)(2,1)S(1)} %bitcast.28), kind=kOutput, calls=%fused_computation.2 | convolution fusion | flops 402653184 | bytes 9273344 | tf_op jit(solution)/shard_map/dot_general | solution.py:310
  56.2 1.5 %fusion.3.refs_4_ = f32[48,512]{1,0:T(8,128)S(1)} fusion(bf16[48,8192]{1,0:T(8,128)(2,1)S(1)} %get-tuple-element.76.refs_2_, bf16[8192,512]{1,0:T(8,128)(2,1)S(1)} %bitcast.28), kind=kOutput, calls=%fused_computation.3 | convolution fusion | flops 402653184 | bytes 9273344 | tf_op jit(solution)/shard_map/dot_general | solution.py:310
  57.7 1.5 %fusion.4.refs_7_ = f32[48,512]{1,0:T(8,128)S(1)} fusion(bf16[48,8192]{1,0:T(8,128)(2,1)S(1)} %get-tuple-element.77, bf16[8192,512]{1,0:T(8,128)(2,1)S(1)} %get-tuple-element.78), kind=kOutput, calls=%fused_computation.4 | convolution fusion | flops 402653184 | bytes 9273344 | tf_op jit(solution)/shard_map/dot_general | solution.py:310
  60.3 14.6 %all_to_all.5 = bf16[8,24,1024]{2,1,0:T(8,128)(2,1)S(1)} all-to-all(bf16[8,24,1024]{2,1,0:T(8,128)(2,1)S(1)} %shard_map.85), channel_id=1, replica_groups={{0,2,4,6,8,10,12,14},{1,3,5,7,9,11,13,15},{16,18,20,22,24,26,28,30},{17..., dimensions={0} | all-to-all | bytes 786432 | tf_op jit(solution)/shard_map/all_to_all | solution.py:358
  (39 shorter events, 7.5 us)
Async XLA Ops:
  0.0 42.6 %collective-permute-start.8 = (bf16[8192,512]{1,0:T(8,128)(2,1)}, bf16[8192,512]{1,0:T(8,128)(2,1)}, u32[]{:S(2)}, u32[]{:S(2)}) collective-permute-start(bf16[8192,512]{1,0:T(8,128)(2,1)} %param.9), channel_id=1, source_target_pairs={{0,1},{1,0},{2,3},{3,2},{4,5},{5,4},{6,7},{7,6},{12,13},{13,12},{1... | collective-permute-start | bytes 25165832 | tf_op jit(solution)/shard_map/ppermute | solution.py:307
  0.5 18.3 %collective-permute-start.3 = (bf16[64,8192]{1,0:T(8,128)(2,1)}, bf16[64,8192]{1,0:T(8,128)(2,1)S(1)}, u32[]{:S(2)}, u32[]{:S(2)}) collective-permute-start(bf16[64,8192]{1,0:T(8,128)(2,1)} %bitcast.20), channel_id=1, source_target_pairs={{0,1},{1,0},{2,3},{3,2},{4,5},{5,4},{6,7},{7,6},{12,13},{13,12},{1... | collective-permute-start | bytes 3145736 | tf_op jit(solution)/shard_map/ppermute | solution.py:307
  2.6 13.7 %collective-permute-start = (bf16[24,8320]{1,0:T(8,128)(2,1)}, bf16[24,8320]{1,0:T(8,128)(2,1)S(1)}, u32[]{:S(2)}, u32[]{:S(2)}) collective-permute-start(bf16[24,8320]{1,0:T(8,128)(2,1)} %shard_map.73.refs_0_), channel_id=1, source_target_pairs={{0,4},{1,5},{2,6},{3,7},{4,12},{5,13},{6,14},{7,15},{12,8},{13,9},... | collective-permute-start | bytes 1198088 | tf_op jit(solution)/shard_map/ppermute | solution.py:307
  5.7 11.6 %collective-permute-start.2 = (bf16[24,8320]{1,0:T(8,128)(2,1)}, bf16[24,8320]{1,0:T(8,128)(2,1)S(1)}, u32[]{:S(2)}, u32[]{:S(2)}) collective-permute-start(bf16[24,8320]{1,0:T(8,128)(2,1)} %shard_map.73.refs_0_), channel_id=1, source_target_pairs={{0,2},{1,3},{2,0},{3,1},{4,6},{5,7},{6,4},{7,5},{12,14},{13,15},{1... | collective-permute-start | bytes 1198088 | tf_op jit(solution)/shard_map/ppermute | solution.py:307
  16.3 11.5 %collective-permute-start.1 = (bf16[24,8320]{1,0:T(8,128)(2,1)S(1)}, bf16[24,8320]{1,0:T(8,128)(2,1)S(1)}, u32[]{:S(2)}, u32[]{:S(2)}) collective-permute-start(bf16[24,8320]{1,0:T(8,128)(2,1)S(1)} %collective-permute-done.block_ref.refs_0_), channel_id=1, source_target_pairs={{0,4},{1,5},{2,6},{3,7},{4,12},{5,13},{6,14},{7,15},{12,8},{13,9},... | collective-permute-start | bytes 1198088 | tf_op jit(solution)/shard_map/ppermute | solution.py:307
  17.2 13.5 %collective-permute-start.5 = (bf16[24,8320]{1,0:T(8,128)(2,1)S(1)}, bf16[24,8320]{1,0:T(8,128)(2,1)S(1)}, u32[]{:S(2)}, u32[]{:S(2)}) collective-permute-start(bf16[24,8320]{1,0:T(8,128)(2,1)S(1)} %collective-permute-done.block_ref.refs_0_), channel_id=1, source_target_pairs={{0,2},{1,3},{2,0},{3,1},{4,6},{5,7},{6,4},{7,5},{12,14},{13,15},{1... | collective-permute-start | bytes 1198088 | tf_op jit(solution)/shard_map/ppermute | solution.py:307
  18.8 1.2 %copy-start = (bf16[1,8192,64]{1,2,0:T(8,128)(2,1)S(1)}, bf16[1,8192,64]{1,2,0:T(8,128)(2,1)}, u32[]{:S(2)}) copy-start(bf16[1,8192,64]{1,2,0:T(8,128)(2,1)} %param.10) | copy-start | bytes 3145732
  20.0 1.0 %copy-start.2 = (bf16[24,8320]{1,0:T(8,128)(2,1)S(1)}, bf16[24,8320]{1,0:T(8,128)(2,1)}, u32[]{:S(2)}) copy-start(bf16[24,8320]{1,0:T(8,128)(2,1)} %shard_map.73.refs_0_) | copy-start | bytes 1198084
  21.0 11.1 %slice-start = ((s8[8388608]{0:T(1024)(128)(4,1)}), s8[4194304]{0:T(1024)(128)(4,1)S(1)}, s32[]{:S(2)}) async-start(s8[8388608]{0:T(1024)(128)(4,1)} %bitcast.27), calls=%async_computation.1 | async-start | bytes 8388608
  21.9 9.3 %copy-start.1 = (bf16[1,8192,64]{1,2,0:T(8,128)(2,1)S(1)}, bf16[1,8192,64]{1,2,0:T(8,128)(2,1)}, u32[]{:S(2)}) copy-start(bf16[1,8192,64]{1,2,0:T(8,128)(2,1)} %param.10) | copy-start | bytes 3145732
  21.9 10.2 %slice-start.1 = ((s8[8388608]{0:T(1024)(128)(4,1)}), s8[4194304]{0:T(1024)(128)(4,1)S(1)}, s32[]{:S(2)}) async-start(s8[8388608]{0:T(1024)(128)(4,1)} %bitcast.27), calls=%async_computation.2 | async-start | bytes 8388608
  27.8 10.6 %collective-permute-start.4 = (bf16[24,8320]{1,0:T(8,128)(2,1)S(1)}, bf16[24,8320]{1,0:T(8,128)(2,1)S(1)}, u32[]{:S(2)}, u32[]{:S(2)}) collective-permute-start(bf16[24,8320]{1,0:T(8,128)(2,1)S(1)} %collective-permute-done.1.block_ref.refs_0_), channel_id=1, source_target_pairs={{0,4},{1,5},{2,6},{3,7},{4,12},{5,13},{6,14},{7,15},{12,8},{13,9},... | collective-permute-start | bytes 1198088 | tf_op jit(solution)/shard_map/ppermute | solution.py:307
  30.7 10.8 %collective-permute-start.6 = (bf16[24,8320]{1,0:T(8,128)(2,1)S(1)}, bf16[24,8320]{1,0:T(8,128)(2,1)S(1)}, u32[]{:S(2)}, u32[]{:S(2)}) collective-permute-start(bf16[24,8320]{1,0:T(8,128)(2,1)S(1)} %collective-permute-done.1.block_ref.refs_0_), channel_id=1, source_target_pairs={{0,2},{1,3},{2,0},{3,1},{4,6},{5,7},{6,4},{7,5},{12,14},{13,15},{1... | collective-permute-start | bytes 1198088 | tf_op jit(solution)/shard_map/ppermute | solution.py:307
  32.1 9.5 %copy-start.3 = (bf16[16,64,512]{2,1,0:T(8,128)(2,1)S(1)}, bf16[16,64,512]{2,1,0:T(8,128)(2,1)}, u32[]{:S(2)}) copy-start(bf16[16,64,512]{2,1,0:T(8,128)(2,1)} %param.11) | copy-start | bytes 3145732
  38.4 9.7 %collective-permute-start.9 = (bf16[24,4224]{1,0:T(8,128)(2,1)S(1)}, bf16[24,4224]{1,0:T(8,128)(2,1)S(1)}, u32[]{:S(2)}, u32[]{:S(2)}) collective-permute-start(bf16[24,4224]{1,0:T(8,128)(2,1)S(1)} %shard_map.82), channel_id=1, source_target_pairs={{0,2},{1,3},{2,0},{3,1},{4,6},{5,7},{6,4},{7,5},{12,14},{13,15},{1... | collective-permute-start | bytes 608264 | tf_op jit(solution)/shard_map/ppermute | solution.py:307
  41.5 6.6 %collective-permute-start.7 = (bf16[24,4096]{1,0:T(8,128)(2,1)S(1)}, bf16[24,4096]{1,0:T(8,128)(2,1)S(1)}, u32[]{:S(2)}, u32[]{:S(2)}) collective-permute-start(bf16[24,4096]{1,0:T(8,128)(2,1)S(1)} %shard_map.79), channel_id=1, source_target_pairs={{0,4},{1,5},{2,6},{3,7},{4,12},{5,13},{6,14},{7,15},{12,8},{13,9},... | collective-permute-start | bytes 589832 | tf_op jit(solution)/shard_map/ppermute | solution.py:307
  41.6 17.7 %collective-permute-start.14 = (bf16[1024,512]{1,0:T(8,128)(2,1)S(1)}, bf16[1024,512]{1,0:T(8,128)(2,1)S(1)}, u32[]{:S(2)}, u32[]{:S(2)}) collective-permute-start(bf16[1024,512]{1,0:T(8,128)(2,1)S(1)} %bitcast.25), channel_id=1, source_target_pairs={{0,1},{1,0},{2,3},{3,2},{4,5},{5,4},{6,7},{7,6},{12,13},{13,12},{1... | collective-permute-start | bytes 3145736 | tf_op jit(solution)/shard_map/ppermute | solution.py:307
  49.1 5.1 %collective-permute-start.10 = (bf16[96,128]{1,0:T(8,128)(2,1)S(1)}, bf16[96,128]{1,0:T(8,128)(2,1)S(1)}, u32[]{:S(2)}, u32[]{:S(2)}) collective-permute-start(bf16[96,128]{1,0:T(8,128)(2,1)S(1)} %get-tuple-element.72.refs_0_), channel_id=1, source_target_pairs={{0,4},{1,5},{2,6},{3,7},{4,12},{5,13},{6,14},{7,15},{12,8},{13,9},... | collective-permute-start | bytes 73736 | tf_op jit(solution)/shard_map/ppermute | solution.py:307
  49.4 5.7 %collective-permute-start.11 = (bf16[96,128]{1,0:T(8,128)(2,1)S(1)}, bf16[96,128]{1,0:T(8,128)(2,1)S(1)}, u32[]{:S(2)}, u32[]{:S(2)}) collective-permute-start(bf16[96,128]{1,0:T(8,128)(2,1)S(1)} %get-tuple-element.72.refs_0_), channel_id=1, source_target_pairs={{0,12},{1,13},{2,14},{3,15},{4,8},{5,9},{6,10},{7,11},{12,0},{13,1... | collective-permute-start | bytes 73736 | tf_op jit(solution)/shard_map/ppermute | solution.py:307
  51.7 3.8 %collective-permute-start.12 = (bf16[96,128]{1,0:T(8,128)(2,1)S(1)}, bf16[96,128]{1,0:T(8,128)(2,1)S(1)}, u32[]{:S(2)}, u32[]{:S(2)}) collective-permute-start(bf16[96,128]{1,0:T(8,128)(2,1)S(1)} %get-tuple-element.72.refs_0_), channel_id=1, source_target_pairs={{0,8},{1,9},{2,10},{3,11},{4,0},{5,1},{6,2},{7,3},{12,4},{13,5},{1... | collective-permute-start | bytes 73736 | tf_op jit(solution)/shard_map/ppermute | solution.py:307
  55.7 3.9 %collective-permute-start.13 = (bf16[96,128]{1,0:T(8,128)(2,1)S(1)}, bf16[96,128]{1,0:T(8,128)(2,1)S(1)}, u32[]{:S(2)}, u32[]{:S(2)}) collective-permute-start(bf16[96,128]{1,0:T(8,128)(2,1)S(1)} %shard_map.84.refs_0_), channel_id=1, source_target_pairs={{0,2},{1,3},{2,0},{3,1},{4,6},{5,7},{6,4},{7,5},{12,14},{13,15},{1... | collective-permute-start | bytes 73736 | tf_op jit(solution)/shard_map/ppermute | solution.py:307

commit v13 on v12

--- a/solution.py
+++ b/solution.py
@@ -31,6 +31,13 @@
         for corner in range(CORNERS):
             out.append((place * CORNERS + corner, target * CORNERS + (corner ^ flip)))
     return out
+
+
+def split_pairs(places):
+    flips, steps = pairs(places, 0, 2), pairs(places, 1, 0)
+    return [pair for pair in flips if pair[0] % CORES == 0] + [
+        pair for pair in steps if pair[0] % CORES
+    ]
 
 
 def ring_chip(places, steps, side):
@@ -109,32 +116,21 @@
     )(*sources)
 
 
-def columns_of(pieces, start):
-    for piece in pieces:
-        if start < piece.shape[1]:
-            return piece[:, start : start + CHUNK].astype(jnp.float32)
-        start -= piece.shape[1]
-
-
-def shrink_kernel(counts, halves, *refs):
-    blocks, refs = [], list(refs)
-    for count in counts:
-        blocks.append(refs[:count])
-        refs = refs[count:]
-    own_ref, other_ref, *before, part_ref, slot_ref, rows_ref = refs
+def shrink_kernel(halves, *refs):
+    blocks, (own_ref, other_ref, *before, part_ref, slot_ref, rows_ref) = refs[:SIDE], refs[SIDE:]
     rank, width = own_ref.shape
     rows = slot_ref.shape[0]
     part = jnp.zeros((rows, 2 * rank), jnp.float32)
     for start in range(0, width, CHUNK):
         lanes = slice(start, start + CHUNK)
-        wide = [columns_of(block, start) for block in blocks]
+        wide = [block[:, lanes].astype(jnp.float32) for block in blocks]
         chunk = jnp.concatenate(wide, axis=0).astype(jnp.bfloat16)
         rows_ref[:, lanes] = chunk
         down = jnp.concatenate([own_ref[:, lanes], other_ref[:, lanes]], axis=0)
         part += lax.dot_general(
             chunk, down, (((1,), (1,)), ((), ())), preferred_element_type=jnp.float32
         )
-    slot = [block[-1][:, block[-1].shape[1] - LANES :].astype(jnp.float32) for block in blocks]
+    slot = [block[:, width:].astype(jnp.float32) for block in blocks]
     slot = jnp.concatenate(slot, axis=0)[:, 0:1].astype(jnp.int32)
     slot_ref[...] = jnp.broadcast_to(slot, slot_ref.shape)
     me = lax.axis_index("adapter")
@@ -150,7 +146,7 @@
 
 
 def shrink_rows(blocks, own, other, before=(), tokens=()):
-    rows = blocks[0][0].shape[0] * len(blocks)
+    rows = blocks[0].shape[0] * SIDE
     rank, width = own.shape
     packed = (rows * (len(before) + 1) // 2, 2 * rank) if before else (rows, rank)
     out_shape = (
@@ -158,12 +154,10 @@
         jax.ShapeDtypeStruct((rows, LANES), jnp.int32),
         jax.ShapeDtypeStruct((rows, width), jnp.bfloat16),
     )
-    counts = [len(block) for block in blocks]
-    pieces = [piece for block in blocks for piece in block]
     return call(
-        lambda *refs: shrink_kernel(counts, bool(before), *refs[len(tokens) :]),
+        lambda *refs: shrink_kernel(bool(before), *refs[len(tokens) :]),
         out_shape,
-        (*tokens, *pieces, own, other, *before),
+        (*tokens, *blocks, own, other, *before),
     )
 
 
@@ -186,18 +180,6 @@
     rows = ref.shape[0] // (places // 2)
     side, first = divmod(step, places // 2)
     return ref[first * rows : (first + 1) * rows, side * rank : (side + 1) * rank].astype(jnp.float32)
-
-
-def cut_kernel(first, block_ref, out_ref):
-    out_ref[...] = block_ref[:, first : first + out_ref.shape[1]]
-
-
-def cut(block, first, last):
-    return call(
-        lambda *refs: cut_kernel(first, *refs),
-        jax.ShapeDtypeStruct((block.shape[0], last - first), block.dtype),
-        (block,),
-    )
 
 
 def base_kernel(*refs):
@@ -251,8 +233,8 @@
 
 def finish_kernel(places, *refs):
     shrink_ref, across_ref, *refs = refs
-    bases, slots = refs[: places + 2], refs[places + 2 : 2 * places + 2]
-    own_ref, other_ref, out_ref = refs[2 * places + 2 :]
+    bases, slots = refs[: places + 3], refs[places + 3 : 2 * places + 3]
+    own_ref, other_ref, out_ref = refs[2 * places + 3 :]
     depth, columns = own_ref.shape
     own_rows = out_ref.shape[1]
     rows = SIDE * own_rows
@@ -274,10 +256,10 @@
             here = slice(step * rows, (step + 1) * rows)
             if which == 0:
                 base = bases[step][...]
-            elif step == places - 1:
-                base = bases[places + 1][...]
+            elif step < places - 2:
+                base = bases[places][here, :]
             else:
-                base = bases[places][here, :]
+                base = bases[step + 3][...]
             query = (base + ADAPTER_SCALE * update[here]).astype(jnp.bfloat16)
             for side in range(SIDE):
                 chip = ring_chip(places, -step, side)
@@ -297,9 +279,9 @@
     hidden, norm_weight, query_weight, down_weights, up_weights, adapter_index, adapter_slot
 ):
     devices = lax.axis_size("adapter")
+    me = lax.axis_index("adapter")
     places = devices // CORNERS
     own_rows, width = hidden.shape
-    half = width // 2
     columns = query_weight.shape[1]
     rank = down_weights.shape[2]
 
@@ -332,16 +314,18 @@
         block.append(move(after(block[step], *tokens[-1:]), 1, 0))
         other.append(move(after(block[step], *other[-1:]), 0, 2))
         if step:
-            meet(after([[block[step - 1]], [other[step - 1]]], block[step]))
+            meet(after([block[step - 1], other[step - 1]], block[step]))
             bases.append(base_rows(rows[-1], query_weight))
-    block[last] = after(block[last], bases[-1])
+    base, weight_other = base_and_weight(after(rows, bases[-1]), weight_other)
+    block[last] = after(block[last], base)
     tokens.append(token(block[last]))
-    low = move(cut(after(other[-1], tokens[-1]), 0, half), 1, 0)
-    high = move(cut(after(block[last], tokens[-1]), half, block[last].shape[1]), 0, 2)
-    meet(after([[block[last - 1]], [other[-1]]], block[last]))
-    base, weight_other = base_and_weight(after(rows, block[last]), weight_other)
-    low, high = after(low, base), after(high, base)
-    meet([[block[last]], [low, high]], parts)
+    source = after(block[last], other[-1], tokens[-1])
+    source = jnp.where((me & 1) == 0, source, other[-1])
+    crossed = lax.ppermute(source, "adapter", split_pairs(places))
+    meet(after([block[last - 1], other[-1]], source))
+    bases.append(base_rows(rows[-1], query_weight))
+    bases_other = [base, base_rows(rows[-1], weight_other)]
+    meet([block[last], after(crossed, bases[-1], bases_other[-1])], parts)
 
     part = parts[-1]
     moved = [part] + [move(part, steps, 0) for steps in range(1, places)]
@@ -351,9 +335,8 @@
         lambda *refs: sum_kernel(places, *refs), jax.ShapeDtypeStruct(part.shape, part.dtype), moved
     )
     across = move(shrink, 0, 2)
-    bases.insert(last - 1, base_rows(after(rows[last - 1], shrink), query_weight))
-    bases += [base, base_rows(after(rows[-1], shrink), weight_other)]
-    query = finish(shrink, across, bases, slots, up, up_other, own_rows)
+    bases_other.append(base_rows(after(rows[-1], shrink), weight_other))
+    query = finish(shrink, across, bases + bases_other, slots, up, up_other, own_rows)
     groups = [list(range(core, devices, CORES)) for core in range(CORES)]
     query = lax.all_to_all(query, "adapter", 0, 0, axis_index_groups=groups, tiled=True)
     return query.transpose(1, 0, 2).reshape(own_rows, devices * columns)

time: 75.9 us -> 74.4 us (0.980)
  waiting for transfers between devices: 19.8 us -> 17.4 us
  blocking collectives: 14.6 us -> 12.8 us
  matrix products: 11.5 us -> 13 us
  starting transfers between devices: 16.2 us -> 17.5 us
    ppermute x15 -> x13, waiting for transfers between devices: 19.8 us -> 14.2 us  [move(): return lax.ppermute(x, 'adapter', pairs(places, steps, flip))]
    ppermute x0 -> x1, waiting for transfers between devices: none -> 3.14 us  [shards(): crossed = lax.ppermute(source, 'adapter', split_pairs(places))]
    all_to_all x1, blocking collectives: 14.6 us -> 12.8 us  [shards(): lax.all_to_all(query, 'adapter', 0, 0, axis_index_groups=groups, tiled=True)]
    dot_general x5 -> x6, matrix products: 11.5 us -> 13 us  [base_rows(): return jnp.dot(rows, weight, preferred_element_type=jnp.float32)]
    ppermute x0 -> x1, starting transfers between devices: none -> 0.77 us  [shards(): crossed = lax.ppermute(source, 'adapter', split_pairs(places))]
    ppermute x15 -> x13, starting transfers between devices: 16.2 us -> 16.7 us  [move(): return lax.ppermute(x, 'adapter', pairs(places, steps, flip))]
    pallas_call x8 -> x6, Pallas kernels: 4.51 us -> 4.48 us  [call(): pl.pallas_call(kernel, out_shape=out_shape, in_specs=[VMEM] * len(operand...]
  transfers between devices with their start and end apart: 15 -> 14, of which waited for: 8 -> 8; matrix products, arithmetic and copies ran while one was open for 15% -> 18% of each run, Pallas kernels for 13% -> 13%
where the time goes in v13:
time: 74.4 us; the launch traced here: 74.2 us
  starting transfers between devices  17.5 us (24%)
  waiting for transfers between devices  17.4 us (23%)
  matrix products  13 us (17%)
  blocking collectives  12.8 us (17%)
  Pallas kernels  10.3 us (14%)
  local copies, waits for them, and re-layouts  3.02 us (4%)
    ppermute x13, starting transfers between devices, move(): return lax.ppermute(x, 'adapter', pairs(places, steps, flip))  16.7 us
    ppermute x13, waiting for transfers between devices, move(): return lax.ppermute(x, 'adapter', pairs(places, steps, flip))  14.2 us
    dot_general x6, matrix products, base_rows(): return jnp.dot(rows, weight, preferred_element_type=jnp.float32)  13 us
    all_to_all x1, blocking collectives, shards(): lax.all_to_all(query, 'adapter', 0, 0, axis_index_groups=groups, tiled=True)  12.8 us
    pallas_call x6, Pallas kernels, call(): pl.pallas_call(kernel, out_shape=out_shape, in_specs=[VMEM] * len(operand...  4.48 us
    pallas_call x1, Pallas kernels, base_and_weight(): pl.pallas_call(base_kernel, out_shape=(jax.ShapeDtypeStruct((rows, weight...  3.79 us
    ppermute x1, waiting for transfers between devices, shards(): crossed = lax.ppermute(source, 'adapter', split_pairs(places))  3.14 us
    unnamed x12, local copies, waits for them, and re-layouts  2.24 us
  transfers between devices with their start and end apart: 14, of which 8 were waited for; matrix products, arithmetic and copies ran while one was open for 18% of the time, Pallas kernels for 13%

profile of v13, /device:TPU:0, one launch (start us, length us, event | category | flops | bytes accessed | tf_op | source)
XLA Modules:
  0.0 74.2 jit_solution(16662837836492626377)
XLA Ops:
  0.5 2.0 %shard_map.73.refs_0_ = bf16[24,8320]{1,0:T(8,128)(2,1)} custom-call(bf16[24,8192]{1,0:T(8,128)(2,1)} %refs_0_.1, f32[1,8192]{1,0:T(1,128)} %bitcast.32, s32[1,24]{1,0:T(1,128)} %bitcast.33, s32[1,16]{1,0:T(1,128)} %bitcast.34), custom_call_target="tpu_custom_call" | custom-call | tf_op jit(solution)/shard_map/pallas_call | solution.py:109
  2.6 3.1 %collective-permute-start = (bf16[24,8320]{1,0:T(8,128)(2,1)}, bf16[24,8320]{1,0:T(8,128)(2,1)S(1)}, u32[]{:S(2)}, u32[]{:S(2)}) collective-permute-start(bf16[24,8320]{1,0:T(8,128)(2,1)} %shard_map.73.refs_0_), channel_id=1, source_target_pairs={{0,4},{1,5},{2,6},{3,7},{4,12},{5,13},{6,14},{7,15},{12,8},{13,9},... | collective-permute-start | bytes 1198088 | tf_op jit(solution)/shard_map/ppermute | solution.py:289
  5.6 1.5 %collective-permute-start.2 = (bf16[24,8320]{1,0:T(8,128)(2,1)}, bf16[24,8320]{1,0:T(8,128)(2,1)S(1)}, u32[]{:S(2)}, u32[]{:S(2)}) collective-permute-start(bf16[24,8320]{1,0:T(8,128)(2,1)} %shard_map.73.refs_0_), channel_id=1, source_target_pairs={{0,2},{1,3},{2,0},{3,1},{4,6},{5,7},{6,4},{7,5},{12,14},{13,15},{1... | collective-permute-start | bytes 1198088 | tf_op jit(solution)/shard_map/ppermute | solution.py:289
  7.2 9.1 %collective-permute-done.block_ref.refs_0_ = bf16[24,8320]{1,0:T(8,128)(2,1)S(1)} collective-permute-done((bf16[24,8320]{1,0:T(8,128)(2,1)}, bf16[24,8320]{1,0:T(8,128)(2,1)S(1)}, u32[]{:S(2)}, u32[]{:S(2)}) %collective-permute-start) | collective-permute-done | bytes 399392 | tf_op jit(solution)/shard_map/ppermute | solution.py:289
  16.7 2.6 %collective-permute-start.1 = (bf16[24,8320]{1,0:T(8,128)(2,1)S(1)}, bf16[24,8320]{1,0:T(8,128)(2,1)S(1)}, u32[]{:S(2)}, u32[]{:S(2)}) collective-permute-start(bf16[24,8320]{1,0:T(8,128)(2,1)S(1)} %collective-permute-done.block_ref.refs_0_), channel_id=1, source_target_pairs={{0,4},{1,5},{2,6},{3,7},{4,12},{5,13},{6,14},{7,15},{12,8},{13,9},... | collective-permute-start | bytes 1198088 | tf_op jit(solution)/shard_map/ppermute | solution.py:289
  19.3 1.5 %collective-permute-start.5 = (bf16[24,8320]{1,0:T(8,128)(2,1)S(1)}, bf16[24,8320]{1,0:T(8,128)(2,1)S(1)}, u32[]{:S(2)}, u32[]{:S(2)}) collective-permute-start(bf16[24,8320]{1,0:T(8,128)(2,1)S(1)} %collective-permute-done.block_ref.refs_0_), channel_id=1, source_target_pairs={{0,2},{1,3},{2,0},{3,1},{4,6},{5,7},{6,4},{7,5},{12,14},{13,15},{1... | collective-permute-start | bytes 1198088 | tf_op jit(solution)/shard_map/ppermute | solution.py:289
  20.8 1.2 %copy-done = bf16[1,8192,64]{1,2,0:T(8,128)(2,1)S(1)} copy-done((bf16[1,8192,64]{1,2,0:T(8,128)(2,1)S(1)}, bf16[1,8192,64]{1,2,0:T(8,128)(2,1)}, u32[]{:S(2)}) %copy-start) | copy-done | bytes 1048600
  22.1 1.0 %copy-done.2 = bf16[24,8320]{1,0:T(8,128)(2,1)S(1)} copy-done((bf16[24,8320]{1,0:T(8,128)(2,1)S(1)}, bf16[24,8320]{1,0:T(8,128)(2,1)}, u32[]{:S(2)}) %copy-start.2) | copy-done | bytes 399384
  24.0 5.4 %fusion.refs_2_ = f32[48,512]{1,0:T(8,128)S(1)} fusion(bf16[48,8192]{1,0:T(8,128)(2,1)S(1)} %get-tuple-element.50.refs_0_, bf16[8192,512]{1,0:T(8,128)(2,1)} %param.9), kind=kOutput, calls=%fused_computation.1 | convolution fusion | flops 402653184 | bytes 9273344 | tf_op jit(solution)/shard_map/dot_general | solution.py:292
  29.5 1.2 %collective-permute-start.4 = (bf16[24,8320]{1,0:T(8,128)(2,1)S(1)}, bf16[24,8320]{1,0:T(8,128)(2,1)S(1)}, u32[]{:S(2)}, u32[]{:S(2)}) collective-permute-start(bf16[24,8320]{1,0:T(8,128)(2,1)S(1)} %collective-permute-done.1.block_ref.refs_0_), channel_id=1, source_target_pairs={{0,4},{1,5},{2,6},{3,7},{4,12},{5,13},{6,14},{7,15},{12,8},{13,9},... | collective-permute-start | bytes 1198088 | tf_op jit(solution)/shard_map/ppermute | solution.py:289
  30.7 1.4 %collective-permute-start.7 = (bf16[24,8320]{1,0:T(8,128)(2,1)S(1)}, bf16[24,8320]{1,0:T(8,128)(2,1)S(1)}, u32[]{:S(2)}, u32[]{:S(2)}) collective-permute-start(bf16[24,8320]{1,0:T(8,128)(2,1)S(1)} %collective-permute-done.1.block_ref.refs_0_), channel_id=1, source_target_pairs={{0,2},{1,3},{2,0},{3,1},{4,6},{5,7},{6,4},{7,5},{12,14},{13,15},{1... | collective-permute-start | bytes 1198088 | tf_op jit(solution)/shard_map/ppermute | solution.py:289
  33.0 1.5 %fusion.1.refs_3_ = f32[48,512]{1,0:T(8,128)S(1)} fusion(bf16[48,8192]{1,0:T(8,128)(2,1)S(1)} %get-tuple-element.51.refs_1_, bf16[8192,512]{1,0:T(8,128)(2,1)S(1)} %bitcast.30), kind=kOutput, calls=%fused_computation.2 | convolution fusion | flops 402653184 | bytes 9273344 | tf_op jit(solution)/shard_map/dot_general | solution.py:292
  34.5 3.8 %shard_map.78 = (f32[96,512]{1,0:T(8,128)S(1)}, bf16[8192,512]{1,0:T(8,128)(2,1)S(1)}) custom-call(bf16[48,8192]{1,0:T(8,128)(2,1)S(1)} %get-tuple-element.50.refs_0_, bf16[48,8192]{1,0:T(8,128)(2,1)S(1)} %get-tuple-element.51.refs_1_, bf16[8192,512]{1,0:T(8,128)(2,1)} %collective-permute-done.6.refs_2_), custom_call_target="tpu_custom_call" | custom-call | flops 1 | bytes 1 | tf_op jit(solution)/shard_map/pallas_call | solution.py:205
  38.3 1.5 %collective-permute-done.4.block_ref.refs_3_ = bf16[24,8320]{1,0:T(8,128)(2,1)S(1)} collective-permute-done((bf16[24,8320]{1,0:T(8,128)(2,1)S(1)}, bf16[24,8320]{1,0:T(8,128)(2,1)S(1)}, u32[]{:S(2)}, u32[]{:S(2)}) %collective-permute-start.4) | collective-permute-done | bytes 399392 | tf_op jit(solution)/shard_map/ppermute | solution.py:289
  41.9 1.5 %fusion.2.refs_4_ = f32[48,512]{1,0:T(8,128)S(1)} fusion(bf16[48,8192]{1,0:T(8,128)(2,1)S(1)} %get-tuple-element.58, bf16[8192,512]{1,0:T(8,128)(2,1)S(1)} %bitcast.30), kind=kOutput, calls=%fused_computation.3 | convolution fusion | flops 402653184 | bytes 9273344 | tf_op jit(solution)/shard_map/dot_general | solution.py:292
  43.4 1.5 %fusion.3.refs_7_ = f32[48,512]{1,0:T(8,128)S(1)} fusion(bf16[48,8192]{1,0:T(8,128)(2,1)S(1)} %get-tuple-element.58, bf16[8192,512]{1,0:T(8,128)(2,1)S(1)} %get-tuple-element.59), kind=kOutput, calls=%fused_computation.4 | convolution fusion | flops 402653184 | bytes 9273344 | tf_op jit(solution)/shard_map/dot_general | solution.py:292
  44.9 3.1 %collective-permute-done.8.refs_4_ = bf16[24,8320]{1,0:T(8,128)(2,1)S(1)} collective-permute-done((bf16[24,8320]{1,0:T(8,128)(2,1)S(1)}, bf16[24,8320]{1,0:T(8,128)(2,1)S(1)}, u32[]{:S(2)}, u32[]{:S(2)}) %collective-permute-start.8) | collective-permute-done | bytes 399392 | tf_op jit(solution)/shard_map/ppermute | solution.py:324
  49.1 1.3 %collective-permute-start.10 = (bf16[96,128]{1,0:T(8,128)(2,1)S(1)}, bf16[96,128]{1,0:T(8,128)(2,1)S(1)}, u32[]{:S(2)}, u32[]{:S(2)}) collective-permute-start(bf16[96,128]{1,0:T(8,128)(2,1)S(1)} %get-tuple-element.66.refs_0_), channel_id=1, source_target_pairs={{0,12},{1,13},{2,14},{3,15},{4,8},{5,9},{6,10},{7,11},{12,0},{13,1... | collective-permute-start | bytes 73736 | tf_op jit(solution)/shard_map/ppermute | solution.py:289
  51.2 1.2 %collective-permute-start.9 = (bf16[96,128]{1,0:T(8,128)(2,1)S(1)}, bf16[96,128]{1,0:T(8,128)(2,1)S(1)}, u32[]{:S(2)}, u32[]{:S(2)}) collective-permute-start(bf16[96,128]{1,0:T(8,128)(2,1)S(1)} %get-tuple-element.66.refs_0_), channel_id=1, source_target_pairs={{0,4},{1,5},{2,6},{3,7},{4,12},{5,13},{6,14},{7,15},{12,8},{13,9},... | collective-permute-start | bytes 73736 | tf_op jit(solution)/shard_map/ppermute | solution.py:289
  52.4 1.5 %fusion.4.refs_5_ = f32[48,512]{1,0:T(8,128)S(1)} fusion(bf16[48,8192]{1,0:T(8,128)(2,1)S(1)} %get-tuple-element.70, bf16[8192,512]{1,0:T(8,128)(2,1)S(1)} %bitcast.30), kind=kOutput, calls=%fused_computation.5 | convolution fusion | flops 402653184 | bytes 9273344 | tf_op jit(solution)/shard_map/dot_general | solution.py:292
  54.7 1.2 %collective-permute-done.9.refs_1_ = bf16[96,128]{1,0:T(8,128)(2,1)S(1)} collective-permute-done((bf16[96,128]{1,0:T(8,128)(2,1)S(1)}, bf16[96,128]{1,0:T(8,128)(2,1)S(1)}, u32[]{:S(2)}, u32[]{:S(2)}) %collective-permute-start.9) | collective-permute-done | bytes 24608 | tf_op jit(solution)/shard_map/ppermute | solution.py:289
  56.1 1.6 %collective-permute-start.12 = (bf16[96,128]{1,0:T(8,128)(2,1)S(1)}, bf16[96,128]{1,0:T(8,128)(2,1)S(1)}, u32[]{:S(2)}, u32[]{:S(2)}) collective-permute-start(bf16[96,128]{1,0:T(8,128)(2,1)S(1)} %shard_map.82.refs_0_), channel_id=1, source_target_pairs={{0,2},{1,3},{2,0},{3,1},{4,6},{5,7},{6,4},{7,5},{12,14},{13,15},{1... | collective-permute-start | bytes 73736 | tf_op jit(solution)/shard_map/ppermute | solution.py:289
  57.6 1.5 %fusion.5.refs_8_ = f32[48,512]{1,0:T(8,128)S(1)} fusion(bf16[48,8192]{1,0:T(8,128)(2,1)S(1)} %get-tuple-element.70, bf16[8192,512]{1,0:T(8,128)(2,1)S(1)} %get-tuple-element.59), kind=kOutput, calls=%fused_computation.6 | convolution fusion | flops 402653184 | bytes 9273344 | tf_op jit(solution)/shard_map/dot_general | solution.py:292
  60.6 12.8 %all_to_all.5 = bf16[8,24,1024]{2,1,0:T(8,128)(2,1)S(1)} all-to-all(bf16[8,24,1024]{2,1,0:T(8,128)(2,1)S(1)} %shard_map.83), channel_id=1, replica_groups={{0,2,4,6,8,10,12,14},{1,3,5,7,9,11,13,15},{16,18,20,22,24,26,28,30},{17..., dimensions={0} | all-to-all | bytes 786432 | tf_op jit(solution)/shard_map/all_to_all | solution.py:341
  (37 shorter events, 9.8 us)
Async XLA Ops:
  0.0 34.5 %collective-permute-start.6 = (bf16[8192,512]{1,0:T(8,128)(2,1)}, bf16[8192,512]{1,0:T(8,128)(2,1)}, u32[]{:S(2)}, u32[]{:S(2)}) collective-permute-start(bf16[8192,512]{1,0:T(8,128)(2,1)} %param.9), channel_id=1, source_target_pairs={{0,1},{1,0},{2,3},{3,2},{4,5},{5,4},{6,7},{7,6},{12,13},{13,12},{1... | collective-permute-start | bytes 25165832 | tf_op jit(solution)/shard_map/ppermute | solution.py:289
  0.5 20.4 %collective-permute-start.3 = (bf16[64,8192]{1,0:T(8,128)(2,1)}, bf16[64,8192]{1,0:T(8,128)(2,1)S(1)}, u32[]{:S(2)}, u32[]{:S(2)}) collective-permute-start(bf16[64,8192]{1,0:T(8,128)(2,1)} %bitcast.22), channel_id=1, source_target_pairs={{0,1},{1,0},{2,3},{3,2},{4,5},{5,4},{6,7},{7,6},{12,13},{13,12},{1... | collective-permute-start | bytes 3145736 | tf_op jit(solution)/shard_map/ppermute | solution.py:289
  2.6 13.7 %collective-permute-start = (bf16[24,8320]{1,0:T(8,128)(2,1)}, bf16[24,8320]{1,0:T(8,128)(2,1)S(1)}, u32[]{:S(2)}, u32[]{:S(2)}) collective-permute-start(bf16[24,8320]{1,0:T(8,128)(2,1)} %shard_map.73.refs_0_), channel_id=1, source_target_pairs={{0,4},{1,5},{2,6},{3,7},{4,12},{5,13},{6,14},{7,15},{12,8},{13,9},... | collective-permute-start | bytes 1198088 | tf_op jit(solution)/shard_map/ppermute | solution.py:289
  5.6 11.1 %collective-permute-start.2 = (bf16[24,8320]{1,0:T(8,128)(2,1)}, bf16[24,8320]{1,0:T(8,128)(2,1)S(1)}, u32[]{:S(2)}, u32[]{:S(2)}) collective-permute-start(bf16[24,8320]{1,0:T(8,128)(2,1)} %shard_map.73.refs_0_), channel_id=1, source_target_pairs={{0,2},{1,3},{2,0},{3,1},{4,6},{5,7},{6,4},{7,5},{12,14},{13,15},{1... | collective-permute-start | bytes 1198088 | tf_op jit(solution)/shard_map/ppermute | solution.py:289
  7.2 52.0 %collective-permute-start.13 = (bf16[1024,512]{1,0:T(8,128)(2,1)}, bf16[1024,512]{1,0:T(8,128)(2,1)S(1)}, u32[]{:S(2)}, u32[]{:S(2)}) collective-permute-start(bf16[1024,512]{1,0:T(8,128)(2,1)} %bitcast.27), channel_id=1, source_target_pairs={{0,1},{1,0},{2,3},{3,2},{4,5},{5,4},{6,7},{7,6},{12,13},{13,12},{1... | collective-permute-start | bytes 3145736 | tf_op jit(solution)/shard_map/ppermute | solution.py:289
  16.7 12.7 %collective-permute-start.1 = (bf16[24,8320]{1,0:T(8,128)(2,1)S(1)}, bf16[24,8320]{1,0:T(8,128)(2,1)S(1)}, u32[]{:S(2)}, u32[]{:S(2)}) collective-permute-start(bf16[24,8320]{1,0:T(8,128)(2,1)S(1)} %collective-permute-done.block_ref.refs_0_), channel_id=1, source_target_pairs={{0,4},{1,5},{2,6},{3,7},{4,12},{5,13},{6,14},{7,15},{12,8},{13,9},... | collective-permute-start | bytes 1198088 | tf_op jit(solution)/shard_map/ppermute | solution.py:289
  19.3 10.1 %collective-permute-start.5 = (bf16[24,8320]{1,0:T(8,128)(2,1)S(1)}, bf16[24,8320]{1,0:T(8,128)(2,1)S(1)}, u32[]{:S(2)}, u32[]{:S(2)}) collective-permute-start(bf16[24,8320]{1,0:T(8,128)(2,1)S(1)} %collective-permute-done.block_ref.refs_0_), channel_id=1, source_target_pairs={{0,2},{1,3},{2,0},{3,1},{4,6},{5,7},{6,4},{7,5},{12,14},{13,15},{1... | collective-permute-start | bytes 1198088 | tf_op jit(solution)/shard_map/ppermute | solution.py:289
  20.8 1.2 %copy-start = (bf16[1,8192,64]{1,2,0:T(8,128)(2,1)S(1)}, bf16[1,8192,64]{1,2,0:T(8,128)(2,1)}, u32[]{:S(2)}) copy-start(bf16[1,8192,64]{1,2,0:T(8,128)(2,1)} %param.10) | copy-start | bytes 3145732
  22.1 1.0 %copy-start.2 = (bf16[24,8320]{1,0:T(8,128)(2,1)S(1)}, bf16[24,8320]{1,0:T(8,128)(2,1)}, u32[]{:S(2)}) copy-start(bf16[24,8320]{1,0:T(8,128)(2,1)} %shard_map.73.refs_0_) | copy-start | bytes 1198084
  23.1 9.9 %slice-start = ((s8[8388608]{0:T(1024)(128)(4,1)}), s8[4194304]{0:T(1024)(128)(4,1)S(1)}, s32[]{:S(2)}) async-start(s8[8388608]{0:T(1024)(128)(4,1)} %bitcast.29), calls=%async_computation.1 | async-start | bytes 8388608
  24.0 8.1 %copy-start.1 = (bf16[1,8192,64]{1,2,0:T(8,128)(2,1)S(1)}, bf16[1,8192,64]{1,2,0:T(8,128)(2,1)}, u32[]{:S(2)}) copy-start(bf16[1,8192,64]{1,2,0:T(8,128)(2,1)} %param.10) | copy-start | bytes 3145732
  24.0 9.0 %slice-start.1 = ((s8[8388608]{0:T(1024)(128)(4,1)}), s8[4194304]{0:T(1024)(128)(4,1)S(1)}, s32[]{:S(2)}) async-start(s8[8388608]{0:T(1024)(128)(4,1)} %bitcast.29), calls=%async_computation.2 | async-start | bytes 8388608
  29.5 10.4 %collective-permute-start.4 = (bf16[24,8320]{1,0:T(8,128)(2,1)S(1)}, bf16[24,8320]{1,0:T(8,128)(2,1)S(1)}, u32[]{:S(2)}, u32[]{:S(2)}) collective-permute-start(bf16[24,8320]{1,0:T(8,128)(2,1)S(1)} %collective-permute-done.1.block_ref.refs_0_), channel_id=1, source_target_pairs={{0,4},{1,5},{2,6},{3,7},{4,12},{5,13},{6,14},{7,15},{12,8},{13,9},... | collective-permute-start | bytes 1198088 | tf_op jit(solution)/shard_map/ppermute | solution.py:289
  30.7 9.5 %collective-permute-start.7 = (bf16[24,8320]{1,0:T(8,128)(2,1)S(1)}, bf16[24,8320]{1,0:T(8,128)(2,1)S(1)}, u32[]{:S(2)}, u32[]{:S(2)}) collective-permute-start(bf16[24,8320]{1,0:T(8,128)(2,1)S(1)} %collective-permute-done.1.block_ref.refs_0_), channel_id=1, source_target_pairs={{0,2},{1,3},{2,0},{3,1},{4,6},{5,7},{6,4},{7,5},{12,14},{13,15},{1... | collective-permute-start | bytes 1198088 | tf_op jit(solution)/shard_map/ppermute | solution.py:289
  40.2 7.9 %collective-permute-start.8 = (bf16[24,8320]{1,0:T(8,128)(2,1)S(1)}, bf16[24,8320]{1,0:T(8,128)(2,1)S(1)}, u32[]{:S(2)}, u32[]{:S(2)}) collective-permute-start(bf16[24,8320]{1,0:T(8,128)(2,1)S(1)} %broadcast_select_fusion), channel_id=1, source_target_pairs={{0,2},{2,0},{4,6},{6,4},{12,14},{14,12},{8,10},{10,8},{1,5},{3,7},... | collective-permute-start | bytes 1198088 | tf_op jit(solution)/shard_map/ppermute | solution.py:324
  49.1 5.7 %collective-permute-start.10 = (bf16[96,128]{1,0:T(8,128)(2,1)S(1)}, bf16[96,128]{1,0:T(8,128)(2,1)S(1)}, u32[]{:S(2)}, u32[]{:S(2)}) collective-permute-start(bf16[96,128]{1,0:T(8,128)(2,1)S(1)} %get-tuple-element.66.refs_0_), channel_id=1, source_target_pairs={{0,12},{1,13},{2,14},{3,15},{4,8},{5,9},{6,10},{7,11},{12,0},{13,1... | collective-permute-start | bytes 73736 | tf_op jit(solution)/shard_map/ppermute | solution.py:289
  50.4 4.3 %collective-permute-start.11 = (bf16[96,128]{1,0:T(8,128)(2,1)S(1)}, bf16[96,128]{1,0:T(8,128)(2,1)S(1)}, u32[]{:S(2)}, u32[]{:S(2)}) collective-permute-start(bf16[96,128]{1,0:T(8,128)(2,1)S(1)} %get-tuple-element.66.refs_0_), channel_id=1, source_target_pairs={{0,8},{1,9},{2,10},{3,11},{4,0},{5,1},{6,2},{7,3},{12,4},{13,5},{1... | collective-permute-start | bytes 73736 | tf_op jit(solution)/shard_map/ppermute | solution.py:289
  51.2 4.7 %collective-permute-start.9 = (bf16[96,128]{1,0:T(8,128)(2,1)S(1)}, bf16[96,128]{1,0:T(8,128)(2,1)S(1)}, u32[]{:S(2)}, u32[]{:S(2)}) collective-permute-start(bf16[96,128]{1,0:T(8,128)(2,1)S(1)} %get-tuple-element.66.refs_0_), channel_id=1, source_target_pairs={{0,4},{1,5},{2,6},{3,7},{4,12},{5,13},{6,14},{7,15},{12,8},{13,9},... | collective-permute-start | bytes 73736 | tf_op jit(solution)/shard_map/ppermute | solution.py:289
  56.0 3.9 %copy-start.3 = (bf16[16,64,512]{2,1,0:T(8,128)(2,1)S(1)}, bf16[16,64,512]{2,1,0:T(8,128)(2,1)}, u32[]{:S(2)}) copy-start(bf16[16,64,512]{2,1,0:T(8,128)(2,1)} %param.11) | copy-start | bytes 3145732
  56.1 3.9 %collective-permute-start.12 = (bf16[96,128]{1,0:T(8,128)(2,1)S(1)}, bf16[96,128]{1,0:T(8,128)(2,1)S(1)}, u32[]{:S(2)}, u32[]{:S(2)}) collective-permute-start(bf16[96,128]{1,0:T(8,128)(2,1)S(1)} %shard_map.82.refs_0_), channel_id=1, source_target_pairs={{0,2},{1,3},{2,0},{3,1},{4,6},{5,7},{6,4},{7,5},{12,14},{13,15},{1... | collective-permute-start | bytes 73736 | tf_op jit(solution)/shard_map/ppermute | solution.py:289

commit v14 on v13

--- a/solution.py
+++ b/solution.py
@@ -13,6 +13,7 @@
 CORNERS = SIDE * CORES
 LANES = 128
 CHUNK = 1024
+PIECES = 4
 VMEM_LIMIT = 24 << 20
 VMEM = pl.BlockSpec(memory_space=pltpu.VMEM)
 
@@ -214,6 +215,35 @@
         compiler_params=pltpu.CompilerParams(vmem_limit_bytes=VMEM_LIMIT),
         cost_estimate=pl.CostEstimate(flops=1, bytes_accessed=1, transcendentals=0),
     )(*blocks, weight)
+
+
+def load_kernel(*refs):
+    *refs, sems = refs
+    count = len(refs) // 2
+    copies = []
+    for number, (source, target) in enumerate(zip(refs[:count], refs[count:])):
+        size = source.shape[0] // PIECES
+        for piece in range(PIECES):
+            here = pl.ds(piece * size, size)
+            copies.append(
+                pltpu.make_async_copy(source.at[here], target.at[here], sems.at[number, piece])
+            )
+    for copy in copies:
+        copy.start()
+    for copy in copies:
+        copy.wait()
+
+
+def load(*arrays):
+    return pl.pallas_call(
+        load_kernel,
+        out_shape=[jax.ShapeDtypeStruct(x.shape, x.dtype) for x in arrays],
+        in_specs=[pl.BlockSpec(memory_space=pltpu.HBM)] * len(arrays),
+        out_specs=[VMEM] * len(arrays),
+        scratch_shapes=[pltpu.SemaphoreType.DMA((len(arrays), PIECES))],
+        compiler_params=pltpu.CompilerParams(vmem_limit_bytes=VMEM_LIMIT),
+        cost_estimate=pl.CostEstimate(flops=1, bytes_accessed=1, transcendentals=0),
+    )(*arrays)
 
 
 def token_kernel(block_ref, out_ref):
@@ -300,6 +330,7 @@
     block, other = [normalize(hidden, norm_weight, adapter_index, adapter_slot)], []
     parts, slots, rows, bases, tokens = [], [], [], [], []
     last = places - 1
+    query_weight, down = load(*after([query_weight, down], block[0]))
 
     def meet(blocks, before=()):
         part, slot, here = shrink_rows(blocks, down, down_other, before, tokens if before else ())
@@ -309,7 +340,7 @@
 
     for step in range(last):
         if step:
-            block[step] = after(block[step], *bases[-1:])
+            block[step] = after(block[step], *(bases[-1:] or [query_weight]))
             tokens.append(token(block[step]))
         block.append(move(after(block[step], *tokens[-1:]), 1, 0))
         other.append(move(after(block[step], *other[-1:]), 0, 2))

time: 74.4 us -> 76 us (1.022)
  waiting for transfers between devices: 17.4 us -> 11.6 us
  local copies, waits for them, and re-layouts: 3.02 us -> 8.61 us
  Pallas kernels: 10.3 us -> 12.2 us
    ppermute x13, waiting for transfers between devices: 14.2 us -> 8.41 us  [move(): return lax.ppermute(x, 'adapter', pairs(places, steps, flip))]
    unnamed x12 -> x14, local copies, waits for them, and re-layouts: 2.24 us -> 7.83 us
    pallas_call x6, Pallas kernels: 4.48 us -> 5.66 us  [call(): pl.pallas_call(kernel, out_shape=out_shape, in_specs=[VMEM] * len(operand...]
  transfers between devices with their start and end apart: 14 -> 14, of which waited for: 8 -> 9; matrix products, arithmetic and copies ran while one was open for 18% -> 17% of each run, Pallas kernels for 13% -> 14%
where the time goes in v14:
time: 76 us; the launch traced here: 75.7 us
  starting transfers between devices  17.2 us (23%)
  blocking collectives  13.1 us (17%)
  matrix products  12.9 us (17%)
  Pallas kernels  12.2 us (16%)
  waiting for transfers between devices  11.6 us (15%)
  local copies, waits for them, and re-layouts  8.61 us (11%)
    ppermute x13, starting transfers between devices, move(): return lax.ppermute(x, 'adapter', pairs(places, steps, flip))  16.4 us
    all_to_all x1, blocking collectives, shards(): lax.all_to_all(query, 'adapter', 0, 0, axis_index_groups=groups, tiled=True)  13.1 us
    dot_general x6, matrix products, base_rows(): return jnp.dot(rows, weight, preferred_element_type=jnp.float32)  12.9 us
    ppermute x13, waiting for transfers between devices, move(): return lax.ppermute(x, 'adapter', pairs(places, steps, flip))  8.41 us
    unnamed x14, local copies, waits for them, and re-layouts  7.83 us
    pallas_call x6, Pallas kernels, call(): pl.pallas_call(kernel, out_shape=out_shape, in_specs=[VMEM] * len(operand...  5.66 us
    pallas_call x1, Pallas kernels, base_and_weight(): pl.pallas_call(base_kernel, out_shape=(jax.ShapeDtypeStruct((rows, weight...  3.78 us
    ppermute x1, waiting for transfers between devices, shards(): crossed = lax.ppermute(source, 'adapter', split_pairs(places))  3.17 us
  transfers between devices with their start and end apart: 14, of which 9 were waited for; matrix products, arithmetic and copies ran while one was open for 17% of the time, Pallas kernels for 14%

profile of v14, /device:TPU:0, one launch (start us, length us, event | category | flops | bytes accessed | tf_op | source)
XLA Modules:
  0.0 75.7 jit_solution(11126507830363701403)
XLA Ops:
  0.5 2.0 %shard_map.73.refs_0_ = bf16[24,8320]{1,0:T(8,128)(2,1)} custom-call(bf16[24,8192]{1,0:T(8,128)(2,1)} %refs_0_.1, f32[1,8192]{1,0:T(1,128)} %bitcast.29, s32[1,24]{1,0:T(1,128)} %bitcast.30, s32[1,16]{1,0:T(1,128)} %bitcast.31), custom_call_target="tpu_custom_call" | custom-call | tf_op jit(solution)/shard_map/pallas_call | solution.py:110
  2.5 3.1 %collective-permute-start = (bf16[24,8320]{1,0:T(8,128)(2,1)}, bf16[24,8320]{1,0:T(8,128)(2,1)S(1)}, u32[]{:S(2)}, u32[]{:S(2)}) collective-permute-start(bf16[24,8320]{1,0:T(8,128)(2,1)} %shard_map.73.refs_0_), channel_id=1, source_target_pairs={{0,4},{1,5},{2,6},{3,7},{4,12},{5,13},{6,14},{7,15},{12,8},{13,9},... | collective-permute-start | bytes 1198088 | tf_op jit(solution)/shard_map/ppermute | solution.py:319
  5.6 1.5 %collective-permute-start.2 = (bf16[24,8320]{1,0:T(8,128)(2,1)}, bf16[24,8320]{1,0:T(8,128)(2,1)S(1)}, u32[]{:S(2)}, u32[]{:S(2)}) collective-permute-start(bf16[24,8320]{1,0:T(8,128)(2,1)} %shard_map.73.refs_0_), channel_id=1, source_target_pairs={{0,2},{1,3},{2,0},{3,1},{4,6},{5,7},{6,4},{7,5},{12,14},{13,15},{1... | collective-permute-start | bytes 1198088 | tf_op jit(solution)/shard_map/ppermute | solution.py:319
  7.1 3.4 %copy-done.1 = bf16[8192,512]{1,0:T(8,128)(2,1)S(1)} copy-done((bf16[8192,512]{1,0:T(8,128)(2,1)S(1)}, bf16[8192,512]{1,0:T(8,128)(2,1)}, u32[]{:S(2)}) %copy-start.1) | copy-done | bytes 8388632
  10.5 1.2 %copy-done.3 = bf16[1,8192,64]{1,2,0:T(8,128)(2,1)S(1)} copy-done((bf16[1,8192,64]{1,2,0:T(8,128)(2,1)S(1)}, bf16[1,8192,64]{1,2,0:T(8,128)(2,1)}, u32[]{:S(2)}) %copy-start.3) | copy-done | bytes 1048600
  12.5 3.2 %copy-done = bf16[8192,512]{1,0:T(8,128)(2,1)} copy-done((bf16[8192,512]{1,0:T(8,128)(2,1)}, bf16[8192,512]{1,0:T(8,128)(2,1)S(1)}, u32[]{:S(2)}) %copy-start) | copy-done | bytes 8388632
  16.7 2.6 %collective-permute-start.1 = (bf16[24,8320]{1,0:T(8,128)(2,1)S(1)}, bf16[24,8320]{1,0:T(8,128)(2,1)S(1)}, u32[]{:S(2)}, u32[]{:S(2)}) collective-permute-start(bf16[24,8320]{1,0:T(8,128)(2,1)S(1)} %collective-permute-done.block_ref.refs_0_), channel_id=1, source_target_pairs={{0,4},{1,5},{2,6},{3,7},{4,12},{5,13},{6,14},{7,15},{12,8},{13,9},... | collective-permute-start | bytes 1198088 | tf_op jit(solution)/shard_map/ppermute | solution.py:319
  19.3 1.5 %collective-permute-start.5 = (bf16[24,8320]{1,0:T(8,128)(2,1)S(1)}, bf16[24,8320]{1,0:T(8,128)(2,1)S(1)}, u32[]{:S(2)}, u32[]{:S(2)}) collective-permute-start(bf16[24,8320]{1,0:T(8,128)(2,1)S(1)} %collective-permute-done.block_ref.refs_0_), channel_id=1, source_target_pairs={{0,2},{1,3},{2,0},{3,1},{4,6},{5,7},{6,4},{7,5},{12,14},{13,15},{1... | collective-permute-start | bytes 1198088 | tf_op jit(solution)/shard_map/ppermute | solution.py:319
  21.7 5.3 %fusion.refs_2_ = f32[48,512]{1,0:T(8,128)S(1)} fusion(bf16[48,8192]{1,0:T(8,128)(2,1)S(1)} %get-tuple-element.60.refs_0_, bf16[8192,512]{1,0:T(8,128)(2,1)} %copy-done), kind=kOutput, calls=%fused_computation.1 | convolution fusion | flops 402653184 | bytes 9273344 | tf_op jit(solution)/shard_map/dot_general | solution.py:322
  27.0 1.3 %collective-permute-done.1.block_ref.refs_0_ = bf16[24,8320]{1,0:T(8,128)(2,1)S(1)} collective-permute-done((bf16[24,8320]{1,0:T(8,128)(2,1)S(1)}, bf16[24,8320]{1,0:T(8,128)(2,1)S(1)}, u32[]{:S(2)}, u32[]{:S(2)}) %collective-permute-start.1) | collective-permute-done | bytes 399392 | tf_op jit(solution)/shard_map/ppermute | solution.py:319
  28.3 1.4 %collective-permute-done.5.refs_1_ = bf16[24,8320]{1,0:T(8,128)(2,1)S(1)} collective-permute-done((bf16[24,8320]{1,0:T(8,128)(2,1)S(1)}, bf16[24,8320]{1,0:T(8,128)(2,1)S(1)}, u32[]{:S(2)}, u32[]{:S(2)}) %collective-permute-start.5) | collective-permute-done | bytes 399392 | tf_op jit(solution)/shard_map/ppermute | solution.py:319
  30.5 1.5 %collective-permute-start.7 = (bf16[24,8320]{1,0:T(8,128)(2,1)S(1)}, bf16[24,8320]{1,0:T(8,128)(2,1)S(1)}, u32[]{:S(2)}, u32[]{:S(2)}) collective-permute-start(bf16[24,8320]{1,0:T(8,128)(2,1)S(1)} %collective-permute-done.1.block_ref.refs_0_), channel_id=1, source_target_pairs={{0,2},{1,3},{2,0},{3,1},{4,6},{5,7},{6,4},{7,5},{12,14},{13,15},{1... | collective-permute-start | bytes 1198088 | tf_op jit(solution)/shard_map/ppermute | solution.py:319
  32.9 1.5 %fusion.1.refs_3_ = f32[48,512]{1,0:T(8,128)S(1)} fusion(bf16[48,8192]{1,0:T(8,128)(2,1)S(1)} %get-tuple-element.61.refs_1_, bf16[8192,512]{1,0:T(8,128)(2,1)S(1)} %bitcast.23), kind=kOutput, calls=%fused_computation.2 | convolution fusion | flops 402653184 | bytes 9273344 | tf_op jit(solution)/shard_map/dot_general | solution.py:322
  34.5 3.8 %shard_map.79 = (f32[96,512]{1,0:T(8,128)S(1)}, bf16[8192,512]{1,0:T(8,128)(2,1)S(1)}) custom-call(bf16[48,8192]{1,0:T(8,128)(2,1)S(1)} %get-tuple-element.60.refs_0_, bf16[48,8192]{1,0:T(8,128)(2,1)S(1)} %get-tuple-element.61.refs_1_, bf16[8192,512]{1,0:T(8,128)(2,1)} %collective-permute-done.6.refs_2_), custom_call_target="tpu_custom_call" | custom-call | flops 1 | bytes 1 | tf_op jit(solution)/shard_map/pallas_call | solution.py:206
  38.3 1.9 %collective-permute-done.4.block_ref.refs_3_ = bf16[24,8320]{1,0:T(8,128)(2,1)S(1)} collective-permute-done((bf16[24,8320]{1,0:T(8,128)(2,1)S(1)}, bf16[24,8320]{1,0:T(8,128)(2,1)S(1)}, u32[]{:S(2)}, u32[]{:S(2)}) %collective-permute-start.4) | collective-permute-done | bytes 399392 | tf_op jit(solution)/shard_map/ppermute | solution.py:319
  41.8 1.5 %fusion.2.refs_4_ = f32[48,512]{1,0:T(8,128)S(1)} fusion(bf16[48,8192]{1,0:T(8,128)(2,1)S(1)} %get-tuple-element.68, bf16[8192,512]{1,0:T(8,128)(2,1)S(1)} %bitcast.23), kind=kOutput, calls=%fused_computation.3 | convolution fusion | flops 402653184 | bytes 9273344 | tf_op jit(solution)/shard_map/dot_general | solution.py:322
  43.4 1.5 %fusion.3.refs_7_ = f32[48,512]{1,0:T(8,128)S(1)} fusion(bf16[48,8192]{1,0:T(8,128)(2,1)S(1)} %get-tuple-element.68, bf16[8192,512]{1,0:T(8,128)(2,1)S(1)} %get-tuple-element.69), kind=kOutput, calls=%fused_computation.4 | convolution fusion | flops 402653184 | bytes 9273344 | tf_op jit(solution)/shard_map/dot_general | solution.py:322
  44.9 3.2 %collective-permute-done.8.refs_4_ = bf16[24,8320]{1,0:T(8,128)(2,1)S(1)} collective-permute-done((bf16[24,8320]{1,0:T(8,128)(2,1)S(1)}, bf16[24,8320]{1,0:T(8,128)(2,1)S(1)}, u32[]{:S(2)}, u32[]{:S(2)}) %collective-permute-start.8) | collective-permute-done | bytes 399392 | tf_op jit(solution)/shard_map/ppermute | solution.py:355
  49.0 1.3 %collective-permute-start.10 = (bf16[96,128]{1,0:T(8,128)(2,1)S(1)}, bf16[96,128]{1,0:T(8,128)(2,1)S(1)}, u32[]{:S(2)}, u32[]{:S(2)}) collective-permute-start(bf16[96,128]{1,0:T(8,128)(2,1)S(1)} %get-tuple-element.76.refs_0_), channel_id=1, source_target_pairs={{0,12},{1,13},{2,14},{3,15},{4,8},{5,9},{6,10},{7,11},{12,0},{13,1... | collective-permute-start | bytes 73736 | tf_op jit(solution)/shard_map/ppermute | solution.py:319
  52.4 1.5 %fusion.4.refs_5_ = f32[48,512]{1,0:T(8,128)S(1)} fusion(bf16[48,8192]{1,0:T(8,128)(2,1)S(1)} %get-tuple-element.80, bf16[8192,512]{1,0:T(8,128)(2,1)S(1)} %bitcast.23), kind=kOutput, calls=%fused_computation.5 | convolution fusion | flops 402653184 | bytes 9273344 | tf_op jit(solution)/shard_map/dot_general | solution.py:322
  56.0 1.6 %collective-permute-start.12 = (bf16[96,128]{1,0:T(8,128)(2,1)S(1)}, bf16[96,128]{1,0:T(8,128)(2,1)S(1)}, u32[]{:S(2)}, u32[]{:S(2)}) collective-permute-start(bf16[96,128]{1,0:T(8,128)(2,1)S(1)} %shard_map.83.refs_0_), channel_id=1, source_target_pairs={{0,2},{1,3},{2,0},{3,1},{4,6},{5,7},{6,4},{7,5},{12,14},{13,15},{1... | collective-permute-start | bytes 73736 | tf_op jit(solution)/shard_map/ppermute | solution.py:319
  57.6 1.5 %fusion.5.refs_8_ = f32[48,512]{1,0:T(8,128)S(1)} fusion(bf16[48,8192]{1,0:T(8,128)(2,1)S(1)} %get-tuple-element.80, bf16[8192,512]{1,0:T(8,128)(2,1)S(1)} %get-tuple-element.69), kind=kOutput, calls=%fused_computation.6 | convolution fusion | flops 402653184 | bytes 9273344 | tf_op jit(solution)/shard_map/dot_general | solution.py:322
  59.9 1.9 %shard_map.84 = bf16[8,24,1024]{2,1,0:T(8,128)(2,1)S(1)} custom-call(bf16[96,128]{1,0:T(8,128)(2,1)S(1)} %shard_map.83.refs_0_, bf16[96,128]{1,0:T(8,128)(2,1)S(1)} %collective-permute-done.12.refs_1_, f32[48,512]{1,0:T(8,128)S(1)} %fusion.refs_2_, f32[48,512]{1,0:T(8,128)S(1)} %fusion.1.refs_3_, f32[48,512]{1,0:T(8,128)S(1)} %fusion.2.refs_4_, ...), custom_call_target="tpu_custom_call" | custom-call | flops 1 | bytes 1 | tf_op jit(solution)/shard_map/pallas_call | solution.py:58
  61.8 13.1 %all_to_all.5 = bf16[8,24,1024]{2,1,0:T(8,128)(2,1)S(1)} all-to-all(bf16[8,24,1024]{2,1,0:T(8,128)(2,1)S(1)} %shard_map.84), channel_id=1, replica_groups={{0,2,4,6,8,10,12,14},{1,3,5,7,9,11,13,15},{16,18,20,22,24,26,28,30},{17..., dimensions={0} | all-to-all | bytes 786432 | tf_op jit(solution)/shard_map/all_to_all | solution.py:372
  (40 shorter events, 13.2 us)
Async XLA Ops:
  0.0 34.5 %collective-permute-start.6 = (bf16[8192,512]{1,0:T(8,128)(2,1)}, bf16[8192,512]{1,0:T(8,128)(2,1)}, u32[]{:S(2)}, u32[]{:S(2)}) collective-permute-start(bf16[8192,512]{1,0:T(8,128)(2,1)} %refs_0_.2), channel_id=1, source_target_pairs={{0,1},{1,0},{2,3},{3,2},{4,5},{5,4},{6,7},{7,6},{12,13},{13,12},{1... | collective-permute-start | bytes 25165832 | tf_op jit(solution)/shard_map/ppermute | solution.py:319
  0.5 20.4 %collective-permute-start.3 = (bf16[64,8192]{1,0:T(8,128)(2,1)}, bf16[64,8192]{1,0:T(8,128)(2,1)S(1)}, u32[]{:S(2)}, u32[]{:S(2)}) collective-permute-start(bf16[64,8192]{1,0:T(8,128)(2,1)} %bitcast.24), channel_id=1, source_target_pairs={{0,1},{1,0},{2,3},{3,2},{4,5},{5,4},{6,7},{7,6},{12,13},{13,12},{1... | collective-permute-start | bytes 3145736 | tf_op jit(solution)/shard_map/ppermute | solution.py:319
  2.5 13.7 %collective-permute-start = (bf16[24,8320]{1,0:T(8,128)(2,1)}, bf16[24,8320]{1,0:T(8,128)(2,1)S(1)}, u32[]{:S(2)}, u32[]{:S(2)}) collective-permute-start(bf16[24,8320]{1,0:T(8,128)(2,1)} %shard_map.73.refs_0_), channel_id=1, source_target_pairs={{0,4},{1,5},{2,6},{3,7},{4,12},{5,13},{6,14},{7,15},{12,8},{13,9},... | collective-permute-start | bytes 1198088 | tf_op jit(solution)/shard_map/ppermute | solution.py:319
  5.6 11.1 %collective-permute-start.2 = (bf16[24,8320]{1,0:T(8,128)(2,1)}, bf16[24,8320]{1,0:T(8,128)(2,1)S(1)}, u32[]{:S(2)}, u32[]{:S(2)}) collective-permute-start(bf16[24,8320]{1,0:T(8,128)(2,1)} %shard_map.73.refs_0_), channel_id=1, source_target_pairs={{0,2},{1,3},{2,0},{3,1},{4,6},{5,7},{6,4},{7,5},{12,14},{13,15},{1... | collective-permute-start | bytes 1198088 | tf_op jit(solution)/shard_map/ppermute | solution.py:319
  7.1 52.0 %collective-permute-start.13 = (bf16[1024,512]{1,0:T(8,128)(2,1)}, bf16[1024,512]{1,0:T(8,128)(2,1)}, u32[]{:S(2)}, u32[]{:S(2)}) collective-permute-start(bf16[1024,512]{1,0:T(8,128)(2,1)} %bitcast.26), channel_id=1, source_target_pairs={{0,1},{1,0},{2,3},{3,2},{4,5},{5,4},{6,7},{7,6},{12,13},{13,12},{1... | collective-permute-start | bytes 3145736 | tf_op jit(solution)/shard_map/ppermute | solution.py:319
  7.1 3.4 %copy-start.1 = (bf16[8192,512]{1,0:T(8,128)(2,1)S(1)}, bf16[8192,512]{1,0:T(8,128)(2,1)}, u32[]{:S(2)}) copy-start(bf16[8192,512]{1,0:T(8,128)(2,1)} %refs_0_.2) | copy-start | bytes 25165828
  10.5 1.2 %copy-start.3 = (bf16[1,8192,64]{1,2,0:T(8,128)(2,1)S(1)}, bf16[1,8192,64]{1,2,0:T(8,128)(2,1)}, u32[]{:S(2)}) copy-start(bf16[1,8192,64]{1,2,0:T(8,128)(2,1)} %param.10) | copy-start | bytes 3145732
  11.7 9.1 %copy-start.2 = (bf16[24,8320]{1,0:T(8,128)(2,1)S(1)}, bf16[24,8320]{1,0:T(8,128)(2,1)}, u32[]{:S(2)}) copy-start(bf16[24,8320]{1,0:T(8,128)(2,1)} %shard_map.73.refs_0_) | copy-start | bytes 1198084
  12.5 3.2 %copy-start = (bf16[8192,512]{1,0:T(8,128)(2,1)}, bf16[8192,512]{1,0:T(8,128)(2,1)S(1)}, u32[]{:S(2)}) copy-start(bf16[8192,512]{1,0:T(8,128)(2,1)S(1)} %get-tuple-element.47) | copy-start | bytes 25165828
  16.7 11.6 %collective-permute-start.1 = (bf16[24,8320]{1,0:T(8,128)(2,1)S(1)}, bf16[24,8320]{1,0:T(8,128)(2,1)S(1)}, u32[]{:S(2)}, u32[]{:S(2)}) collective-permute-start(bf16[24,8320]{1,0:T(8,128)(2,1)S(1)} %collective-permute-done.block_ref.refs_0_), channel_id=1, source_target_pairs={{0,4},{1,5},{2,6},{3,7},{4,12},{5,13},{6,14},{7,15},{12,8},{13,9},... | collective-permute-start | bytes 1198088 | tf_op jit(solution)/shard_map/ppermute | solution.py:319
  19.3 10.4 %collective-permute-start.5 = (bf16[24,8320]{1,0:T(8,128)(2,1)S(1)}, bf16[24,8320]{1,0:T(8,128)(2,1)S(1)}, u32[]{:S(2)}, u32[]{:S(2)}) collective-permute-start(bf16[24,8320]{1,0:T(8,128)(2,1)S(1)} %collective-permute-done.block_ref.refs_0_), channel_id=1, source_target_pairs={{0,2},{1,3},{2,0},{3,1},{4,6},{5,7},{6,4},{7,5},{12,14},{13,15},{1... | collective-permute-start | bytes 1198088 | tf_op jit(solution)/shard_map/ppermute | solution.py:319
  20.8 12.1 %slice-start = ((s8[8388608]{0:T(1024)(128)(4,1)}), s8[4194304]{0:T(1024)(128)(4,1)S(1)}, s32[]{:S(2)}) async-start(s8[8388608]{0:T(1024)(128)(4,1)} %bitcast.22), calls=%async_computation.1 | async-start | bytes 8388608
  21.7 11.2 %slice-start.1 = ((s8[8388608]{0:T(1024)(128)(4,1)}), s8[4194304]{0:T(1024)(128)(4,1)S(1)}, s32[]{:S(2)}) async-start(s8[8388608]{0:T(1024)(128)(4,1)} %bitcast.22), calls=%async_computation.2 | async-start | bytes 8388608
  29.7 10.4 %collective-permute-start.4 = (bf16[24,8320]{1,0:T(8,128)(2,1)S(1)}, bf16[24,8320]{1,0:T(8,128)(2,1)S(1)}, u32[]{:S(2)}, u32[]{:S(2)}) collective-permute-start(bf16[24,8320]{1,0:T(8,128)(2,1)S(1)} %collective-permute-done.1.block_ref.refs_0_), channel_id=1, source_target_pairs={{0,4},{1,5},{2,6},{3,7},{4,12},{5,13},{6,14},{7,15},{12,8},{13,9},... | collective-permute-start | bytes 1198088 | tf_op jit(solution)/shard_map/ppermute | solution.py:319
  30.5 9.6 %collective-permute-start.7 = (bf16[24,8320]{1,0:T(8,128)(2,1)S(1)}, bf16[24,8320]{1,0:T(8,128)(2,1)S(1)}, u32[]{:S(2)}, u32[]{:S(2)}) collective-permute-start(bf16[24,8320]{1,0:T(8,128)(2,1)S(1)} %collective-permute-done.1.block_ref.refs_0_), channel_id=1, source_target_pairs={{0,2},{1,3},{2,0},{3,1},{4,6},{5,7},{6,4},{7,5},{12,14},{13,15},{1... | collective-permute-start | bytes 1198088 | tf_op jit(solution)/shard_map/ppermute | solution.py:319
  40.2 7.9 %collective-permute-start.8 = (bf16[24,8320]{1,0:T(8,128)(2,1)S(1)}, bf16[24,8320]{1,0:T(8,128)(2,1)S(1)}, u32[]{:S(2)}, u32[]{:S(2)}) collective-permute-start(bf16[24,8320]{1,0:T(8,128)(2,1)S(1)} %broadcast_select_fusion), channel_id=1, source_target_pairs={{0,2},{2,0},{4,6},{6,4},{12,14},{14,12},{8,10},{10,8},{1,5},{3,7},... | collective-permute-start | bytes 1198088 | tf_op jit(solution)/shard_map/ppermute | solution.py:355
  49.0 5.7 %collective-permute-start.10 = (bf16[96,128]{1,0:T(8,128)(2,1)S(1)}, bf16[96,128]{1,0:T(8,128)(2,1)S(1)}, u32[]{:S(2)}, u32[]{:S(2)}) collective-permute-start(bf16[96,128]{1,0:T(8,128)(2,1)S(1)} %get-tuple-element.76.refs_0_), channel_id=1, source_target_pairs={{0,12},{1,13},{2,14},{3,15},{4,8},{5,9},{6,10},{7,11},{12,0},{13,1... | collective-permute-start | bytes 73736 | tf_op jit(solution)/shard_map/ppermute | solution.py:319
  50.3 4.4 %collective-permute-start.11 = (bf16[96,128]{1,0:T(8,128)(2,1)S(1)}, bf16[96,128]{1,0:T(8,128)(2,1)S(1)}, u32[]{:S(2)}, u32[]{:S(2)}) collective-permute-start(bf16[96,128]{1,0:T(8,128)(2,1)S(1)} %get-tuple-element.76.refs_0_), channel_id=1, source_target_pairs={{0,8},{1,9},{2,10},{3,11},{4,0},{5,1},{6,2},{7,3},{12,4},{13,5},{1... | collective-permute-start | bytes 73736 | tf_op jit(solution)/shard_map/ppermute | solution.py:319
  51.2 4.7 %collective-permute-start.9 = (bf16[96,128]{1,0:T(8,128)(2,1)S(1)}, bf16[96,128]{1,0:T(8,128)(2,1)S(1)}, u32[]{:S(2)}, u32[]{:S(2)}) collective-permute-start(bf16[96,128]{1,0:T(8,128)(2,1)S(1)} %get-tuple-element.76.refs_0_), channel_id=1, source_target_pairs={{0,4},{1,5},{2,6},{3,7},{4,12},{5,13},{6,14},{7,15},{12,8},{13,9},... | collective-permute-start | bytes 73736 | tf_op jit(solution)/shard_map/ppermute | solution.py:319
  56.0 3.9 %copy-start.4 = (bf16[16,64,512]{2,1,0:T(8,128)(2,1)S(1)}, bf16[16,64,512]{2,1,0:T(8,128)(2,1)}, u32[]{:S(2)}) copy-start(bf16[16,64,512]{2,1,0:T(8,128)(2,1)} %param.11) | copy-start | bytes 3145732
  56.0 3.9 %collective-permute-start.12 = (bf16[96,128]{1,0:T(8,128)(2,1)S(1)}, bf16[96,128]{1,0:T(8,128)(2,1)S(1)}, u32[]{:S(2)}, u32[]{:S(2)}) collective-permute-start(bf16[96,128]{1,0:T(8,128)(2,1)S(1)} %shard_map.83.refs_0_), channel_id=1, source_target_pairs={{0,2},{1,3},{2,0},{3,1},{4,6},{5,7},{6,4},{7,5},{12,14},{13,15},{1... | collective-permute-start | bytes 73736 | tf_op jit(solution)/shard_map/ppermute | solution.py:319

commit v15 on v13

--- a/solution.py
+++ b/solution.py
@@ -64,101 +64,154 @@
     )(*operands)
 
 
-def norm_kernel(*refs):
-    sources, (out_ref, *buffers, sems) = refs[:4], refs[4:]
+def slots_kernel(index_hbm, slot_hbm, out_ref, index_ref, slot_ref, sems):
     copies = [
-        pltpu.make_async_copy(source, buffer, sems.at[number])
-        for number, (source, buffer) in enumerate(zip(sources, buffers))
+        pltpu.make_async_copy(index_hbm, index_ref, sems.at[0]),
+        pltpu.make_async_copy(slot_hbm, slot_ref, sems.at[1]),
     ]
     for copy in copies:
         copy.start()
     for copy in copies:
         copy.wait()
-    hidden_ref, gain_ref, index_ref, slot_ref = buffers
-    rows, width = hidden_ref.shape
-    squares = jnp.zeros((rows, LANES), jnp.float32)
-    for start in range(0, width, CHUNK):
-        wide = hidden_ref[:, start : start + CHUNK].astype(jnp.float32)
-        wide = wide * wide
-        for lane in range(0, CHUNK, LANES):
-            squares = squares + wide[:, lane : lane + LANES]
-    inv_rms = lax.rsqrt(jnp.sum(squares, axis=1, keepdims=True) / width + EPS)
-    for start in range(0, width, CHUNK):
-        lanes = slice(start, start + CHUNK)
-        wide = hidden_ref[:, lanes].astype(jnp.float32)
-        out_ref[:, lanes] = (wide * inv_rms * gain_ref[:, lanes]).astype(jnp.bfloat16)
     index = index_ref[...]
     slot = jnp.zeros(index.shape, jnp.float32)
     for name in range(slot_ref.shape[1]):
         slot = jnp.where(index == name, slot_ref[0, name].astype(jnp.float32), slot)
-    across = lax.broadcasted_iota(jnp.int32, (rows, rows), 1)
-    down = lax.broadcasted_iota(jnp.int32, (rows, rows), 0)
-    column = jnp.sum(jnp.where(across == down, slot, 0.0), axis=1, keepdims=True)
-    out_ref[:, width:] = jnp.broadcast_to(column, (rows, LANES)).astype(jnp.bfloat16)
-
-
-def normalize(hidden, norm_weight, adapter_index, adapter_slot):
-    rows, width = hidden.shape
-    sources = (
-        hidden,
-        norm_weight.reshape(1, width),
-        adapter_index.reshape(1, rows),
-        adapter_slot.reshape(1, -1),
-    )
-    spaces = (pltpu.VMEM, pltpu.VMEM, pltpu.VMEM, pltpu.SMEM)
+    out_ref[...] = jnp.zeros(out_ref.shape, jnp.float32)
+    out_ref[0:1, 0 : index.shape[1]] = slot
+
+
+def own_slots(adapter_index, adapter_slot, places):
+    sources = (adapter_index.reshape(1, -1), adapter_slot.reshape(1, -1))
     return pl.pallas_call(
-        norm_kernel,
-        out_shape=jax.ShapeDtypeStruct((rows, width + LANES), jnp.bfloat16),
-        in_specs=[pl.BlockSpec(memory_space=pltpu.HBM)] * len(sources),
+        slots_kernel,
+        out_shape=jax.ShapeDtypeStruct((-(-places // 8) * 8, LANES), jnp.float32),
+        in_specs=[pl.BlockSpec(memory_space=pltpu.HBM)] * 2,
         out_specs=VMEM,
-        scratch_shapes=[space(x.shape, x.dtype) for space, x in zip(spaces, sources)]
-        + [pltpu.SemaphoreType.DMA((len(sources),))],
+        scratch_shapes=[
+            pltpu.VMEM(sources[0].shape, sources[0].dtype),
+            pltpu.SMEM(sources[1].shape, sources[1].dtype),
+            pltpu.SemaphoreType.DMA((2,)),
+        ],
     )(*sources)
 
 
-def shrink_kernel(halves, *refs):
-    blocks, (own_ref, other_ref, *before, part_ref, slot_ref, rows_ref) = refs[:SIDE], refs[SIDE:]
-    rank, width = own_ref.shape
-    rows = slot_ref.shape[0]
-    part = jnp.zeros((rows, 2 * rank), jnp.float32)
+def merge_kernel(count, near_ref, far_ref, out_ref):
+    out_ref[...] = near_ref[...]
+    out_ref[count : 2 * count, :] = far_ref[0:count, :]
+
+
+def merge(near, far, count):
+    out_shape = jax.ShapeDtypeStruct(near.shape, near.dtype)
+    return call(lambda *refs: merge_kernel(count, *refs), out_shape, (near, far))
+
+
+def slot_column(step, near_ref, across_ref, own_rows):
+    across = lax.broadcasted_iota(jnp.int32, (own_rows, LANES), 1)
+    down = lax.broadcasted_iota(jnp.int32, (own_rows, LANES), 0)
+    column = [
+        jnp.sum(jnp.where(across == down, ref[step : step + 1, :], 0.0), axis=1, keepdims=True)
+        for ref in (near_ref, across_ref)
+    ]
+    return jnp.concatenate(column, axis=0).astype(jnp.int32)
+
+
+def inverse_rms(block):
+    rows, width = block.shape
+    squares = jnp.zeros((rows, LANES), jnp.float32)
     for start in range(0, width, CHUNK):
+        wide = block[:, start : start + CHUNK].astype(jnp.float32)
+        wide = wide * wide
+        for lane in range(0, CHUNK, LANES):
+            squares = squares + wide[:, lane : lane + LANES]
+    return lax.rsqrt(jnp.sum(squares, axis=1, keepdims=True) / width + EPS)
+
+
+def normalized(blocks, inverse, gain_ref, lanes):
+    gain = gain_ref[:, lanes]
+    wide = [block[:, lanes].astype(jnp.float32) * inv * gain for block, inv in zip(blocks, inverse)]
+    return jnp.concatenate(wide, axis=0).astype(jnp.bfloat16)
+
+
+def norm_kernel(*refs):
+    *blocks, gain_ref, rows_ref = refs
+    inverse = [inverse_rms(block) for block in blocks]
+    for start in range(0, rows_ref.shape[1], CHUNK):
         lanes = slice(start, start + CHUNK)
-        wide = [block[:, lanes].astype(jnp.float32) for block in blocks]
-        chunk = jnp.concatenate(wide, axis=0).astype(jnp.bfloat16)
-        rows_ref[:, lanes] = chunk
-        down = jnp.concatenate([own_ref[:, lanes], other_ref[:, lanes]], axis=0)
-        part += lax.dot_general(
-            chunk, down, (((1,), (1,)), ((), ())), preferred_element_type=jnp.float32
-        )
-    slot = [block[:, width:].astype(jnp.float32) for block in blocks]
-    slot = jnp.concatenate(slot, axis=0)[:, 0:1].astype(jnp.int32)
-    slot_ref[...] = jnp.broadcast_to(slot, slot_ref.shape)
+        rows_ref[:, lanes] = normalized(blocks, inverse, gain_ref, lanes)
+
+
+def norm_rows(blocks, gain):
+    rows, width = blocks[0].shape
+    out_shape = jax.ShapeDtypeStruct((rows * len(blocks), width), jnp.bfloat16)
+    return call(norm_kernel, out_shape, (*blocks, gain))
+
+
+def held(part, slot):
+    rank = part.shape[1] // 2
     me = lax.axis_index("adapter")
     lanes = lax.broadcasted_iota(jnp.int32, part.shape, 1)
     part = jnp.where(slot == jnp.where(lanes < rank, me, me ^ 1), part, 0.0)
-    part = part[:, :rank] + part[:, rank:]
-    if halves:
-        steps = [ref[...].astype(jnp.float32) for ref in before] + [part]
-        middle = len(steps) // 2
-        halves = [jnp.concatenate(steps[:middle], axis=0), jnp.concatenate(steps[middle:], axis=0)]
-        part = jnp.concatenate(halves, axis=1)
-    part_ref[...] = part.astype(jnp.bfloat16)
-
-
-def shrink_rows(blocks, own, other, before=(), tokens=()):
-    rows = blocks[0].shape[0] * SIDE
+    return part[:, :rank] + part[:, rank:]
+
+
+def down_chunk(own_ref, other_ref, lanes):
+    return jnp.concatenate([own_ref[:, lanes], other_ref[:, lanes]], axis=0)
+
+
+def times_down(rows, down):
+    return lax.dot_general(rows, down, (((1,), (1,)), ((), ())), preferred_element_type=jnp.float32)
+
+
+def shrink_kernel(*refs):
+    *rows, own_ref, other_ref, near_ref, across_ref, part_ref = refs
+    rank, width = own_ref.shape
+    part = jnp.zeros((part_ref.shape[0], 2 * rank), jnp.float32)
+    for start in range(0, width, CHUNK):
+        lanes = slice(start, start + CHUNK)
+        chunk = jnp.concatenate([ref[:, lanes] for ref in rows], axis=0)
+        part += times_down(chunk, down_chunk(own_ref, other_ref, lanes))
+    own_rows = rows[0].shape[0] // SIDE
+    slot = [slot_column(step, near_ref, across_ref, own_rows) for step in range(len(rows))]
+    part_ref[...] = held(part, jnp.concatenate(slot, axis=0)).astype(jnp.bfloat16)
+
+
+def shrink_rows(rows, own, other, near, across):
+    out_shape = jax.ShapeDtypeStruct((sum(x.shape[0] for x in rows), own.shape[0]), jnp.bfloat16)
+    return call(shrink_kernel, out_shape, (*rows, own, other, near, across))
+
+
+def last_kernel(*refs):
+    block, crossed, gain_ref, rows_ref, own_ref, other_ref, before, near_ref, across_ref, *outs = refs
+    part_ref, out_ref = outs[-2:]
+    rank, width = own_ref.shape
+    blocks = (block, crossed)
+    inverse = [inverse_rms(block) for block in blocks]
+    part = jnp.zeros((2 * out_ref.shape[0], 2 * rank), jnp.float32)
+    for start in range(0, width, CHUNK):
+        lanes = slice(start, start + CHUNK)
+        here = normalized(blocks, inverse, gain_ref, lanes)
+        out_ref[:, lanes] = here
+        chunk = jnp.concatenate([rows_ref[:, lanes], here], axis=0)
+        part += times_down(chunk, down_chunk(own_ref, other_ref, lanes))
+    own_rows = block.shape[0]
+    first = before.shape[0] // rows_ref.shape[0]
+    slot = [slot_column(step, near_ref, across_ref, own_rows) for step in (first, first + 1)]
+    part = held(part, jnp.concatenate(slot, axis=0))
+    part = jnp.concatenate([before[...].astype(jnp.float32), part], axis=0)
+    half = part.shape[0] // 2
+    part_ref[...] = jnp.concatenate([part[:half], part[half:]], axis=1).astype(jnp.bfloat16)
+
+
+def last_rows(blocks, gain, rows, own, other, before, near, across, tokens):
     rank, width = own.shape
-    packed = (rows * (len(before) + 1) // 2, 2 * rank) if before else (rows, rank)
+    total = before.shape[0] + 2 * rows.shape[0]
     out_shape = (
-        jax.ShapeDtypeStruct(packed, jnp.bfloat16),
-        jax.ShapeDtypeStruct((rows, LANES), jnp.int32),
-        jax.ShapeDtypeStruct((rows, width), jnp.bfloat16),
+        jax.ShapeDtypeStruct((total // 2, 2 * rank), jnp.bfloat16),
+        jax.ShapeDtypeStruct(rows.shape, jnp.bfloat16),
     )
-    return call(
-        lambda *refs: shrink_kernel(bool(before), *refs[len(tokens) :]),
-        out_shape,
-        (*tokens, *blocks, own, other, *before),
-    )
+    operands = (*blocks, gain, rows, own, other, before, near, across, *tokens)
+    return call(last_kernel, out_shape, operands)
 
 
 def sum_kernel(places, *refs):
@@ -232,9 +285,7 @@
 
 
 def finish_kernel(places, *refs):
-    shrink_ref, across_ref, *refs = refs
-    bases, slots = refs[: places + 3], refs[places + 3 : 2 * places + 3]
-    own_ref, other_ref, out_ref = refs[2 * places + 3 :]
+    shrink_ref, across_ref, near_slots, across_slots, *bases, own_ref, other_ref, out_ref = refs
     depth, columns = own_ref.shape
     own_rows = out_ref.shape[1]
     rows = SIDE * own_rows
@@ -245,7 +296,8 @@
         swapped = jnp.concatenate([across[own_rows:], across[:own_rows]], axis=0)
         shrinks.append(packed_step(shrink_ref, step, places) + swapped)
     shrink = jnp.concatenate(shrinks, axis=0)
-    slot = jnp.concatenate([ref[:, 0:1] for ref in slots], axis=0)
+    slot = [slot_column(step, near_slots, across_slots, own_rows) for step in range(places)]
+    slot = jnp.concatenate(slot, axis=0)
     wide = jnp.concatenate([shrink] * (depth // shrink.shape[1]), axis=1)
     lanes = lax.broadcasted_iota(jnp.int32, wide.shape, 1)
     spread = jnp.where(lanes // shrink.shape[1] == slot, wide, 0.0).astype(jnp.bfloat16)
@@ -266,12 +318,11 @@
                 out_ref[chip, :, pl.ds(at, columns)] = query[side * own_rows : (side + 1) * own_rows]
 
 
-def finish(shrink, across, bases, slots, own, other, own_rows):
-    places = len(slots)
+def finish(places, shrink, across, slots, bases, own, other, own_rows):
     return call(
         lambda *refs: finish_kernel(places, *refs),
         jax.ShapeDtypeStruct((places * SIDE, own_rows, CORES * own.shape[1]), jnp.bfloat16),
-        (shrink, across, *bases, *slots, own, other),
+        (shrink, across, *slots, *bases, own, other),
     )
 
 
@@ -293,19 +344,14 @@
 
     down = down_weights[0].T
     up = up_weights.reshape(devices * rank, columns)
-    down_other = move(down, 0, 1)
-    up_other = move(up, 0, 1)
+    block, other = [hidden], []
+    rows, bases, tokens = [], [], []
+    gain = norm_weight.reshape(1, width)
+    last = places - 1
+
     weight_other = move(query_weight, 0, 1)
-
-    block, other = [normalize(hidden, norm_weight, adapter_index, adapter_slot)], []
-    parts, slots, rows, bases, tokens = [], [], [], [], []
-    last = places - 1
-
-    def meet(blocks, before=()):
-        part, slot, here = shrink_rows(blocks, down, down_other, before, tokens if before else ())
-        parts.append(part)
-        slots.append(slot)
-        rows.append(here)
+    near, count = own_slots(adapter_index, adapter_slot, places), 1
+    far = move(near, count, 0)
 
     for step in range(last):
         if step:
@@ -314,20 +360,28 @@
         block.append(move(after(block[step], *tokens[-1:]), 1, 0))
         other.append(move(after(block[step], *other[-1:]), 0, 2))
         if step:
-            meet(after([block[step - 1], other[step - 1]], block[step]))
+            rows.append(norm_rows(after([block[step - 1], other[step - 1]], block[step]), gain))
             bases.append(base_rows(rows[-1], query_weight))
+            if count < places:
+                near, count = merge(near, after(far, block[step]), count), 2 * count
+                far = move(near, count, 0) if count < places else None
+    across_slots = move(near, 0, 2)
+    up_other = move(after(up, bases[-1]), 0, 1)
+    down_other = move(after(down, bases[0]), 0, 1)
     base, weight_other = base_and_weight(after(rows, bases[-1]), weight_other)
     block[last] = after(block[last], base)
     tokens.append(token(block[last]))
     source = after(block[last], other[-1], tokens[-1])
     source = jnp.where((me & 1) == 0, source, other[-1])
     crossed = lax.ppermute(source, "adapter", split_pairs(places))
-    meet(after([block[last - 1], other[-1]], source))
+    part = shrink_rows(after(rows, source), down, down_other, near, across_slots)
+    rows.append(norm_rows(after([block[last - 1], other[-1]], source), gain))
     bases.append(base_rows(rows[-1], query_weight))
     bases_other = [base, base_rows(rows[-1], weight_other)]
-    meet([block[last], after(crossed, bases[-1], bases_other[-1])], parts)
-
-    part = parts[-1]
+    ends = [block[last], after(crossed, part, bases[-1], bases_other[-1])]
+    part, here = last_rows(ends, gain, rows[-1], down, down_other, part, near, across_slots, tokens)
+    rows.append(here)
+
     moved = [part] + [move(part, steps, 0) for steps in range(1, places)]
     bases.append(base_rows(rows[-1], query_weight))
     moved = after(moved, bases[-1])
@@ -336,7 +390,8 @@
     )
     across = move(shrink, 0, 2)
     bases_other.append(base_rows(after(rows[-1], shrink), weight_other))
-    query = finish(shrink, across, bases + bases_other, slots, up, up_other, own_rows)
+    slots = (near, across_slots)
+    query = finish(places, shrink, across, slots, bases + bases_other, up, up_other, own_rows)
     groups = [list(range(core, devices, CORES)) for core in range(CORES)]
     query = lax.all_to_all(query, "adapter", 0, 0, axis_index_groups=groups, tiled=True)
     return query.transpose(1, 0, 2).reshape(own_rows, devices * columns)

time: 74.4 us -> 75.6 us (1.016)
  starting transfers between devices: 17.5 us -> 21 us
  waiting for transfers between devices: 17.4 us -> 16.2 us
  Pallas kernels: 10.3 us -> 9.35 us
    ppermute x13 -> x16, starting transfers between devices: 16.7 us -> 20.4 us  [move(): return lax.ppermute(x, 'adapter', pairs(places, steps, flip))]
    ppermute x13 -> x16, waiting for transfers between devices: 14.2 us -> 13.2 us  [move(): return lax.ppermute(x, 'adapter', pairs(places, steps, flip))]
    pallas_call x6 -> x9, Pallas kernels: 4.48 us -> 4.14 us  [call(): pl.pallas_call(kernel, out_shape=out_shape, in_specs=[VMEM] * len(operand...]
    unnamed x12 -> x16, local copies, waits for them, and re-layouts: 2.24 us -> 2.48 us
  transfers between devices with their start and end apart: 14 -> 17, of which waited for: 8 -> 6; matrix products, arithmetic and copies ran while one was open for 18% -> 17% of each run, Pallas kernels for 13% -> 11%
where the time goes in v15:
time: 75.6 us; the launch traced here: 75.3 us
  starting transfers between devices  21 us (28%)
  waiting for transfers between devices  16.2 us (21%)
  matrix products  12.7 us (17%)
  blocking collectives  12.6 us (17%)
  Pallas kernels  9.35 us (12%)
  local copies, waits for them, and re-layouts  3.26 us (4%)
    ppermute x16, starting transfers between devices, move(): return lax.ppermute(x, 'adapter', pairs(places, steps, flip))  20.4 us
    ppermute x16, waiting for transfers between devices, move(): return lax.ppermute(x, 'adapter', pairs(places, steps, flip))  13.2 us
    dot_general x6, matrix products, base_rows(): return jnp.dot(rows, weight, preferred_element_type=jnp.float32)  12.7 us
    all_to_all x1, blocking collectives, shards(): lax.all_to_all(query, 'adapter', 0, 0, axis_index_groups=groups, tiled=True)  12.6 us
    pallas_call x9, Pallas kernels, call(): pl.pallas_call(kernel, out_shape=out_shape, in_specs=[VMEM] * len(operand...  4.14 us
    pallas_call x1, Pallas kernels, base_and_weight(): pl.pallas_call(base_kernel, out_shape=(jax.ShapeDtypeStruct((rows, weight...  3.78 us
    ppermute x1, waiting for transfers between devices, shards(): crossed = lax.ppermute(source, 'adapter', split_pairs(places))  2.91 us
    unnamed x16, local copies, waits for them, and re-layouts  2.48 us
  transfers between devices with their start and end apart: 17, of which 6 were waited for; matrix products, arithmetic and copies ran while one was open for 17% of the time, Pallas kernels for 11%

profile of v15, /device:TPU:0, one launch (start us, length us, event | category | flops | bytes accessed | tf_op | source)
XLA Modules:
  0.0 75.3 jit_solution(8703695784688225016)
XLA Ops:
  0.5 2.6 %collective-permute-start = (bf16[24,8192]{1,0:T(8,128)(2,1)}, bf16[24,8192]{1,0:T(8,128)(2,1)S(1)}, u32[]{:S(2)}, u32[]{:S(2)}) collective-permute-start(bf16[24,8192]{1,0:T(8,128)(2,1)} %refs_0_), channel_id=1, source_target_pairs={{0,4},{1,5},{2,6},{3,7},{4,12},{5,13},{6,14},{7,15},{12,8},{13,9},... | collective-permute-start | bytes 1179656 | tf_op jit(solution)/shard_map/ppermute | solution.py:340
  3.0 1.5 %collective-permute-start.2 = (bf16[24,8192]{1,0:T(8,128)(2,1)}, bf16[24,8192]{1,0:T(8,128)(2,1)S(1)}, u32[]{:S(2)}, u32[]{:S(2)}) collective-permute-start(bf16[24,8192]{1,0:T(8,128)(2,1)} %refs_0_), channel_id=1, source_target_pairs={{0,2},{1,3},{2,0},{3,1},{4,6},{5,7},{6,4},{7,5},{12,14},{13,15},{1... | collective-permute-start | bytes 1179656 | tf_op jit(solution)/shard_map/ppermute | solution.py:340
  4.5 1.4 %shard_map.79.refs_0_ = f32[8,128]{1,0:T(8,128)} custom-call(s32[1,24]{1,0:T(1,128)} %bitcast.34, s32[1,16]{1,0:T(1,128)} %bitcast.35), custom_call_target="tpu_custom_call" | custom-call | tf_op jit(solution)/shard_map/pallas_call | solution.py:86
  6.0 2.6 %collective-permute-start.9 = (f32[8,128]{1,0:T(8,128)}, f32[8,128]{1,0:T(8,128)S(1)}, u32[]{:S(2)}, u32[]{:S(2)}) collective-permute-start(f32[8,128]{1,0:T(8,128)} %shard_map.79.refs_0_), channel_id=1, source_target_pairs={{0,4},{1,5},{2,6},{3,7},{4,12},{5,13},{6,14},{7,15},{12,8},{13,9},... | collective-permute-start | bytes 12296 | tf_op jit(solution)/shard_map/ppermute | solution.py:340
  8.6 5.5 %collective-permute-done.block_ref.refs_0_ = bf16[24,8192]{1,0:T(8,128)(2,1)S(1)} collective-permute-done((bf16[24,8192]{1,0:T(8,128)(2,1)}, bf16[24,8192]{1,0:T(8,128)(2,1)S(1)}, u32[]{:S(2)}, u32[]{:S(2)}) %collective-permute-start) | collective-permute-done | bytes 393248 | tf_op jit(solution)/shard_map/ppermute | solution.py:340
  14.5 2.6 %collective-permute-start.1 = (bf16[24,8192]{1,0:T(8,128)(2,1)S(1)}, bf16[24,8192]{1,0:T(8,128)(2,1)S(1)}, u32[]{:S(2)}, u32[]{:S(2)}) collective-permute-start(bf16[24,8192]{1,0:T(8,128)(2,1)S(1)} %collective-permute-done.block_ref.refs_0_), channel_id=1, source_target_pairs={{0,4},{1,5},{2,6},{3,7},{4,12},{5,13},{6,14},{7,15},{12,8},{13,9},... | collective-permute-start | bytes 1179656 | tf_op jit(solution)/shard_map/ppermute | solution.py:340
  17.1 1.5 %collective-permute-start.4 = (bf16[24,8192]{1,0:T(8,128)(2,1)S(1)}, bf16[24,8192]{1,0:T(8,128)(2,1)S(1)}, u32[]{:S(2)}, u32[]{:S(2)}) collective-permute-start(bf16[24,8192]{1,0:T(8,128)(2,1)S(1)} %collective-permute-done.block_ref.refs_0_), channel_id=1, source_target_pairs={{0,2},{1,3},{2,0},{3,1},{4,6},{5,7},{6,4},{7,5},{12,14},{13,15},{1... | collective-permute-start | bytes 1179656 | tf_op jit(solution)/shard_map/ppermute | solution.py:340
  20.8 1.0 %copy-done.4 = bf16[24,8192]{1,0:T(8,128)(2,1)S(1)} copy-done((bf16[24,8192]{1,0:T(8,128)(2,1)S(1)}, bf16[24,8192]{1,0:T(8,128)(2,1)}, u32[]{:S(2)}) %copy-start.4) | copy-done | bytes 393240
  22.2 5.1 %fusion.refs_4_ = f32[48,512]{1,0:T(8,128)S(1)} fusion(bf16[48,8192]{1,0:T(8,128)(2,1)S(1)} %shard_map.74.refs_0_, bf16[8192,512]{1,0:T(8,128)(2,1)} %param.9), kind=kOutput, calls=%fused_computation.1 | convolution fusion | flops 402653184 | bytes 9273344 | tf_op jit(solution)/shard_map/dot_general | solution.py:343
  28.0 1.1 %collective-permute-start.6 = (bf16[24,8192]{1,0:T(8,128)(2,1)S(1)}, bf16[24,8192]{1,0:T(8,128)(2,1)S(1)}, u32[]{:S(2)}, u32[]{:S(2)}) collective-permute-start(bf16[24,8192]{1,0:T(8,128)(2,1)S(1)} %collective-permute-done.1.block_ref.refs_0_), channel_id=1, source_target_pairs={{0,2},{1,3},{2,0},{3,1},{4,6},{5,7},{6,4},{7,5},{12,14},{13,15},{1... | collective-permute-start | bytes 1179656 | tf_op jit(solution)/shard_map/ppermute | solution.py:340
  29.5 1.5 %fusion.1.refs_5_ = f32[48,512]{1,0:T(8,128)S(1)} fusion(bf16[48,8192]{1,0:T(8,128)(2,1)S(1)} %shard_map.76.refs_1_, bf16[8192,512]{1,0:T(8,128)(2,1)S(1)} %bitcast.32), kind=kOutput, calls=%fused_computation.2 | convolution fusion | flops 402653184 | bytes 9273344 | tf_op jit(solution)/shard_map/dot_general | solution.py:343
  32.0 3.8 %shard_map.77 = (f32[96,512]{1,0:T(8,128)S(1)}, bf16[8192,512]{1,0:T(8,128)(2,1)S(1)}) custom-call(bf16[48,8192]{1,0:T(8,128)(2,1)S(1)} %shard_map.74.refs_0_, bf16[48,8192]{1,0:T(8,128)(2,1)S(1)} %shard_map.76.refs_1_, bf16[8192,512]{1,0:T(8,128)(2,1)} %collective-permute-done.5.refs_2_), custom_call_target="tpu_custom_call" | custom-call | flops 1 | bytes 1 | tf_op jit(solution)/shard_map/pallas_call | solution.py:258
  35.8 4.1 %collective-permute-done.3.block_ref.refs_0_ = bf16[24,8192]{1,0:T(8,128)(2,1)S(1)} collective-permute-done((bf16[24,8192]{1,0:T(8,128)(2,1)S(1)}, bf16[24,8192]{1,0:T(8,128)(2,1)S(1)}, u32[]{:S(2)}, u32[]{:S(2)}) %collective-permute-start.3) | collective-permute-done | bytes 393248 | tf_op jit(solution)/shard_map/ppermute | solution.py:340
  40.9 1.5 %fusion.2.refs_6_ = f32[48,512]{1,0:T(8,128)S(1)} fusion(bf16[48,8192]{1,0:T(8,128)(2,1)S(1)} %shard_map.83.refs_3_, bf16[8192,512]{1,0:T(8,128)(2,1)S(1)} %bitcast.32), kind=kOutput, calls=%fused_computation.3 | convolution fusion | flops 402653184 | bytes 9273344 | tf_op jit(solution)/shard_map/dot_general | solution.py:343
  43.3 1.5 %fusion.3.refs_9_ = f32[48,512]{1,0:T(8,128)S(1)} fusion(bf16[48,8192]{1,0:T(8,128)(2,1)S(1)} %shard_map.83.refs_3_, bf16[8192,512]{1,0:T(8,128)(2,1)S(1)} %get-tuple-element.57), kind=kOutput, calls=%fused_computation.4 | convolution fusion | flops 402653184 | bytes 9273344 | tf_op jit(solution)/shard_map/dot_general | solution.py:343
  44.8 2.9 %collective-permute-done.7.refs_1_ = bf16[24,8192]{1,0:T(8,128)(2,1)S(1)} collective-permute-done((bf16[24,8192]{1,0:T(8,128)(2,1)S(1)}, bf16[24,8192]{1,0:T(8,128)(2,1)S(1)}, u32[]{:S(2)}, u32[]{:S(2)}) %collective-permute-start.7) | collective-permute-done | bytes 393248 | tf_op jit(solution)/shard_map/ppermute | solution.py:376
  47.8 1.2 %shard_map.84 = (bf16[96,128]{1,0:T(8,128)(2,1)S(1)}, bf16[48,8192]{1,0:T(8,128)(2,1)S(1)}) custom-call(bf16[24,8192]{1,0:T(8,128)(2,1)S(1)} %collective-permute-done.3.block_ref.refs_0_, bf16[24,8192]{1,0:T(8,128)(2,1)S(1)} %collective-permute-done.7.refs_1_, f32[1,8192]{1,0:T(1,128)S(1)} %bitcast.30, bf16[48,8192]{1,0:T(8,128)(2,1)S(1)} %shard_map.83.refs_3_, ...), custom_call_target="tpu_custom_call" | custom-call | flops 1 | bytes 1 | tf_op jit(solution)/shard_map/pallas_call | solution.py:57
  49.0 2.6 %collective-permute-start.12 = (bf16[96,128]{1,0:T(8,128)(2,1)S(1)}, bf16[96,128]{1,0:T(8,128)(2,1)S(1)}, u32[]{:S(2)}, u32[]{:S(2)}) collective-permute-start(bf16[96,128]{1,0:T(8,128)(2,1)S(1)} %get-tuple-element.61.refs_0_), channel_id=1, source_target_pairs={{0,4},{1,5},{2,6},{3,7},{4,12},{5,13},{6,14},{7,15},{12,8},{13,9},... | collective-permute-start | bytes 73736 | tf_op jit(solution)/shard_map/ppermute | solution.py:340
  52.2 1.9 %collective-permute-start.14 = (bf16[96,128]{1,0:T(8,128)(2,1)S(1)}, bf16[96,128]{1,0:T(8,128)(2,1)S(1)}, u32[]{:S(2)}, u32[]{:S(2)}) collective-permute-start(bf16[96,128]{1,0:T(8,128)(2,1)S(1)} %get-tuple-element.61.refs_0_), channel_id=1, source_target_pairs={{0,8},{1,9},{2,10},{3,11},{4,0},{5,1},{6,2},{7,3},{12,4},{13,5},{1... | collective-permute-start | bytes 73736 | tf_op jit(solution)/shard_map/ppermute | solution.py:340
  54.1 1.5 %fusion.4.refs_7_ = f32[48,512]{1,0:T(8,128)S(1)} fusion(bf16[48,8192]{1,0:T(8,128)(2,1)S(1)} %get-tuple-element.65, bf16[8192,512]{1,0:T(8,128)(2,1)S(1)} %bitcast.32), kind=kOutput, calls=%fused_computation.5 | convolution fusion | flops 402653184 | bytes 9273344 | tf_op jit(solution)/shard_map/dot_general | solution.py:343
  55.7 1.5 %collective-permute-done.13.refs_2_ = bf16[96,128]{1,0:T(8,128)(2,1)S(1)} collective-permute-done((bf16[96,128]{1,0:T(8,128)(2,1)S(1)}, bf16[96,128]{1,0:T(8,128)(2,1)S(1)}, u32[]{:S(2)}, u32[]{:S(2)}) %collective-permute-start.13) | collective-permute-done | bytes 24608 | tf_op jit(solution)/shard_map/ppermute | solution.py:340
  57.8 1.5 %fusion.5.refs_10_ = f32[48,512]{1,0:T(8,128)S(1)} fusion(bf16[48,8192]{1,0:T(8,128)(2,1)S(1)} %get-tuple-element.65, bf16[8192,512]{1,0:T(8,128)(2,1)S(1)} %get-tuple-element.57), kind=kOutput, calls=%fused_computation.6 | convolution fusion | flops 402653184 | bytes 9273344 | tf_op jit(solution)/shard_map/dot_general | solution.py:343
  59.4 1.8 %collective-permute-done.15.refs_1_ = bf16[96,128]{1,0:T(8,128)(2,1)S(1)} collective-permute-done((bf16[96,128]{1,0:T(8,128)(2,1)S(1)}, bf16[96,128]{1,0:T(8,128)(2,1)S(1)}, u32[]{:S(2)}, u32[]{:S(2)}) %collective-permute-start.15) | collective-permute-done | bytes 24608 | tf_op jit(solution)/shard_map/ppermute | solution.py:340
  62.0 12.6 %all_to_all.5 = bf16[8,24,1024]{2,1,0:T(8,128)(2,1)S(1)} all-to-all(bf16[8,24,1024]{2,1,0:T(8,128)(2,1)S(1)} %shard_map.86), channel_id=1, replica_groups={{0,2,4,6,8,10,12,14},{1,3,5,7,9,11,13,15},{16,18,20,22,24,26,28,30},{17..., dimensions={0} | all-to-all | bytes 786432 | tf_op jit(solution)/shard_map/all_to_all | solution.py:396
  (50 shorter events, 10.4 us)
Async XLA Ops:
  0.0 32.0 %collective-permute-start.5 = (bf16[8192,512]{1,0:T(8,128)(2,1)}, bf16[8192,512]{1,0:T(8,128)(2,1)}, u32[]{:S(2)}, u32[]{:S(2)}) collective-permute-start(bf16[8192,512]{1,0:T(8,128)(2,1)} %param.9), channel_id=1, source_target_pairs={{0,1},{1,0},{2,3},{3,2},{4,5},{5,4},{6,7},{7,6},{12,13},{13,12},{1... | collective-permute-start | bytes 25165832 | tf_op jit(solution)/shard_map/ppermute | solution.py:340
  0.5 13.6 %collective-permute-start = (bf16[24,8192]{1,0:T(8,128)(2,1)}, bf16[24,8192]{1,0:T(8,128)(2,1)S(1)}, u32[]{:S(2)}, u32[]{:S(2)}) collective-permute-start(bf16[24,8192]{1,0:T(8,128)(2,1)} %refs_0_), channel_id=1, source_target_pairs={{0,4},{1,5},{2,6},{3,7},{4,12},{5,13},{6,14},{7,15},{12,8},{13,9},... | collective-permute-start | bytes 1179656 | tf_op jit(solution)/shard_map/ppermute | solution.py:340
  3.0 11.5 %collective-permute-start.2 = (bf16[24,8192]{1,0:T(8,128)(2,1)}, bf16[24,8192]{1,0:T(8,128)(2,1)S(1)}, u32[]{:S(2)}, u32[]{:S(2)}) collective-permute-start(bf16[24,8192]{1,0:T(8,128)(2,1)} %refs_0_), channel_id=1, source_target_pairs={{0,2},{1,3},{2,0},{3,1},{4,6},{5,7},{6,4},{7,5},{12,14},{13,15},{1... | collective-permute-start | bytes 1179656 | tf_op jit(solution)/shard_map/ppermute | solution.py:340
  6.0 12.6 %collective-permute-start.9 = (f32[8,128]{1,0:T(8,128)}, f32[8,128]{1,0:T(8,128)S(1)}, u32[]{:S(2)}, u32[]{:S(2)}) collective-permute-start(f32[8,128]{1,0:T(8,128)} %shard_map.79.refs_0_), channel_id=1, source_target_pairs={{0,4},{1,5},{2,6},{3,7},{4,12},{5,13},{6,14},{7,15},{12,8},{13,9},... | collective-permute-start | bytes 12296 | tf_op jit(solution)/shard_map/ppermute | solution.py:340
  14.5 12.9 %collective-permute-start.1 = (bf16[24,8192]{1,0:T(8,128)(2,1)S(1)}, bf16[24,8192]{1,0:T(8,128)(2,1)S(1)}, u32[]{:S(2)}, u32[]{:S(2)}) collective-permute-start(bf16[24,8192]{1,0:T(8,128)(2,1)S(1)} %collective-permute-done.block_ref.refs_0_), channel_id=1, source_target_pairs={{0,4},{1,5},{2,6},{3,7},{4,12},{5,13},{6,14},{7,15},{12,8},{13,9},... | collective-permute-start | bytes 1179656 | tf_op jit(solution)/shard_map/ppermute | solution.py:340
  17.1 10.9 %collective-permute-start.4 = (bf16[24,8192]{1,0:T(8,128)(2,1)S(1)}, bf16[24,8192]{1,0:T(8,128)(2,1)S(1)}, u32[]{:S(2)}, u32[]{:S(2)}) collective-permute-start(bf16[24,8192]{1,0:T(8,128)(2,1)S(1)} %collective-permute-done.block_ref.refs_0_), channel_id=1, source_target_pairs={{0,2},{1,3},{2,0},{3,1},{4,6},{5,7},{6,4},{7,5},{12,14},{13,15},{1... | collective-permute-start | bytes 1179656 | tf_op jit(solution)/shard_map/ppermute | solution.py:340
  19.3 9.8 %collective-permute-start.10 = (f32[8,128]{1,0:T(8,128)S(1)}, f32[8,128]{1,0:T(8,128)S(1)}, u32[]{:S(2)}, u32[]{:S(2)}) collective-permute-start(f32[8,128]{1,0:T(8,128)S(1)} %shard_map.80.refs_0_), channel_id=1, source_target_pairs={{0,12},{1,13},{2,14},{3,15},{4,8},{5,9},{6,10},{7,11},{12,0},{13,1... | collective-permute-start | bytes 12296 | tf_op jit(solution)/shard_map/ppermute | solution.py:340
  20.0 0.8 %copy-start.2 = (f32[8192]{0:T(1024)S(1)}, f32[8192]{0:T(1024)}, u32[]{:S(2)}) copy-start(f32[8192]{0:T(1024)} %param.8) | copy-start | bytes 98308
  20.8 1.0 %copy-start.4 = (bf16[24,8192]{1,0:T(8,128)(2,1)S(1)}, bf16[24,8192]{1,0:T(8,128)(2,1)}, u32[]{:S(2)}) copy-start(bf16[24,8192]{1,0:T(8,128)(2,1)} %refs_0_) | copy-start | bytes 1179652
  21.8 7.7 %slice-start = ((s8[8388608]{0:T(1024)(128)(4,1)}), s8[4194304]{0:T(1024)(128)(4,1)S(1)}, s32[]{:S(2)}) async-start(s8[8388608]{0:T(1024)(128)(4,1)} %bitcast.31), calls=%async_computation.1 | async-start | bytes 8388608
  22.2 5.2 %copy-start = (bf16[1,8192,64]{1,2,0:T(8,128)(2,1)S(1)}, bf16[1,8192,64]{1,2,0:T(8,128)(2,1)}, u32[]{:S(2)}) copy-start(bf16[1,8192,64]{1,2,0:T(8,128)(2,1)} %param.10) | copy-start | bytes 3145732
  22.2 6.9 %copy-start.3 = (f32[8192]{0:T(1024)S(1)}, f32[8192]{0:T(1024)}, u32[]{:S(2)}) copy-start(f32[8192]{0:T(1024)} %param.8) | copy-start | bytes 98308
  22.2 7.3 %slice-start.1 = ((s8[8388608]{0:T(1024)(128)(4,1)}), s8[4194304]{0:T(1024)(128)(4,1)S(1)}, s32[]{:S(2)}) async-start(s8[8388608]{0:T(1024)(128)(4,1)} %bitcast.31), calls=%async_computation.2 | async-start | bytes 8388608
  27.4 15.1 %collective-permute-start.8 = (bf16[64,8192]{1,0:T(8,128)(2,1)S(1)}, bf16[64,8192]{1,0:T(8,128)(2,1)S(1)}, u32[]{:S(2)}, u32[]{:S(2)}) collective-permute-start(bf16[64,8192]{1,0:T(8,128)(2,1)S(1)} %bitcast.22), channel_id=1, source_target_pairs={{0,1},{1,0},{2,3},{3,2},{4,5},{5,4},{6,7},{7,6},{12,13},{13,12},{1... | collective-permute-start | bytes 3145736 | tf_op jit(solution)/shard_map/ppermute | solution.py:340
  27.5 12.4 %collective-permute-start.3 = (bf16[24,8192]{1,0:T(8,128)(2,1)S(1)}, bf16[24,8192]{1,0:T(8,128)(2,1)S(1)}, u32[]{:S(2)}, u32[]{:S(2)}) collective-permute-start(bf16[24,8192]{1,0:T(8,128)(2,1)S(1)} %collective-permute-done.1.block_ref.refs_0_), channel_id=1, source_target_pairs={{0,4},{1,5},{2,6},{3,7},{4,12},{5,13},{6,14},{7,15},{12,8},{13,9},... | collective-permute-start | bytes 1179656 | tf_op jit(solution)/shard_map/ppermute | solution.py:340
  28.0 11.9 %collective-permute-start.6 = (bf16[24,8192]{1,0:T(8,128)(2,1)S(1)}, bf16[24,8192]{1,0:T(8,128)(2,1)S(1)}, u32[]{:S(2)}, u32[]{:S(2)}) collective-permute-start(bf16[24,8192]{1,0:T(8,128)(2,1)S(1)} %collective-permute-done.1.block_ref.refs_0_), channel_id=1, source_target_pairs={{0,2},{1,3},{2,0},{3,1},{4,6},{5,7},{6,4},{7,5},{12,14},{13,15},{1... | collective-permute-start | bytes 1179656 | tf_op jit(solution)/shard_map/ppermute | solution.py:340
  29.5 2.5 %copy-start.1 = (bf16[16,64,512]{2,1,0:T(8,128)(2,1)S(1)}, bf16[16,64,512]{2,1,0:T(8,128)(2,1)}, u32[]{:S(2)}) copy-start(bf16[16,64,512]{2,1,0:T(8,128)(2,1)} %param.11) | copy-start | bytes 3145732
  31.0 11.4 %collective-permute-start.11 = (f32[8,128]{1,0:T(8,128)S(1)}, f32[8,128]{1,0:T(8,128)S(1)}, u32[]{:S(2)}, u32[]{:S(2)}) collective-permute-start(f32[8,128]{1,0:T(8,128)S(1)} %shard_map.81.refs_4_.refs_7_.refs_2_), channel_id=1, source_target_pairs={{0,2},{1,3},{2,0},{3,1},{4,6},{5,7},{6,4},{7,5},{12,14},{13,15},{1... | collective-permute-start | bytes 12296 | tf_op jit(solution)/shard_map/ppermute | solution.py:340
  32.0 27.3 %collective-permute-start.16 = (bf16[1024,512]{1,0:T(8,128)(2,1)S(1)}, bf16[1024,512]{1,0:T(8,128)(2,1)S(1)}, u32[]{:S(2)}, u32[]{:S(2)}) collective-permute-start(bf16[1024,512]{1,0:T(8,128)(2,1)S(1)} %bitcast.25), channel_id=1, source_target_pairs={{0,1},{1,0},{2,3},{3,2},{4,5},{5,4},{6,7},{7,6},{12,13},{13,12},{1... | collective-permute-start | bytes 3145736 | tf_op jit(solution)/shard_map/ppermute | solution.py:340
  39.9 7.8 %collective-permute-start.7 = (bf16[24,8192]{1,0:T(8,128)(2,1)S(1)}, bf16[24,8192]{1,0:T(8,128)(2,1)S(1)}, u32[]{:S(2)}, u32[]{:S(2)}) collective-permute-start(bf16[24,8192]{1,0:T(8,128)(2,1)S(1)} %broadcast_select_fusion), channel_id=1, source_target_pairs={{0,2},{2,0},{4,6},{6,4},{12,14},{14,12},{8,10},{10,8},{1,5},{3,7},... | collective-permute-start | bytes 1179656 | tf_op jit(solution)/shard_map/ppermute | solution.py:376
  49.0 6.7 %collective-permute-start.12 = (bf16[96,128]{1,0:T(8,128)(2,1)S(1)}, bf16[96,128]{1,0:T(8,128)(2,1)S(1)}, u32[]{:S(2)}, u32[]{:S(2)}) collective-permute-start(bf16[96,128]{1,0:T(8,128)(2,1)S(1)} %get-tuple-element.61.refs_0_), channel_id=1, source_target_pairs={{0,4},{1,5},{2,6},{3,7},{4,12},{5,13},{6,14},{7,15},{12,8},{13,9},... | collective-permute-start | bytes 73736 | tf_op jit(solution)/shard_map/ppermute | solution.py:340
  51.5 5.6 %collective-permute-start.13 = (bf16[96,128]{1,0:T(8,128)(2,1)S(1)}, bf16[96,128]{1,0:T(8,128)(2,1)S(1)}, u32[]{:S(2)}, u32[]{:S(2)}) collective-permute-start(bf16[96,128]{1,0:T(8,128)(2,1)S(1)} %get-tuple-element.61.refs_0_), channel_id=1, source_target_pairs={{0,12},{1,13},{2,14},{3,15},{4,8},{5,9},{6,10},{7,11},{12,0},{13,1... | collective-permute-start | bytes 73736 | tf_op jit(solution)/shard_map/ppermute | solution.py:340
  52.2 4.9 %collective-permute-start.14 = (bf16[96,128]{1,0:T(8,128)(2,1)S(1)}, bf16[96,128]{1,0:T(8,128)(2,1)S(1)}, u32[]{:S(2)}, u32[]{:S(2)}) collective-permute-start(bf16[96,128]{1,0:T(8,128)(2,1)S(1)} %get-tuple-element.61.refs_0_), channel_id=1, source_target_pairs={{0,8},{1,9},{2,10},{3,11},{4,0},{5,1},{6,2},{7,3},{12,4},{13,5},{1... | collective-permute-start | bytes 73736 | tf_op jit(solution)/shard_map/ppermute | solution.py:340
  57.3 3.9 %collective-permute-start.15 = (bf16[96,128]{1,0:T(8,128)(2,1)S(1)}, bf16[96,128]{1,0:T(8,128)(2,1)S(1)}, u32[]{:S(2)}, u32[]{:S(2)}) collective-permute-start(bf16[96,128]{1,0:T(8,128)(2,1)S(1)} %shard_map.85.refs_0_), channel_id=1, source_target_pairs={{0,2},{1,3},{2,0},{3,1},{4,6},{5,7},{6,4},{7,5},{12,14},{13,15},{1... | collective-permute-start | bytes 73736 | tf_op jit(solution)/shard_map/ppermute | solution.py:340
  (1 other events, 0.7 us)

commit v16 on v15

--- a/solution.py
+++ b/solution.py
@@ -306,12 +306,14 @@
         at = pl.multiple_of((core ^ which) * columns, columns)
         for step in range(places):
             here = slice(step * rows, (step + 1) * rows)
-            if which == 0:
-                base = bases[step][...]
+            if which == 0 and step:
+                base = bases[step + 1][...]
+            elif which == 0:
+                base = jnp.concatenate([bases[0][...], bases[1][...]], axis=0)
             elif step < places - 2:
-                base = bases[places][here, :]
+                base = bases[places + 1][here, :]
             else:
-                base = bases[step + 3][...]
+                base = bases[step + 4][...]
             query = (base + ADAPTER_SCALE * update[here]).astype(jnp.bfloat16)
             for side in range(SIDE):
                 chip = ring_chip(places, -step, side)
@@ -345,29 +347,30 @@
     down = down_weights[0].T
     up = up_weights.reshape(devices * rank, columns)
     block, other = [hidden], []
-    rows, bases, tokens = [], [], []
+    rows, tokens = [], []
     gain = norm_weight.reshape(1, width)
+    bases = [base_rows(norm_rows([hidden], gain), query_weight)]
     last = places - 1
 
     weight_other = move(query_weight, 0, 1)
+    down_other = move(down, 0, 1)
     near, count = own_slots(adapter_index, adapter_slot, places), 1
     far = move(near, count, 0)
 
     for step in range(last):
         if step:
-            block[step] = after(block[step], *bases[-1:])
+            block[step] = after(block[step], bases[-1])
             tokens.append(token(block[step]))
         block.append(move(after(block[step], *tokens[-1:]), 1, 0))
         other.append(move(after(block[step], *other[-1:]), 0, 2))
         if step:
             rows.append(norm_rows(after([block[step - 1], other[step - 1]], block[step]), gain))
-            bases.append(base_rows(rows[-1], query_weight))
+            here = rows[-1] if len(rows) > 1 else rows[0][own_rows:]
+            bases.append(base_rows(here, query_weight))
             if count < places:
                 near, count = merge(near, after(far, block[step]), count), 2 * count
                 far = move(near, count, 0) if count < places else None
     across_slots = move(near, 0, 2)
-    up_other = move(after(up, bases[-1]), 0, 1)
-    down_other = move(after(down, bases[0]), 0, 1)
     base, weight_other = base_and_weight(after(rows, bases[-1]), weight_other)
     block[last] = after(block[last], base)
     tokens.append(token(block[last]))
@@ -378,6 +381,7 @@
     rows.append(norm_rows(after([block[last - 1], other[-1]], source), gain))
     bases.append(base_rows(rows[-1], query_weight))
     bases_other = [base, base_rows(rows[-1], weight_other)]
+    up_other = move(after(up, part), 0, 1)
     ends = [block[last], after(crossed, part, bases[-1], bases_other[-1])]
     part, here = last_rows(ends, gain, rows[-1], down, down_other, part, near, across_slots, tokens)
     rows.append(here)

time: 75.6 us -> 75.5 us (level)
  matrix products: 12.7 us -> 20.4 us
  waiting for transfers between devices: 16.2 us -> 9.75 us
  starting transfers between devices: 21 us -> 19.7 us
    dot_general x6 -> x7, matrix products: 12.7 us -> 20.4 us  [base_rows(): return jnp.dot(rows, weight, preferred_element_type=jnp.float32)]
    ppermute x16, waiting for transfers between devices: 13.2 us -> 7.38 us  [move(): return lax.ppermute(x, 'adapter', pairs(places, steps, flip))]
    ppermute x16, starting transfers between devices: 20.4 us -> 18.7 us  [move(): return lax.ppermute(x, 'adapter', pairs(places, steps, flip))]
    unnamed x16 -> x18, local copies, waits for them, and re-layouts: 2.48 us -> 1.8 us
    pallas_call x9 -> x10, Pallas kernels: 4.14 us -> 4.33 us  [call(): pl.pallas_call(kernel, out_shape=out_shape, in_specs=[VMEM] * len(operand...]
  transfers between devices with their start and end apart: 17 -> 17, of which waited for: 6 -> 6; matrix products, arithmetic and copies ran while one was open for 17% -> 27% of each run, Pallas kernels for 11% -> 12%
where the time goes in v16:
time: 75.5 us; the launch traced here: 75.2 us
  matrix products  20.4 us (27%)
  starting transfers between devices  19.7 us (26%)
  blocking collectives  13 us (17%)
  waiting for transfers between devices  9.75 us (13%)
  Pallas kernels  9.53 us (13%)
  local copies, waits for them, and re-layouts  2.57 us (3%)
    dot_general x7, matrix products, base_rows(): return jnp.dot(rows, weight, preferred_element_type=jnp.float32)  20.4 us
    ppermute x16, starting transfers between devices, move(): return lax.ppermute(x, 'adapter', pairs(places, steps, flip))  18.7 us
    all_to_all x1, blocking collectives, shards(): lax.all_to_all(query, 'adapter', 0, 0, axis_index_groups=groups, tiled=True)  13 us
    ppermute x16, waiting for transfers between devices, move(): return lax.ppermute(x, 'adapter', pairs(places, steps, flip))  7.38 us
    pallas_call x10, Pallas kernels, call(): pl.pallas_call(kernel, out_shape=out_shape, in_specs=[VMEM] * len(operand...  4.33 us
    pallas_call x1, Pallas kernels, base_and_weight(): pl.pallas_call(base_kernel, out_shape=(jax.ShapeDtypeStruct((rows, weight...  3.78 us
    ppermute x1, waiting for transfers between devices, shards(): crossed = lax.ppermute(source, 'adapter', split_pairs(places))  2.37 us
    unnamed x18, local copies, waits for them, and re-layouts  1.8 us
  transfers between devices with their start and end apart: 17, of which 6 were waited for; matrix products, arithmetic and copies ran while one was open for 27% of the time, Pallas kernels for 12%

profile of v16, /device:TPU:0, one launch (start us, length us, event | category | flops | bytes accessed | tf_op | source)
XLA Modules:
  0.0 75.2 jit_solution(391551319707016280)
XLA Ops:
  0.5 2.6 %collective-permute-start = (bf16[24,8192]{1,0:T(8,128)(2,1)}, bf16[24,8192]{1,0:T(8,128)(2,1)S(1)}, u32[]{:S(2)}, u32[]{:S(2)}) collective-permute-start(bf16[24,8192]{1,0:T(8,128)(2,1)} %refs_0_.2), channel_id=1, source_target_pairs={{0,4},{1,5},{2,6},{3,7},{4,12},{5,13},{6,14},{7,15},{12,8},{13,9},... | collective-permute-start | bytes 1179656 | tf_op jit(solution)/shard_map/ppermute | solution.py:342
  3.0 1.5 %collective-permute-start.2 = (bf16[24,8192]{1,0:T(8,128)(2,1)}, bf16[24,8192]{1,0:T(8,128)(2,1)S(1)}, u32[]{:S(2)}, u32[]{:S(2)}) collective-permute-start(bf16[24,8192]{1,0:T(8,128)(2,1)} %refs_0_.2), channel_id=1, source_target_pairs={{0,2},{1,3},{2,0},{3,1},{4,6},{5,7},{6,4},{7,5},{12,14},{13,15},{1... | collective-permute-start | bytes 1179656 | tf_op jit(solution)/shard_map/ppermute | solution.py:342
  4.5 1.4 %shard_map.80.refs_0_ = f32[8,128]{1,0:T(8,128)} custom-call(s32[1,24]{1,0:T(1,128)} %bitcast.36, s32[1,16]{1,0:T(1,128)} %bitcast.37), custom_call_target="tpu_custom_call" | custom-call | tf_op jit(solution)/shard_map/pallas_call | solution.py:86
  6.0 2.6 %collective-permute-start.9 = (f32[8,128]{1,0:T(8,128)}, f32[8,128]{1,0:T(8,128)S(1)}, u32[]{:S(2)}, u32[]{:S(2)}) collective-permute-start(f32[8,128]{1,0:T(8,128)} %shard_map.80.refs_0_), channel_id=1, source_target_pairs={{0,4},{1,5},{2,6},{3,7},{4,12},{5,13},{6,14},{7,15},{12,8},{13,9},... | collective-permute-start | bytes 12296 | tf_op jit(solution)/shard_map/ppermute | solution.py:342
  10.7 4.6 %fusion.2.refs_4_ = f32[24,512]{1,0:T(8,128)S(1)} fusion(bf16[24,8192]{1,0:T(8,128)(2,1)S(1)} %shard_map.73, bf16[8192,512]{1,0:T(8,128)(2,1)} %param.9), kind=kOutput, calls=%fused_computation.3 | convolution fusion | flops 201326592 | bytes 8830976 | tf_op jit(solution)/shard_map/dot_general | solution.py:345
  15.3 1.8 %collective-permute-start.1 = (bf16[24,8192]{1,0:T(8,128)(2,1)S(1)}, bf16[24,8192]{1,0:T(8,128)(2,1)S(1)}, u32[]{:S(2)}, u32[]{:S(2)}) collective-permute-start(bf16[24,8192]{1,0:T(8,128)(2,1)S(1)} %collective-permute-done.block_ref.refs_0_), channel_id=1, source_target_pairs={{0,4},{1,5},{2,6},{3,7},{4,12},{5,13},{6,14},{7,15},{12,8},{13,9},... | collective-permute-start | bytes 1179656 | tf_op jit(solution)/shard_map/ppermute | solution.py:342
  17.1 1.5 %collective-permute-start.4 = (bf16[24,8192]{1,0:T(8,128)(2,1)S(1)}, bf16[24,8192]{1,0:T(8,128)(2,1)S(1)}, u32[]{:S(2)}, u32[]{:S(2)}) collective-permute-start(bf16[24,8192]{1,0:T(8,128)(2,1)S(1)} %collective-permute-done.block_ref.refs_0_), channel_id=1, source_target_pairs={{0,2},{1,3},{2,0},{3,1},{4,6},{5,7},{6,4},{7,5},{12,14},{13,15},{1... | collective-permute-start | bytes 1179656 | tf_op jit(solution)/shard_map/ppermute | solution.py:342
  19.8 4.6 %fusion.refs_5_ = f32[24,512]{1,0:T(8,128)S(1)} fusion(bf16[8192,512]{1,0:T(8,128)(2,1)} %param.9, bf16[48,8192]{1,0:T(8,128)(2,1)S(1)} %shard_map.75.refs_0_), kind=kOutput, calls=%fused_computation | convolution fusion | flops 201326592 | bytes 8830976 | tf_op jit(solution)/shard_map/dot_general | solution.py:345
  24.4 3.5 %collective-permute-done.1.block_ref.refs_0_ = bf16[24,8192]{1,0:T(8,128)(2,1)S(1)} collective-permute-done((bf16[24,8192]{1,0:T(8,128)(2,1)S(1)}, bf16[24,8192]{1,0:T(8,128)(2,1)S(1)}, u32[]{:S(2)}, u32[]{:S(2)}) %collective-permute-start.1) | collective-permute-done | bytes 393248 | tf_op jit(solution)/shard_map/ppermute | solution.py:342
  27.9 1.1 %collective-permute-start.6 = (bf16[24,8192]{1,0:T(8,128)(2,1)S(1)}, bf16[24,8192]{1,0:T(8,128)(2,1)S(1)}, u32[]{:S(2)}, u32[]{:S(2)}) collective-permute-start(bf16[24,8192]{1,0:T(8,128)(2,1)S(1)} %collective-permute-done.1.block_ref.refs_0_), channel_id=1, source_target_pairs={{0,2},{1,3},{2,0},{3,1},{4,6},{5,7},{6,4},{7,5},{12,14},{13,15},{1... | collective-permute-start | bytes 1179656 | tf_op jit(solution)/shard_map/ppermute | solution.py:342
  29.5 5.1 %fusion.3.refs_6_ = f32[48,512]{1,0:T(8,128)S(1)} fusion(bf16[48,8192]{1,0:T(8,128)(2,1)S(1)} %shard_map.77.refs_1_, bf16[8192,512]{1,0:T(8,128)(2,1)} %param.9), kind=kOutput, calls=%fused_computation.4 | convolution fusion | flops 402653184 | bytes 9273344 | tf_op jit(solution)/shard_map/dot_general | solution.py:345
  35.6 3.8 %shard_map.78 = (f32[96,512]{1,0:T(8,128)S(1)}, bf16[8192,512]{1,0:T(8,128)(2,1)S(1)}) custom-call(bf16[48,8192]{1,0:T(8,128)(2,1)S(1)} %shard_map.75.refs_0_, bf16[48,8192]{1,0:T(8,128)(2,1)S(1)} %shard_map.77.refs_1_, bf16[8192,512]{1,0:T(8,128)(2,1)} %collective-permute-done.5.refs_2_), custom_call_target="tpu_custom_call" | custom-call | flops 1 | bytes 1 | tf_op jit(solution)/shard_map/pallas_call | solution.py:258
  41.0 1.5 %fusion.4.refs_7_ = f32[48,512]{1,0:T(8,128)S(1)} fusion(bf16[48,8192]{1,0:T(8,128)(2,1)S(1)} %shard_map.84.refs_3_, bf16[8192,512]{1,0:T(8,128)(2,1)S(1)} %bitcast.34), kind=kOutput, calls=%fused_computation.5 | convolution fusion | flops 402653184 | bytes 9273344 | tf_op jit(solution)/shard_map/dot_general | solution.py:345
  43.5 1.5 %fusion.5.refs_10_ = f32[48,512]{1,0:T(8,128)S(1)} fusion(bf16[48,8192]{1,0:T(8,128)(2,1)S(1)} %shard_map.84.refs_3_, bf16[8192,512]{1,0:T(8,128)(2,1)S(1)} %get-tuple-element.57), kind=kOutput, calls=%fused_computation.6 | convolution fusion | flops 402653184 | bytes 9273344 | tf_op jit(solution)/shard_map/dot_general | solution.py:345
  45.0 2.4 %collective-permute-done.7.refs_1_ = bf16[24,8192]{1,0:T(8,128)(2,1)S(1)} collective-permute-done((bf16[24,8192]{1,0:T(8,128)(2,1)S(1)}, bf16[24,8192]{1,0:T(8,128)(2,1)S(1)}, u32[]{:S(2)}, u32[]{:S(2)}) %collective-permute-start.7) | collective-permute-done | bytes 393248 | tf_op jit(solution)/shard_map/ppermute | solution.py:379
  47.4 1.2 %shard_map.85 = (bf16[96,128]{1,0:T(8,128)(2,1)S(1)}, bf16[48,8192]{1,0:T(8,128)(2,1)S(1)}) custom-call(bf16[24,8192]{1,0:T(8,128)(2,1)S(1)} %collective-permute-done.3.block_ref.refs_0_, bf16[24,8192]{1,0:T(8,128)(2,1)S(1)} %collective-permute-done.7.refs_1_, f32[1,8192]{1,0:T(1,128)S(1)} %bitcast.32, bf16[48,8192]{1,0:T(8,128)(2,1)S(1)} %shard_map.84.refs_3_, ...), custom_call_target="tpu_custom_call" | custom-call | flops 1 | bytes 1 | tf_op jit(solution)/shard_map/pallas_call | solution.py:57
  48.6 1.9 %collective-permute-start.12 = (bf16[96,128]{1,0:T(8,128)(2,1)S(1)}, bf16[96,128]{1,0:T(8,128)(2,1)S(1)}, u32[]{:S(2)}, u32[]{:S(2)}) collective-permute-start(bf16[96,128]{1,0:T(8,128)(2,1)S(1)} %get-tuple-element.61.refs_0_), channel_id=1, source_target_pairs={{0,4},{1,5},{2,6},{3,7},{4,12},{5,13},{6,14},{7,15},{12,8},{13,9},... | collective-permute-start | bytes 73736 | tf_op jit(solution)/shard_map/ppermute | solution.py:342
  50.5 2.3 %collective-permute-start.13 = (bf16[96,128]{1,0:T(8,128)(2,1)S(1)}, bf16[96,128]{1,0:T(8,128)(2,1)S(1)}, u32[]{:S(2)}, u32[]{:S(2)}) collective-permute-start(bf16[96,128]{1,0:T(8,128)(2,1)S(1)} %get-tuple-element.61.refs_0_), channel_id=1, source_target_pairs={{0,12},{1,13},{2,14},{3,15},{4,8},{5,9},{6,10},{7,11},{12,0},{13,1... | collective-permute-start | bytes 73736 | tf_op jit(solution)/shard_map/ppermute | solution.py:342
  52.8 1.5 %fusion.6.refs_8_ = f32[48,512]{1,0:T(8,128)S(1)} fusion(bf16[48,8192]{1,0:T(8,128)(2,1)S(1)} %get-tuple-element.65, bf16[8192,512]{1,0:T(8,128)(2,1)S(1)} %bitcast.34), kind=kOutput, calls=%fused_computation.7 | convolution fusion | flops 402653184 | bytes 9273344 | tf_op jit(solution)/shard_map/dot_general | solution.py:345
  54.4 1.8 %collective-permute-done.13.refs_2_ = bf16[96,128]{1,0:T(8,128)(2,1)S(1)} collective-permute-done((bf16[96,128]{1,0:T(8,128)(2,1)S(1)}, bf16[96,128]{1,0:T(8,128)(2,1)S(1)}, u32[]{:S(2)}, u32[]{:S(2)}) %collective-permute-start.13) | collective-permute-done | bytes 24608 | tf_op jit(solution)/shard_map/ppermute | solution.py:342
  56.8 1.1 %collective-permute-start.15 = (bf16[96,128]{1,0:T(8,128)(2,1)S(1)}, bf16[96,128]{1,0:T(8,128)(2,1)S(1)}, u32[]{:S(2)}, u32[]{:S(2)}) collective-permute-start(bf16[96,128]{1,0:T(8,128)(2,1)S(1)} %shard_map.86.refs_0_), channel_id=1, source_target_pairs={{0,2},{1,3},{2,0},{3,1},{4,6},{5,7},{6,4},{7,5},{12,14},{13,15},{1... | collective-permute-start | bytes 73736 | tf_op jit(solution)/shard_map/ppermute | solution.py:342
  57.8 1.5 %fusion.7.refs_11_ = f32[48,512]{1,0:T(8,128)S(1)} fusion(bf16[48,8192]{1,0:T(8,128)(2,1)S(1)} %get-tuple-element.65, bf16[8192,512]{1,0:T(8,128)(2,1)S(1)} %get-tuple-element.57), kind=kOutput, calls=%fused_computation.8 | convolution fusion | flops 402653184 | bytes 9273344 | tf_op jit(solution)/shard_map/dot_general | solution.py:345
  59.4 1.3 %collective-permute-done.15.refs_1_ = bf16[96,128]{1,0:T(8,128)(2,1)S(1)} collective-permute-done((bf16[96,128]{1,0:T(8,128)(2,1)S(1)}, bf16[96,128]{1,0:T(8,128)(2,1)S(1)}, u32[]{:S(2)}, u32[]{:S(2)}) %collective-permute-start.15) | collective-permute-done | bytes 24608 | tf_op jit(solution)/shard_map/ppermute | solution.py:342
  61.5 13.0 %all_to_all.5 = bf16[8,24,1024]{2,1,0:T(8,128)(2,1)S(1)} all-to-all(bf16[8,24,1024]{2,1,0:T(8,128)(2,1)S(1)} %shard_map.87), channel_id=1, replica_groups={{0,2,4,6,8,10,12,14},{1,3,5,7,9,11,13,15},{16,18,20,22,24,26,28,30},{17..., dimensions={0} | all-to-all | bytes 786432 | tf_op jit(solution)/shard_map/all_to_all | solution.py:400
  (54 shorter events, 9.8 us)
Async XLA Ops:
  0.0 35.6 %collective-permute-start.5 = (bf16[8192,512]{1,0:T(8,128)(2,1)}, bf16[8192,512]{1,0:T(8,128)(2,1)}, u32[]{:S(2)}, u32[]{:S(2)}) collective-permute-start(bf16[8192,512]{1,0:T(8,128)(2,1)} %param.9), channel_id=1, source_target_pairs={{0,1},{1,0},{2,3},{3,2},{4,5},{5,4},{6,7},{7,6},{12,13},{13,12},{1... | collective-permute-start | bytes 25165832 | tf_op jit(solution)/shard_map/ppermute | solution.py:342
  0.5 14.8 %collective-permute-start = (bf16[24,8192]{1,0:T(8,128)(2,1)}, bf16[24,8192]{1,0:T(8,128)(2,1)S(1)}, u32[]{:S(2)}, u32[]{:S(2)}) collective-permute-start(bf16[24,8192]{1,0:T(8,128)(2,1)} %refs_0_.2), channel_id=1, source_target_pairs={{0,4},{1,5},{2,6},{3,7},{4,12},{5,13},{6,14},{7,15},{12,8},{13,9},... | collective-permute-start | bytes 1179656 | tf_op jit(solution)/shard_map/ppermute | solution.py:342
  3.0 12.3 %collective-permute-start.2 = (bf16[24,8192]{1,0:T(8,128)(2,1)}, bf16[24,8192]{1,0:T(8,128)(2,1)S(1)}, u32[]{:S(2)}, u32[]{:S(2)}) collective-permute-start(bf16[24,8192]{1,0:T(8,128)(2,1)} %refs_0_.2), channel_id=1, source_target_pairs={{0,2},{1,3},{2,0},{3,1},{4,6},{5,7},{6,4},{7,5},{12,14},{13,15},{1... | collective-permute-start | bytes 1179656 | tf_op jit(solution)/shard_map/ppermute | solution.py:342
  6.0 12.6 %collective-permute-start.9 = (f32[8,128]{1,0:T(8,128)}, f32[8,128]{1,0:T(8,128)S(1)}, u32[]{:S(2)}, u32[]{:S(2)}) collective-permute-start(f32[8,128]{1,0:T(8,128)} %shard_map.80.refs_0_), channel_id=1, source_target_pairs={{0,4},{1,5},{2,6},{3,7},{4,12},{5,13},{6,14},{7,15},{12,8},{13,9},... | collective-permute-start | bytes 12296 | tf_op jit(solution)/shard_map/ppermute | solution.py:342
  8.6 33.9 %collective-permute-start.8 = (bf16[64,8192]{1,0:T(8,128)(2,1)}, bf16[64,8192]{1,0:T(8,128)(2,1)S(1)}, u32[]{:S(2)}, u32[]{:S(2)}) collective-permute-start(bf16[64,8192]{1,0:T(8,128)(2,1)} %bitcast.23), channel_id=1, source_target_pairs={{0,1},{1,0},{2,3},{3,2},{4,5},{5,4},{6,7},{7,6},{12,13},{13,12},{1... | collective-permute-start | bytes 3145736 | tf_op jit(solution)/shard_map/ppermute | solution.py:342
  10.6 8.0 %copy-start.6 = (f32[8,128]{1,0:T(8,128)S(1)}, f32[8,128]{1,0:T(8,128)}, u32[]{:S(2)}) copy-start(f32[8,128]{1,0:T(8,128)} %shard_map.80.refs_0_) | copy-start | bytes 12292
  10.6 8.8 %copy-start.2 = (bf16[24,8192]{1,0:T(8,128)(2,1)S(1)}, bf16[24,8192]{1,0:T(8,128)(2,1)}, u32[]{:S(2)}) copy-start(bf16[24,8192]{1,0:T(8,128)(2,1)} %refs_0_.2) | copy-start | bytes 1179652
  10.6 8.8 %copy-start.5 = (f32[8192]{0:T(1024)S(1)}, f32[8192]{0:T(1024)}, u32[]{:S(2)}) copy-start(f32[8192]{0:T(1024)} %param.8) | copy-start | bytes 98308
  15.3 12.6 %collective-permute-start.1 = (bf16[24,8192]{1,0:T(8,128)(2,1)S(1)}, bf16[24,8192]{1,0:T(8,128)(2,1)S(1)}, u32[]{:S(2)}, u32[]{:S(2)}) collective-permute-start(bf16[24,8192]{1,0:T(8,128)(2,1)S(1)} %collective-permute-done.block_ref.refs_0_), channel_id=1, source_target_pairs={{0,4},{1,5},{2,6},{3,7},{4,12},{5,13},{6,14},{7,15},{12,8},{13,9},... | collective-permute-start | bytes 1179656 | tf_op jit(solution)/shard_map/ppermute | solution.py:342
  17.1 10.9 %collective-permute-start.4 = (bf16[24,8192]{1,0:T(8,128)(2,1)S(1)}, bf16[24,8192]{1,0:T(8,128)(2,1)S(1)}, u32[]{:S(2)}, u32[]{:S(2)}) collective-permute-start(bf16[24,8192]{1,0:T(8,128)(2,1)S(1)} %collective-permute-done.block_ref.refs_0_), channel_id=1, source_target_pairs={{0,2},{1,3},{2,0},{3,1},{4,6},{5,7},{6,4},{7,5},{12,14},{13,15},{1... | collective-permute-start | bytes 1179656 | tf_op jit(solution)/shard_map/ppermute | solution.py:342
  18.6 10.5 %collective-permute-start.10 = (f32[8,128]{1,0:T(8,128)S(1)}, f32[8,128]{1,0:T(8,128)S(1)}, u32[]{:S(2)}, u32[]{:S(2)}) collective-permute-start(f32[8,128]{1,0:T(8,128)S(1)} %shard_map.81.refs_0_), channel_id=1, source_target_pairs={{0,12},{1,13},{2,14},{3,15},{4,8},{5,9},{6,10},{7,11},{12,0},{13,1... | collective-permute-start | bytes 12296 | tf_op jit(solution)/shard_map/ppermute | solution.py:342
  27.9 11.6 %collective-permute-start.3 = (bf16[24,8192]{1,0:T(8,128)(2,1)S(1)}, bf16[24,8192]{1,0:T(8,128)(2,1)S(1)}, u32[]{:S(2)}, u32[]{:S(2)}) collective-permute-start(bf16[24,8192]{1,0:T(8,128)(2,1)S(1)} %collective-permute-done.1.block_ref.refs_0_), channel_id=1, source_target_pairs={{0,4},{1,5},{2,6},{3,7},{4,12},{5,13},{6,14},{7,15},{12,8},{13,9},... | collective-permute-start | bytes 1179656 | tf_op jit(solution)/shard_map/ppermute | solution.py:342
  27.9 11.6 %collective-permute-start.6 = (bf16[24,8192]{1,0:T(8,128)(2,1)S(1)}, bf16[24,8192]{1,0:T(8,128)(2,1)S(1)}, u32[]{:S(2)}, u32[]{:S(2)}) collective-permute-start(bf16[24,8192]{1,0:T(8,128)(2,1)S(1)} %collective-permute-done.1.block_ref.refs_0_), channel_id=1, source_target_pairs={{0,2},{1,3},{2,0},{3,1},{4,6},{5,7},{6,4},{7,5},{12,14},{13,15},{1... | collective-permute-start | bytes 1179656 | tf_op jit(solution)/shard_map/ppermute | solution.py:342
  29.1 11.9 %slice-start = ((s8[8388608]{0:T(1024)(128)(4,1)}), s8[4194304]{0:T(1024)(128)(4,1)S(1)}, s32[]{:S(2)}) async-start(s8[8388608]{0:T(1024)(128)(4,1)} %bitcast.33), calls=%async_computation.1 | async-start | bytes 8388608
  29.5 11.5 %slice-start.1 = ((s8[8388608]{0:T(1024)(128)(4,1)}), s8[4194304]{0:T(1024)(128)(4,1)S(1)}, s32[]{:S(2)}) async-start(s8[8388608]{0:T(1024)(128)(4,1)} %bitcast.33), calls=%async_computation.2 | async-start | bytes 8388608
  34.6 8.0 %collective-permute-start.11 = (f32[8,128]{1,0:T(8,128)S(1)}, f32[8,128]{1,0:T(8,128)S(1)}, u32[]{:S(2)}, u32[]{:S(2)}) collective-permute-start(f32[8,128]{1,0:T(8,128)S(1)} %shard_map.82.refs_4_.refs_7_.refs_2_), channel_id=1, source_target_pairs={{0,2},{1,3},{2,0},{3,1},{4,6},{5,7},{6,4},{7,5},{12,14},{13,15},{1... | collective-permute-start | bytes 12296 | tf_op jit(solution)/shard_map/ppermute | solution.py:342
  39.6 7.8 %collective-permute-start.7 = (bf16[24,8192]{1,0:T(8,128)(2,1)S(1)}, bf16[24,8192]{1,0:T(8,128)(2,1)S(1)}, u32[]{:S(2)}, u32[]{:S(2)}) collective-permute-start(bf16[24,8192]{1,0:T(8,128)(2,1)S(1)} %broadcast_select_fusion), channel_id=1, source_target_pairs={{0,2},{2,0},{4,6},{6,4},{12,14},{14,12},{8,10},{10,8},{1,5},{3,7},... | collective-permute-start | bytes 1179656 | tf_op jit(solution)/shard_map/ppermute | solution.py:379
  41.0 1.6 %copy-start = (bf16[1,8192,64]{1,2,0:T(8,128)(2,1)S(1)}, bf16[1,8192,64]{1,2,0:T(8,128)(2,1)}, u32[]{:S(2)}) copy-start(bf16[1,8192,64]{1,2,0:T(8,128)(2,1)} %param.10) | copy-start | bytes 3145732
  41.0 2.5 %copy-start.3 = (bf16[16,64,512]{2,1,0:T(8,128)(2,1)S(1)}, bf16[16,64,512]{2,1,0:T(8,128)(2,1)}, u32[]{:S(2)}) copy-start(bf16[16,64,512]{2,1,0:T(8,128)(2,1)} %param.11) | copy-start | bytes 3145732
  43.4 17.2 %collective-permute-start.16 = (bf16[1024,512]{1,0:T(8,128)(2,1)S(1)}, bf16[1024,512]{1,0:T(8,128)(2,1)S(1)}, u32[]{:S(2)}, u32[]{:S(2)}) collective-permute-start(bf16[1024,512]{1,0:T(8,128)(2,1)S(1)} %bitcast.26), channel_id=1, source_target_pairs={{0,1},{1,0},{2,3},{3,2},{4,5},{5,4},{6,7},{7,6},{12,13},{13,12},{1... | collective-permute-start | bytes 3145736 | tf_op jit(solution)/shard_map/ppermute | solution.py:342
  48.6 5.8 %collective-permute-start.12 = (bf16[96,128]{1,0:T(8,128)(2,1)S(1)}, bf16[96,128]{1,0:T(8,128)(2,1)S(1)}, u32[]{:S(2)}, u32[]{:S(2)}) collective-permute-start(bf16[96,128]{1,0:T(8,128)(2,1)S(1)} %get-tuple-element.61.refs_0_), channel_id=1, source_target_pairs={{0,4},{1,5},{2,6},{3,7},{4,12},{5,13},{6,14},{7,15},{12,8},{13,9},... | collective-permute-start | bytes 73736 | tf_op jit(solution)/shard_map/ppermute | solution.py:342
  50.5 5.6 %collective-permute-start.13 = (bf16[96,128]{1,0:T(8,128)(2,1)S(1)}, bf16[96,128]{1,0:T(8,128)(2,1)S(1)}, u32[]{:S(2)}, u32[]{:S(2)}) collective-permute-start(bf16[96,128]{1,0:T(8,128)(2,1)S(1)} %get-tuple-element.61.refs_0_), channel_id=1, source_target_pairs={{0,12},{1,13},{2,14},{3,15},{4,8},{5,9},{6,10},{7,11},{12,0},{13,1... | collective-permute-start | bytes 73736 | tf_op jit(solution)/shard_map/ppermute | solution.py:342
  52.8 3.8 %collective-permute-start.14 = (bf16[96,128]{1,0:T(8,128)(2,1)S(1)}, bf16[96,128]{1,0:T(8,128)(2,1)S(1)}, u32[]{:S(2)}, u32[]{:S(2)}) collective-permute-start(bf16[96,128]{1,0:T(8,128)(2,1)S(1)} %get-tuple-element.61.refs_0_), channel_id=1, source_target_pairs={{0,8},{1,9},{2,10},{3,11},{4,0},{5,1},{6,2},{7,3},{12,4},{13,5},{1... | collective-permute-start | bytes 73736 | tf_op jit(solution)/shard_map/ppermute | solution.py:342
  56.8 3.9 %collective-permute-start.15 = (bf16[96,128]{1,0:T(8,128)(2,1)S(1)}, bf16[96,128]{1,0:T(8,128)(2,1)S(1)}, u32[]{:S(2)}, u32[]{:S(2)}) collective-permute-start(bf16[96,128]{1,0:T(8,128)(2,1)S(1)} %shard_map.86.refs_0_), channel_id=1, source_target_pairs={{0,2},{1,3},{2,0},{3,1},{4,6},{5,7},{6,4},{7,5},{12,14},{13,15},{1... | collective-permute-start | bytes 73736 | tf_op jit(solution)/shard_map/ppermute | solution.py:342
  (2 other events, 1.8 us)

commit v17 on v14

--- a/solution.py
+++ b/solution.py
@@ -14,7 +14,7 @@
 LANES = 128
 CHUNK = 1024
 PIECES = 4
-VMEM_LIMIT = 24 << 20
+VMEM_LIMIT = 12 << 20
 VMEM = pl.BlockSpec(memory_space=pltpu.VMEM)
 
 

time: 76 us -> 76 us (level)
  no operation moved by 1% of the time
where the time goes in v17:
time: 76 us; the launch traced here: 75.7 us
  starting transfers between devices  17.2 us (23%)
  blocking collectives  13.1 us (17%)
  matrix products  12.9 us (17%)
  Pallas kernels  12.2 us (16%)
  waiting for transfers between devices  11.6 us (15%)
  local copies, waits for them, and re-layouts  8.61 us (11%)
    ppermute x13, starting transfers between devices, move(): return lax.ppermute(x, 'adapter', pairs(places, steps, flip))  16.4 us
    all_to_all x1, blocking collectives, shards(): lax.all_to_all(query, 'adapter', 0, 0, axis_index_groups=groups, tiled=True)  13.1 us
    dot_general x6, matrix products, base_rows(): return jnp.dot(rows, weight, preferred_element_type=jnp.float32)  12.9 us
    ppermute x13, waiting for transfers between devices, move(): return lax.ppermute(x, 'adapter', pairs(places, steps, flip))  8.4 us
    unnamed x14, local copies, waits for them, and re-layouts  7.83 us
    pallas_call x6, Pallas kernels, call(): pl.pallas_call(kernel, out_shape=out_shape, in_specs=[VMEM] * len(operand...  5.67 us
    pallas_call x1, Pallas kernels, base_and_weight(): pl.pallas_call(base_kernel, out_shape=(jax.ShapeDtypeStruct((rows, weight...  3.78 us
    ppermute x1, waiting for transfers between devices, shards(): crossed = lax.ppermute(source, 'adapter', split_pairs(places))  3.18 us
  transfers between devices with their start and end apart: 14, of which 9 were waited for; matrix products, arithmetic and copies ran while one was open for 17% of the time, Pallas kernels for 14%

profile of v17, /device:TPU:0, one launch (start us, length us, event | category | flops | bytes accessed | tf_op | source)
XLA Modules:
  0.0 75.7 jit_solution(9814381514844550586)
XLA Ops:
  0.5 2.0 %shard_map.73.refs_0_ = bf16[24,8320]{1,0:T(8,128)(2,1)} custom-call(bf16[24,8192]{1,0:T(8,128)(2,1)} %refs_0_.1, f32[1,8192]{1,0:T(1,128)} %bitcast.29, s32[1,24]{1,0:T(1,128)} %bitcast.30, s32[1,16]{1,0:T(1,128)} %bitcast.31), custom_call_target="tpu_custom_call" | custom-call | tf_op jit(solution)/shard_map/pallas_call | solution.py:110
  2.5 3.1 %collective-permute-start = (bf16[24,8320]{1,0:T(8,128)(2,1)}, bf16[24,8320]{1,0:T(8,128)(2,1)S(1)}, u32[]{:S(2)}, u32[]{:S(2)}) collective-permute-start(bf16[24,8320]{1,0:T(8,128)(2,1)} %shard_map.73.refs_0_), channel_id=1, source_target_pairs={{0,4},{1,5},{2,6},{3,7},{4,12},{5,13},{6,14},{7,15},{12,8},{13,9},... | collective-permute-start | bytes 1198088 | tf_op jit(solution)/shard_map/ppermute | solution.py:319
  5.6 1.5 %collective-permute-start.2 = (bf16[24,8320]{1,0:T(8,128)(2,1)}, bf16[24,8320]{1,0:T(8,128)(2,1)S(1)}, u32[]{:S(2)}, u32[]{:S(2)}) collective-permute-start(bf16[24,8320]{1,0:T(8,128)(2,1)} %shard_map.73.refs_0_), channel_id=1, source_target_pairs={{0,2},{1,3},{2,0},{3,1},{4,6},{5,7},{6,4},{7,5},{12,14},{13,15},{1... | collective-permute-start | bytes 1198088 | tf_op jit(solution)/shard_map/ppermute | solution.py:319
  7.1 3.4 %copy-done.1 = bf16[8192,512]{1,0:T(8,128)(2,1)S(1)} copy-done((bf16[8192,512]{1,0:T(8,128)(2,1)S(1)}, bf16[8192,512]{1,0:T(8,128)(2,1)}, u32[]{:S(2)}) %copy-start.1) | copy-done | bytes 8388632
  10.5 1.2 %copy-done.3 = bf16[1,8192,64]{1,2,0:T(8,128)(2,1)S(1)} copy-done((bf16[1,8192,64]{1,2,0:T(8,128)(2,1)S(1)}, bf16[1,8192,64]{1,2,0:T(8,128)(2,1)}, u32[]{:S(2)}) %copy-start.3) | copy-done | bytes 1048600
  12.5 3.2 %copy-done = bf16[8192,512]{1,0:T(8,128)(2,1)} copy-done((bf16[8192,512]{1,0:T(8,128)(2,1)}, bf16[8192,512]{1,0:T(8,128)(2,1)S(1)}, u32[]{:S(2)}) %copy-start) | copy-done | bytes 8388632
  16.7 2.6 %collective-permute-start.1 = (bf16[24,8320]{1,0:T(8,128)(2,1)S(1)}, bf16[24,8320]{1,0:T(8,128)(2,1)S(1)}, u32[]{:S(2)}, u32[]{:S(2)}) collective-permute-start(bf16[24,8320]{1,0:T(8,128)(2,1)S(1)} %collective-permute-done.block_ref.refs_0_), channel_id=1, source_target_pairs={{0,4},{1,5},{2,6},{3,7},{4,12},{5,13},{6,14},{7,15},{12,8},{13,9},... | collective-permute-start | bytes 1198088 | tf_op jit(solution)/shard_map/ppermute | solution.py:319
  19.3 1.5 %collective-permute-start.5 = (bf16[24,8320]{1,0:T(8,128)(2,1)S(1)}, bf16[24,8320]{1,0:T(8,128)(2,1)S(1)}, u32[]{:S(2)}, u32[]{:S(2)}) collective-permute-start(bf16[24,8320]{1,0:T(8,128)(2,1)S(1)} %collective-permute-done.block_ref.refs_0_), channel_id=1, source_target_pairs={{0,2},{1,3},{2,0},{3,1},{4,6},{5,7},{6,4},{7,5},{12,14},{13,15},{1... | collective-permute-start | bytes 1198088 | tf_op jit(solution)/shard_map/ppermute | solution.py:319
  21.7 5.3 %fusion.refs_2_ = f32[48,512]{1,0:T(8,128)S(1)} fusion(bf16[48,8192]{1,0:T(8,128)(2,1)S(1)} %get-tuple-element.60.refs_0_, bf16[8192,512]{1,0:T(8,128)(2,1)} %copy-done), kind=kOutput, calls=%fused_computation.1 | convolution fusion | flops 402653184 | bytes 9273344 | tf_op jit(solution)/shard_map/dot_general | solution.py:322
  27.0 1.3 %collective-permute-done.1.block_ref.refs_0_ = bf16[24,8320]{1,0:T(8,128)(2,1)S(1)} collective-permute-done((bf16[24,8320]{1,0:T(8,128)(2,1)S(1)}, bf16[24,8320]{1,0:T(8,128)(2,1)S(1)}, u32[]{:S(2)}, u32[]{:S(2)}) %collective-permute-start.1) | collective-permute-done | bytes 399392 | tf_op jit(solution)/shard_map/ppermute | solution.py:319
  28.3 1.4 %collective-permute-done.5.refs_1_ = bf16[24,8320]{1,0:T(8,128)(2,1)S(1)} collective-permute-done((bf16[24,8320]{1,0:T(8,128)(2,1)S(1)}, bf16[24,8320]{1,0:T(8,128)(2,1)S(1)}, u32[]{:S(2)}, u32[]{:S(2)}) %collective-permute-start.5) | collective-permute-done | bytes 399392 | tf_op jit(solution)/shard_map/ppermute | solution.py:319
  30.5 1.5 %collective-permute-start.7 = (bf16[24,8320]{1,0:T(8,128)(2,1)S(1)}, bf16[24,8320]{1,0:T(8,128)(2,1)S(1)}, u32[]{:S(2)}, u32[]{:S(2)}) collective-permute-start(bf16[24,8320]{1,0:T(8,128)(2,1)S(1)} %collective-permute-done.1.block_ref.refs_0_), channel_id=1, source_target_pairs={{0,2},{1,3},{2,0},{3,1},{4,6},{5,7},{6,4},{7,5},{12,14},{13,15},{1... | collective-permute-start | bytes 1198088 | tf_op jit(solution)/shard_map/ppermute | solution.py:319
  32.9 1.5 %fusion.1.refs_3_ = f32[48,512]{1,0:T(8,128)S(1)} fusion(bf16[48,8192]{1,0:T(8,128)(2,1)S(1)} %get-tuple-element.61.refs_1_, bf16[8192,512]{1,0:T(8,128)(2,1)S(1)} %bitcast.23), kind=kOutput, calls=%fused_computation.2 | convolution fusion | flops 402653184 | bytes 9273344 | tf_op jit(solution)/shard_map/dot_general | solution.py:322
  34.5 3.8 %shard_map.79 = (f32[96,512]{1,0:T(8,128)S(1)}, bf16[8192,512]{1,0:T(8,128)(2,1)S(1)}) custom-call(bf16[48,8192]{1,0:T(8,128)(2,1)S(1)} %get-tuple-element.60.refs_0_, bf16[48,8192]{1,0:T(8,128)(2,1)S(1)} %get-tuple-element.61.refs_1_, bf16[8192,512]{1,0:T(8,128)(2,1)} %collective-permute-done.6.refs_2_), custom_call_target="tpu_custom_call" | custom-call | flops 1 | bytes 1 | tf_op jit(solution)/shard_map/pallas_call | solution.py:206
  38.3 1.8 %collective-permute-done.4.block_ref.refs_3_ = bf16[24,8320]{1,0:T(8,128)(2,1)S(1)} collective-permute-done((bf16[24,8320]{1,0:T(8,128)(2,1)S(1)}, bf16[24,8320]{1,0:T(8,128)(2,1)S(1)}, u32[]{:S(2)}, u32[]{:S(2)}) %collective-permute-start.4) | collective-permute-done | bytes 399392 | tf_op jit(solution)/shard_map/ppermute | solution.py:319
  41.8 1.5 %fusion.2.refs_4_ = f32[48,512]{1,0:T(8,128)S(1)} fusion(bf16[48,8192]{1,0:T(8,128)(2,1)S(1)} %get-tuple-element.68, bf16[8192,512]{1,0:T(8,128)(2,1)S(1)} %bitcast.23), kind=kOutput, calls=%fused_computation.3 | convolution fusion | flops 402653184 | bytes 9273344 | tf_op jit(solution)/shard_map/dot_general | solution.py:322
  43.4 1.5 %fusion.3.refs_7_ = f32[48,512]{1,0:T(8,128)S(1)} fusion(bf16[48,8192]{1,0:T(8,128)(2,1)S(1)} %get-tuple-element.68, bf16[8192,512]{1,0:T(8,128)(2,1)S(1)} %get-tuple-element.69), kind=kOutput, calls=%fused_computation.4 | convolution fusion | flops 402653184 | bytes 9273344 | tf_op jit(solution)/shard_map/dot_general | solution.py:322
  44.9 3.2 %collective-permute-done.8.refs_4_ = bf16[24,8320]{1,0:T(8,128)(2,1)S(1)} collective-permute-done((bf16[24,8320]{1,0:T(8,128)(2,1)S(1)}, bf16[24,8320]{1,0:T(8,128)(2,1)S(1)}, u32[]{:S(2)}, u32[]{:S(2)}) %collective-permute-start.8) | collective-permute-done | bytes 399392 | tf_op jit(solution)/shard_map/ppermute | solution.py:355
  49.0 1.3 %collective-permute-start.10 = (bf16[96,128]{1,0:T(8,128)(2,1)S(1)}, bf16[96,128]{1,0:T(8,128)(2,1)S(1)}, u32[]{:S(2)}, u32[]{:S(2)}) collective-permute-start(bf16[96,128]{1,0:T(8,128)(2,1)S(1)} %get-tuple-element.76.refs_0_), channel_id=1, source_target_pairs={{0,12},{1,13},{2,14},{3,15},{4,8},{5,9},{6,10},{7,11},{12,0},{13,1... | collective-permute-start | bytes 73736 | tf_op jit(solution)/shard_map/ppermute | solution.py:319
  52.4 1.5 %fusion.4.refs_5_ = f32[48,512]{1,0:T(8,128)S(1)} fusion(bf16[48,8192]{1,0:T(8,128)(2,1)S(1)} %get-tuple-element.80, bf16[8192,512]{1,0:T(8,128)(2,1)S(1)} %bitcast.23), kind=kOutput, calls=%fused_computation.5 | convolution fusion | flops 402653184 | bytes 9273344 | tf_op jit(solution)/shard_map/dot_general | solution.py:322
  56.0 1.6 %collective-permute-start.12 = (bf16[96,128]{1,0:T(8,128)(2,1)S(1)}, bf16[96,128]{1,0:T(8,128)(2,1)S(1)}, u32[]{:S(2)}, u32[]{:S(2)}) collective-permute-start(bf16[96,128]{1,0:T(8,128)(2,1)S(1)} %shard_map.83.refs_0_), channel_id=1, source_target_pairs={{0,2},{1,3},{2,0},{3,1},{4,6},{5,7},{6,4},{7,5},{12,14},{13,15},{1... | collective-permute-start | bytes 73736 | tf_op jit(solution)/shard_map/ppermute | solution.py:319
  57.6 1.5 %fusion.5.refs_8_ = f32[48,512]{1,0:T(8,128)S(1)} fusion(bf16[48,8192]{1,0:T(8,128)(2,1)S(1)} %get-tuple-element.80, bf16[8192,512]{1,0:T(8,128)(2,1)S(1)} %get-tuple-element.69), kind=kOutput, calls=%fused_computation.6 | convolution fusion | flops 402653184 | bytes 9273344 | tf_op jit(solution)/shard_map/dot_general | solution.py:322
  59.9 1.9 %shard_map.84 = bf16[8,24,1024]{2,1,0:T(8,128)(2,1)S(1)} custom-call(bf16[96,128]{1,0:T(8,128)(2,1)S(1)} %shard_map.83.refs_0_, bf16[96,128]{1,0:T(8,128)(2,1)S(1)} %collective-permute-done.12.refs_1_, f32[48,512]{1,0:T(8,128)S(1)} %fusion.refs_2_, f32[48,512]{1,0:T(8,128)S(1)} %fusion.1.refs_3_, f32[48,512]{1,0:T(8,128)S(1)} %fusion.2.refs_4_, ...), custom_call_target="tpu_custom_call" | custom-call | flops 1 | bytes 1 | tf_op jit(solution)/shard_map/pallas_call | solution.py:58
  61.8 13.1 %all_to_all.5 = bf16[8,24,1024]{2,1,0:T(8,128)(2,1)S(1)} all-to-all(bf16[8,24,1024]{2,1,0:T(8,128)(2,1)S(1)} %shard_map.84), channel_id=1, replica_groups={{0,2,4,6,8,10,12,14},{1,3,5,7,9,11,13,15},{16,18,20,22,24,26,28,30},{17..., dimensions={0} | all-to-all | bytes 786432 | tf_op jit(solution)/shard_map/all_to_all | solution.py:372
  (40 shorter events, 13.2 us)
Async XLA Ops:
  0.0 34.5 %collective-permute-start.6 = (bf16[8192,512]{1,0:T(8,128)(2,1)}, bf16[8192,512]{1,0:T(8,128)(2,1)}, u32[]{:S(2)}, u32[]{:S(2)}) collective-permute-start(bf16[8192,512]{1,0:T(8,128)(2,1)} %refs_0_.2), channel_id=1, source_target_pairs={{0,1},{1,0},{2,3},{3,2},{4,5},{5,4},{6,7},{7,6},{12,13},{13,12},{1... | collective-permute-start | bytes 25165832 | tf_op jit(solution)/shard_map/ppermute | solution.py:319
  0.5 20.4 %collective-permute-start.3 = (bf16[64,8192]{1,0:T(8,128)(2,1)}, bf16[64,8192]{1,0:T(8,128)(2,1)S(1)}, u32[]{:S(2)}, u32[]{:S(2)}) collective-permute-start(bf16[64,8192]{1,0:T(8,128)(2,1)} %bitcast.24), channel_id=1, source_target_pairs={{0,1},{1,0},{2,3},{3,2},{4,5},{5,4},{6,7},{7,6},{12,13},{13,12},{1... | collective-permute-start | bytes 3145736 | tf_op jit(solution)/shard_map/ppermute | solution.py:319
  2.5 13.7 %collective-permute-start = (bf16[24,8320]{1,0:T(8,128)(2,1)}, bf16[24,8320]{1,0:T(8,128)(2,1)S(1)}, u32[]{:S(2)}, u32[]{:S(2)}) collective-permute-start(bf16[24,8320]{1,0:T(8,128)(2,1)} %shard_map.73.refs_0_), channel_id=1, source_target_pairs={{0,4},{1,5},{2,6},{3,7},{4,12},{5,13},{6,14},{7,15},{12,8},{13,9},... | collective-permute-start | bytes 1198088 | tf_op jit(solution)/shard_map/ppermute | solution.py:319
  5.6 11.1 %collective-permute-start.2 = (bf16[24,8320]{1,0:T(8,128)(2,1)}, bf16[24,8320]{1,0:T(8,128)(2,1)S(1)}, u32[]{:S(2)}, u32[]{:S(2)}) collective-permute-start(bf16[24,8320]{1,0:T(8,128)(2,1)} %shard_map.73.refs_0_), channel_id=1, source_target_pairs={{0,2},{1,3},{2,0},{3,1},{4,6},{5,7},{6,4},{7,5},{12,14},{13,15},{1... | collective-permute-start | bytes 1198088 | tf_op jit(solution)/shard_map/ppermute | solution.py:319
  7.1 52.0 %collective-permute-start.13 = (bf16[1024,512]{1,0:T(8,128)(2,1)}, bf16[1024,512]{1,0:T(8,128)(2,1)}, u32[]{:S(2)}, u32[]{:S(2)}) collective-permute-start(bf16[1024,512]{1,0:T(8,128)(2,1)} %bitcast.26), channel_id=1, source_target_pairs={{0,1},{1,0},{2,3},{3,2},{4,5},{5,4},{6,7},{7,6},{12,13},{13,12},{1... | collective-permute-start | bytes 3145736 | tf_op jit(solution)/shard_map/ppermute | solution.py:319
  7.1 3.4 %copy-start.1 = (bf16[8192,512]{1,0:T(8,128)(2,1)S(1)}, bf16[8192,512]{1,0:T(8,128)(2,1)}, u32[]{:S(2)}) copy-start(bf16[8192,512]{1,0:T(8,128)(2,1)} %refs_0_.2) | copy-start | bytes 25165828
  10.5 1.2 %copy-start.3 = (bf16[1,8192,64]{1,2,0:T(8,128)(2,1)S(1)}, bf16[1,8192,64]{1,2,0:T(8,128)(2,1)}, u32[]{:S(2)}) copy-start(bf16[1,8192,64]{1,2,0:T(8,128)(2,1)} %param.10) | copy-start | bytes 3145732
  11.7 9.1 %copy-start.2 = (bf16[24,8320]{1,0:T(8,128)(2,1)S(1)}, bf16[24,8320]{1,0:T(8,128)(2,1)}, u32[]{:S(2)}) copy-start(bf16[24,8320]{1,0:T(8,128)(2,1)} %shard_map.73.refs_0_) | copy-start | bytes 1198084
  12.5 3.2 %copy-start = (bf16[8192,512]{1,0:T(8,128)(2,1)}, bf16[8192,512]{1,0:T(8,128)(2,1)S(1)}, u32[]{:S(2)}) copy-start(bf16[8192,512]{1,0:T(8,128)(2,1)S(1)} %get-tuple-element.47) | copy-start | bytes 25165828
  16.7 11.6 %collective-permute-start.1 = (bf16[24,8320]{1,0:T(8,128)(2,1)S(1)}, bf16[24,8320]{1,0:T(8,128)(2,1)S(1)}, u32[]{:S(2)}, u32[]{:S(2)}) collective-permute-start(bf16[24,8320]{1,0:T(8,128)(2,1)S(1)} %collective-permute-done.block_ref.refs_0_), channel_id=1, source_target_pairs={{0,4},{1,5},{2,6},{3,7},{4,12},{5,13},{6,14},{7,15},{12,8},{13,9},... | collective-permute-start | bytes 1198088 | tf_op jit(solution)/shard_map/ppermute | solution.py:319
  19.3 10.4 %collective-permute-start.5 = (bf16[24,8320]{1,0:T(8,128)(2,1)S(1)}, bf16[24,8320]{1,0:T(8,128)(2,1)S(1)}, u32[]{:S(2)}, u32[]{:S(2)}) collective-permute-start(bf16[24,8320]{1,0:T(8,128)(2,1)S(1)} %collective-permute-done.block_ref.refs_0_), channel_id=1, source_target_pairs={{0,2},{1,3},{2,0},{3,1},{4,6},{5,7},{6,4},{7,5},{12,14},{13,15},{1... | collective-permute-start | bytes 1198088 | tf_op jit(solution)/shard_map/ppermute | solution.py:319
  20.8 12.1 %slice-start = ((s8[8388608]{0:T(1024)(128)(4,1)}), s8[4194304]{0:T(1024)(128)(4,1)S(1)}, s32[]{:S(2)}) async-start(s8[8388608]{0:T(1024)(128)(4,1)} %bitcast.22), calls=%async_computation.1 | async-start | bytes 8388608
  21.7 11.2 %slice-start.1 = ((s8[8388608]{0:T(1024)(128)(4,1)}), s8[4194304]{0:T(1024)(128)(4,1)S(1)}, s32[]{:S(2)}) async-start(s8[8388608]{0:T(1024)(128)(4,1)} %bitcast.22), calls=%async_computation.2 | async-start | bytes 8388608
  29.7 10.4 %collective-permute-start.4 = (bf16[24,8320]{1,0:T(8,128)(2,1)S(1)}, bf16[24,8320]{1,0:T(8,128)(2,1)S(1)}, u32[]{:S(2)}, u32[]{:S(2)}) collective-permute-start(bf16[24,8320]{1,0:T(8,128)(2,1)S(1)} %collective-permute-done.1.block_ref.refs_0_), channel_id=1, source_target_pairs={{0,4},{1,5},{2,6},{3,7},{4,12},{5,13},{6,14},{7,15},{12,8},{13,9},... | collective-permute-start | bytes 1198088 | tf_op jit(solution)/shard_map/ppermute | solution.py:319
  30.5 9.6 %collective-permute-start.7 = (bf16[24,8320]{1,0:T(8,128)(2,1)S(1)}, bf16[24,8320]{1,0:T(8,128)(2,1)S(1)}, u32[]{:S(2)}, u32[]{:S(2)}) collective-permute-start(bf16[24,8320]{1,0:T(8,128)(2,1)S(1)} %collective-permute-done.1.block_ref.refs_0_), channel_id=1, source_target_pairs={{0,2},{1,3},{2,0},{3,1},{4,6},{5,7},{6,4},{7,5},{12,14},{13,15},{1... | collective-permute-start | bytes 1198088 | tf_op jit(solution)/shard_map/ppermute | solution.py:319
  40.2 7.9 %collective-permute-start.8 = (bf16[24,8320]{1,0:T(8,128)(2,1)S(1)}, bf16[24,8320]{1,0:T(8,128)(2,1)S(1)}, u32[]{:S(2)}, u32[]{:S(2)}) collective-permute-start(bf16[24,8320]{1,0:T(8,128)(2,1)S(1)} %broadcast_select_fusion), channel_id=1, source_target_pairs={{0,2},{2,0},{4,6},{6,4},{12,14},{14,12},{8,10},{10,8},{1,5},{3,7},... | collective-permute-start | bytes 1198088 | tf_op jit(solution)/shard_map/ppermute | solution.py:355
  49.0 5.7 %collective-permute-start.10 = (bf16[96,128]{1,0:T(8,128)(2,1)S(1)}, bf16[96,128]{1,0:T(8,128)(2,1)S(1)}, u32[]{:S(2)}, u32[]{:S(2)}) collective-permute-start(bf16[96,128]{1,0:T(8,128)(2,1)S(1)} %get-tuple-element.76.refs_0_), channel_id=1, source_target_pairs={{0,12},{1,13},{2,14},{3,15},{4,8},{5,9},{6,10},{7,11},{12,0},{13,1... | collective-permute-start | bytes 73736 | tf_op jit(solution)/shard_map/ppermute | solution.py:319
  50.3 4.4 %collective-permute-start.11 = (bf16[96,128]{1,0:T(8,128)(2,1)S(1)}, bf16[96,128]{1,0:T(8,128)(2,1)S(1)}, u32[]{:S(2)}, u32[]{:S(2)}) collective-permute-start(bf16[96,128]{1,0:T(8,128)(2,1)S(1)} %get-tuple-element.76.refs_0_), channel_id=1, source_target_pairs={{0,8},{1,9},{2,10},{3,11},{4,0},{5,1},{6,2},{7,3},{12,4},{13,5},{1... | collective-permute-start | bytes 73736 | tf_op jit(solution)/shard_map/ppermute | solution.py:319
  51.2 4.7 %collective-permute-start.9 = (bf16[96,128]{1,0:T(8,128)(2,1)S(1)}, bf16[96,128]{1,0:T(8,128)(2,1)S(1)}, u32[]{:S(2)}, u32[]{:S(2)}) collective-permute-start(bf16[96,128]{1,0:T(8,128)(2,1)S(1)} %get-tuple-element.76.refs_0_), channel_id=1, source_target_pairs={{0,4},{1,5},{2,6},{3,7},{4,12},{5,13},{6,14},{7,15},{12,8},{13,9},... | collective-permute-start | bytes 73736 | tf_op jit(solution)/shard_map/ppermute | solution.py:319
  56.0 3.9 %copy-start.4 = (bf16[16,64,512]{2,1,0:T(8,128)(2,1)S(1)}, bf16[16,64,512]{2,1,0:T(8,128)(2,1)}, u32[]{:S(2)}) copy-start(bf16[16,64,512]{2,1,0:T(8,128)(2,1)} %param.11) | copy-start | bytes 3145732
  56.0 3.9 %collective-permute-start.12 = (bf16[96,128]{1,0:T(8,128)(2,1)S(1)}, bf16[96,128]{1,0:T(8,128)(2,1)S(1)}, u32[]{:S(2)}, u32[]{:S(2)}) collective-permute-start(bf16[96,128]{1,0:T(8,128)(2,1)S(1)} %shard_map.83.refs_0_), channel_id=1, source_target_pairs={{0,2},{1,3},{2,0},{3,1},{4,6},{5,7},{6,4},{7,5},{12,14},{13,15},{1... | collective-permute-start | bytes 73736 | tf_op jit(solution)/shard_map/ppermute | solution.py:319

commit v18 on v13

--- a/solution.py
+++ b/solution.py
@@ -13,6 +13,7 @@
 CORNERS = SIDE * CORES
 LANES = 128
 CHUNK = 1024
+PIECE = 2048
 VMEM_LIMIT = 24 << 20
 VMEM = pl.BlockSpec(memory_space=pltpu.VMEM)
 
@@ -65,28 +66,44 @@
 
 
 def norm_kernel(*refs):
-    sources, (out_ref, *buffers, sems) = refs[:4], refs[4:]
-    copies = [
-        pltpu.make_async_copy(source, buffer, sems.at[number])
-        for number, (source, buffer) in enumerate(zip(sources, buffers))
-    ]
-    for copy in copies:
-        copy.start()
-    for copy in copies:
-        copy.wait()
+    sources, out_hbm, buffers, out_ref, in_sems, out_sems = refs[:4], refs[4], refs[5:9], *refs[9:]
     hidden_ref, gain_ref, index_ref, slot_ref = buffers
     rows, width = hidden_ref.shape
+    chunks = [pl.ds(start, PIECE) for start in range(0, width, PIECE)]
+    arriving = [
+        pltpu.make_async_copy(
+            sources[0].at[:, chunk], hidden_ref.at[:, chunk], in_sems.at[len(buffers) + number]
+        )
+        for number, chunk in enumerate(chunks)
+    ]
+    others = [
+        pltpu.make_async_copy(source, buffer, in_sems.at[number])
+        for number, (source, buffer) in enumerate(zip(sources, buffers))
+        if number
+    ]
+    for copy in arriving + others:
+        copy.start()
     squares = jnp.zeros((rows, LANES), jnp.float32)
-    for start in range(0, width, CHUNK):
-        wide = hidden_ref[:, start : start + CHUNK].astype(jnp.float32)
-        wide = wide * wide
-        for lane in range(0, CHUNK, LANES):
-            squares = squares + wide[:, lane : lane + LANES]
+    for number, copy in enumerate(arriving):
+        copy.wait()
+        for start in range(number * PIECE, (number + 1) * PIECE, CHUNK):
+            wide = hidden_ref[:, start : start + CHUNK].astype(jnp.float32)
+            wide = wide * wide
+            for lane in range(0, CHUNK, LANES):
+                squares = squares + wide[:, lane : lane + LANES]
     inv_rms = lax.rsqrt(jnp.sum(squares, axis=1, keepdims=True) / width + EPS)
-    for start in range(0, width, CHUNK):
-        lanes = slice(start, start + CHUNK)
-        wide = hidden_ref[:, lanes].astype(jnp.float32)
-        out_ref[:, lanes] = (wide * inv_rms * gain_ref[:, lanes]).astype(jnp.bfloat16)
+    for copy in others:
+        copy.wait()
+    leaving = []
+    for number, chunk in enumerate(chunks):
+        for start in range(number * PIECE, (number + 1) * PIECE, CHUNK):
+            lanes = slice(start, start + CHUNK)
+            wide = hidden_ref[:, lanes].astype(jnp.float32)
+            out_ref[:, lanes] = (wide * inv_rms * gain_ref[:, lanes]).astype(jnp.bfloat16)
+        leaving.append(
+            pltpu.make_async_copy(out_ref.at[:, chunk], out_hbm.at[:, chunk], out_sems.at[number])
+        )
+        leaving[-1].start()
     index = index_ref[...]
     slot = jnp.zeros(index.shape, jnp.float32)
     for name in range(slot_ref.shape[1]):
@@ -95,6 +112,13 @@
     down = lax.broadcasted_iota(jnp.int32, (rows, rows), 0)
     column = jnp.sum(jnp.where(across == down, slot, 0.0), axis=1, keepdims=True)
     out_ref[:, width:] = jnp.broadcast_to(column, (rows, LANES)).astype(jnp.bfloat16)
+    end = pl.ds(width, LANES)
+    leaving.append(
+        pltpu.make_async_copy(out_ref.at[:, end], out_hbm.at[:, end], out_sems.at[len(chunks)])
+    )
+    leaving[-1].start()
+    for copy in leaving:
+        copy.wait()
 
 
 def normalize(hidden, norm_weight, adapter_index, adapter_slot):
@@ -106,13 +130,19 @@
         adapter_slot.reshape(1, -1),
     )
     spaces = (pltpu.VMEM, pltpu.VMEM, pltpu.VMEM, pltpu.SMEM)
+    out_shape = jax.ShapeDtypeStruct((rows, width + LANES), jnp.bfloat16)
+    pieces = width // PIECE
     return pl.pallas_call(
         norm_kernel,
-        out_shape=jax.ShapeDtypeStruct((rows, width + LANES), jnp.bfloat16),
+        out_shape=out_shape,
         in_specs=[pl.BlockSpec(memory_space=pltpu.HBM)] * len(sources),
-        out_specs=VMEM,
+        out_specs=pl.BlockSpec(memory_space=pltpu.HBM),
         scratch_shapes=[space(x.shape, x.dtype) for space, x in zip(spaces, sources)]
-        + [pltpu.SemaphoreType.DMA((len(sources),))],
+        + [
+            pltpu.VMEM(out_shape.shape, out_shape.dtype),
+            pltpu.SemaphoreType.DMA((len(sources) + pieces,)),
+            pltpu.SemaphoreType.DMA((pieces + 1,)),
+        ],
     )(*sources)
 
 

time: 74.4 us -> 74.5 us (level)
  no operation moved by 1% of the time
where the time goes in v18:
time: 74.5 us; the launch traced here: 74.2 us
  starting transfers between devices  17.5 us (23%)
  waiting for transfers between devices  17.4 us (23%)
  matrix products  13 us (17%)
  blocking collectives  12.8 us (17%)
  Pallas kernels  10.4 us (14%)
  local copies, waits for them, and re-layouts  3.02 us (4%)
    ppermute x13, starting transfers between devices, move(): return lax.ppermute(x, 'adapter', pairs(places, steps, flip))  16.7 us
    ppermute x13, waiting for transfers between devices, move(): return lax.ppermute(x, 'adapter', pairs(places, steps, flip))  14.2 us
    dot_general x6, matrix products, base_rows(): return jnp.dot(rows, weight, preferred_element_type=jnp.float32)  13 us
    all_to_all x1, blocking collectives, shards(): lax.all_to_all(query, 'adapter', 0, 0, axis_index_groups=groups, tiled=True)  12.8 us
    pallas_call x6, Pallas kernels, call(): pl.pallas_call(kernel, out_shape=out_shape, in_specs=[VMEM] * len(operand...  4.48 us
    pallas_call x1, Pallas kernels, base_and_weight(): pl.pallas_call(base_kernel, out_shape=(jax.ShapeDtypeStruct((rows, weight...  3.79 us
    ppermute x1, waiting for transfers between devices, shards(): crossed = lax.ppermute(source, 'adapter', split_pairs(places))  3.15 us
    unnamed x12, local copies, waits for them, and re-layouts  2.24 us
  transfers between devices with their start and end apart: 14, of which 8 were waited for; matrix products, arithmetic and copies ran while one was open for 18% of the time, Pallas kernels for 13%

profile of v18, /device:TPU:0, one launch (start us, length us, event | category | flops | bytes accessed | tf_op | source)
XLA Modules:
  0.0 74.2 jit_solution(2326876484826075832)
XLA Ops:
  0.5 2.1 %shard_map.73.refs_0_ = bf16[24,8320]{1,0:T(8,128)(2,1)} custom-call(bf16[24,8192]{1,0:T(8,128)(2,1)} %refs_0_.1, f32[1,8192]{1,0:T(1,128)} %bitcast.32, s32[1,24]{1,0:T(1,128)} %bitcast.33, s32[1,16]{1,0:T(1,128)} %bitcast.34), custom_call_target="tpu_custom_call" | custom-call | tf_op jit(solution)/shard_map/pallas_call | solution.py:135
  2.6 3.1 %collective-permute-start = (bf16[24,8320]{1,0:T(8,128)(2,1)}, bf16[24,8320]{1,0:T(8,128)(2,1)S(1)}, u32[]{:S(2)}, u32[]{:S(2)}) collective-permute-start(bf16[24,8320]{1,0:T(8,128)(2,1)} %shard_map.73.refs_0_), channel_id=1, source_target_pairs={{0,4},{1,5},{2,6},{3,7},{4,12},{5,13},{6,14},{7,15},{12,8},{13,9},... | collective-permute-start | bytes 1198088 | tf_op jit(solution)/shard_map/ppermute | solution.py:319
  5.7 1.5 %collective-permute-start.2 = (bf16[24,8320]{1,0:T(8,128)(2,1)}, bf16[24,8320]{1,0:T(8,128)(2,1)S(1)}, u32[]{:S(2)}, u32[]{:S(2)}) collective-permute-start(bf16[24,8320]{1,0:T(8,128)(2,1)} %shard_map.73.refs_0_), channel_id=1, source_target_pairs={{0,2},{1,3},{2,0},{3,1},{4,6},{5,7},{6,4},{7,5},{12,14},{13,15},{1... | collective-permute-start | bytes 1198088 | tf_op jit(solution)/shard_map/ppermute | solution.py:319
  7.2 9.1 %collective-permute-done.block_ref.refs_0_ = bf16[24,8320]{1,0:T(8,128)(2,1)S(1)} collective-permute-done((bf16[24,8320]{1,0:T(8,128)(2,1)}, bf16[24,8320]{1,0:T(8,128)(2,1)S(1)}, u32[]{:S(2)}, u32[]{:S(2)}) %collective-permute-start) | collective-permute-done | bytes 399392 | tf_op jit(solution)/shard_map/ppermute | solution.py:319
  16.8 2.6 %collective-permute-start.1 = (bf16[24,8320]{1,0:T(8,128)(2,1)S(1)}, bf16[24,8320]{1,0:T(8,128)(2,1)S(1)}, u32[]{:S(2)}, u32[]{:S(2)}) collective-permute-start(bf16[24,8320]{1,0:T(8,128)(2,1)S(1)} %collective-permute-done.block_ref.refs_0_), channel_id=1, source_target_pairs={{0,4},{1,5},{2,6},{3,7},{4,12},{5,13},{6,14},{7,15},{12,8},{13,9},... | collective-permute-start | bytes 1198088 | tf_op jit(solution)/shard_map/ppermute | solution.py:319
  19.4 1.5 %collective-permute-start.5 = (bf16[24,8320]{1,0:T(8,128)(2,1)S(1)}, bf16[24,8320]{1,0:T(8,128)(2,1)S(1)}, u32[]{:S(2)}, u32[]{:S(2)}) collective-permute-start(bf16[24,8320]{1,0:T(8,128)(2,1)S(1)} %collective-permute-done.block_ref.refs_0_), channel_id=1, source_target_pairs={{0,2},{1,3},{2,0},{3,1},{4,6},{5,7},{6,4},{7,5},{12,14},{13,15},{1... | collective-permute-start | bytes 1198088 | tf_op jit(solution)/shard_map/ppermute | solution.py:319
  20.9 1.2 %copy-done = bf16[1,8192,64]{1,2,0:T(8,128)(2,1)S(1)} copy-done((bf16[1,8192,64]{1,2,0:T(8,128)(2,1)S(1)}, bf16[1,8192,64]{1,2,0:T(8,128)(2,1)}, u32[]{:S(2)}) %copy-start) | copy-done | bytes 1048600
  22.1 1.0 %copy-done.2 = bf16[24,8320]{1,0:T(8,128)(2,1)S(1)} copy-done((bf16[24,8320]{1,0:T(8,128)(2,1)S(1)}, bf16[24,8320]{1,0:T(8,128)(2,1)}, u32[]{:S(2)}) %copy-start.2) | copy-done | bytes 399384
  24.0 5.4 %fusion.refs_2_ = f32[48,512]{1,0:T(8,128)S(1)} fusion(bf16[48,8192]{1,0:T(8,128)(2,1)S(1)} %get-tuple-element.50.refs_0_, bf16[8192,512]{1,0:T(8,128)(2,1)} %param.9), kind=kOutput, calls=%fused_computation.1 | convolution fusion | flops 402653184 | bytes 9273344 | tf_op jit(solution)/shard_map/dot_general | solution.py:322
  29.5 1.2 %collective-permute-start.4 = (bf16[24,8320]{1,0:T(8,128)(2,1)S(1)}, bf16[24,8320]{1,0:T(8,128)(2,1)S(1)}, u32[]{:S(2)}, u32[]{:S(2)}) collective-permute-start(bf16[24,8320]{1,0:T(8,128)(2,1)S(1)} %collective-permute-done.1.block_ref.refs_0_), channel_id=1, source_target_pairs={{0,4},{1,5},{2,6},{3,7},{4,12},{5,13},{6,14},{7,15},{12,8},{13,9},... | collective-permute-start | bytes 1198088 | tf_op jit(solution)/shard_map/ppermute | solution.py:319
  30.7 1.4 %collective-permute-start.7 = (bf16[24,8320]{1,0:T(8,128)(2,1)S(1)}, bf16[24,8320]{1,0:T(8,128)(2,1)S(1)}, u32[]{:S(2)}, u32[]{:S(2)}) collective-permute-start(bf16[24,8320]{1,0:T(8,128)(2,1)S(1)} %collective-permute-done.1.block_ref.refs_0_), channel_id=1, source_target_pairs={{0,2},{1,3},{2,0},{3,1},{4,6},{5,7},{6,4},{7,5},{12,14},{13,15},{1... | collective-permute-start | bytes 1198088 | tf_op jit(solution)/shard_map/ppermute | solution.py:319
  33.0 1.5 %fusion.1.refs_3_ = f32[48,512]{1,0:T(8,128)S(1)} fusion(bf16[48,8192]{1,0:T(8,128)(2,1)S(1)} %get-tuple-element.51.refs_1_, bf16[8192,512]{1,0:T(8,128)(2,1)S(1)} %bitcast.30), kind=kOutput, calls=%fused_computation.2 | convolution fusion | flops 402653184 | bytes 9273344 | tf_op jit(solution)/shard_map/dot_general | solution.py:322
  34.6 3.8 %shard_map.78 = (f32[96,512]{1,0:T(8,128)S(1)}, bf16[8192,512]{1,0:T(8,128)(2,1)S(1)}) custom-call(bf16[48,8192]{1,0:T(8,128)(2,1)S(1)} %get-tuple-element.50.refs_0_, bf16[48,8192]{1,0:T(8,128)(2,1)S(1)} %get-tuple-element.51.refs_1_, bf16[8192,512]{1,0:T(8,128)(2,1)} %collective-permute-done.6.refs_2_), custom_call_target="tpu_custom_call" | custom-call | flops 1 | bytes 1 | tf_op jit(solution)/shard_map/pallas_call | solution.py:235
  38.4 1.5 %collective-permute-done.4.block_ref.refs_3_ = bf16[24,8320]{1,0:T(8,128)(2,1)S(1)} collective-permute-done((bf16[24,8320]{1,0:T(8,128)(2,1)S(1)}, bf16[24,8320]{1,0:T(8,128)(2,1)S(1)}, u32[]{:S(2)}, u32[]{:S(2)}) %collective-permute-start.4) | collective-permute-done | bytes 399392 | tf_op jit(solution)/shard_map/ppermute | solution.py:319
  41.9 1.5 %fusion.2.refs_4_ = f32[48,512]{1,0:T(8,128)S(1)} fusion(bf16[48,8192]{1,0:T(8,128)(2,1)S(1)} %get-tuple-element.58, bf16[8192,512]{1,0:T(8,128)(2,1)S(1)} %bitcast.30), kind=kOutput, calls=%fused_computation.3 | convolution fusion | flops 402653184 | bytes 9273344 | tf_op jit(solution)/shard_map/dot_general | solution.py:322
  43.4 1.5 %fusion.3.refs_7_ = f32[48,512]{1,0:T(8,128)S(1)} fusion(bf16[48,8192]{1,0:T(8,128)(2,1)S(1)} %get-tuple-element.58, bf16[8192,512]{1,0:T(8,128)(2,1)S(1)} %get-tuple-element.59), kind=kOutput, calls=%fused_computation.4 | convolution fusion | flops 402653184 | bytes 9273344 | tf_op jit(solution)/shard_map/dot_general | solution.py:322
  45.0 3.1 %collective-permute-done.8.refs_4_ = bf16[24,8320]{1,0:T(8,128)(2,1)S(1)} collective-permute-done((bf16[24,8320]{1,0:T(8,128)(2,1)S(1)}, bf16[24,8320]{1,0:T(8,128)(2,1)S(1)}, u32[]{:S(2)}, u32[]{:S(2)}) %collective-permute-start.8) | collective-permute-done | bytes 399392 | tf_op jit(solution)/shard_map/ppermute | solution.py:354
  49.1 1.3 %collective-permute-start.10 = (bf16[96,128]{1,0:T(8,128)(2,1)S(1)}, bf16[96,128]{1,0:T(8,128)(2,1)S(1)}, u32[]{:S(2)}, u32[]{:S(2)}) collective-permute-start(bf16[96,128]{1,0:T(8,128)(2,1)S(1)} %get-tuple-element.66.refs_0_), channel_id=1, source_target_pairs={{0,12},{1,13},{2,14},{3,15},{4,8},{5,9},{6,10},{7,11},{12,0},{13,1... | collective-permute-start | bytes 73736 | tf_op jit(solution)/shard_map/ppermute | solution.py:319
  51.3 1.2 %collective-permute-start.9 = (bf16[96,128]{1,0:T(8,128)(2,1)S(1)}, bf16[96,128]{1,0:T(8,128)(2,1)S(1)}, u32[]{:S(2)}, u32[]{:S(2)}) collective-permute-start(bf16[96,128]{1,0:T(8,128)(2,1)S(1)} %get-tuple-element.66.refs_0_), channel_id=1, source_target_pairs={{0,4},{1,5},{2,6},{3,7},{4,12},{5,13},{6,14},{7,15},{12,8},{13,9},... | collective-permute-start | bytes 73736 | tf_op jit(solution)/shard_map/ppermute | solution.py:319
  52.4 1.5 %fusion.4.refs_5_ = f32[48,512]{1,0:T(8,128)S(1)} fusion(bf16[48,8192]{1,0:T(8,128)(2,1)S(1)} %get-tuple-element.70, bf16[8192,512]{1,0:T(8,128)(2,1)S(1)} %bitcast.30), kind=kOutput, calls=%fused_computation.5 | convolution fusion | flops 402653184 | bytes 9273344 | tf_op jit(solution)/shard_map/dot_general | solution.py:322
  54.8 1.2 %collective-permute-done.9.refs_1_ = bf16[96,128]{1,0:T(8,128)(2,1)S(1)} collective-permute-done((bf16[96,128]{1,0:T(8,128)(2,1)S(1)}, bf16[96,128]{1,0:T(8,128)(2,1)S(1)}, u32[]{:S(2)}, u32[]{:S(2)}) %collective-permute-start.9) | collective-permute-done | bytes 24608 | tf_op jit(solution)/shard_map/ppermute | solution.py:319
  56.1 1.6 %collective-permute-start.12 = (bf16[96,128]{1,0:T(8,128)(2,1)S(1)}, bf16[96,128]{1,0:T(8,128)(2,1)S(1)}, u32[]{:S(2)}, u32[]{:S(2)}) collective-permute-start(bf16[96,128]{1,0:T(8,128)(2,1)S(1)} %shard_map.82.refs_0_), channel_id=1, source_target_pairs={{0,2},{1,3},{2,0},{3,1},{4,6},{5,7},{6,4},{7,5},{12,14},{13,15},{1... | collective-permute-start | bytes 73736 | tf_op jit(solution)/shard_map/ppermute | solution.py:319
  57.7 1.5 %fusion.5.refs_8_ = f32[48,512]{1,0:T(8,128)S(1)} fusion(bf16[48,8192]{1,0:T(8,128)(2,1)S(1)} %get-tuple-element.70, bf16[8192,512]{1,0:T(8,128)(2,1)S(1)} %get-tuple-element.59), kind=kOutput, calls=%fused_computation.6 | convolution fusion | flops 402653184 | bytes 9273344 | tf_op jit(solution)/shard_map/dot_general | solution.py:322
  60.7 12.8 %all_to_all.5 = bf16[8,24,1024]{2,1,0:T(8,128)(2,1)S(1)} all-to-all(bf16[8,24,1024]{2,1,0:T(8,128)(2,1)S(1)} %shard_map.83), channel_id=1, replica_groups={{0,2,4,6,8,10,12,14},{1,3,5,7,9,11,13,15},{16,18,20,22,24,26,28,30},{17..., dimensions={0} | all-to-all | bytes 786432 | tf_op jit(solution)/shard_map/all_to_all | solution.py:371
  (37 shorter events, 9.8 us)
Async XLA Ops:
  0.0 34.6 %collective-permute-start.6 = (bf16[8192,512]{1,0:T(8,128)(2,1)}, bf16[8192,512]{1,0:T(8,128)(2,1)}, u32[]{:S(2)}, u32[]{:S(2)}) collective-permute-start(bf16[8192,512]{1,0:T(8,128)(2,1)} %param.9), channel_id=1, source_target_pairs={{0,1},{1,0},{2,3},{3,2},{4,5},{5,4},{6,7},{7,6},{12,13},{13,12},{1... | collective-permute-start | bytes 25165832 | tf_op jit(solution)/shard_map/ppermute | solution.py:319
  0.5 20.4 %collective-permute-start.3 = (bf16[64,8192]{1,0:T(8,128)(2,1)}, bf16[64,8192]{1,0:T(8,128)(2,1)S(1)}, u32[]{:S(2)}, u32[]{:S(2)}) collective-permute-start(bf16[64,8192]{1,0:T(8,128)(2,1)} %bitcast.22), channel_id=1, source_target_pairs={{0,1},{1,0},{2,3},{3,2},{4,5},{5,4},{6,7},{7,6},{12,13},{13,12},{1... | collective-permute-start | bytes 3145736 | tf_op jit(solution)/shard_map/ppermute | solution.py:319
  2.6 13.7 %collective-permute-start = (bf16[24,8320]{1,0:T(8,128)(2,1)}, bf16[24,8320]{1,0:T(8,128)(2,1)S(1)}, u32[]{:S(2)}, u32[]{:S(2)}) collective-permute-start(bf16[24,8320]{1,0:T(8,128)(2,1)} %shard_map.73.refs_0_), channel_id=1, source_target_pairs={{0,4},{1,5},{2,6},{3,7},{4,12},{5,13},{6,14},{7,15},{12,8},{13,9},... | collective-permute-start | bytes 1198088 | tf_op jit(solution)/shard_map/ppermute | solution.py:319
  5.7 11.1 %collective-permute-start.2 = (bf16[24,8320]{1,0:T(8,128)(2,1)}, bf16[24,8320]{1,0:T(8,128)(2,1)S(1)}, u32[]{:S(2)}, u32[]{:S(2)}) collective-permute-start(bf16[24,8320]{1,0:T(8,128)(2,1)} %shard_map.73.refs_0_), channel_id=1, source_target_pairs={{0,2},{1,3},{2,0},{3,1},{4,6},{5,7},{6,4},{7,5},{12,14},{13,15},{1... | collective-permute-start | bytes 1198088 | tf_op jit(solution)/shard_map/ppermute | solution.py:319
  7.2 52.0 %collective-permute-start.13 = (bf16[1024,512]{1,0:T(8,128)(2,1)}, bf16[1024,512]{1,0:T(8,128)(2,1)S(1)}, u32[]{:S(2)}, u32[]{:S(2)}) collective-permute-start(bf16[1024,512]{1,0:T(8,128)(2,1)} %bitcast.27), channel_id=1, source_target_pairs={{0,1},{1,0},{2,3},{3,2},{4,5},{5,4},{6,7},{7,6},{12,13},{13,12},{1... | collective-permute-start | bytes 3145736 | tf_op jit(solution)/shard_map/ppermute | solution.py:319
  16.8 12.7 %collective-permute-start.1 = (bf16[24,8320]{1,0:T(8,128)(2,1)S(1)}, bf16[24,8320]{1,0:T(8,128)(2,1)S(1)}, u32[]{:S(2)}, u32[]{:S(2)}) collective-permute-start(bf16[24,8320]{1,0:T(8,128)(2,1)S(1)} %collective-permute-done.block_ref.refs_0_), channel_id=1, source_target_pairs={{0,4},{1,5},{2,6},{3,7},{4,12},{5,13},{6,14},{7,15},{12,8},{13,9},... | collective-permute-start | bytes 1198088 | tf_op jit(solution)/shard_map/ppermute | solution.py:319
  19.4 10.1 %collective-permute-start.5 = (bf16[24,8320]{1,0:T(8,128)(2,1)S(1)}, bf16[24,8320]{1,0:T(8,128)(2,1)S(1)}, u32[]{:S(2)}, u32[]{:S(2)}) collective-permute-start(bf16[24,8320]{1,0:T(8,128)(2,1)S(1)} %collective-permute-done.block_ref.refs_0_), channel_id=1, source_target_pairs={{0,2},{1,3},{2,0},{3,1},{4,6},{5,7},{6,4},{7,5},{12,14},{13,15},{1... | collective-permute-start | bytes 1198088 | tf_op jit(solution)/shard_map/ppermute | solution.py:319
  20.9 1.2 %copy-start = (bf16[1,8192,64]{1,2,0:T(8,128)(2,1)S(1)}, bf16[1,8192,64]{1,2,0:T(8,128)(2,1)}, u32[]{:S(2)}) copy-start(bf16[1,8192,64]{1,2,0:T(8,128)(2,1)} %param.10) | copy-start | bytes 3145732
  22.1 1.0 %copy-start.2 = (bf16[24,8320]{1,0:T(8,128)(2,1)S(1)}, bf16[24,8320]{1,0:T(8,128)(2,1)}, u32[]{:S(2)}) copy-start(bf16[24,8320]{1,0:T(8,128)(2,1)} %shard_map.73.refs_0_) | copy-start | bytes 1198084
  23.1 9.9 %slice-start = ((s8[8388608]{0:T(1024)(128)(4,1)}), s8[4194304]{0:T(1024)(128)(4,1)S(1)}, s32[]{:S(2)}) async-start(s8[8388608]{0:T(1024)(128)(4,1)} %bitcast.29), calls=%async_computation.1 | async-start | bytes 8388608
  24.0 8.1 %copy-start.1 = (bf16[1,8192,64]{1,2,0:T(8,128)(2,1)S(1)}, bf16[1,8192,64]{1,2,0:T(8,128)(2,1)}, u32[]{:S(2)}) copy-start(bf16[1,8192,64]{1,2,0:T(8,128)(2,1)} %param.10) | copy-start | bytes 3145732
  24.0 9.0 %slice-start.1 = ((s8[8388608]{0:T(1024)(128)(4,1)}), s8[4194304]{0:T(1024)(128)(4,1)S(1)}, s32[]{:S(2)}) async-start(s8[8388608]{0:T(1024)(128)(4,1)} %bitcast.29), calls=%async_computation.2 | async-start | bytes 8388608
  29.5 10.4 %collective-permute-start.4 = (bf16[24,8320]{1,0:T(8,128)(2,1)S(1)}, bf16[24,8320]{1,0:T(8,128)(2,1)S(1)}, u32[]{:S(2)}, u32[]{:S(2)}) collective-permute-start(bf16[24,8320]{1,0:T(8,128)(2,1)S(1)} %collective-permute-done.1.block_ref.refs_0_), channel_id=1, source_target_pairs={{0,4},{1,5},{2,6},{3,7},{4,12},{5,13},{6,14},{7,15},{12,8},{13,9},... | collective-permute-start | bytes 1198088 | tf_op jit(solution)/shard_map/ppermute | solution.py:319
  30.7 9.5 %collective-permute-start.7 = (bf16[24,8320]{1,0:T(8,128)(2,1)S(1)}, bf16[24,8320]{1,0:T(8,128)(2,1)S(1)}, u32[]{:S(2)}, u32[]{:S(2)}) collective-permute-start(bf16[24,8320]{1,0:T(8,128)(2,1)S(1)} %collective-permute-done.1.block_ref.refs_0_), channel_id=1, source_target_pairs={{0,2},{1,3},{2,0},{3,1},{4,6},{5,7},{6,4},{7,5},{12,14},{13,15},{1... | collective-permute-start | bytes 1198088 | tf_op jit(solution)/shard_map/ppermute | solution.py:319
  40.2 7.9 %collective-permute-start.8 = (bf16[24,8320]{1,0:T(8,128)(2,1)S(1)}, bf16[24,8320]{1,0:T(8,128)(2,1)S(1)}, u32[]{:S(2)}, u32[]{:S(2)}) collective-permute-start(bf16[24,8320]{1,0:T(8,128)(2,1)S(1)} %broadcast_select_fusion), channel_id=1, source_target_pairs={{0,2},{2,0},{4,6},{6,4},{12,14},{14,12},{8,10},{10,8},{1,5},{3,7},... | collective-permute-start | bytes 1198088 | tf_op jit(solution)/shard_map/ppermute | solution.py:354
  49.1 5.7 %collective-permute-start.10 = (bf16[96,128]{1,0:T(8,128)(2,1)S(1)}, bf16[96,128]{1,0:T(8,128)(2,1)S(1)}, u32[]{:S(2)}, u32[]{:S(2)}) collective-permute-start(bf16[96,128]{1,0:T(8,128)(2,1)S(1)} %get-tuple-element.66.refs_0_), channel_id=1, source_target_pairs={{0,12},{1,13},{2,14},{3,15},{4,8},{5,9},{6,10},{7,11},{12,0},{13,1... | collective-permute-start | bytes 73736 | tf_op jit(solution)/shard_map/ppermute | solution.py:319
  50.4 4.3 %collective-permute-start.11 = (bf16[96,128]{1,0:T(8,128)(2,1)S(1)}, bf16[96,128]{1,0:T(8,128)(2,1)S(1)}, u32[]{:S(2)}, u32[]{:S(2)}) collective-permute-start(bf16[96,128]{1,0:T(8,128)(2,1)S(1)} %get-tuple-element.66.refs_0_), channel_id=1, source_target_pairs={{0,8},{1,9},{2,10},{3,11},{4,0},{5,1},{6,2},{7,3},{12,4},{13,5},{1... | collective-permute-start | bytes 73736 | tf_op jit(solution)/shard_map/ppermute | solution.py:319
  51.3 4.7 %collective-permute-start.9 = (bf16[96,128]{1,0:T(8,128)(2,1)S(1)}, bf16[96,128]{1,0:T(8,128)(2,1)S(1)}, u32[]{:S(2)}, u32[]{:S(2)}) collective-permute-start(bf16[96,128]{1,0:T(8,128)(2,1)S(1)} %get-tuple-element.66.refs_0_), channel_id=1, source_target_pairs={{0,4},{1,5},{2,6},{3,7},{4,12},{5,13},{6,14},{7,15},{12,8},{13,9},... | collective-permute-start | bytes 73736 | tf_op jit(solution)/shard_map/ppermute | solution.py:319
  56.1 3.9 %copy-start.3 = (bf16[16,64,512]{2,1,0:T(8,128)(2,1)S(1)}, bf16[16,64,512]{2,1,0:T(8,128)(2,1)}, u32[]{:S(2)}) copy-start(bf16[16,64,512]{2,1,0:T(8,128)(2,1)} %param.11) | copy-start | bytes 3145732
  56.1 3.9 %collective-permute-start.12 = (bf16[96,128]{1,0:T(8,128)(2,1)S(1)}, bf16[96,128]{1,0:T(8,128)(2,1)S(1)}, u32[]{:S(2)}, u32[]{:S(2)}) collective-permute-start(bf16[96,128]{1,0:T(8,128)(2,1)S(1)} %shard_map.82.refs_0_), channel_id=1, source_target_pairs={{0,2},{1,3},{2,0},{3,1},{4,6},{5,7},{6,4},{7,5},{12,14},{13,15},{1... | collective-permute-start | bytes 73736 | tf_op jit(solution)/shard_map/ppermute | solution.py:319

commit v19 on v13

--- a/solution.py
+++ b/solution.py
@@ -14,6 +14,7 @@
 LANES = 128
 CHUNK = 1024
 VMEM_LIMIT = 24 << 20
+LARGE = 44 << 20
 VMEM = pl.BlockSpec(memory_space=pltpu.VMEM)
 
 
@@ -200,7 +201,7 @@
         out_ref[...] += jnp.dot(rows, kept_ref[lanes, :], preferred_element_type=jnp.float32)
 
 
-def base_and_weight(blocks, weight):
+def base_and_weight(blocks, weight, limit=VMEM_LIMIT):
     rows = blocks[0].shape[0] * len(blocks)
     return pl.pallas_call(
         base_kernel,
@@ -211,7 +212,7 @@
         in_specs=[VMEM] * len(blocks) + [pl.BlockSpec(memory_space=pltpu.HBM)],
         out_specs=(VMEM, VMEM),
         scratch_shapes=[pltpu.SemaphoreType.DMA((weight.shape[0] // CHUNK,))],
-        compiler_params=pltpu.CompilerParams(vmem_limit_bytes=VMEM_LIMIT),
+        compiler_params=pltpu.CompilerParams(vmem_limit_bytes=limit),
         cost_estimate=pl.CostEstimate(flops=1, bytes_accessed=1, transcendentals=0),
     )(*blocks, weight)
 
@@ -315,7 +316,11 @@
         other.append(move(after(block[step], *other[-1:]), 0, 2))
         if step:
             meet(after([block[step - 1], other[step - 1]], block[step]))
-            bases.append(base_rows(rows[-1], query_weight))
+            if step == 1:
+                base, query_weight = base_and_weight(rows, query_weight, LARGE)
+            else:
+                base = base_rows(rows[-1], query_weight)
+            bases.append(base)
     base, weight_other = base_and_weight(after(rows, bases[-1]), weight_other)
     block[last] = after(block[last], base)
     tokens.append(token(block[last]))

time: 74.4 us -> 77.4 us (1.040)
  Pallas kernels: 10.3 us -> 16.4 us
  matrix products: 13 us -> 7.62 us
  local copies, waits for them, and re-layouts: 3.02 us -> 4.78 us
  waiting for transfers between devices: 17.4 us -> 19.1 us
  starting transfers between devices: 17.5 us -> 16.4 us
    dot_general x6 -> x5, matrix products: 13 us -> 7.62 us  [base_rows(): return jnp.dot(rows, weight, preferred_element_type=jnp.float32)]
    pallas_call x1 -> x2, Pallas kernels: 3.79 us -> 7.55 us  [base_and_weight(): pl.pallas_call(base_kernel, out_shape=(jax.ShapeDtypeStruct((rows, weight...]
    pallas_call x6, Pallas kernels: 4.48 us -> 6.77 us  [call(): pl.pallas_call(kernel, out_shape=out_shape, in_specs=[VMEM] * len(operand...]
    unnamed x12, local copies, waits for them, and re-layouts: 2.24 us -> 4 us
    ppermute x13, waiting for transfers between devices: 14.2 us -> 15.8 us  [move(): return lax.ppermute(x, 'adapter', pairs(places, steps, flip))]
    ppermute x13, starting transfers between devices: 16.7 us -> 15.9 us  [move(): return lax.ppermute(x, 'adapter', pairs(places, steps, flip))]
  transfers between devices with their start and end apart: 14 -> 14, of which waited for: 8 -> 8; matrix products, arithmetic and copies ran while one was open for 18% -> 10% of each run, Pallas kernels for 13% -> 19%
where the time goes in v19:
time: 77.4 us; the launch traced here: 77 us
  waiting for transfers between devices  19.1 us (25%)
  starting transfers between devices  16.4 us (21%)
  Pallas kernels  16.4 us (21%)
  blocking collectives  12.5 us (16%)
  matrix products  7.62 us (10%)
  local copies, waits for them, and re-layouts  4.78 us (6%)
    ppermute x13, starting transfers between devices, move(): return lax.ppermute(x, 'adapter', pairs(places, steps, flip))  15.9 us
    ppermute x13, waiting for transfers between devices, move(): return lax.ppermute(x, 'adapter', pairs(places, steps, flip))  15.8 us
    all_to_all x1, blocking collectives, shards(): lax.all_to_all(query, 'adapter', 0, 0, axis_index_groups=groups, tiled=True)  12.5 us
    dot_general x5, matrix products, base_rows(): return jnp.dot(rows, weight, preferred_element_type=jnp.float32)  7.62 us
    pallas_call x2, Pallas kernels, base_and_weight(): pl.pallas_call(base_kernel, out_shape=(jax.ShapeDtypeStruct((rows, weight...  7.55 us
    pallas_call x6, Pallas kernels, call(): pl.pallas_call(kernel, out_shape=out_shape, in_specs=[VMEM] * len(operand...  6.77 us
    unnamed x12, local copies, waits for them, and re-layouts  4 us
    ppermute x1, waiting for transfers between devices, shards(): crossed = lax.ppermute(source, 'adapter', split_pairs(places))  3.38 us
  transfers between devices with their start and end apart: 14, of which 8 were waited for; matrix products, arithmetic and copies ran while one was open for 10% of the time, Pallas kernels for 19%

profile of v19, /device:TPU:0, one launch (start us, length us, event | category | flops | bytes accessed | tf_op | source)
XLA Modules:
  0.0 77.0 jit_solution(4117099993958282879)
XLA Ops:
  0.5 2.0 %shard_map.73.refs_0_ = bf16[24,8320]{1,0:T(8,128)(2,1)} custom-call(bf16[24,8192]{1,0:T(8,128)(2,1)} %refs_0_.1, f32[1,8192]{1,0:T(1,128)} %bitcast.28, s32[1,24]{1,0:T(1,128)} %bitcast.29, s32[1,16]{1,0:T(1,128)} %bitcast.30), custom_call_target="tpu_custom_call" | custom-call | tf_op jit(solution)/shard_map/pallas_call | solution.py:110
  2.6 3.1 %collective-permute-start = (bf16[24,8320]{1,0:T(8,128)(2,1)}, bf16[24,8320]{1,0:T(8,128)(2,1)}, u32[]{:S(2)}, u32[]{:S(2)}) collective-permute-start(bf16[24,8320]{1,0:T(8,128)(2,1)} %shard_map.73.refs_0_), channel_id=1, source_target_pairs={{0,4},{1,5},{2,6},{3,7},{4,12},{5,13},{6,14},{7,15},{12,8},{13,9},... | collective-permute-start | bytes 1198088 | tf_op jit(solution)/shard_map/ppermute | solution.py:290
  5.6 1.5 %collective-permute-start.2 = (bf16[24,8320]{1,0:T(8,128)(2,1)}, bf16[24,8320]{1,0:T(8,128)(2,1)S(1)}, u32[]{:S(2)}, u32[]{:S(2)}) collective-permute-start(bf16[24,8320]{1,0:T(8,128)(2,1)} %shard_map.73.refs_0_), channel_id=1, source_target_pairs={{0,2},{1,3},{2,0},{3,1},{4,6},{5,7},{6,4},{7,5},{12,14},{13,15},{1... | collective-permute-start | bytes 1198088 | tf_op jit(solution)/shard_map/ppermute | solution.py:290
  7.1 9.3 %collective-permute-done.block_ref.refs_0_ = bf16[24,8320]{1,0:T(8,128)(2,1)} collective-permute-done((bf16[24,8320]{1,0:T(8,128)(2,1)}, bf16[24,8320]{1,0:T(8,128)(2,1)}, u32[]{:S(2)}, u32[]{:S(2)}) %collective-permute-start) | collective-permute-done | bytes 399392 | tf_op jit(solution)/shard_map/ppermute | solution.py:290
  18.0 1.5 %collective-permute-start.5 = (bf16[24,8320]{1,0:T(8,128)(2,1)}, bf16[24,8320]{1,0:T(8,128)(2,1)}, u32[]{:S(2)}, u32[]{:S(2)}) collective-permute-start(bf16[24,8320]{1,0:T(8,128)(2,1)} %collective-permute-done.block_ref.refs_0_), channel_id=1, source_target_pairs={{0,2},{1,3},{2,0},{3,1},{4,6},{5,7},{6,4},{7,5},{12,14},{13,15},{1... | collective-permute-start | bytes 1198088 | tf_op jit(solution)/shard_map/ppermute | solution.py:290
  19.6 1.2 %copy-done = bf16[1,8192,64]{1,2,0:T(8,128)(2,1)S(1)} copy-done((bf16[1,8192,64]{1,2,0:T(8,128)(2,1)S(1)}, bf16[1,8192,64]{1,2,0:T(8,128)(2,1)}, u32[]{:S(2)}) %copy-start) | copy-done | bytes 1048600
  20.8 1.0 %copy-done.2 = bf16[24,8320]{1,0:T(8,128)(2,1)S(1)} copy-done((bf16[24,8320]{1,0:T(8,128)(2,1)S(1)}, bf16[24,8320]{1,0:T(8,128)(2,1)}, u32[]{:S(2)}) %copy-start.2) | copy-done | bytes 399384
  23.7 3.8 %shard_map.76 = (f32[48,512]{1,0:T(8,128)S(1)}, bf16[8192,512]{1,0:T(8,128)(2,1)S(1)}) custom-call(bf16[48,8192]{1,0:T(8,128)(2,1)S(1)} %get-tuple-element.54.refs_0_, bf16[8192,512]{1,0:T(8,128)(2,1)} %refs_1_.1), custom_call_target="tpu_custom_call" | custom-call | flops 1 | bytes 1 | tf_op jit(solution)/shard_map/pallas_call | solution.py:206
  28.5 3.4 %collective-permute-start.4 = (bf16[24,8320]{1,0:T(8,128)(2,1)S(1)}, bf16[24,8320]{1,0:T(8,128)(2,1)S(1)}, u32[]{:S(2)}, u32[]{:S(2)}) collective-permute-start(bf16[24,8320]{1,0:T(8,128)(2,1)S(1)} %collective-permute-done.1.block_ref.refs_0_), channel_id=1, source_target_pairs={{0,4},{1,5},{2,6},{3,7},{4,12},{5,13},{6,14},{7,15},{12,8},{13,9},... | collective-permute-start | bytes 1198088 | tf_op jit(solution)/shard_map/ppermute | solution.py:290
  31.8 1.5 %collective-permute-start.7 = (bf16[24,8320]{1,0:T(8,128)(2,1)S(1)}, bf16[24,8320]{1,0:T(8,128)(2,1)S(1)}, u32[]{:S(2)}, u32[]{:S(2)}) collective-permute-start(bf16[24,8320]{1,0:T(8,128)(2,1)S(1)} %collective-permute-done.1.block_ref.refs_0_), channel_id=1, source_target_pairs={{0,2},{1,3},{2,0},{3,1},{4,6},{5,7},{6,4},{7,5},{12,14},{13,15},{1... | collective-permute-start | bytes 1198088 | tf_op jit(solution)/shard_map/ppermute | solution.py:290
  33.4 2.0 %shard_map.78 = (bf16[48,64]{1,0:T(8,128)(2,1)S(1)}, s32[48,128]{1,0:T(8,128)S(1)}, bf16[48,8192]{1,0:T(8,128)(2,1)S(1)}) custom-call(bf16[24,8320]{1,0:T(8,128)(2,1)} %collective-permute-done.block_ref.refs_0_, bf16[24,8320]{1,0:T(8,128)(2,1)} %collective-permute-done.5.refs_1_, bf16[64,8192]{1,0:T(8,128)(2,1)S(1)} %bitcast.22, ...), custom_call_target="tpu_custom_call" | custom-call | flops 1 | bytes 1 | tf_op jit(solution)/shard_map/pallas_call | solution.py:58
  35.4 1.5 %fusion.refs_3_ = f32[48,512]{1,0:T(8,128)S(1)} fusion(bf16[48,8192]{1,0:T(8,128)(2,1)S(1)} %get-tuple-element.55.refs_1_, bf16[8192,512]{1,0:T(8,128)(2,1)S(1)} %get-tuple-element.53), kind=kOutput, calls=%fused_computation.1 | convolution fusion | flops 402653184 | bytes 9273344 | tf_op jit(solution)/shard_map/dot_general | solution.py:293
  36.9 3.8 %shard_map.79 = (f32[96,512]{1,0:T(8,128)S(1)}, bf16[8192,512]{1,0:T(8,128)(2,1)S(1)}) custom-call(bf16[48,8192]{1,0:T(8,128)(2,1)S(1)} %get-tuple-element.54.refs_0_, bf16[48,8192]{1,0:T(8,128)(2,1)S(1)} %get-tuple-element.55.refs_1_, bf16[8192,512]{1,0:T(8,128)(2,1)} %collective-permute-done.6.refs_2_), custom_call_target="tpu_custom_call" | custom-call | flops 1 | bytes 1 | tf_op jit(solution)/shard_map/pallas_call | solution.py:206
  40.7 1.6 %collective-permute-done.7.refs_1_ = bf16[24,8320]{1,0:T(8,128)(2,1)S(1)} collective-permute-done((bf16[24,8320]{1,0:T(8,128)(2,1)S(1)}, bf16[24,8320]{1,0:T(8,128)(2,1)S(1)}, u32[]{:S(2)}, u32[]{:S(2)}) %collective-permute-start.7) | collective-permute-done | bytes 399392 | tf_op jit(solution)/shard_map/ppermute | solution.py:290
  43.8 1.5 %fusion.1.refs_4_ = f32[48,512]{1,0:T(8,128)S(1)} fusion(bf16[48,8192]{1,0:T(8,128)(2,1)S(1)} %get-tuple-element.62, bf16[8192,512]{1,0:T(8,128)(2,1)S(1)} %get-tuple-element.53), kind=kOutput, calls=%fused_computation.2 | convolution fusion | flops 402653184 | bytes 9273344 | tf_op jit(solution)/shard_map/dot_general | solution.py:293
  45.3 1.5 %fusion.2.refs_7_ = f32[48,512]{1,0:T(8,128)S(1)} fusion(bf16[48,8192]{1,0:T(8,128)(2,1)S(1)} %get-tuple-element.62, bf16[8192,512]{1,0:T(8,128)(2,1)S(1)} %get-tuple-element.63), kind=kOutput, calls=%fused_computation.3 | convolution fusion | flops 402653184 | bytes 9273344 | tf_op jit(solution)/shard_map/dot_general | solution.py:293
  46.9 3.4 %collective-permute-done.8.refs_4_ = bf16[24,8320]{1,0:T(8,128)(2,1)S(1)} collective-permute-done((bf16[24,8320]{1,0:T(8,128)(2,1)S(1)}, bf16[24,8320]{1,0:T(8,128)(2,1)S(1)}, u32[]{:S(2)}, u32[]{:S(2)}) %collective-permute-start.8) | collective-permute-done | bytes 399392 | tf_op jit(solution)/shard_map/ppermute | solution.py:329
  53.1 1.1 %collective-permute-start.9 = (bf16[96,128]{1,0:T(8,128)(2,1)S(1)}, bf16[96,128]{1,0:T(8,128)(2,1)S(1)}, u32[]{:S(2)}, u32[]{:S(2)}) collective-permute-start(bf16[96,128]{1,0:T(8,128)(2,1)S(1)} %get-tuple-element.70.refs_0_), channel_id=1, source_target_pairs={{0,4},{1,5},{2,6},{3,7},{4,12},{5,13},{6,14},{7,15},{12,8},{13,9},... | collective-permute-start | bytes 73736 | tf_op jit(solution)/shard_map/ppermute | solution.py:290
  54.2 1.5 %fusion.3.refs_5_ = f32[48,512]{1,0:T(8,128)S(1)} fusion(bf16[48,8192]{1,0:T(8,128)(2,1)S(1)} %get-tuple-element.74, bf16[8192,512]{1,0:T(8,128)(2,1)S(1)} %get-tuple-element.53), kind=kOutput, calls=%fused_computation.4 | convolution fusion | flops 402653184 | bytes 9273344 | tf_op jit(solution)/shard_map/dot_general | solution.py:293
  55.7 1.2 %collective-permute-done.10.refs_2_ = bf16[96,128]{1,0:T(8,128)(2,1)S(1)} collective-permute-done((bf16[96,128]{1,0:T(8,128)(2,1)S(1)}, bf16[96,128]{1,0:T(8,128)(2,1)S(1)}, u32[]{:S(2)}, u32[]{:S(2)}) %collective-permute-start.10) | collective-permute-done | bytes 24608 | tf_op jit(solution)/shard_map/ppermute | solution.py:290
  58.5 1.5 %fusion.4.refs_8_ = f32[48,512]{1,0:T(8,128)S(1)} fusion(bf16[48,8192]{1,0:T(8,128)(2,1)S(1)} %get-tuple-element.74, bf16[8192,512]{1,0:T(8,128)(2,1)S(1)} %get-tuple-element.63), kind=kOutput, calls=%fused_computation.5 | convolution fusion | flops 402653184 | bytes 9273344 | tf_op jit(solution)/shard_map/dot_general | solution.py:293
  60.0 1.8 %collective-permute-done.12.refs_1_ = bf16[96,128]{1,0:T(8,128)(2,1)S(1)} collective-permute-done((bf16[96,128]{1,0:T(8,128)(2,1)S(1)}, bf16[96,128]{1,0:T(8,128)(2,1)S(1)}, u32[]{:S(2)}, u32[]{:S(2)}) %collective-permute-start.12) | collective-permute-done | bytes 24608 | tf_op jit(solution)/shard_map/ppermute | solution.py:290
  61.8 1.9 %shard_map.84 = bf16[8,24,1024]{2,1,0:T(8,128)(2,1)S(1)} custom-call(bf16[96,128]{1,0:T(8,128)(2,1)S(1)} %shard_map.83.refs_0_, bf16[96,128]{1,0:T(8,128)(2,1)S(1)} %collective-permute-done.12.refs_1_, f32[48,512]{1,0:T(8,128)S(1)} %get-tuple-element.46.refs_2_, f32[48,512]{1,0:T(8,128)S(1)} %fusion.refs_3_, f32[48,512]{1,0:T(8,128)S(1)} %fusion.1.refs_4_, ...), custom_call_target="tpu_custom_call" | custom-call | flops 1 | bytes 1 | tf_op jit(solution)/shard_map/pallas_call | solution.py:58
  63.7 12.5 %all_to_all.5 = bf16[8,24,1024]{2,1,0:T(8,128)(2,1)S(1)} all-to-all(bf16[8,24,1024]{2,1,0:T(8,128)(2,1)S(1)} %shard_map.84), channel_id=1, replica_groups={{0,2,4,6,8,10,12,14},{1,3,5,7,9,11,13,15},{16,18,20,22,24,26,28,30},{17..., dimensions={0} | all-to-all | bytes 786432 | tf_op jit(solution)/shard_map/all_to_all | solution.py:346
  (36 shorter events, 11.7 us)
Async XLA Ops:
  0.0 33.4 %copy-start.1 = (bf16[1,8192,64]{1,2,0:T(8,128)(2,1)S(1)}, bf16[1,8192,64]{1,2,0:T(8,128)(2,1)}, u32[]{:S(2)}) copy-start(bf16[1,8192,64]{1,2,0:T(8,128)(2,1)} %param.10) | copy-start | bytes 3145732
  0.0 36.9 %collective-permute-start.6 = (bf16[8192,512]{1,0:T(8,128)(2,1)}, bf16[8192,512]{1,0:T(8,128)(2,1)}, u32[]{:S(2)}, u32[]{:S(2)}) collective-permute-start(bf16[8192,512]{1,0:T(8,128)(2,1)} %refs_1_.1), channel_id=1, source_target_pairs={{0,1},{1,0},{2,3},{3,2},{4,5},{5,4},{6,7},{7,6},{12,13},{13,12},{1... | collective-permute-start | bytes 25165832 | tf_op jit(solution)/shard_map/ppermute | solution.py:290
  0.5 19.1 %collective-permute-start.3 = (bf16[64,8192]{1,0:T(8,128)(2,1)}, bf16[64,8192]{1,0:T(8,128)(2,1)S(1)}, u32[]{:S(2)}, u32[]{:S(2)}) collective-permute-start(bf16[64,8192]{1,0:T(8,128)(2,1)} %bitcast.20), channel_id=1, source_target_pairs={{0,1},{1,0},{2,3},{3,2},{4,5},{5,4},{6,7},{7,6},{12,13},{13,12},{1... | collective-permute-start | bytes 3145736 | tf_op jit(solution)/shard_map/ppermute | solution.py:290
  2.6 13.9 %collective-permute-start = (bf16[24,8320]{1,0:T(8,128)(2,1)}, bf16[24,8320]{1,0:T(8,128)(2,1)}, u32[]{:S(2)}, u32[]{:S(2)}) collective-permute-start(bf16[24,8320]{1,0:T(8,128)(2,1)} %shard_map.73.refs_0_), channel_id=1, source_target_pairs={{0,4},{1,5},{2,6},{3,7},{4,12},{5,13},{6,14},{7,15},{12,8},{13,9},... | collective-permute-start | bytes 1198088 | tf_op jit(solution)/shard_map/ppermute | solution.py:290
  5.6 11.6 %collective-permute-start.2 = (bf16[24,8320]{1,0:T(8,128)(2,1)}, bf16[24,8320]{1,0:T(8,128)(2,1)S(1)}, u32[]{:S(2)}, u32[]{:S(2)}) collective-permute-start(bf16[24,8320]{1,0:T(8,128)(2,1)} %shard_map.73.refs_0_), channel_id=1, source_target_pairs={{0,2},{1,3},{2,0},{3,1},{4,6},{5,7},{6,4},{7,5},{12,14},{13,15},{1... | collective-permute-start | bytes 1198088 | tf_op jit(solution)/shard_map/ppermute | solution.py:290
  16.4 11.8 %collective-permute-start.1 = (bf16[24,8320]{1,0:T(8,128)(2,1)}, bf16[24,8320]{1,0:T(8,128)(2,1)S(1)}, u32[]{:S(2)}, u32[]{:S(2)}) collective-permute-start(bf16[24,8320]{1,0:T(8,128)(2,1)} %collective-permute-done.block_ref.refs_0_), channel_id=1, source_target_pairs={{0,4},{1,5},{2,6},{3,7},{4,12},{5,13},{6,14},{7,15},{12,8},{13,9},... | collective-permute-start | bytes 1198088 | tf_op jit(solution)/shard_map/ppermute | solution.py:290
  17.3 0.8 %copy-start.4 = (bf16[24,8320]{1,0:T(8,128)(2,1)}, bf16[24,8320]{1,0:T(8,128)(2,1)S(1)}, u32[]{:S(2)}) copy-start(bf16[24,8320]{1,0:T(8,128)(2,1)S(1)} %collective-permute-done.2.refs_1_) | copy-start | bytes 1198084
  18.0 10.4 %collective-permute-start.5 = (bf16[24,8320]{1,0:T(8,128)(2,1)}, bf16[24,8320]{1,0:T(8,128)(2,1)}, u32[]{:S(2)}, u32[]{:S(2)}) collective-permute-start(bf16[24,8320]{1,0:T(8,128)(2,1)} %collective-permute-done.block_ref.refs_0_), channel_id=1, source_target_pairs={{0,2},{1,3},{2,0},{3,1},{4,6},{5,7},{6,4},{7,5},{12,14},{13,15},{1... | collective-permute-start | bytes 1198088 | tf_op jit(solution)/shard_map/ppermute | solution.py:290
  19.6 40.5 %collective-permute-start.13 = (bf16[1024,512]{1,0:T(8,128)(2,1)}, bf16[1024,512]{1,0:T(8,128)(2,1)}, u32[]{:S(2)}, u32[]{:S(2)}) collective-permute-start(bf16[1024,512]{1,0:T(8,128)(2,1)} %bitcast.25), channel_id=1, source_target_pairs={{0,1},{1,0},{2,3},{3,2},{4,5},{5,4},{6,7},{7,6},{12,13},{13,12},{1... | collective-permute-start | bytes 3145736 | tf_op jit(solution)/shard_map/ppermute | solution.py:290
  19.6 1.2 %copy-start = (bf16[1,8192,64]{1,2,0:T(8,128)(2,1)S(1)}, bf16[1,8192,64]{1,2,0:T(8,128)(2,1)}, u32[]{:S(2)}) copy-start(bf16[1,8192,64]{1,2,0:T(8,128)(2,1)} %param.10) | copy-start | bytes 3145732
  20.8 1.0 %copy-start.2 = (bf16[24,8320]{1,0:T(8,128)(2,1)S(1)}, bf16[24,8320]{1,0:T(8,128)(2,1)}, u32[]{:S(2)}) copy-start(bf16[24,8320]{1,0:T(8,128)(2,1)} %shard_map.73.refs_0_) | copy-start | bytes 1198084
  21.8 1.0 %copy-start.5 = (bf16[24,8320]{1,0:T(8,128)(2,1)S(1)}, bf16[24,8320]{1,0:T(8,128)(2,1)}, u32[]{:S(2)}) copy-start(bf16[24,8320]{1,0:T(8,128)(2,1)} %copy-done.4) | copy-start | bytes 1198084
  28.5 12.3 %collective-permute-start.4 = (bf16[24,8320]{1,0:T(8,128)(2,1)S(1)}, bf16[24,8320]{1,0:T(8,128)(2,1)S(1)}, u32[]{:S(2)}, u32[]{:S(2)}) collective-permute-start(bf16[24,8320]{1,0:T(8,128)(2,1)S(1)} %collective-permute-done.1.block_ref.refs_0_), channel_id=1, source_target_pairs={{0,4},{1,5},{2,6},{3,7},{4,12},{5,13},{6,14},{7,15},{12,8},{13,9},... | collective-permute-start | bytes 1198088 | tf_op jit(solution)/shard_map/ppermute | solution.py:290
  31.8 10.5 %collective-permute-start.7 = (bf16[24,8320]{1,0:T(8,128)(2,1)S(1)}, bf16[24,8320]{1,0:T(8,128)(2,1)S(1)}, u32[]{:S(2)}, u32[]{:S(2)}) collective-permute-start(bf16[24,8320]{1,0:T(8,128)(2,1)S(1)} %collective-permute-done.1.block_ref.refs_0_), channel_id=1, source_target_pairs={{0,2},{1,3},{2,0},{3,1},{4,6},{5,7},{6,4},{7,5},{12,14},{13,15},{1... | collective-permute-start | bytes 1198088 | tf_op jit(solution)/shard_map/ppermute | solution.py:290
  42.4 7.9 %collective-permute-start.8 = (bf16[24,8320]{1,0:T(8,128)(2,1)S(1)}, bf16[24,8320]{1,0:T(8,128)(2,1)S(1)}, u32[]{:S(2)}, u32[]{:S(2)}) collective-permute-start(bf16[24,8320]{1,0:T(8,128)(2,1)S(1)} %broadcast_select_fusion), channel_id=1, source_target_pairs={{0,2},{2,0},{4,6},{6,4},{12,14},{14,12},{8,10},{10,8},{1,5},{3,7},... | collective-permute-start | bytes 1198088 | tf_op jit(solution)/shard_map/ppermute | solution.py:329
  51.2 5.7 %collective-permute-start.10 = (bf16[96,128]{1,0:T(8,128)(2,1)S(1)}, bf16[96,128]{1,0:T(8,128)(2,1)S(1)}, u32[]{:S(2)}, u32[]{:S(2)}) collective-permute-start(bf16[96,128]{1,0:T(8,128)(2,1)S(1)} %get-tuple-element.70.refs_0_), channel_id=1, source_target_pairs={{0,12},{1,13},{2,14},{3,15},{4,8},{5,9},{6,10},{7,11},{12,0},{13,1... | collective-permute-start | bytes 73736 | tf_op jit(solution)/shard_map/ppermute | solution.py:290
  52.2 4.7 %collective-permute-start.11 = (bf16[96,128]{1,0:T(8,128)(2,1)S(1)}, bf16[96,128]{1,0:T(8,128)(2,1)S(1)}, u32[]{:S(2)}, u32[]{:S(2)}) collective-permute-start(bf16[96,128]{1,0:T(8,128)(2,1)S(1)} %get-tuple-element.70.refs_0_), channel_id=1, source_target_pairs={{0,8},{1,9},{2,10},{3,11},{4,0},{5,1},{6,2},{7,3},{12,4},{13,5},{1... | collective-permute-start | bytes 73736 | tf_op jit(solution)/shard_map/ppermute | solution.py:290
  53.1 4.7 %collective-permute-start.9 = (bf16[96,128]{1,0:T(8,128)(2,1)S(1)}, bf16[96,128]{1,0:T(8,128)(2,1)S(1)}, u32[]{:S(2)}, u32[]{:S(2)}) collective-permute-start(bf16[96,128]{1,0:T(8,128)(2,1)S(1)} %get-tuple-element.70.refs_0_), channel_id=1, source_target_pairs={{0,4},{1,5},{2,6},{3,7},{4,12},{5,13},{6,14},{7,15},{12,8},{13,9},... | collective-permute-start | bytes 73736 | tf_op jit(solution)/shard_map/ppermute | solution.py:290
  57.9 3.9 %copy-start.3 = (bf16[16,64,512]{2,1,0:T(8,128)(2,1)S(1)}, bf16[16,64,512]{2,1,0:T(8,128)(2,1)}, u32[]{:S(2)}) copy-start(bf16[16,64,512]{2,1,0:T(8,128)(2,1)} %param.11) | copy-start | bytes 3145732
  57.9 3.9 %collective-permute-start.12 = (bf16[96,128]{1,0:T(8,128)(2,1)S(1)}, bf16[96,128]{1,0:T(8,128)(2,1)S(1)}, u32[]{:S(2)}, u32[]{:S(2)}) collective-permute-start(bf16[96,128]{1,0:T(8,128)(2,1)S(1)} %shard_map.83.refs_0_), channel_id=1, source_target_pairs={{0,2},{1,3},{2,0},{3,1},{4,6},{5,7},{6,4},{7,5},{12,14},{13,15},{1... | collective-permute-start | bytes 73736 | tf_op jit(solution)/shard_map/ppermute | solution.py:290

commit v20 on v13

--- a/solution.py
+++ b/solution.py
@@ -234,9 +234,9 @@
 def finish_kernel(places, *refs):
     shrink_ref, across_ref, *refs = refs
     bases, slots = refs[: places + 3], refs[places + 3 : 2 * places + 3]
-    own_ref, other_ref, out_ref = refs[2 * places + 3 :]
+    own_ref, other_ref, *outs = refs[2 * places + 3 :]
     depth, columns = own_ref.shape
-    own_rows = out_ref.shape[1]
+    own_rows = outs[0].shape[0]
     rows = SIDE * own_rows
     core = lax.axis_index("adapter") % CORES
     shrinks = []
@@ -262,17 +262,32 @@
                 base = bases[step + 3][...]
             query = (base + ADAPTER_SCALE * update[here]).astype(jnp.bfloat16)
             for side in range(SIDE):
-                chip = ring_chip(places, -step, side)
-                out_ref[chip, :, pl.ds(at, columns)] = query[side * own_rows : (side + 1) * own_rows]
+                out_ref = outs[step * SIDE + side]
+                out_ref[:, pl.ds(at, columns)] = query[side * own_rows : (side + 1) * own_rows]
 
 
 def finish(shrink, across, bases, slots, own, other, own_rows):
     places = len(slots)
     return call(
         lambda *refs: finish_kernel(places, *refs),
-        jax.ShapeDtypeStruct((places * SIDE, own_rows, CORES * own.shape[1]), jnp.bfloat16),
+        [jax.ShapeDtypeStruct((own_rows, CORES * own.shape[1]), jnp.bfloat16)] * (places * SIDE),
         (shrink, across, *bases, *slots, own, other),
     )
+
+
+def assemble_kernel(places, *refs):
+    *blocks, out_ref = refs
+    columns = blocks[0].shape[1]
+    for step in range(places):
+        for side in range(SIDE):
+            at = pl.multiple_of(ring_chip(places, step, side) * columns, columns)
+            out_ref[:, pl.ds(at, columns)] = blocks[step * SIDE + side][...]
+
+
+def assemble(places, blocks):
+    rows, columns = blocks[0].shape
+    out_shape = jax.ShapeDtypeStruct((rows, columns * len(blocks)), jnp.bfloat16)
+    return call(lambda *refs: assemble_kernel(places, *refs), out_shape, blocks)
 
 
 def shards(
@@ -336,10 +351,13 @@
     )
     across = move(shrink, 0, 2)
     bases_other.append(base_rows(after(rows[-1], shrink), weight_other))
-    query = finish(shrink, across, bases + bases_other, slots, up, up_other, own_rows)
-    groups = [list(range(core, devices, CORES)) for core in range(CORES)]
-    query = lax.all_to_all(query, "adapter", 0, 0, axis_index_groups=groups, tiled=True)
-    return query.transpose(1, 0, 2).reshape(own_rows, devices * columns)
+    query = list(finish(shrink, across, bases + bases_other, slots, up, up_other, own_rows))
+    for step in sorted(range(places), key=lambda step: -min(step, places - step)):
+        for side in (1, 0):
+            if step or side:
+                at = step * SIDE + side
+                query[at] = move(query[at], -step, 2 * side)
+    return assemble(places, query)
 
 
 def solution(mesh):

time: 74.4 us -> 76.2 us (1.024)
  blocking collectives: 12.8 us -> 0 us
  starting transfers between devices: 17.5 us -> 28.7 us
  waiting for transfers between devices: 17.4 us -> 20.7 us
  Pallas kernels: 10.3 us -> 11.1 us
  local copies, waits for them, and re-layouts: 3.02 us -> 2.24 us
    all_to_all x1 -> x0, blocking collectives: 12.8 us -> none  [shards(): lax.all_to_all(query, 'adapter', 0, 0, axis_index_groups=groups, tiled=True)]
    ppermute x13 -> x20, starting transfers between devices: 16.7 us -> 27.9 us  [move(): return lax.ppermute(x, 'adapter', pairs(places, steps, flip))]
    ppermute x13 -> x20, waiting for transfers between devices: 14.2 us -> 17.6 us  [move(): return lax.ppermute(x, 'adapter', pairs(places, steps, flip))]
    pallas_call x6 -> x7, Pallas kernels: 4.48 us -> 5.27 us  [call(): pl.pallas_call(kernel, out_shape=out_shape, in_specs=[VMEM] * len(operand...]
    reshape x1 -> x0, local copies, waits for them, and re-layouts: 0.77 us -> none  [shards(): return query.transpose(1, 0, 2).reshape(own_rows, devices * columns)]
  transfers between devices with their start and end apart: 14 -> 21, of which waited for: 8 -> 11; matrix products, arithmetic and copies ran while one was open for 18% -> 17% of each run, Pallas kernels for 13% -> 13%
where the time goes in v20:
time: 76.2 us; the launch traced here: 76 us
  starting transfers between devices  28.7 us (38%)
  waiting for transfers between devices  20.7 us (27%)
  matrix products  13 us (17%)
  Pallas kernels  11.1 us (15%)
  local copies, waits for them, and re-layouts  2.24 us (3%)
    ppermute x20, starting transfers between devices, move(): return lax.ppermute(x, 'adapter', pairs(places, steps, flip))  27.9 us
    ppermute x20, waiting for transfers between devices, move(): return lax.ppermute(x, 'adapter', pairs(places, steps, flip))  17.6 us
    dot_general x6, matrix products, base_rows(): return jnp.dot(rows, weight, preferred_element_type=jnp.float32)  13 us
    pallas_call x7, Pallas kernels, call(): pl.pallas_call(kernel, out_shape=out_shape, in_specs=[VMEM] * len(operand...  5.27 us
    pallas_call x1, Pallas kernels, base_and_weight(): pl.pallas_call(base_kernel, out_shape=(jax.ShapeDtypeStruct((rows, weight...  3.78 us
    ppermute x1, waiting for transfers between devices, shards(): crossed = lax.ppermute(source, 'adapter', split_pairs(places))  3.14 us
    unnamed x12, local copies, waits for them, and re-layouts  2.24 us
    pallas_call x1, Pallas kernels, normalize(): pl.pallas_call(norm_kernel, out_shape=jax.ShapeDtypeStruct((rows, width +...  2.06 us
  transfers between devices with their start and end apart: 21, of which 11 were waited for; matrix products, arithmetic and copies ran while one was open for 17% of the time, Pallas kernels for 13%

profile of v20, /device:TPU:0, one launch (start us, length us, event | category | flops | bytes accessed | tf_op | source)
XLA Modules:
  0.0 76.0 jit_solution(9114745991010512492)
XLA Ops:
  0.5 2.1 %shard_map.73.refs_0_ = bf16[24,8320]{1,0:T(8,128)(2,1)} custom-call(bf16[24,8192]{1,0:T(8,128)(2,1)} %refs_0_.1, f32[1,8192]{1,0:T(1,128)} %bitcast.28, s32[1,24]{1,0:T(1,128)} %bitcast.29, s32[1,16]{1,0:T(1,128)} %bitcast.30), custom_call_target="tpu_custom_call" | custom-call | tf_op jit(solution)/shard_map/pallas_call | solution.py:109
  2.6 3.1 %collective-permute-start = (bf16[24,8320]{1,0:T(8,128)(2,1)}, bf16[24,8320]{1,0:T(8,128)(2,1)S(1)}, u32[]{:S(2)}, u32[]{:S(2)}) collective-permute-start(bf16[24,8320]{1,0:T(8,128)(2,1)} %shard_map.73.refs_0_), channel_id=1, source_target_pairs={{0,4},{1,5},{2,6},{3,7},{4,12},{5,13},{6,14},{7,15},{12,8},{13,9},... | collective-permute-start | bytes 1198088 | tf_op jit(solution)/shard_map/ppermute | solution.py:304
  5.7 1.5 %collective-permute-start.2 = (bf16[24,8320]{1,0:T(8,128)(2,1)}, bf16[24,8320]{1,0:T(8,128)(2,1)S(1)}, u32[]{:S(2)}, u32[]{:S(2)}) collective-permute-start(bf16[24,8320]{1,0:T(8,128)(2,1)} %shard_map.73.refs_0_), channel_id=1, source_target_pairs={{0,2},{1,3},{2,0},{3,1},{4,6},{5,7},{6,4},{7,5},{12,14},{13,15},{1... | collective-permute-start | bytes 1198088 | tf_op jit(solution)/shard_map/ppermute | solution.py:304
  7.2 9.1 %collective-permute-done.block_ref.refs_0_ = bf16[24,8320]{1,0:T(8,128)(2,1)S(1)} collective-permute-done((bf16[24,8320]{1,0:T(8,128)(2,1)}, bf16[24,8320]{1,0:T(8,128)(2,1)S(1)}, u32[]{:S(2)}, u32[]{:S(2)}) %collective-permute-start) | collective-permute-done | bytes 399392 | tf_op jit(solution)/shard_map/ppermute | solution.py:304
  16.7 2.6 %collective-permute-start.1 = (bf16[24,8320]{1,0:T(8,128)(2,1)S(1)}, bf16[24,8320]{1,0:T(8,128)(2,1)S(1)}, u32[]{:S(2)}, u32[]{:S(2)}) collective-permute-start(bf16[24,8320]{1,0:T(8,128)(2,1)S(1)} %collective-permute-done.block_ref.refs_0_), channel_id=1, source_target_pairs={{0,4},{1,5},{2,6},{3,7},{4,12},{5,13},{6,14},{7,15},{12,8},{13,9},... | collective-permute-start | bytes 1198088 | tf_op jit(solution)/shard_map/ppermute | solution.py:304
  19.3 1.5 %collective-permute-start.5 = (bf16[24,8320]{1,0:T(8,128)(2,1)S(1)}, bf16[24,8320]{1,0:T(8,128)(2,1)S(1)}, u32[]{:S(2)}, u32[]{:S(2)}) collective-permute-start(bf16[24,8320]{1,0:T(8,128)(2,1)S(1)} %collective-permute-done.block_ref.refs_0_), channel_id=1, source_target_pairs={{0,2},{1,3},{2,0},{3,1},{4,6},{5,7},{6,4},{7,5},{12,14},{13,15},{1... | collective-permute-start | bytes 1198088 | tf_op jit(solution)/shard_map/ppermute | solution.py:304
  24.0 5.4 %fusion.refs_2_ = f32[48,512]{1,0:T(8,128)S(1)} fusion(bf16[48,8192]{1,0:T(8,128)(2,1)S(1)} %get-tuple-element.58.refs_0_, bf16[8192,512]{1,0:T(8,128)(2,1)} %param.9), kind=kOutput, calls=%fused_computation.1 | convolution fusion | flops 402653184 | bytes 9273344 | tf_op jit(solution)/shard_map/dot_general | solution.py:307
  30.7 1.4 %collective-permute-start.7 = (bf16[24,8320]{1,0:T(8,128)(2,1)S(1)}, bf16[24,8320]{1,0:T(8,128)(2,1)S(1)}, u32[]{:S(2)}, u32[]{:S(2)}) collective-permute-start(bf16[24,8320]{1,0:T(8,128)(2,1)S(1)} %collective-permute-done.1.block_ref.refs_0_), channel_id=1, source_target_pairs={{0,2},{1,3},{2,0},{3,1},{4,6},{5,7},{6,4},{7,5},{12,14},{13,15},{1... | collective-permute-start | bytes 1198088 | tf_op jit(solution)/shard_map/ppermute | solution.py:304
  33.0 1.5 %fusion.1.refs_3_ = f32[48,512]{1,0:T(8,128)S(1)} fusion(bf16[48,8192]{1,0:T(8,128)(2,1)S(1)} %get-tuple-element.59.refs_1_, bf16[8192,512]{1,0:T(8,128)(2,1)S(1)} %bitcast.27), kind=kOutput, calls=%fused_computation.2 | convolution fusion | flops 402653184 | bytes 9273344 | tf_op jit(solution)/shard_map/dot_general | solution.py:307
  34.5 3.8 %shard_map.78 = (f32[96,512]{1,0:T(8,128)S(1)}, bf16[8192,512]{1,0:T(8,128)(2,1)S(1)}) custom-call(bf16[48,8192]{1,0:T(8,128)(2,1)S(1)} %get-tuple-element.58.refs_0_, bf16[48,8192]{1,0:T(8,128)(2,1)S(1)} %get-tuple-element.59.refs_1_, bf16[8192,512]{1,0:T(8,128)(2,1)} %collective-permute-done.6.refs_2_), custom_call_target="tpu_custom_call" | custom-call | flops 1 | bytes 1 | tf_op jit(solution)/shard_map/pallas_call | solution.py:205
  38.3 1.5 %collective-permute-done.4.block_ref.refs_3_ = bf16[24,8320]{1,0:T(8,128)(2,1)S(1)} collective-permute-done((bf16[24,8320]{1,0:T(8,128)(2,1)S(1)}, bf16[24,8320]{1,0:T(8,128)(2,1)S(1)}, u32[]{:S(2)}, u32[]{:S(2)}) %collective-permute-start.4) | collective-permute-done | bytes 399392 | tf_op jit(solution)/shard_map/ppermute | solution.py:304
  41.9 1.5 %fusion.2.refs_4_ = f32[48,512]{1,0:T(8,128)S(1)} fusion(bf16[48,8192]{1,0:T(8,128)(2,1)S(1)} %get-tuple-element.66, bf16[8192,512]{1,0:T(8,128)(2,1)S(1)} %bitcast.27), kind=kOutput, calls=%fused_computation.3 | convolution fusion | flops 402653184 | bytes 9273344 | tf_op jit(solution)/shard_map/dot_general | solution.py:307
  43.4 1.5 %fusion.3.refs_7_ = f32[48,512]{1,0:T(8,128)S(1)} fusion(bf16[48,8192]{1,0:T(8,128)(2,1)S(1)} %get-tuple-element.66, bf16[8192,512]{1,0:T(8,128)(2,1)S(1)} %get-tuple-element.67), kind=kOutput, calls=%fused_computation.4 | convolution fusion | flops 402653184 | bytes 9273344 | tf_op jit(solution)/shard_map/dot_general | solution.py:307
  45.0 3.1 %collective-permute-done.8.refs_4_ = bf16[24,8320]{1,0:T(8,128)(2,1)S(1)} collective-permute-done((bf16[24,8320]{1,0:T(8,128)(2,1)S(1)}, bf16[24,8320]{1,0:T(8,128)(2,1)S(1)}, u32[]{:S(2)}, u32[]{:S(2)}) %collective-permute-start.8) | collective-permute-done | bytes 399392 | tf_op jit(solution)/shard_map/ppermute | solution.py:339
  49.1 1.3 %collective-permute-start.10 = (bf16[96,128]{1,0:T(8,128)(2,1)S(1)}, bf16[96,128]{1,0:T(8,128)(2,1)S(1)}, u32[]{:S(2)}, u32[]{:S(2)}) collective-permute-start(bf16[96,128]{1,0:T(8,128)(2,1)S(1)} %get-tuple-element.74.refs_0_), channel_id=1, source_target_pairs={{0,12},{1,13},{2,14},{3,15},{4,8},{5,9},{6,10},{7,11},{12,0},{13,1... | collective-permute-start | bytes 73736 | tf_op jit(solution)/shard_map/ppermute | solution.py:304
  52.4 1.5 %fusion.4.refs_5_ = f32[48,512]{1,0:T(8,128)S(1)} fusion(bf16[48,8192]{1,0:T(8,128)(2,1)S(1)} %get-tuple-element.78, bf16[8192,512]{1,0:T(8,128)(2,1)S(1)} %bitcast.27), kind=kOutput, calls=%fused_computation.5 | convolution fusion | flops 402653184 | bytes 9273344 | tf_op jit(solution)/shard_map/dot_general | solution.py:307
  56.1 1.6 %collective-permute-start.12 = (bf16[96,128]{1,0:T(8,128)(2,1)S(1)}, bf16[96,128]{1,0:T(8,128)(2,1)S(1)}, u32[]{:S(2)}, u32[]{:S(2)}) collective-permute-start(bf16[96,128]{1,0:T(8,128)(2,1)S(1)} %shard_map.82.refs_0_), channel_id=1, source_target_pairs={{0,2},{1,3},{2,0},{3,1},{4,6},{5,7},{6,4},{7,5},{12,14},{13,15},{1... | collective-permute-start | bytes 73736 | tf_op jit(solution)/shard_map/ppermute | solution.py:304
  57.6 1.5 %fusion.5.refs_8_ = f32[48,512]{1,0:T(8,128)S(1)} fusion(bf16[48,8192]{1,0:T(8,128)(2,1)S(1)} %get-tuple-element.78, bf16[8192,512]{1,0:T(8,128)(2,1)S(1)} %get-tuple-element.67), kind=kOutput, calls=%fused_computation.6 | convolution fusion | flops 402653184 | bytes 9273344 | tf_op jit(solution)/shard_map/dot_general | solution.py:307
  60.7 1.6 %collective-permute-start.14 = (bf16[24,1024]{1,0:T(8,128)(2,1)S(1)}, bf16[24,1024]{1,0:T(8,128)(2,1)S(1)}, u32[]{:S(2)}, u32[]{:S(2)}) collective-permute-start(bf16[24,1024]{1,0:T(8,128)(2,1)S(1)} %get-tuple-element.84), channel_id=1, source_target_pairs={{0,2},{1,3},{2,0},{3,1},{4,6},{5,7},{6,4},{7,5},{12,14},{13,15},{1... | collective-permute-start | bytes 147464 | tf_op jit(solution)/shard_map/ppermute | solution.py:304
  62.8 2.2 %collective-permute-start.16 = (bf16[24,1024]{1,0:T(8,128)(2,1)S(1)}, bf16[24,1024]{1,0:T(8,128)(2,1)S(1)}, u32[]{:S(2)}, u32[]{:S(2)}) collective-permute-start(bf16[24,1024]{1,0:T(8,128)(2,1)S(1)} %get-tuple-element.86), channel_id=1, source_target_pairs={{0,10},{1,11},{2,8},{3,9},{4,2},{5,3},{6,0},{7,1},{12,6},{13,7},{1... | collective-permute-start | bytes 147464 | tf_op jit(solution)/shard_map/ppermute | solution.py:304
  65.0 1.6 %collective-permute-start.17 = (bf16[24,1024]{1,0:T(8,128)(2,1)S(1)}, bf16[24,1024]{1,0:T(8,128)(2,1)S(1)}, u32[]{:S(2)}, u32[]{:S(2)}) collective-permute-start(bf16[24,1024]{1,0:T(8,128)(2,1)S(1)} %get-tuple-element.87), channel_id=1, source_target_pairs={{0,12},{1,13},{2,14},{3,15},{4,8},{5,9},{6,10},{7,11},{12,0},{13,1... | collective-permute-start | bytes 147464 | tf_op jit(solution)/shard_map/ppermute | solution.py:304
  66.6 2.2 %collective-permute-start.18 = (bf16[24,1024]{1,0:T(8,128)(2,1)S(1)}, bf16[24,1024]{1,0:T(8,128)(2,1)S(1)}, u32[]{:S(2)}, u32[]{:S(2)}) collective-permute-start(bf16[24,1024]{1,0:T(8,128)(2,1)S(1)} %get-tuple-element.88), channel_id=1, source_target_pairs={{0,14},{1,15},{2,12},{3,13},{4,10},{5,11},{6,8},{7,9},{12,2},{13,3... | collective-permute-start | bytes 147464 | tf_op jit(solution)/shard_map/ppermute | solution.py:304
  68.8 3.1 %collective-permute-start.20 = (bf16[24,1024]{1,0:T(8,128)(2,1)S(1)}, bf16[24,1024]{1,0:T(8,128)(2,1)S(1)}, u32[]{:S(2)}, u32[]{:S(2)}) collective-permute-start(bf16[24,1024]{1,0:T(8,128)(2,1)S(1)} %get-tuple-element.90), channel_id=1, source_target_pairs={{0,6},{1,7},{2,4},{3,5},{4,14},{5,15},{6,12},{7,13},{12,10},{13,11... | collective-permute-start | bytes 147464 | tf_op jit(solution)/shard_map/ppermute | solution.py:304
  71.9 1.5 %collective-permute-done.18.refs_5_ = bf16[24,1024]{1,0:T(8,128)(2,1)S(1)} collective-permute-done((bf16[24,1024]{1,0:T(8,128)(2,1)S(1)}, bf16[24,1024]{1,0:T(8,128)(2,1)S(1)}, u32[]{:S(2)}, u32[]{:S(2)}) %collective-permute-start.18) | collective-permute-done | bytes 49184 | tf_op jit(solution)/shard_map/ppermute | solution.py:304
  (50 shorter events, 18.2 us)
Async XLA Ops:
  0.0 34.5 %collective-permute-start.6 = (bf16[8192,512]{1,0:T(8,128)(2,1)}, bf16[8192,512]{1,0:T(8,128)(2,1)}, u32[]{:S(2)}, u32[]{:S(2)}) collective-permute-start(bf16[8192,512]{1,0:T(8,128)(2,1)} %param.9), channel_id=1, source_target_pairs={{0,1},{1,0},{2,3},{3,2},{4,5},{5,4},{6,7},{7,6},{12,13},{13,12},{1... | collective-permute-start | bytes 25165832 | tf_op jit(solution)/shard_map/ppermute | solution.py:304
  0.5 20.4 %collective-permute-start.3 = (bf16[64,8192]{1,0:T(8,128)(2,1)}, bf16[64,8192]{1,0:T(8,128)(2,1)S(1)}, u32[]{:S(2)}, u32[]{:S(2)}) collective-permute-start(bf16[64,8192]{1,0:T(8,128)(2,1)} %bitcast.19), channel_id=1, source_target_pairs={{0,1},{1,0},{2,3},{3,2},{4,5},{5,4},{6,7},{7,6},{12,13},{13,12},{1... | collective-permute-start | bytes 3145736 | tf_op jit(solution)/shard_map/ppermute | solution.py:304
  2.6 13.7 %collective-permute-start = (bf16[24,8320]{1,0:T(8,128)(2,1)}, bf16[24,8320]{1,0:T(8,128)(2,1)S(1)}, u32[]{:S(2)}, u32[]{:S(2)}) collective-permute-start(bf16[24,8320]{1,0:T(8,128)(2,1)} %shard_map.73.refs_0_), channel_id=1, source_target_pairs={{0,4},{1,5},{2,6},{3,7},{4,12},{5,13},{6,14},{7,15},{12,8},{13,9},... | collective-permute-start | bytes 1198088 | tf_op jit(solution)/shard_map/ppermute | solution.py:304
  5.7 11.1 %collective-permute-start.2 = (bf16[24,8320]{1,0:T(8,128)(2,1)}, bf16[24,8320]{1,0:T(8,128)(2,1)S(1)}, u32[]{:S(2)}, u32[]{:S(2)}) collective-permute-start(bf16[24,8320]{1,0:T(8,128)(2,1)} %shard_map.73.refs_0_), channel_id=1, source_target_pairs={{0,2},{1,3},{2,0},{3,1},{4,6},{5,7},{6,4},{7,5},{12,14},{13,15},{1... | collective-permute-start | bytes 1198088 | tf_op jit(solution)/shard_map/ppermute | solution.py:304
  7.2 52.0 %collective-permute-start.13 = (bf16[1024,512]{1,0:T(8,128)(2,1)}, bf16[1024,512]{1,0:T(8,128)(2,1)S(1)}, u32[]{:S(2)}, u32[]{:S(2)}) collective-permute-start(bf16[1024,512]{1,0:T(8,128)(2,1)} %bitcast.24), channel_id=1, source_target_pairs={{0,1},{1,0},{2,3},{3,2},{4,5},{5,4},{6,7},{7,6},{12,13},{13,12},{1... | collective-permute-start | bytes 3145736 | tf_op jit(solution)/shard_map/ppermute | solution.py:304
  16.7 12.7 %collective-permute-start.1 = (bf16[24,8320]{1,0:T(8,128)(2,1)S(1)}, bf16[24,8320]{1,0:T(8,128)(2,1)S(1)}, u32[]{:S(2)}, u32[]{:S(2)}) collective-permute-start(bf16[24,8320]{1,0:T(8,128)(2,1)S(1)} %collective-permute-done.block_ref.refs_0_), channel_id=1, source_target_pairs={{0,4},{1,5},{2,6},{3,7},{4,12},{5,13},{6,14},{7,15},{12,8},{13,9},... | collective-permute-start | bytes 1198088 | tf_op jit(solution)/shard_map/ppermute | solution.py:304
  19.3 10.1 %collective-permute-start.5 = (bf16[24,8320]{1,0:T(8,128)(2,1)S(1)}, bf16[24,8320]{1,0:T(8,128)(2,1)S(1)}, u32[]{:S(2)}, u32[]{:S(2)}) collective-permute-start(bf16[24,8320]{1,0:T(8,128)(2,1)S(1)} %collective-permute-done.block_ref.refs_0_), channel_id=1, source_target_pairs={{0,2},{1,3},{2,0},{3,1},{4,6},{5,7},{6,4},{7,5},{12,14},{13,15},{1... | collective-permute-start | bytes 1198088 | tf_op jit(solution)/shard_map/ppermute | solution.py:304
  23.1 9.9 %slice-start = ((s8[8388608]{0:T(1024)(128)(4,1)}), s8[4194304]{0:T(1024)(128)(4,1)S(1)}, s32[]{:S(2)}) async-start(s8[8388608]{0:T(1024)(128)(4,1)} %bitcast.26), calls=%async_computation | async-start | bytes 8388608
  24.0 8.1 %copy-start.1 = (bf16[1,8192,64]{1,2,0:T(8,128)(2,1)S(1)}, bf16[1,8192,64]{1,2,0:T(8,128)(2,1)}, u32[]{:S(2)}) copy-start(bf16[1,8192,64]{1,2,0:T(8,128)(2,1)} %param.10) | copy-start | bytes 3145732
  24.0 9.0 %slice-start.1 = ((s8[8388608]{0:T(1024)(128)(4,1)}), s8[4194304]{0:T(1024)(128)(4,1)S(1)}, s32[]{:S(2)}) async-start(s8[8388608]{0:T(1024)(128)(4,1)} %bitcast.26), calls=%async_computation.1 | async-start | bytes 8388608
  29.5 10.4 %collective-permute-start.4 = (bf16[24,8320]{1,0:T(8,128)(2,1)S(1)}, bf16[24,8320]{1,0:T(8,128)(2,1)S(1)}, u32[]{:S(2)}, u32[]{:S(2)}) collective-permute-start(bf16[24,8320]{1,0:T(8,128)(2,1)S(1)} %collective-permute-done.1.block_ref.refs_0_), channel_id=1, source_target_pairs={{0,4},{1,5},{2,6},{3,7},{4,12},{5,13},{6,14},{7,15},{12,8},{13,9},... | collective-permute-start | bytes 1198088 | tf_op jit(solution)/shard_map/ppermute | solution.py:304
  30.7 9.5 %collective-permute-start.7 = (bf16[24,8320]{1,0:T(8,128)(2,1)S(1)}, bf16[24,8320]{1,0:T(8,128)(2,1)S(1)}, u32[]{:S(2)}, u32[]{:S(2)}) collective-permute-start(bf16[24,8320]{1,0:T(8,128)(2,1)S(1)} %collective-permute-done.1.block_ref.refs_0_), channel_id=1, source_target_pairs={{0,2},{1,3},{2,0},{3,1},{4,6},{5,7},{6,4},{7,5},{12,14},{13,15},{1... | collective-permute-start | bytes 1198088 | tf_op jit(solution)/shard_map/ppermute | solution.py:304
  40.2 7.9 %collective-permute-start.8 = (bf16[24,8320]{1,0:T(8,128)(2,1)S(1)}, bf16[24,8320]{1,0:T(8,128)(2,1)S(1)}, u32[]{:S(2)}, u32[]{:S(2)}) collective-permute-start(bf16[24,8320]{1,0:T(8,128)(2,1)S(1)} %broadcast_select_fusion), channel_id=1, source_target_pairs={{0,2},{2,0},{4,6},{6,4},{12,14},{14,12},{8,10},{10,8},{1,5},{3,7},... | collective-permute-start | bytes 1198088 | tf_op jit(solution)/shard_map/ppermute | solution.py:339
  49.1 5.7 %collective-permute-start.10 = (bf16[96,128]{1,0:T(8,128)(2,1)S(1)}, bf16[96,128]{1,0:T(8,128)(2,1)S(1)}, u32[]{:S(2)}, u32[]{:S(2)}) collective-permute-start(bf16[96,128]{1,0:T(8,128)(2,1)S(1)} %get-tuple-element.74.refs_0_), channel_id=1, source_target_pairs={{0,12},{1,13},{2,14},{3,15},{4,8},{5,9},{6,10},{7,11},{12,0},{13,1... | collective-permute-start | bytes 73736 | tf_op jit(solution)/shard_map/ppermute | solution.py:304
  50.4 4.3 %collective-permute-start.11 = (bf16[96,128]{1,0:T(8,128)(2,1)S(1)}, bf16[96,128]{1,0:T(8,128)(2,1)S(1)}, u32[]{:S(2)}, u32[]{:S(2)}) collective-permute-start(bf16[96,128]{1,0:T(8,128)(2,1)S(1)} %get-tuple-element.74.refs_0_), channel_id=1, source_target_pairs={{0,8},{1,9},{2,10},{3,11},{4,0},{5,1},{6,2},{7,3},{12,4},{13,5},{1... | collective-permute-start | bytes 73736 | tf_op jit(solution)/shard_map/ppermute | solution.py:304
  51.2 4.7 %collective-permute-start.9 = (bf16[96,128]{1,0:T(8,128)(2,1)S(1)}, bf16[96,128]{1,0:T(8,128)(2,1)S(1)}, u32[]{:S(2)}, u32[]{:S(2)}) collective-permute-start(bf16[96,128]{1,0:T(8,128)(2,1)S(1)} %get-tuple-element.74.refs_0_), channel_id=1, source_target_pairs={{0,4},{1,5},{2,6},{3,7},{4,12},{5,13},{6,14},{7,15},{12,8},{13,9},... | collective-permute-start | bytes 73736 | tf_op jit(solution)/shard_map/ppermute | solution.py:304
  56.1 3.9 %collective-permute-start.12 = (bf16[96,128]{1,0:T(8,128)(2,1)S(1)}, bf16[96,128]{1,0:T(8,128)(2,1)S(1)}, u32[]{:S(2)}, u32[]{:S(2)}) collective-permute-start(bf16[96,128]{1,0:T(8,128)(2,1)S(1)} %shard_map.82.refs_0_), channel_id=1, source_target_pairs={{0,2},{1,3},{2,0},{3,1},{4,6},{5,7},{6,4},{7,5},{12,14},{13,15},{1... | collective-permute-start | bytes 73736 | tf_op jit(solution)/shard_map/ppermute | solution.py:304
  60.7 8.1 %collective-permute-start.14 = (bf16[24,1024]{1,0:T(8,128)(2,1)S(1)}, bf16[24,1024]{1,0:T(8,128)(2,1)S(1)}, u32[]{:S(2)}, u32[]{:S(2)}) collective-permute-start(bf16[24,1024]{1,0:T(8,128)(2,1)S(1)} %get-tuple-element.84), channel_id=1, source_target_pairs={{0,2},{1,3},{2,0},{3,1},{4,6},{5,7},{6,4},{7,5},{12,14},{13,15},{1... | collective-permute-start | bytes 147464 | tf_op jit(solution)/shard_map/ppermute | solution.py:304
  62.2 6.5 %collective-permute-start.15 = (bf16[24,1024]{1,0:T(8,128)(2,1)S(1)}, bf16[24,1024]{1,0:T(8,128)(2,1)S(1)}, u32[]{:S(2)}, u32[]{:S(2)}) collective-permute-start(bf16[24,1024]{1,0:T(8,128)(2,1)S(1)} %get-tuple-element.85), channel_id=1, source_target_pairs={{0,8},{1,9},{2,10},{3,11},{4,0},{5,1},{6,2},{7,3},{12,4},{13,5},{1... | collective-permute-start | bytes 147464 | tf_op jit(solution)/shard_map/ppermute | solution.py:304
  62.8 9.1 %collective-permute-start.16 = (bf16[24,1024]{1,0:T(8,128)(2,1)S(1)}, bf16[24,1024]{1,0:T(8,128)(2,1)S(1)}, u32[]{:S(2)}, u32[]{:S(2)}) collective-permute-start(bf16[24,1024]{1,0:T(8,128)(2,1)S(1)} %get-tuple-element.86), channel_id=1, source_target_pairs={{0,10},{1,11},{2,8},{3,9},{4,2},{5,3},{6,0},{7,1},{12,6},{13,7},{1... | collective-permute-start | bytes 147464 | tf_op jit(solution)/shard_map/ppermute | solution.py:304
  65.0 6.9 %collective-permute-start.17 = (bf16[24,1024]{1,0:T(8,128)(2,1)S(1)}, bf16[24,1024]{1,0:T(8,128)(2,1)S(1)}, u32[]{:S(2)}, u32[]{:S(2)}) collective-permute-start(bf16[24,1024]{1,0:T(8,128)(2,1)S(1)} %get-tuple-element.87), channel_id=1, source_target_pairs={{0,12},{1,13},{2,14},{3,15},{4,8},{5,9},{6,10},{7,11},{12,0},{13,1... | collective-permute-start | bytes 147464 | tf_op jit(solution)/shard_map/ppermute | solution.py:304
  66.6 6.8 %collective-permute-start.18 = (bf16[24,1024]{1,0:T(8,128)(2,1)S(1)}, bf16[24,1024]{1,0:T(8,128)(2,1)S(1)}, u32[]{:S(2)}, u32[]{:S(2)}) collective-permute-start(bf16[24,1024]{1,0:T(8,128)(2,1)S(1)} %get-tuple-element.88), channel_id=1, source_target_pairs={{0,14},{1,15},{2,12},{3,13},{4,10},{5,11},{6,8},{7,9},{12,2},{13,3... | collective-permute-start | bytes 147464 | tf_op jit(solution)/shard_map/ppermute | solution.py:304
  68.7 5.2 %collective-permute-start.19 = (bf16[24,1024]{1,0:T(8,128)(2,1)S(1)}, bf16[24,1024]{1,0:T(8,128)(2,1)S(1)}, u32[]{:S(2)}, u32[]{:S(2)}) collective-permute-start(bf16[24,1024]{1,0:T(8,128)(2,1)S(1)} %get-tuple-element.89), channel_id=1, source_target_pairs={{0,4},{1,5},{2,6},{3,7},{4,12},{5,13},{6,14},{7,15},{12,8},{13,9},... | collective-permute-start | bytes 147464 | tf_op jit(solution)/shard_map/ppermute | solution.py:304
  68.8 6.5 %collective-permute-start.20 = (bf16[24,1024]{1,0:T(8,128)(2,1)S(1)}, bf16[24,1024]{1,0:T(8,128)(2,1)S(1)}, u32[]{:S(2)}, u32[]{:S(2)}) collective-permute-start(bf16[24,1024]{1,0:T(8,128)(2,1)S(1)} %get-tuple-element.90), channel_id=1, source_target_pairs={{0,6},{1,7},{2,4},{3,5},{4,14},{5,15},{6,12},{7,13},{12,10},{13,11... | collective-permute-start | bytes 147464 | tf_op jit(solution)/shard_map/ppermute | solution.py:304
  (3 other events, 6.1 us)

commit v21 on v13

--- a/solution.py
+++ b/solution.py
@@ -316,12 +316,12 @@
         if step:
             meet(after([block[step - 1], other[step - 1]], block[step]))
             bases.append(base_rows(rows[-1], query_weight))
-    base, weight_other = base_and_weight(after(rows, bases[-1]), weight_other)
-    block[last] = after(block[last], base)
+    block[last] = after(block[last], bases[-1])
     tokens.append(token(block[last]))
     source = after(block[last], other[-1], tokens[-1])
     source = jnp.where((me & 1) == 0, source, other[-1])
     crossed = lax.ppermute(source, "adapter", split_pairs(places))
+    base, weight_other = base_and_weight(after(rows, source), weight_other)
     meet(after([block[last - 1], other[-1]], source))
     bases.append(base_rows(rows[-1], query_weight))
     bases_other = [base, base_rows(rows[-1], weight_other)]

time: 74.4 us -> 75.8 us (1.019)
  waiting for transfers between devices: 17.4 us -> 19 us
    ppermute x13, waiting for transfers between devices: 14.2 us -> 19 us  [move(): return lax.ppermute(x, 'adapter', pairs(places, steps, flip))]
    ppermute x1, waiting for transfers between devices: 3.14 us -> 0.01 us  [shards(): crossed = lax.ppermute(source, 'adapter', split_pairs(places))]
  transfers between devices with their start and end apart: 14 -> 14, of which waited for: 8 -> 7; matrix products, arithmetic and copies ran while one was open for 18% -> 17% of each run, Pallas kernels for 13% -> 13%
where the time goes in v21:
time: 75.8 us; the launch traced here: 75.6 us
  waiting for transfers between devices  19 us (25%)
  starting transfers between devices  17.3 us (23%)
  matrix products  13 us (17%)
  blocking collectives  12.7 us (17%)
  Pallas kernels  10.3 us (14%)
  local copies, waits for them, and re-layouts  3.02 us (4%)
    ppermute x13, waiting for transfers between devices, move(): return lax.ppermute(x, 'adapter', pairs(places, steps, flip))  19 us
    ppermute x13, starting transfers between devices, move(): return lax.ppermute(x, 'adapter', pairs(places, steps, flip))  16.5 us
    dot_general x6, matrix products, base_rows(): return jnp.dot(rows, weight, preferred_element_type=jnp.float32)  13 us
    all_to_all x1, blocking collectives, shards(): lax.all_to_all(query, 'adapter', 0, 0, axis_index_groups=groups, tiled=True)  12.7 us
    pallas_call x6, Pallas kernels, call(): pl.pallas_call(kernel, out_shape=out_shape, in_specs=[VMEM] * len(operand...  4.48 us
    pallas_call x1, Pallas kernels, base_and_weight(): pl.pallas_call(base_kernel, out_shape=(jax.ShapeDtypeStruct((rows, weight...  3.79 us
    unnamed x12, local copies, waits for them, and re-layouts  2.24 us
    pallas_call x1, Pallas kernels, normalize(): pl.pallas_call(norm_kernel, out_shape=jax.ShapeDtypeStruct((rows, width +...  2.05 us
  transfers between devices with their start and end apart: 14, of which 7 were waited for; matrix products, arithmetic and copies ran while one was open for 17% of the time, Pallas kernels for 13%

profile of v21, /device:TPU:0, one launch (start us, length us, event | category | flops | bytes accessed | tf_op | source)
XLA Modules:
  0.0 75.6 jit_solution(5524906270174453659)
XLA Ops:
  0.5 2.0 %shard_map.73.refs_0_ = bf16[24,8320]{1,0:T(8,128)(2,1)} custom-call(bf16[24,8192]{1,0:T(8,128)(2,1)} %refs_0_.1, f32[1,8192]{1,0:T(1,128)} %bitcast.32, s32[1,24]{1,0:T(1,128)} %bitcast.33, s32[1,16]{1,0:T(1,128)} %bitcast.34), custom_call_target="tpu_custom_call" | custom-call | tf_op jit(solution)/shard_map/pallas_call | solution.py:109
  2.6 3.1 %collective-permute-start = (bf16[24,8320]{1,0:T(8,128)(2,1)}, bf16[24,8320]{1,0:T(8,128)(2,1)S(1)}, u32[]{:S(2)}, u32[]{:S(2)}) collective-permute-start(bf16[24,8320]{1,0:T(8,128)(2,1)} %shard_map.73.refs_0_), channel_id=1, source_target_pairs={{0,4},{1,5},{2,6},{3,7},{4,12},{5,13},{6,14},{7,15},{12,8},{13,9},... | collective-permute-start | bytes 1198088 | tf_op jit(solution)/shard_map/ppermute | solution.py:289
  5.6 1.5 %collective-permute-start.2 = (bf16[24,8320]{1,0:T(8,128)(2,1)}, bf16[24,8320]{1,0:T(8,128)(2,1)S(1)}, u32[]{:S(2)}, u32[]{:S(2)}) collective-permute-start(bf16[24,8320]{1,0:T(8,128)(2,1)} %shard_map.73.refs_0_), channel_id=1, source_target_pairs={{0,2},{1,3},{2,0},{3,1},{4,6},{5,7},{6,4},{7,5},{12,14},{13,15},{1... | collective-permute-start | bytes 1198088 | tf_op jit(solution)/shard_map/ppermute | solution.py:289
  7.2 9.1 %collective-permute-done.block_ref.refs_0_ = bf16[24,8320]{1,0:T(8,128)(2,1)S(1)} collective-permute-done((bf16[24,8320]{1,0:T(8,128)(2,1)}, bf16[24,8320]{1,0:T(8,128)(2,1)S(1)}, u32[]{:S(2)}, u32[]{:S(2)}) %collective-permute-start) | collective-permute-done | bytes 399392 | tf_op jit(solution)/shard_map/ppermute | solution.py:289
  16.7 2.6 %collective-permute-start.1 = (bf16[24,8320]{1,0:T(8,128)(2,1)S(1)}, bf16[24,8320]{1,0:T(8,128)(2,1)S(1)}, u32[]{:S(2)}, u32[]{:S(2)}) collective-permute-start(bf16[24,8320]{1,0:T(8,128)(2,1)S(1)} %collective-permute-done.block_ref.refs_0_), channel_id=1, source_target_pairs={{0,4},{1,5},{2,6},{3,7},{4,12},{5,13},{6,14},{7,15},{12,8},{13,9},... | collective-permute-start | bytes 1198088 | tf_op jit(solution)/shard_map/ppermute | solution.py:289
  19.3 1.5 %collective-permute-start.5 = (bf16[24,8320]{1,0:T(8,128)(2,1)S(1)}, bf16[24,8320]{1,0:T(8,128)(2,1)S(1)}, u32[]{:S(2)}, u32[]{:S(2)}) collective-permute-start(bf16[24,8320]{1,0:T(8,128)(2,1)S(1)} %collective-permute-done.block_ref.refs_0_), channel_id=1, source_target_pairs={{0,2},{1,3},{2,0},{3,1},{4,6},{5,7},{6,4},{7,5},{12,14},{13,15},{1... | collective-permute-start | bytes 1198088 | tf_op jit(solution)/shard_map/ppermute | solution.py:289
  20.8 1.2 %copy-done = bf16[1,8192,64]{1,2,0:T(8,128)(2,1)S(1)} copy-done((bf16[1,8192,64]{1,2,0:T(8,128)(2,1)S(1)}, bf16[1,8192,64]{1,2,0:T(8,128)(2,1)}, u32[]{:S(2)}) %copy-start) | copy-done | bytes 1048600
  22.1 1.0 %copy-done.2 = bf16[24,8320]{1,0:T(8,128)(2,1)S(1)} copy-done((bf16[24,8320]{1,0:T(8,128)(2,1)S(1)}, bf16[24,8320]{1,0:T(8,128)(2,1)}, u32[]{:S(2)}) %copy-start.2) | copy-done | bytes 399384
  24.0 5.4 %fusion.refs_2_ = f32[48,512]{1,0:T(8,128)S(1)} fusion(bf16[48,8192]{1,0:T(8,128)(2,1)S(1)} %get-tuple-element.56.refs_0_, bf16[8192,512]{1,0:T(8,128)(2,1)} %param.9), kind=kOutput, calls=%fused_computation.1 | convolution fusion | flops 402653184 | bytes 9273344 | tf_op jit(solution)/shard_map/dot_general | solution.py:292
  29.5 1.2 %collective-permute-start.4 = (bf16[24,8320]{1,0:T(8,128)(2,1)S(1)}, bf16[24,8320]{1,0:T(8,128)(2,1)S(1)}, u32[]{:S(2)}, u32[]{:S(2)}) collective-permute-start(bf16[24,8320]{1,0:T(8,128)(2,1)S(1)} %collective-permute-done.1.block_ref.refs_0_), channel_id=1, source_target_pairs={{0,4},{1,5},{2,6},{3,7},{4,12},{5,13},{6,14},{7,15},{12,8},{13,9},... | collective-permute-start | bytes 1198088 | tf_op jit(solution)/shard_map/ppermute | solution.py:289
  30.7 1.4 %collective-permute-start.6 = (bf16[24,8320]{1,0:T(8,128)(2,1)S(1)}, bf16[24,8320]{1,0:T(8,128)(2,1)S(1)}, u32[]{:S(2)}, u32[]{:S(2)}) collective-permute-start(bf16[24,8320]{1,0:T(8,128)(2,1)S(1)} %collective-permute-done.1.block_ref.refs_0_), channel_id=1, source_target_pairs={{0,2},{1,3},{2,0},{3,1},{4,6},{5,7},{6,4},{7,5},{12,14},{13,15},{1... | collective-permute-start | bytes 1198088 | tf_op jit(solution)/shard_map/ppermute | solution.py:289
  33.0 1.5 %fusion.1.refs_3_ = f32[48,512]{1,0:T(8,128)S(1)} fusion(bf16[48,8192]{1,0:T(8,128)(2,1)S(1)} %get-tuple-element.57.refs_1_, bf16[8192,512]{1,0:T(8,128)(2,1)S(1)} %bitcast.30), kind=kOutput, calls=%fused_computation.2 | convolution fusion | flops 402653184 | bytes 9273344 | tf_op jit(solution)/shard_map/dot_general | solution.py:292
  34.5 5.3 %collective-permute-done.4.block_ref.refs_3_ = bf16[24,8320]{1,0:T(8,128)(2,1)S(1)} collective-permute-done((bf16[24,8320]{1,0:T(8,128)(2,1)S(1)}, bf16[24,8320]{1,0:T(8,128)(2,1)S(1)}, u32[]{:S(2)}, u32[]{:S(2)}) %collective-permute-start.4) | collective-permute-done | bytes 399392 | tf_op jit(solution)/shard_map/ppermute | solution.py:289
  41.9 1.5 %fusion.2.refs_4_ = f32[48,512]{1,0:T(8,128)S(1)} fusion(bf16[48,8192]{1,0:T(8,128)(2,1)S(1)} %get-tuple-element.55, bf16[8192,512]{1,0:T(8,128)(2,1)S(1)} %bitcast.30), kind=kOutput, calls=%fused_computation.3 | convolution fusion | flops 402653184 | bytes 9273344 | tf_op jit(solution)/shard_map/dot_general | solution.py:292
  43.4 3.8 %shard_map.80 = (f32[96,512]{1,0:T(8,128)S(1)}, bf16[8192,512]{1,0:T(8,128)(2,1)S(1)}) custom-call(bf16[48,8192]{1,0:T(8,128)(2,1)S(1)} %get-tuple-element.56.refs_0_, bf16[48,8192]{1,0:T(8,128)(2,1)S(1)} %get-tuple-element.57.refs_1_, bf16[8192,512]{1,0:T(8,128)(2,1)} %collective-permute-done.8.refs_2_), custom_call_target="tpu_custom_call" | custom-call | flops 1 | bytes 1 | tf_op jit(solution)/shard_map/pallas_call | solution.py:205
  47.2 1.5 %fusion.3.refs_7_ = f32[48,512]{1,0:T(8,128)S(1)} fusion(bf16[48,8192]{1,0:T(8,128)(2,1)S(1)} %get-tuple-element.55, bf16[8192,512]{1,0:T(8,128)(2,1)S(1)} %get-tuple-element.58), kind=kOutput, calls=%fused_computation.4 | convolution fusion | flops 402653184 | bytes 9273344 | tf_op jit(solution)/shard_map/dot_general | solution.py:292
  48.8 1.0 %shard_map.81 = (bf16[96,128]{1,0:T(8,128)(2,1)S(1)}, s32[48,128]{1,0:T(8,128)S(1)}, bf16[48,8192]{1,0:T(8,128)(2,1)S(1)}) custom-call(f32[8,128]{1,0:T(8,128)S(1)} %shard_map.74.refs_0_, f32[8,128]{1,0:T(8,128)S(1)} %shard_map.76.refs_1_, f32[8,128]{1,0:T(8,128)S(1)} %shard_map.78.refs_2_, bf16[24,8320]{1,0:T(8,128)(2,1)S(1)} %collective-permute-done.4.block_ref.refs_3_, ...), custom_call_target="tpu_custom_call" | custom-call | flops 1 | bytes 1 | tf_op jit(solution)/shard_map/pallas_call | solution.py:57
  49.7 2.1 %collective-permute-start.10 = (bf16[96,128]{1,0:T(8,128)(2,1)S(1)}, bf16[96,128]{1,0:T(8,128)(2,1)S(1)}, u32[]{:S(2)}, u32[]{:S(2)}) collective-permute-start(bf16[96,128]{1,0:T(8,128)(2,1)S(1)} %get-tuple-element.65.refs_0_), channel_id=1, source_target_pairs={{0,12},{1,13},{2,14},{3,15},{4,8},{5,9},{6,10},{7,11},{12,0},{13,1... | collective-permute-start | bytes 73736 | tf_op jit(solution)/shard_map/ppermute | solution.py:289
  52.7 1.2 %collective-permute-start.9 = (bf16[96,128]{1,0:T(8,128)(2,1)S(1)}, bf16[96,128]{1,0:T(8,128)(2,1)S(1)}, u32[]{:S(2)}, u32[]{:S(2)}) collective-permute-start(bf16[96,128]{1,0:T(8,128)(2,1)S(1)} %get-tuple-element.65.refs_0_), channel_id=1, source_target_pairs={{0,4},{1,5},{2,6},{3,7},{4,12},{5,13},{6,14},{7,15},{12,8},{13,9},... | collective-permute-start | bytes 73736 | tf_op jit(solution)/shard_map/ppermute | solution.py:289
  53.9 1.5 %fusion.4.refs_5_ = f32[48,512]{1,0:T(8,128)S(1)} fusion(bf16[48,8192]{1,0:T(8,128)(2,1)S(1)} %get-tuple-element.70, bf16[8192,512]{1,0:T(8,128)(2,1)S(1)} %bitcast.30), kind=kOutput, calls=%fused_computation.5 | convolution fusion | flops 402653184 | bytes 9273344 | tf_op jit(solution)/shard_map/dot_general | solution.py:292
  55.7 1.7 %collective-permute-done.9.refs_1_ = bf16[96,128]{1,0:T(8,128)(2,1)S(1)} collective-permute-done((bf16[96,128]{1,0:T(8,128)(2,1)S(1)}, bf16[96,128]{1,0:T(8,128)(2,1)S(1)}, u32[]{:S(2)}, u32[]{:S(2)}) %collective-permute-start.9) | collective-permute-done | bytes 24608 | tf_op jit(solution)/shard_map/ppermute | solution.py:289
  58.1 1.5 %fusion.5.refs_8_ = f32[48,512]{1,0:T(8,128)S(1)} fusion(bf16[48,8192]{1,0:T(8,128)(2,1)S(1)} %get-tuple-element.70, bf16[8192,512]{1,0:T(8,128)(2,1)S(1)} %get-tuple-element.58), kind=kOutput, calls=%fused_computation.6 | convolution fusion | flops 402653184 | bytes 9273344 | tf_op jit(solution)/shard_map/dot_general | solution.py:292
  59.6 1.8 %collective-permute-done.12.refs_1_ = bf16[96,128]{1,0:T(8,128)(2,1)S(1)} collective-permute-done((bf16[96,128]{1,0:T(8,128)(2,1)S(1)}, bf16[96,128]{1,0:T(8,128)(2,1)S(1)}, u32[]{:S(2)}, u32[]{:S(2)}) %collective-permute-start.12) | collective-permute-done | bytes 24608 | tf_op jit(solution)/shard_map/ppermute | solution.py:289
  62.1 12.7 %all_to_all.5 = bf16[8,24,1024]{2,1,0:T(8,128)(2,1)S(1)} all-to-all(bf16[8,24,1024]{2,1,0:T(8,128)(2,1)S(1)} %shard_map.83), channel_id=1, replica_groups={{0,2,4,6,8,10,12,14},{1,3,5,7,9,11,13,15},{16,18,20,22,24,26,28,30},{17..., dimensions={0} | all-to-all | bytes 786432 | tf_op jit(solution)/shard_map/all_to_all | solution.py:341
  (37 shorter events, 8.2 us)
Async XLA Ops:
  0.0 43.4 %collective-permute-start.8 = (bf16[8192,512]{1,0:T(8,128)(2,1)}, bf16[8192,512]{1,0:T(8,128)(2,1)}, u32[]{:S(2)}, u32[]{:S(2)}) collective-permute-start(bf16[8192,512]{1,0:T(8,128)(2,1)} %param.9), channel_id=1, source_target_pairs={{0,1},{1,0},{2,3},{3,2},{4,5},{5,4},{6,7},{7,6},{12,13},{13,12},{1... | collective-permute-start | bytes 25165832 | tf_op jit(solution)/shard_map/ppermute | solution.py:289
  0.5 20.4 %collective-permute-start.3 = (bf16[64,8192]{1,0:T(8,128)(2,1)}, bf16[64,8192]{1,0:T(8,128)(2,1)S(1)}, u32[]{:S(2)}, u32[]{:S(2)}) collective-permute-start(bf16[64,8192]{1,0:T(8,128)(2,1)} %bitcast.22), channel_id=1, source_target_pairs={{0,1},{1,0},{2,3},{3,2},{4,5},{5,4},{6,7},{7,6},{12,13},{13,12},{1... | collective-permute-start | bytes 3145736 | tf_op jit(solution)/shard_map/ppermute | solution.py:289
  2.6 13.7 %collective-permute-start = (bf16[24,8320]{1,0:T(8,128)(2,1)}, bf16[24,8320]{1,0:T(8,128)(2,1)S(1)}, u32[]{:S(2)}, u32[]{:S(2)}) collective-permute-start(bf16[24,8320]{1,0:T(8,128)(2,1)} %shard_map.73.refs_0_), channel_id=1, source_target_pairs={{0,4},{1,5},{2,6},{3,7},{4,12},{5,13},{6,14},{7,15},{12,8},{13,9},... | collective-permute-start | bytes 1198088 | tf_op jit(solution)/shard_map/ppermute | solution.py:289
  5.6 11.1 %collective-permute-start.2 = (bf16[24,8320]{1,0:T(8,128)(2,1)}, bf16[24,8320]{1,0:T(8,128)(2,1)S(1)}, u32[]{:S(2)}, u32[]{:S(2)}) collective-permute-start(bf16[24,8320]{1,0:T(8,128)(2,1)} %shard_map.73.refs_0_), channel_id=1, source_target_pairs={{0,2},{1,3},{2,0},{3,1},{4,6},{5,7},{6,4},{7,5},{12,14},{13,15},{1... | collective-permute-start | bytes 1198088 | tf_op jit(solution)/shard_map/ppermute | solution.py:289
  7.2 52.5 %collective-permute-start.13 = (bf16[1024,512]{1,0:T(8,128)(2,1)}, bf16[1024,512]{1,0:T(8,128)(2,1)S(1)}, u32[]{:S(2)}, u32[]{:S(2)}) collective-permute-start(bf16[1024,512]{1,0:T(8,128)(2,1)} %bitcast.27), channel_id=1, source_target_pairs={{0,1},{1,0},{2,3},{3,2},{4,5},{5,4},{6,7},{7,6},{12,13},{13,12},{1... | collective-permute-start | bytes 3145736 | tf_op jit(solution)/shard_map/ppermute | solution.py:289
  16.7 12.7 %collective-permute-start.1 = (bf16[24,8320]{1,0:T(8,128)(2,1)S(1)}, bf16[24,8320]{1,0:T(8,128)(2,1)S(1)}, u32[]{:S(2)}, u32[]{:S(2)}) collective-permute-start(bf16[24,8320]{1,0:T(8,128)(2,1)S(1)} %collective-permute-done.block_ref.refs_0_), channel_id=1, source_target_pairs={{0,4},{1,5},{2,6},{3,7},{4,12},{5,13},{6,14},{7,15},{12,8},{13,9},... | collective-permute-start | bytes 1198088 | tf_op jit(solution)/shard_map/ppermute | solution.py:289
  19.3 10.1 %collective-permute-start.5 = (bf16[24,8320]{1,0:T(8,128)(2,1)S(1)}, bf16[24,8320]{1,0:T(8,128)(2,1)S(1)}, u32[]{:S(2)}, u32[]{:S(2)}) collective-permute-start(bf16[24,8320]{1,0:T(8,128)(2,1)S(1)} %collective-permute-done.block_ref.refs_0_), channel_id=1, source_target_pairs={{0,2},{1,3},{2,0},{3,1},{4,6},{5,7},{6,4},{7,5},{12,14},{13,15},{1... | collective-permute-start | bytes 1198088 | tf_op jit(solution)/shard_map/ppermute | solution.py:289
  20.8 1.2 %copy-start = (bf16[1,8192,64]{1,2,0:T(8,128)(2,1)S(1)}, bf16[1,8192,64]{1,2,0:T(8,128)(2,1)}, u32[]{:S(2)}) copy-start(bf16[1,8192,64]{1,2,0:T(8,128)(2,1)} %param.10) | copy-start | bytes 3145732
  22.1 1.0 %copy-start.2 = (bf16[24,8320]{1,0:T(8,128)(2,1)S(1)}, bf16[24,8320]{1,0:T(8,128)(2,1)}, u32[]{:S(2)}) copy-start(bf16[24,8320]{1,0:T(8,128)(2,1)} %shard_map.73.refs_0_) | copy-start | bytes 1198084
  23.1 9.9 %slice-start = ((s8[8388608]{0:T(1024)(128)(4,1)}), s8[4194304]{0:T(1024)(128)(4,1)S(1)}, s32[]{:S(2)}) async-start(s8[8388608]{0:T(1024)(128)(4,1)} %bitcast.29), calls=%async_computation.1 | async-start | bytes 8388608
  24.0 8.1 %copy-start.1 = (bf16[1,8192,64]{1,2,0:T(8,128)(2,1)S(1)}, bf16[1,8192,64]{1,2,0:T(8,128)(2,1)}, u32[]{:S(2)}) copy-start(bf16[1,8192,64]{1,2,0:T(8,128)(2,1)} %param.10) | copy-start | bytes 3145732
  24.0 9.0 %slice-start.1 = ((s8[8388608]{0:T(1024)(128)(4,1)}), s8[4194304]{0:T(1024)(128)(4,1)S(1)}, s32[]{:S(2)}) async-start(s8[8388608]{0:T(1024)(128)(4,1)} %bitcast.29), calls=%async_computation.2 | async-start | bytes 8388608
  29.5 10.4 %collective-permute-start.4 = (bf16[24,8320]{1,0:T(8,128)(2,1)S(1)}, bf16[24,8320]{1,0:T(8,128)(2,1)S(1)}, u32[]{:S(2)}, u32[]{:S(2)}) collective-permute-start(bf16[24,8320]{1,0:T(8,128)(2,1)S(1)} %collective-permute-done.1.block_ref.refs_0_), channel_id=1, source_target_pairs={{0,4},{1,5},{2,6},{3,7},{4,12},{5,13},{6,14},{7,15},{12,8},{13,9},... | collective-permute-start | bytes 1198088 | tf_op jit(solution)/shard_map/ppermute | solution.py:289
  30.7 9.5 %collective-permute-start.6 = (bf16[24,8320]{1,0:T(8,128)(2,1)S(1)}, bf16[24,8320]{1,0:T(8,128)(2,1)S(1)}, u32[]{:S(2)}, u32[]{:S(2)}) collective-permute-start(bf16[24,8320]{1,0:T(8,128)(2,1)S(1)} %collective-permute-done.1.block_ref.refs_0_), channel_id=1, source_target_pairs={{0,2},{1,3},{2,0},{3,1},{4,6},{5,7},{6,4},{7,5},{12,14},{13,15},{1... | collective-permute-start | bytes 1198088 | tf_op jit(solution)/shard_map/ppermute | solution.py:289
  40.2 8.6 %collective-permute-start.7 = (bf16[24,8320]{1,0:T(8,128)(2,1)S(1)}, bf16[24,8320]{1,0:T(8,128)(2,1)S(1)}, u32[]{:S(2)}, u32[]{:S(2)}) collective-permute-start(bf16[24,8320]{1,0:T(8,128)(2,1)S(1)} %broadcast_select_fusion), channel_id=1, source_target_pairs={{0,2},{2,0},{4,6},{6,4},{12,14},{14,12},{8,10},{10,8},{1,5},{3,7},... | collective-permute-start | bytes 1198088 | tf_op jit(solution)/shard_map/ppermute | solution.py:323
  49.7 5.7 %collective-permute-start.10 = (bf16[96,128]{1,0:T(8,128)(2,1)S(1)}, bf16[96,128]{1,0:T(8,128)(2,1)S(1)}, u32[]{:S(2)}, u32[]{:S(2)}) collective-permute-start(bf16[96,128]{1,0:T(8,128)(2,1)S(1)} %get-tuple-element.65.refs_0_), channel_id=1, source_target_pairs={{0,12},{1,13},{2,14},{3,15},{4,8},{5,9},{6,10},{7,11},{12,0},{13,1... | collective-permute-start | bytes 73736 | tf_op jit(solution)/shard_map/ppermute | solution.py:289
  51.8 3.8 %collective-permute-start.11 = (bf16[96,128]{1,0:T(8,128)(2,1)S(1)}, bf16[96,128]{1,0:T(8,128)(2,1)S(1)}, u32[]{:S(2)}, u32[]{:S(2)}) collective-permute-start(bf16[96,128]{1,0:T(8,128)(2,1)S(1)} %get-tuple-element.65.refs_0_), channel_id=1, source_target_pairs={{0,8},{1,9},{2,10},{3,11},{4,0},{5,1},{6,2},{7,3},{12,4},{13,5},{1... | collective-permute-start | bytes 73736 | tf_op jit(solution)/shard_map/ppermute | solution.py:289
  52.7 4.7 %collective-permute-start.9 = (bf16[96,128]{1,0:T(8,128)(2,1)S(1)}, bf16[96,128]{1,0:T(8,128)(2,1)S(1)}, u32[]{:S(2)}, u32[]{:S(2)}) collective-permute-start(bf16[96,128]{1,0:T(8,128)(2,1)S(1)} %get-tuple-element.65.refs_0_), channel_id=1, source_target_pairs={{0,4},{1,5},{2,6},{3,7},{4,12},{5,13},{6,14},{7,15},{12,8},{13,9},... | collective-permute-start | bytes 73736 | tf_op jit(solution)/shard_map/ppermute | solution.py:289
  57.5 3.9 %copy-start.3 = (bf16[16,64,512]{2,1,0:T(8,128)(2,1)S(1)}, bf16[16,64,512]{2,1,0:T(8,128)(2,1)}, u32[]{:S(2)}) copy-start(bf16[16,64,512]{2,1,0:T(8,128)(2,1)} %param.11) | copy-start | bytes 3145732
  57.5 3.9 %collective-permute-start.12 = (bf16[96,128]{1,0:T(8,128)(2,1)S(1)}, bf16[96,128]{1,0:T(8,128)(2,1)S(1)}, u32[]{:S(2)}, u32[]{:S(2)}) collective-permute-start(bf16[96,128]{1,0:T(8,128)(2,1)S(1)} %shard_map.82.refs_0_), channel_id=1, source_target_pairs={{0,2},{1,3},{2,0},{3,1},{4,6},{5,7},{6,4},{7,5},{12,14},{13,15},{1... | collective-permute-start | bytes 73736 | tf_op jit(solution)/shard_map/ppermute | solution.py:289

commit v22 on v13

--- a/solution.py
+++ b/solution.py
@@ -13,7 +13,7 @@
 CORNERS = SIDE * CORES
 LANES = 128
 CHUNK = 1024
-VMEM_LIMIT = 24 << 20
+VMEM_LIMIT = 16 << 20
 VMEM = pl.BlockSpec(memory_space=pltpu.VMEM)
 
 

time: 74.4 us -> 74.4 us (level)
  no operation moved by 1% of the time
where the time goes in v22:
time: 74.4 us; the launch traced here: 74.2 us
  starting transfers between devices  17.5 us (24%)
  waiting for transfers between devices  17.4 us (23%)
  matrix products  13 us (17%)
  blocking collectives  12.8 us (17%)
  Pallas kernels  10.3 us (14%)
  local copies, waits for them, and re-layouts  3.02 us (4%)
    ppermute x13, starting transfers between devices, move(): return lax.ppermute(x, 'adapter', pairs(places, steps, flip))  16.7 us
    ppermute x13, waiting for transfers between devices, move(): return lax.ppermute(x, 'adapter', pairs(places, steps, flip))  14.2 us
    dot_general x6, matrix products, base_rows(): return jnp.dot(rows, weight, preferred_element_type=jnp.float32)  13 us
    all_to_all x1, blocking collectives, shards(): lax.all_to_all(query, 'adapter', 0, 0, axis_index_groups=groups, tiled=True)  12.8 us
    pallas_call x6, Pallas kernels, call(): pl.pallas_call(kernel, out_shape=out_shape, in_specs=[VMEM] * len(operand...  4.47 us
    pallas_call x1, Pallas kernels, base_and_weight(): pl.pallas_call(base_kernel, out_shape=(jax.ShapeDtypeStruct((rows, weight...  3.78 us
    ppermute x1, waiting for transfers between devices, shards(): crossed = lax.ppermute(source, 'adapter', split_pairs(places))  3.17 us
    unnamed x12, local copies, waits for them, and re-layouts  2.24 us
  transfers between devices with their start and end apart: 14, of which 8 were waited for; matrix products, arithmetic and copies ran while one was open for 18% of the time, Pallas kernels for 13%

profile of v22, /device:TPU:0, one launch (start us, length us, event | category | flops | bytes accessed | tf_op | source)
XLA Modules:
  0.0 74.2 jit_solution(4115514104004673226)
XLA Ops:
  0.5 2.0 %shard_map.73.refs_0_ = bf16[24,8320]{1,0:T(8,128)(2,1)} custom-call(bf16[24,8192]{1,0:T(8,128)(2,1)} %refs_0_.1, f32[1,8192]{1,0:T(1,128)} %bitcast.32, s32[1,24]{1,0:T(1,128)} %bitcast.33, s32[1,16]{1,0:T(1,128)} %bitcast.34), custom_call_target="tpu_custom_call" | custom-call | tf_op jit(solution)/shard_map/pallas_call | solution.py:109
  2.6 3.1 %collective-permute-start = (bf16[24,8320]{1,0:T(8,128)(2,1)}, bf16[24,8320]{1,0:T(8,128)(2,1)S(1)}, u32[]{:S(2)}, u32[]{:S(2)}) collective-permute-start(bf16[24,8320]{1,0:T(8,128)(2,1)} %shard_map.73.refs_0_), channel_id=1, source_target_pairs={{0,4},{1,5},{2,6},{3,7},{4,12},{5,13},{6,14},{7,15},{12,8},{13,9},... | collective-permute-start | bytes 1198088 | tf_op jit(solution)/shard_map/ppermute | solution.py:289
  5.6 1.5 %collective-permute-start.2 = (bf16[24,8320]{1,0:T(8,128)(2,1)}, bf16[24,8320]{1,0:T(8,128)(2,1)S(1)}, u32[]{:S(2)}, u32[]{:S(2)}) collective-permute-start(bf16[24,8320]{1,0:T(8,128)(2,1)} %shard_map.73.refs_0_), channel_id=1, source_target_pairs={{0,2},{1,3},{2,0},{3,1},{4,6},{5,7},{6,4},{7,5},{12,14},{13,15},{1... | collective-permute-start | bytes 1198088 | tf_op jit(solution)/shard_map/ppermute | solution.py:289
  7.2 9.1 %collective-permute-done.block_ref.refs_0_ = bf16[24,8320]{1,0:T(8,128)(2,1)S(1)} collective-permute-done((bf16[24,8320]{1,0:T(8,128)(2,1)}, bf16[24,8320]{1,0:T(8,128)(2,1)S(1)}, u32[]{:S(2)}, u32[]{:S(2)}) %collective-permute-start) | collective-permute-done | bytes 399392 | tf_op jit(solution)/shard_map/ppermute | solution.py:289
  16.7 2.6 %collective-permute-start.1 = (bf16[24,8320]{1,0:T(8,128)(2,1)S(1)}, bf16[24,8320]{1,0:T(8,128)(2,1)S(1)}, u32[]{:S(2)}, u32[]{:S(2)}) collective-permute-start(bf16[24,8320]{1,0:T(8,128)(2,1)S(1)} %collective-permute-done.block_ref.refs_0_), channel_id=1, source_target_pairs={{0,4},{1,5},{2,6},{3,7},{4,12},{5,13},{6,14},{7,15},{12,8},{13,9},... | collective-permute-start | bytes 1198088 | tf_op jit(solution)/shard_map/ppermute | solution.py:289
  19.3 1.5 %collective-permute-start.5 = (bf16[24,8320]{1,0:T(8,128)(2,1)S(1)}, bf16[24,8320]{1,0:T(8,128)(2,1)S(1)}, u32[]{:S(2)}, u32[]{:S(2)}) collective-permute-start(bf16[24,8320]{1,0:T(8,128)(2,1)S(1)} %collective-permute-done.block_ref.refs_0_), channel_id=1, source_target_pairs={{0,2},{1,3},{2,0},{3,1},{4,6},{5,7},{6,4},{7,5},{12,14},{13,15},{1... | collective-permute-start | bytes 1198088 | tf_op jit(solution)/shard_map/ppermute | solution.py:289
  20.8 1.2 %copy-done = bf16[1,8192,64]{1,2,0:T(8,128)(2,1)S(1)} copy-done((bf16[1,8192,64]{1,2,0:T(8,128)(2,1)S(1)}, bf16[1,8192,64]{1,2,0:T(8,128)(2,1)}, u32[]{:S(2)}) %copy-start) | copy-done | bytes 1048600
  22.1 1.0 %copy-done.2 = bf16[24,8320]{1,0:T(8,128)(2,1)S(1)} copy-done((bf16[24,8320]{1,0:T(8,128)(2,1)S(1)}, bf16[24,8320]{1,0:T(8,128)(2,1)}, u32[]{:S(2)}) %copy-start.2) | copy-done | bytes 399384
  24.0 5.4 %fusion.refs_2_ = f32[48,512]{1,0:T(8,128)S(1)} fusion(bf16[48,8192]{1,0:T(8,128)(2,1)S(1)} %get-tuple-element.50.refs_0_, bf16[8192,512]{1,0:T(8,128)(2,1)} %param.9), kind=kOutput, calls=%fused_computation.1 | convolution fusion | flops 402653184 | bytes 9273344 | tf_op jit(solution)/shard_map/dot_general | solution.py:292
  29.5 1.2 %collective-permute-start.4 = (bf16[24,8320]{1,0:T(8,128)(2,1)S(1)}, bf16[24,8320]{1,0:T(8,128)(2,1)S(1)}, u32[]{:S(2)}, u32[]{:S(2)}) collective-permute-start(bf16[24,8320]{1,0:T(8,128)(2,1)S(1)} %collective-permute-done.1.block_ref.refs_0_), channel_id=1, source_target_pairs={{0,4},{1,5},{2,6},{3,7},{4,12},{5,13},{6,14},{7,15},{12,8},{13,9},... | collective-permute-start | bytes 1198088 | tf_op jit(solution)/shard_map/ppermute | solution.py:289
  30.7 1.4 %collective-permute-start.7 = (bf16[24,8320]{1,0:T(8,128)(2,1)S(1)}, bf16[24,8320]{1,0:T(8,128)(2,1)S(1)}, u32[]{:S(2)}, u32[]{:S(2)}) collective-permute-start(bf16[24,8320]{1,0:T(8,128)(2,1)S(1)} %collective-permute-done.1.block_ref.refs_0_), channel_id=1, source_target_pairs={{0,2},{1,3},{2,0},{3,1},{4,6},{5,7},{6,4},{7,5},{12,14},{13,15},{1... | collective-permute-start | bytes 1198088 | tf_op jit(solution)/shard_map/ppermute | solution.py:289
  33.0 1.5 %fusion.1.refs_3_ = f32[48,512]{1,0:T(8,128)S(1)} fusion(bf16[48,8192]{1,0:T(8,128)(2,1)S(1)} %get-tuple-element.51.refs_1_, bf16[8192,512]{1,0:T(8,128)(2,1)S(1)} %bitcast.30), kind=kOutput, calls=%fused_computation.2 | convolution fusion | flops 402653184 | bytes 9273344 | tf_op jit(solution)/shard_map/dot_general | solution.py:292
  34.5 3.8 %shard_map.78 = (f32[96,512]{1,0:T(8,128)S(1)}, bf16[8192,512]{1,0:T(8,128)(2,1)S(1)}) custom-call(bf16[48,8192]{1,0:T(8,128)(2,1)S(1)} %get-tuple-element.50.refs_0_, bf16[48,8192]{1,0:T(8,128)(2,1)S(1)} %get-tuple-element.51.refs_1_, bf16[8192,512]{1,0:T(8,128)(2,1)} %collective-permute-done.6.refs_2_), custom_call_target="tpu_custom_call" | custom-call | flops 1 | bytes 1 | tf_op jit(solution)/shard_map/pallas_call | solution.py:205
  38.3 1.5 %collective-permute-done.4.block_ref.refs_3_ = bf16[24,8320]{1,0:T(8,128)(2,1)S(1)} collective-permute-done((bf16[24,8320]{1,0:T(8,128)(2,1)S(1)}, bf16[24,8320]{1,0:T(8,128)(2,1)S(1)}, u32[]{:S(2)}, u32[]{:S(2)}) %collective-permute-start.4) | collective-permute-done | bytes 399392 | tf_op jit(solution)/shard_map/ppermute | solution.py:289
  41.9 1.5 %fusion.2.refs_4_ = f32[48,512]{1,0:T(8,128)S(1)} fusion(bf16[48,8192]{1,0:T(8,128)(2,1)S(1)} %get-tuple-element.58, bf16[8192,512]{1,0:T(8,128)(2,1)S(1)} %bitcast.30), kind=kOutput, calls=%fused_computation.3 | convolution fusion | flops 402653184 | bytes 9273344 | tf_op jit(solution)/shard_map/dot_general | solution.py:292
  43.4 1.5 %fusion.3.refs_7_ = f32[48,512]{1,0:T(8,128)S(1)} fusion(bf16[48,8192]{1,0:T(8,128)(2,1)S(1)} %get-tuple-element.58, bf16[8192,512]{1,0:T(8,128)(2,1)S(1)} %get-tuple-element.59), kind=kOutput, calls=%fused_computation.4 | convolution fusion | flops 402653184 | bytes 9273344 | tf_op jit(solution)/shard_map/dot_general | solution.py:292
  44.9 3.2 %collective-permute-done.8.refs_4_ = bf16[24,8320]{1,0:T(8,128)(2,1)S(1)} collective-permute-done((bf16[24,8320]{1,0:T(8,128)(2,1)S(1)}, bf16[24,8320]{1,0:T(8,128)(2,1)S(1)}, u32[]{:S(2)}, u32[]{:S(2)}) %collective-permute-start.8) | collective-permute-done | bytes 399392 | tf_op jit(solution)/shard_map/ppermute | solution.py:324
  49.1 1.3 %collective-permute-start.10 = (bf16[96,128]{1,0:T(8,128)(2,1)S(1)}, bf16[96,128]{1,0:T(8,128)(2,1)S(1)}, u32[]{:S(2)}, u32[]{:S(2)}) collective-permute-start(bf16[96,128]{1,0:T(8,128)(2,1)S(1)} %get-tuple-element.66.refs_0_), channel_id=1, source_target_pairs={{0,12},{1,13},{2,14},{3,15},{4,8},{5,9},{6,10},{7,11},{12,0},{13,1... | collective-permute-start | bytes 73736 | tf_op jit(solution)/shard_map/ppermute | solution.py:289
  51.2 1.2 %collective-permute-start.9 = (bf16[96,128]{1,0:T(8,128)(2,1)S(1)}, bf16[96,128]{1,0:T(8,128)(2,1)S(1)}, u32[]{:S(2)}, u32[]{:S(2)}) collective-permute-start(bf16[96,128]{1,0:T(8,128)(2,1)S(1)} %get-tuple-element.66.refs_0_), channel_id=1, source_target_pairs={{0,4},{1,5},{2,6},{3,7},{4,12},{5,13},{6,14},{7,15},{12,8},{13,9},... | collective-permute-start | bytes 73736 | tf_op jit(solution)/shard_map/ppermute | solution.py:289
  52.4 1.5 %fusion.4.refs_5_ = f32[48,512]{1,0:T(8,128)S(1)} fusion(bf16[48,8192]{1,0:T(8,128)(2,1)S(1)} %get-tuple-element.70, bf16[8192,512]{1,0:T(8,128)(2,1)S(1)} %bitcast.30), kind=kOutput, calls=%fused_computation.5 | convolution fusion | flops 402653184 | bytes 9273344 | tf_op jit(solution)/shard_map/dot_general | solution.py:292
  54.7 1.2 %collective-permute-done.9.refs_1_ = bf16[96,128]{1,0:T(8,128)(2,1)S(1)} collective-permute-done((bf16[96,128]{1,0:T(8,128)(2,1)S(1)}, bf16[96,128]{1,0:T(8,128)(2,1)S(1)}, u32[]{:S(2)}, u32[]{:S(2)}) %collective-permute-start.9) | collective-permute-done | bytes 24608 | tf_op jit(solution)/shard_map/ppermute | solution.py:289
  56.1 1.6 %collective-permute-start.12 = (bf16[96,128]{1,0:T(8,128)(2,1)S(1)}, bf16[96,128]{1,0:T(8,128)(2,1)S(1)}, u32[]{:S(2)}, u32[]{:S(2)}) collective-permute-start(bf16[96,128]{1,0:T(8,128)(2,1)S(1)} %shard_map.82.refs_0_), channel_id=1, source_target_pairs={{0,2},{1,3},{2,0},{3,1},{4,6},{5,7},{6,4},{7,5},{12,14},{13,15},{1... | collective-permute-start | bytes 73736 | tf_op jit(solution)/shard_map/ppermute | solution.py:289
  57.6 1.5 %fusion.5.refs_8_ = f32[48,512]{1,0:T(8,128)S(1)} fusion(bf16[48,8192]{1,0:T(8,128)(2,1)S(1)} %get-tuple-element.70, bf16[8192,512]{1,0:T(8,128)(2,1)S(1)} %get-tuple-element.59), kind=kOutput, calls=%fused_computation.6 | convolution fusion | flops 402653184 | bytes 9273344 | tf_op jit(solution)/shard_map/dot_general | solution.py:292
  60.6 12.8 %all_to_all.5 = bf16[8,24,1024]{2,1,0:T(8,128)(2,1)S(1)} all-to-all(bf16[8,24,1024]{2,1,0:T(8,128)(2,1)S(1)} %shard_map.83), channel_id=1, replica_groups={{0,2,4,6,8,10,12,14},{1,3,5,7,9,11,13,15},{16,18,20,22,24,26,28,30},{17..., dimensions={0} | all-to-all | bytes 786432 | tf_op jit(solution)/shard_map/all_to_all | solution.py:341
  (37 shorter events, 9.8 us)
Async XLA Ops:
  0.0 34.5 %collective-permute-start.6 = (bf16[8192,512]{1,0:T(8,128)(2,1)}, bf16[8192,512]{1,0:T(8,128)(2,1)}, u32[]{:S(2)}, u32[]{:S(2)}) collective-permute-start(bf16[8192,512]{1,0:T(8,128)(2,1)} %param.9), channel_id=1, source_target_pairs={{0,1},{1,0},{2,3},{3,2},{4,5},{5,4},{6,7},{7,6},{12,13},{13,12},{1... | collective-permute-start | bytes 25165832 | tf_op jit(solution)/shard_map/ppermute | solution.py:289
  0.5 20.4 %collective-permute-start.3 = (bf16[64,8192]{1,0:T(8,128)(2,1)}, bf16[64,8192]{1,0:T(8,128)(2,1)S(1)}, u32[]{:S(2)}, u32[]{:S(2)}) collective-permute-start(bf16[64,8192]{1,0:T(8,128)(2,1)} %bitcast.22), channel_id=1, source_target_pairs={{0,1},{1,0},{2,3},{3,2},{4,5},{5,4},{6,7},{7,6},{12,13},{13,12},{1... | collective-permute-start | bytes 3145736 | tf_op jit(solution)/shard_map/ppermute | solution.py:289
  2.6 13.7 %collective-permute-start = (bf16[24,8320]{1,0:T(8,128)(2,1)}, bf16[24,8320]{1,0:T(8,128)(2,1)S(1)}, u32[]{:S(2)}, u32[]{:S(2)}) collective-permute-start(bf16[24,8320]{1,0:T(8,128)(2,1)} %shard_map.73.refs_0_), channel_id=1, source_target_pairs={{0,4},{1,5},{2,6},{3,7},{4,12},{5,13},{6,14},{7,15},{12,8},{13,9},... | collective-permute-start | bytes 1198088 | tf_op jit(solution)/shard_map/ppermute | solution.py:289
  5.6 11.1 %collective-permute-start.2 = (bf16[24,8320]{1,0:T(8,128)(2,1)}, bf16[24,8320]{1,0:T(8,128)(2,1)S(1)}, u32[]{:S(2)}, u32[]{:S(2)}) collective-permute-start(bf16[24,8320]{1,0:T(8,128)(2,1)} %shard_map.73.refs_0_), channel_id=1, source_target_pairs={{0,2},{1,3},{2,0},{3,1},{4,6},{5,7},{6,4},{7,5},{12,14},{13,15},{1... | collective-permute-start | bytes 1198088 | tf_op jit(solution)/shard_map/ppermute | solution.py:289
  7.2 52.0 %collective-permute-start.13 = (bf16[1024,512]{1,0:T(8,128)(2,1)}, bf16[1024,512]{1,0:T(8,128)(2,1)S(1)}, u32[]{:S(2)}, u32[]{:S(2)}) collective-permute-start(bf16[1024,512]{1,0:T(8,128)(2,1)} %bitcast.27), channel_id=1, source_target_pairs={{0,1},{1,0},{2,3},{3,2},{4,5},{5,4},{6,7},{7,6},{12,13},{13,12},{1... | collective-permute-start | bytes 3145736 | tf_op jit(solution)/shard_map/ppermute | solution.py:289
  16.7 12.7 %collective-permute-start.1 = (bf16[24,8320]{1,0:T(8,128)(2,1)S(1)}, bf16[24,8320]{1,0:T(8,128)(2,1)S(1)}, u32[]{:S(2)}, u32[]{:S(2)}) collective-permute-start(bf16[24,8320]{1,0:T(8,128)(2,1)S(1)} %collective-permute-done.block_ref.refs_0_), channel_id=1, source_target_pairs={{0,4},{1,5},{2,6},{3,7},{4,12},{5,13},{6,14},{7,15},{12,8},{13,9},... | collective-permute-start | bytes 1198088 | tf_op jit(solution)/shard_map/ppermute | solution.py:289
  19.3 10.1 %collective-permute-start.5 = (bf16[24,8320]{1,0:T(8,128)(2,1)S(1)}, bf16[24,8320]{1,0:T(8,128)(2,1)S(1)}, u32[]{:S(2)}, u32[]{:S(2)}) collective-permute-start(bf16[24,8320]{1,0:T(8,128)(2,1)S(1)} %collective-permute-done.block_ref.refs_0_), channel_id=1, source_target_pairs={{0,2},{1,3},{2,0},{3,1},{4,6},{5,7},{6,4},{7,5},{12,14},{13,15},{1... | collective-permute-start | bytes 1198088 | tf_op jit(solution)/shard_map/ppermute | solution.py:289
  20.8 1.2 %copy-start = (bf16[1,8192,64]{1,2,0:T(8,128)(2,1)S(1)}, bf16[1,8192,64]{1,2,0:T(8,128)(2,1)}, u32[]{:S(2)}) copy-start(bf16[1,8192,64]{1,2,0:T(8,128)(2,1)} %param.10) | copy-start | bytes 3145732
  22.1 1.0 %copy-start.2 = (bf16[24,8320]{1,0:T(8,128)(2,1)S(1)}, bf16[24,8320]{1,0:T(8,128)(2,1)}, u32[]{:S(2)}) copy-start(bf16[24,8320]{1,0:T(8,128)(2,1)} %shard_map.73.refs_0_) | copy-start | bytes 1198084
  23.1 9.9 %slice-start = ((s8[8388608]{0:T(1024)(128)(4,1)}), s8[4194304]{0:T(1024)(128)(4,1)S(1)}, s32[]{:S(2)}) async-start(s8[8388608]{0:T(1024)(128)(4,1)} %bitcast.29), calls=%async_computation.1 | async-start | bytes 8388608
  24.0 8.1 %copy-start.1 = (bf16[1,8192,64]{1,2,0:T(8,128)(2,1)S(1)}, bf16[1,8192,64]{1,2,0:T(8,128)(2,1)}, u32[]{:S(2)}) copy-start(bf16[1,8192,64]{1,2,0:T(8,128)(2,1)} %param.10) | copy-start | bytes 3145732
  24.0 9.0 %slice-start.1 = ((s8[8388608]{0:T(1024)(128)(4,1)}), s8[4194304]{0:T(1024)(128)(4,1)S(1)}, s32[]{:S(2)}) async-start(s8[8388608]{0:T(1024)(128)(4,1)} %bitcast.29), calls=%async_computation.2 | async-start | bytes 8388608
  29.5 10.4 %collective-permute-start.4 = (bf16[24,8320]{1,0:T(8,128)(2,1)S(1)}, bf16[24,8320]{1,0:T(8,128)(2,1)S(1)}, u32[]{:S(2)}, u32[]{:S(2)}) collective-permute-start(bf16[24,8320]{1,0:T(8,128)(2,1)S(1)} %collective-permute-done.1.block_ref.refs_0_), channel_id=1, source_target_pairs={{0,4},{1,5},{2,6},{3,7},{4,12},{5,13},{6,14},{7,15},{12,8},{13,9},... | collective-permute-start | bytes 1198088 | tf_op jit(solution)/shard_map/ppermute | solution.py:289
  30.7 9.5 %collective-permute-start.7 = (bf16[24,8320]{1,0:T(8,128)(2,1)S(1)}, bf16[24,8320]{1,0:T(8,128)(2,1)S(1)}, u32[]{:S(2)}, u32[]{:S(2)}) collective-permute-start(bf16[24,8320]{1,0:T(8,128)(2,1)S(1)} %collective-permute-done.1.block_ref.refs_0_), channel_id=1, source_target_pairs={{0,2},{1,3},{2,0},{3,1},{4,6},{5,7},{6,4},{7,5},{12,14},{13,15},{1... | collective-permute-start | bytes 1198088 | tf_op jit(solution)/shard_map/ppermute | solution.py:289
  40.2 7.9 %collective-permute-start.8 = (bf16[24,8320]{1,0:T(8,128)(2,1)S(1)}, bf16[24,8320]{1,0:T(8,128)(2,1)S(1)}, u32[]{:S(2)}, u32[]{:S(2)}) collective-permute-start(bf16[24,8320]{1,0:T(8,128)(2,1)S(1)} %broadcast_select_fusion), channel_id=1, source_target_pairs={{0,2},{2,0},{4,6},{6,4},{12,14},{14,12},{8,10},{10,8},{1,5},{3,7},... | collective-permute-start | bytes 1198088 | tf_op jit(solution)/shard_map/ppermute | solution.py:324
  49.1 5.7 %collective-permute-start.10 = (bf16[96,128]{1,0:T(8,128)(2,1)S(1)}, bf16[96,128]{1,0:T(8,128)(2,1)S(1)}, u32[]{:S(2)}, u32[]{:S(2)}) collective-permute-start(bf16[96,128]{1,0:T(8,128)(2,1)S(1)} %get-tuple-element.66.refs_0_), channel_id=1, source_target_pairs={{0,12},{1,13},{2,14},{3,15},{4,8},{5,9},{6,10},{7,11},{12,0},{13,1... | collective-permute-start | bytes 73736 | tf_op jit(solution)/shard_map/ppermute | solution.py:289
  50.4 4.4 %collective-permute-start.11 = (bf16[96,128]{1,0:T(8,128)(2,1)S(1)}, bf16[96,128]{1,0:T(8,128)(2,1)S(1)}, u32[]{:S(2)}, u32[]{:S(2)}) collective-permute-start(bf16[96,128]{1,0:T(8,128)(2,1)S(1)} %get-tuple-element.66.refs_0_), channel_id=1, source_target_pairs={{0,8},{1,9},{2,10},{3,11},{4,0},{5,1},{6,2},{7,3},{12,4},{13,5},{1... | collective-permute-start | bytes 73736 | tf_op jit(solution)/shard_map/ppermute | solution.py:289
  51.2 4.7 %collective-permute-start.9 = (bf16[96,128]{1,0:T(8,128)(2,1)S(1)}, bf16[96,128]{1,0:T(8,128)(2,1)S(1)}, u32[]{:S(2)}, u32[]{:S(2)}) collective-permute-start(bf16[96,128]{1,0:T(8,128)(2,1)S(1)} %get-tuple-element.66.refs_0_), channel_id=1, source_target_pairs={{0,4},{1,5},{2,6},{3,7},{4,12},{5,13},{6,14},{7,15},{12,8},{13,9},... | collective-permute-start | bytes 73736 | tf_op jit(solution)/shard_map/ppermute | solution.py:289
  56.0 3.9 %copy-start.3 = (bf16[16,64,512]{2,1,0:T(8,128)(2,1)S(1)}, bf16[16,64,512]{2,1,0:T(8,128)(2,1)}, u32[]{:S(2)}) copy-start(bf16[16,64,512]{2,1,0:T(8,128)(2,1)} %param.11) | copy-start | bytes 3145732
  56.1 3.9 %collective-permute-start.12 = (bf16[96,128]{1,0:T(8,128)(2,1)S(1)}, bf16[96,128]{1,0:T(8,128)(2,1)S(1)}, u32[]{:S(2)}, u32[]{:S(2)}) collective-permute-start(bf16[96,128]{1,0:T(8,128)(2,1)S(1)} %shard_map.82.refs_0_), channel_id=1, source_target_pairs={{0,2},{1,3},{2,0},{3,1},{4,6},{5,7},{6,4},{7,5},{12,14},{13,15},{1... | collective-permute-start | bytes 73736 | tf_op jit(solution)/shard_map/ppermute | solution.py:289
